TPU v7x, 256 devices: a whole 4x4x8 slice. The times are simulated.
256 devices in a mesh: lat: 4 (over y_hi, core), lon: 32 (over z, x), tp: 2 (over y_lo).
Axes of the slice: x: 4, y: 4 (y_hi: 2, y_lo: 2; y = y_hi * 2 + y_lo), z: 8, core: 2. Of those that a mesh axis runs over, the one named last changes fastest.
Arguments:
- inputs: bfloat16 [8, 24, 384, 192], P(None, 'lat', 'lon'), may hold values from -6 to 6
- residual_mid: bfloat16 [8, 24, 384, 192], P(None, 'lat', 'lon'), may hold values from -6 to 6
- grad_out: bfloat16 [8, 24, 384, 192], P(None, 'lat', 'lon'), may hold values from -6 to 6
- mask_ids: int32 [8, 24, 384], P(None, 'lat', 'lon'), may hold values from 0 to 2
- key_valid: int32 [8, 24, 384], P(None, 'lat', 'lon'), may hold values 0 or 1
- bias_index: int32 [144, 144], replicated, may hold values from 0 to 3311
- pos_bias: float32 [4, 4, 6, 3312], P('lat', None, 'tp'), may hold values from -3 to 257
- norm1_gain: float32 [192], replicated, may hold values from 0.1 to 1.9
- qkv_weight: bfloat16 [3, 192, 192], P(None, None, 'tp'), may hold values from -0.4375 to 0.4375
- proj_weight: bfloat16 [192, 192], P('tp'), may hold values from -0.4375 to 0.4375
- norm2_gain: float32 [192], replicated, may hold values from 0.1 to 1.9
- fc1_weight: bfloat16 [192, 768], P(None, 'tp'), may hold values from -0.4375 to 0.4375
- fc2_weight: bfloat16 [768, 192], P('tp'), may hold values from -0.21875 to 0.21875
Outputs:
- grad_inputs: bfloat16 [8, 24, 384, 192], P(None, 'lat', 'lon')
- qkv_grad: float32 [3, 192, 192], P(None, None, 'tp')
- proj_grad: float32 [192, 192], P('tp')
- fc1_grad: float32 [192, 768], P(None, 'tp')
- fc2_grad: float32 [768, 192], P('tp')
- norm1_gain_grad: float32 [192], P('tp')
- norm2_gain_grad: float32 [192], P('tp')
- pos_bias_grad: float32 [4, 4, 6, 3312], P('lat', None, 'tp')
All inputs are finite; a program needn't handle non-finite values. No bound on the sum of `key_valid` on one device may be relied on, other than what follows from the above.
Results may differ from a plain program's by a relative error of at most 0.024.
Values may be sent and summed in bfloat16 or wider, within the bound.
No kernel may reach another device: no remote copies, remote signals or barrier semaphores. Data moves between devices by JAX's collectives and lax.ppermute only.
A program may use at most 128 MiB of HBM per device.

v0:
```python
import jax
import jax.numpy as jnp
from jax import lax
from jax.sharding import PartitionSpec as P

HD = 32
WZ = 2
WLAT = 6
WLON = 12
WIN = 144


EPSILON = 1e-05
EXCLUDED = -1e30


def shifted(value, axis, steps):
    count = lax.axis_size(axis)
    pairs = [(source, (source + steps) % count) for source in range(count)]
    return lax.ppermute(value, axis, pairs)


def layer_stats(field_rows):
    mean_value = jnp.mean(field_rows, axis=-1, keepdims=True)
    centred = field_rows - mean_value
    inverse = lax.rsqrt(jnp.mean(centred * centred, axis=-1, keepdims=True) + EPSILON)
    return (centred * inverse, inverse)


def norm_backward(grad_normed, gain, normed, inverse):
    scaled = grad_normed * gain
    first = jnp.mean(scaled, axis=-1, keepdims=True)
    second = jnp.mean(scaled * normed, axis=-1, keepdims=True)
    return (scaled - first - normed * second) * inverse


def gelu_pair(pre_act):
    normal_cdf = 0.5 * (1.0 + lax.erf(pre_act * 0.7071067811865476))
    normal_pdf = 0.3989422804014327 * jnp.exp(-0.5 * pre_act * pre_act)
    return (pre_act * normal_cdf, normal_cdf + pre_act * normal_pdf)


def grid_windows(field):
    levels, lat_cells, lon_cells, depth = field.shape
    parts = field.reshape(levels // WZ, WZ, lat_cells // WLAT, WLAT, lon_cells // WLON, WLON, depth)
    return parts.transpose(2, 0, 4, 1, 3, 5, 6).reshape(
        lat_cells // WLAT, levels // WZ, lon_cells // WLON, WIN, depth
    )


def window_grid(windows, levels, lat_cells, lon_cells):
    depth = windows.shape[-1]
    parts = windows.reshape(
        lat_cells // WLAT, levels // WZ, lon_cells // WLON, WZ, WLAT, WLON, depth
    )
    return parts.transpose(1, 3, 0, 4, 2, 5, 6).reshape(levels, lat_cells, lon_cells, depth)


def roll_cells(field, direction):
    half_lat = WLAT // 2
    half_lon = WLON // 2
    field = jnp.roll(field, direction * (WZ // 2), axis=-4)
    lat_piece = field[..., :half_lat, :, :] if direction < 0 else field[..., -half_lat:, :, :]
    lat_moved = shifted(lat_piece, "lat", direction)
    if direction < 0:
        field = jnp.concatenate([field[..., half_lat:, :, :], lat_moved], axis=-3)
    else:
        field = jnp.concatenate([lat_moved, field[..., :-half_lat, :, :]], axis=-3)
    lon_piece = field[..., :half_lon, :] if direction < 0 else field[..., -half_lon:, :]
    lon_moved = shifted(lon_piece, "lon", direction)
    if direction < 0:
        field = jnp.concatenate([field[..., half_lon:, :], lon_moved], axis=-2)
    else:
        field = jnp.concatenate([lon_moved, field[..., :-half_lon, :]], axis=-2)
    return field


def head_sum(rounded_part):
    return lax.psum(rounded_part.astype(jnp.float32).astype(jnp.bfloat16), "tp").astype(jnp.float32)


def attend_local(
    shifted_low, shifted_grad, mask_ids, key_valid, bias_index, pos_bias, qkv_weight, proj_weight
):
    levels, lat_cells, lon_cells, channels = shifted_low.shape
    local_width = qkv_weight.shape[2]
    local_heads = local_width // HD
    attn_scale = HD ** (-0.5)
    window_shape = (lat_cells // WLAT, levels // WZ, lon_cells // WLON, WIN)
    heads_shape = window_shape + (local_heads, HD)
    win_low = grid_windows(shifted_low).reshape(-1, channels)
    win_grad = grid_windows(shifted_grad).reshape(-1, channels)
    ids_win = grid_windows(mask_ids[..., None])[..., 0]
    valid_win = grid_windows(key_valid[..., None])[..., 0]
    query = (
        jnp.dot(win_low, qkv_weight[0], preferred_element_type=jnp.float32)
        .astype(jnp.bfloat16)
        .reshape(heads_shape)
    )
    keys = (
        jnp.dot(win_low, qkv_weight[1], preferred_element_type=jnp.float32)
        .astype(jnp.bfloat16)
        .reshape(heads_shape)
    )
    values = (
        jnp.dot(win_low, qkv_weight[2], preferred_element_type=jnp.float32)
        .astype(jnp.bfloat16)
        .reshape(heads_shape)
    )
    scores = (
        jnp.einsum("abcqhd,abckhd->abchqk", query, keys, preferred_element_type=jnp.float32)
        * attn_scale
    )
    table = jnp.take(pos_bias, bias_index, axis=3)
    scores = scores + table[:, :, None]
    allowed = (ids_win[..., :, None] == ids_win[..., None, :]) & (valid_win[..., None, :] > 0)
    allowed = allowed | jnp.eye(WIN, dtype=bool)
    scores = jnp.where(allowed[:, :, :, None], scores, EXCLUDED)
    top = jnp.max(scores, axis=-1, keepdims=True)
    expo = jnp.exp(scores - top)
    prob = expo / jnp.sum(expo, axis=-1, keepdims=True)
    prob_low = prob.astype(jnp.bfloat16)
    attended = jnp.einsum(
        "abchqk,abckhd->abcqhd", prob_low, values, preferred_element_type=jnp.float32
    )
    attended = attended.astype(jnp.bfloat16).reshape(-1, local_width)
    grad_proj = jnp.dot(attended.T, win_grad, preferred_element_type=jnp.float32)
    grad_att = (
        jnp.dot(win_grad, proj_weight.T, preferred_element_type=jnp.float32)
        .astype(jnp.bfloat16)
        .reshape(heads_shape)
    )
    grad_value = jnp.einsum(
        "abchqk,abcqhd->abckhd", prob_low, grad_att, preferred_element_type=jnp.float32
    )
    grad_value = grad_value.astype(jnp.bfloat16).reshape(-1, local_width)
    grad_prob = jnp.einsum(
        "abcqhd,abckhd->abchqk", grad_att, values, preferred_element_type=jnp.float32
    )
    grad_score = prob * (grad_prob - jnp.sum(grad_prob * prob, axis=-1, keepdims=True))
    table_terms = jnp.sum(grad_score, axis=2).reshape(-1, WIN * WIN)
    grad_table = jax.ops.segment_sum(
        table_terms.T, bias_index.reshape(-1), num_segments=pos_bias.shape[3]
    ).T.reshape(pos_bias.shape)
    score_low = (grad_score * attn_scale).astype(jnp.bfloat16)
    grad_query = jnp.einsum(
        "abchqk,abckhd->abcqhd", score_low, keys, preferred_element_type=jnp.float32
    )
    grad_query = grad_query.astype(jnp.bfloat16).reshape(-1, local_width)
    grad_key = jnp.einsum(
        "abchqk,abcqhd->abckhd", score_low, query, preferred_element_type=jnp.float32
    )
    grad_key = grad_key.astype(jnp.bfloat16).reshape(-1, local_width)
    grad_qkv = jnp.stack(
        [
            jnp.dot(win_low.T, grad_query, preferred_element_type=jnp.float32),
            jnp.dot(win_low.T, grad_key, preferred_element_type=jnp.float32),
            jnp.dot(win_low.T, grad_value, preferred_element_type=jnp.float32),
        ]
    )
    partial_value = jnp.dot(grad_query, qkv_weight[0].T, preferred_element_type=jnp.float32)
    partial_value = partial_value + jnp.dot(
        grad_key, qkv_weight[1].T, preferred_element_type=jnp.float32
    )
    partial_value = partial_value + jnp.dot(
        grad_value, qkv_weight[2].T, preferred_element_type=jnp.float32
    )
    part_grid = window_grid(
        partial_value.astype(jnp.bfloat16).reshape(window_shape + (channels,)),
        levels,
        lat_cells,
        lon_cells,
    )
    return (grad_qkv, grad_proj, grad_table, part_grid)


def local(
    inputs,
    residual_mid,
    grad_out,
    mask_ids,
    key_valid,
    bias_index,
    pos_bias,
    norm1_gain,
    qkv_weight,
    proj_weight,
    norm2_gain,
    fc1_weight,
    fc2_weight,
):
    levels, lat_cells, lon_cells, channels = inputs.shape
    cell_count = levels * lat_cells * lon_cells
    weight_scale = (cell_count * lax.axis_size("lat") * lax.axis_size("lon")) ** (-0.5)
    table_scale = (lon_cells * lax.axis_size("lon") // WLON) ** (-0.5)
    inputs_here, middle_here, upstream = (inputs, residual_mid, grad_out)
    flat_mid = middle_here.reshape(cell_count, channels).astype(jnp.float32)
    flat_upstream = upstream.reshape(cell_count, channels)
    normed2, inverse2 = layer_stats(flat_mid)
    lowered2 = (normed2 * norm2_gain).astype(jnp.bfloat16)
    pre_act = jnp.dot(lowered2, fc1_weight, preferred_element_type=jnp.float32)
    active, slopes = gelu_pair(pre_act)
    active = active.astype(jnp.bfloat16)
    grad_down = jnp.dot(active.T, flat_upstream, preferred_element_type=jnp.float32)
    grad_pre = (
        jnp.dot(flat_upstream, fc2_weight.T, preferred_element_type=jnp.float32) * slopes
    ).astype(jnp.bfloat16)
    grad_up = jnp.dot(lowered2.T, grad_pre, preferred_element_type=jnp.float32)
    part_normed2 = jnp.dot(grad_pre, fc1_weight.T, preferred_element_type=jnp.float32).astype(
        jnp.bfloat16
    )
    grad_normed2 = head_sum(part_normed2)
    grad_gain2 = jnp.sum(grad_normed2 * normed2, axis=0)
    grad_mid = flat_upstream.astype(jnp.float32) + norm_backward(
        grad_normed2, norm2_gain, normed2, inverse2
    )
    grad_mid = grad_mid.astype(jnp.bfloat16)
    grad_mid = grad_mid.reshape(levels, lat_cells, lon_cells, channels)
    normed1, inverse1 = layer_stats(inputs_here.reshape(cell_count, channels).astype(jnp.float32))
    lowered1 = (
        (normed1 * norm1_gain).astype(jnp.bfloat16).reshape(levels, lat_cells, lon_cells, channels)
    )
    shifted_low = roll_cells(lowered1, -1)
    shifted_grad = roll_cells(grad_mid, -1)
    grad_qkv, grad_proj, grad_table, part_grid = attend_local(
        shifted_low,
        shifted_grad,
        mask_ids,
        key_valid,
        bias_index,
        pos_bias,
        qkv_weight,
        proj_weight,
    )
    placed_part = roll_cells(part_grid, 1)
    flat_part = placed_part.reshape(cell_count, channels)
    flat_mid_grad = grad_mid.reshape(cell_count, channels)
    flat_grad = head_sum(flat_part)
    grad_gain1 = jnp.sum(flat_grad * normed1, axis=0)
    result = flat_mid_grad.astype(jnp.float32) + norm_backward(
        flat_grad, norm1_gain, normed1, inverse1
    )
    result = result.astype(jnp.bfloat16)
    result = result.reshape(levels, lat_cells, lon_cells, channels)
    share = channels // lax.axis_size("tp")
    start = lax.axis_index("tp") * share
    gain_one = lax.dynamic_slice_in_dim(grad_gain1, start, share)
    gain_two = lax.dynamic_slice_in_dim(grad_gain2, start, share)
    qkv_total, proj_total, up_total, down_total, one_total, two_total = lax.psum(
        (grad_qkv, grad_proj, grad_up, grad_down, gain_one, gain_two), ("lat", "lon")
    )
    table_total = lax.psum(grad_table.astype(jnp.bfloat16), "lon").astype(jnp.float32)
    return (
        result,
        qkv_total * weight_scale,
        proj_total * weight_scale,
        up_total * weight_scale,
        down_total * weight_scale,
        one_total * weight_scale,
        two_total * weight_scale,
        table_total * table_scale,
    )


def solution(mesh):
    return jax.shard_map(
        local,
        mesh=mesh,
        in_specs=(
            P(None, "lat", "lon", None),
            P(None, "lat", "lon", None),
            P(None, "lat", "lon", None),
            P(None, "lat", "lon"),
            P(None, "lat", "lon"),
            P(),
            P("lat", None, "tp", None),
            P(),
            P(None, None, "tp"),
            P("tp", None),
            P(),
            P(None, "tp"),
            P("tp", None),
        ),
        out_specs=(
            P(None, "lat", "lon", None),
            P(None, None, "tp"),
            P("tp", None),
            P(None, "tp"),
            P("tp", None),
            P("tp"),
            P("tp"),
            P("lat", None, "tp", None),
        ),
        check_vma=False,
    )
```

profile of v0, /device:TPU:24, one launch (start us, length us, event | category | flops | bytes accessed | tf_op | source)
XLA Modules:
  0.0 1772.4 jit_solution(2849738347952083265)
XLA Ops:
  7.2 1.1 copy.139
  8.3 1.2 convert_reduce_fusion
  15.3 1.0 convolution_convert_fusion
  16.5 1.1 fusion.63
  17.6 1.1 fusion.32
  20.2 8.3 collective-permute-start.1
  29.5 4.8 copy.153
  34.2 60.8 %gather_fusion = f32[20736,4,3]{2,1,0:T(4,128)} fusion(f32[4,3,3312]{1,0,2:T(4,128)} %bitcast.91, s32[21504]{0:T(1024)S(1)} %pad_clamp_fusion), kind=kCustom, calls=%fused_computation | custom fusion | bytes 2073600 | tf_op jit(solution)/shard_map/jit(_take)/gather | solution.py:114
  95.0 50.1 %copy.155 = f32[144,144,4,3]{0,1,3,2:T(8,128)} copy(f32[144,144,4,3]{3,2,1,0:T(4,128)} %bitcast.90) | data formatting | bytes 1990656 | tf_op jit(solution)/shard_map/jit(_take)/gather | solution.py:114
  146.1 1.2 fusion.25
  147.3 1.1 fusion.23
  149.6 2.1 fusion.1
  151.7 1.7 fusion.68
  153.4 1.1 copy.156
  155.3 1.7 constant_dynamic-update-slice_fusion.3
  157.8 1.7 fusion.66
  161.0 2.4 collective-permute-done.2
  163.4 1.8 fusion.37
  166.2 2.2 fusion.7
  168.3 1.2 copy.175
  170.4 1.2 collective-permute-done.3
  171.6 1.9 pad_maximum_fusion.2
  173.5 1.1 reshape_reshape_transpose_reshape.7
  174.7 1.1 convolution_convert_fusion.6
  176.6 1.6 multiply_reduce_fusion
  178.8 1.1 fusion.5
  179.9 3.3 fusion.6
  184.5 1.1 reshape.275
  185.6 1.1 copy.168
  190.8 2.0 copy.176
  194.5 1.8 fusion.65
  196.3 1.5 collective-permute-start.4
  197.9 2.2 reshape.280
  200.1 6.8 copy.177
  206.9 112.8 %scatter_custom_fusion = f32[3312,12]{1,0:T(8,128)S(1)} fusion(s32[20736]{0:T(1024)} %reshape.295, f32[20736,12]{1,0:T(8,128)} %copy.177, f32[]{:T(128)} %constant.19.clone.1), kind=kCustom, calls=%fused_computation.39 | custom fusion | flops 248832 | bytes 159488 | tf_op jit(solution)/shard_map/scatter-add | solution.py:142
  321.3 1.1 fusion.36
  323.9 8.4 collective-permute-done.5
  332.3 1.1 fusion.35
  335.4 125.1 %all-reduce.11.cloned.1.call-done = bf16[1,4,3,3312]{3,2,1,0:T(4,128)(2,1)} async-done(((bf16[1,4,3,3312]{3,2,1,0:T(4,128)(2,1)}), bf16[1,4,3,3312]{3,2,1,0:T(4,128)(2,1)}) %all-reduce.11.cloned.1.call-update) | async-done | bytes 79504 | tf_op jit(solution)/shard_map/psum | solution.py:252
  462.1 32.8 %all-reduce.9.cloned.1.call-done = bf16[576,192]{0,1:T(8,128)(2,1)} async-done(((bf16[576,192]{0,1:T(8,128)(2,1)}), bf16[576,192]{0,1:T(8,128)(2,1)}) %all-reduce.9.cloned.1.call-update) | async-done | bytes 221200 | tf_op jit(solution)/shard_map/psum | solution.py:79
  495.0 1.2 fusion.31
  496.2 1.2 fusion.29
  498.5 328.8 %all-reduce = (f32[96]{0:T(128)S(1)}, f32[96]{0:T(128)S(1)}) all-reduce(f32[96]{0:T(128)S(1)} %dynamic_slice.6, f32[96]{0:T(128)S(1)} %dynamic_slice.7), channel_id=1, replica_groups=mesh['lat'=4,'lon'=32,'tp'=2] {'lat','lon'}, use_global_device_ids=true, to_apply=%region_18.19 | all-reduce | flops 192 | bytes 1536 | tf_op jit(solution)/shard_map/psum | solution.py:249
  828.4 930.8 %all-reduce.13.cloned.1.call-done = (f32[3,192,96]{2,1,0:T(8,128)}, f32[96,192]{1,0:T(8,128)}, f32[192,384]{1,0:T(8,128)}, f32[384,192]{0,1:T(8,128)}) async-done(((f32[3,192,96]{2,1,0:T(8,128)}, f32[96,192]{1,0:T(8,128)}, f32[192,384]{1,0:T(8,128)}, f32[384,192]{0,1:T(8,128)}), (f32[3,192,96]{2,1,0:T(8,128)}, f32[96,192]{1,0:T(8,128)}, f32[192,384]{1,0:T(8,128)}, ...) | async-done | bytes 884752 | tf_op jit(solution)/shard_map/psum | solution.py:249
  1759.2 1.7 broadcast_multiply_fusion.2
  1760.9 1.5 broadcast_multiply_fusion.3
  1762.4 1.7 broadcast_multiply_fusion.1
  1764.1 1.7 broadcast_multiply_fusion
  (191 shorter events, 32.3 us)
Async XLA Ops:
  7.2 7.3 copy-start
  7.2 138.9 %all-reduce.7.cloned.1.call-start = ((), (), s32[]{:S(2)}) async-start(), calls=%async_computation | async-start | bytes 491520 | tf_op jit(solution)/shard_map/psum | solution.py:79
  8.3 1.7 copy-start.6
  8.3 2.4 copy-start.29
  10.8 1.9 copy-start.7
  11.2 2.1 copy-start.22
  12.1 8.0 collective-permute-start
  13.3 1.1 copy-start.27
  13.6 1.3 copy-start.31
  15.3 3.4 copy-start.13
  16.4 2.5 copy-start.25
  16.4 2.6 copy-start.26
  16.4 444.0 %all-reduce.11.cloned.1.call-start = ((), (), s32[]{:S(2)}) async-start(), calls=%async_computation.2 | async-start | bytes 212992 | tf_op jit(solution)/shard_map/psum | solution.py:252
  17.6 11.9 copy-start.24
  20.2 125.1 %collective-permute-start.1 = (bf16[8,6,6,192]{3,2,1,0:T(8,128)(2,1)S(1)}, bf16[8,6,6,192]{3,2,1,0:T(8,128)(2,1)S(1)}, u32[]{:S(2)}, u32[]{:S(2)}) collective-permute-start(bf16[8,6,6,192]{3,2,1,0:T(8,128)(2,1)S(1)} %get-tuple-element.59), channel_id=1, source_target_pairs={{0,62},{2,0},{4,2},{6,4},{8,6},{10,8},{12,10},{14,12},{16,14},{18,... | collective-permute-start | bytes 331784 | tf_op jit(solution)/shard_map/ppermute | solution.py:20
  95.0 50.5 %copy-start.17 = (bf16[3,192,96]{2,1,0:T(8,128)(2,1)S(1)}, bf16[3,192,96]{2,1,0:T(8,128)(2,1)}, u32[]{:S(2)}) copy-start(bf16[3,192,96]{2,1,0:T(8,128)(2,1)} %param.21) | copy-start | bytes 331780
  145.1 1.0 copy-start.28
  145.8 3.8 copy-start.18
  148.4 3.2 copy-start.10
  151.7 14.5 copy-start.2
  153.4 3.6 slice-start
  159.5 3.9 collective-permute-start.2
  165.2 6.4 collective-permute-start.3
  168.3 8.3 copy-start.4
  174.7 3.6 copy-start.8
  176.6 1.7 copy-start.5
  178.8 1.1 copy-start.23
  179.9 3.8 copy-start.16
  183.4 2.2 copy-start.14
  192.8 5.0 copy-start.3
  196.3 124.9 %collective-permute-start.4 = (bf16[8,3,12,192]{3,2,1,0:T(8,128)(2,1)}, bf16[8,3,12,192]{3,2,1,0:T(8,128)(2,1)}, u32[]{:S(2)}, u32[]{:S(2)}) collective-permute-start(bf16[8,3,12,192]{3,2,1,0:T(8,128)(2,1)} %get-tuple-element.52), channel_id=1, source_target_pairs={{0,64},{64,128},{128,192},{192,0},{1,65},{65,129},{129,193},{193,1... | collective-permute-start | bytes 331784 | tf_op jit(solution)/shard_map/ppermute | solution.py:20
  319.7 1.3 copy-start.15
  319.8 1.5 copy-start.12
  319.8 3.4 copy-start.20
  319.9 3.4 copy-start.21
  320.9 174.0 %all-reduce.9.cloned.1.call-start = ((), (), s32[]{:S(2)}) async-start(), calls=%async_computation.1 | async-start | bytes 491520 | tf_op jit(solution)/shard_map/psum | solution.py:79
  321.3 13.2 copy-start.9
  321.3 13.2 copy-start.19
  322.4 9.9 collective-permute-start.5
  333.4 161.5 %copy-start.30 = (f32[192]{0:T(256)S(1)}, f32[192]{0:T(256)}, u32[]{:S(2)}) copy-start(f32[192]{0:T(256)} %param.20) | copy-start | bytes 2308
  333.6 162.6 %copy-start.11 = (bf16[576,192]{0,1:T(8,128)(2,1)S(1)}, bf16[576,192]{0,1:T(8,128)(2,1)}, u32[]{:S(2)}) copy-start(bf16[576,192]{0,1:T(8,128)(2,1)} %copy-done.10) | copy-start | bytes 663556
  334.5 1424.7 %all-reduce.13.cloned.1.call-start = ((), (), s32[]{:S(2)}) async-start(), calls=%async_computation.3 | async-start | bytes 1966080 | tf_op jit(solution)/shard_map/psum | solution.py:249
  497.3 1268.5 %copy-start.1 = (bf16[192,384]{1,0:T(8,128)(2,1)S(1)}, bf16[192,384]{1,0:T(8,128)(2,1)}, u32[]{:S(2)}) copy-start(bf16[192,384]{1,0:T(8,128)(2,1)} %param.24) | copy-start | bytes 442372
Sparse Core Ops, SparseCore 0:
  16.5 36.5 all-reduce.6
  321.1 139.3 all-reduce.10
  463.3 31.6 all-reduce.8
  498.5 1260.6 all-reduce.12
where the time goes:
time: 1770 us
  waiting for transfers between devices  1100 us (62%)
  blocking collectives  329 us (19%)
  local copies, waits for them, and re-layouts  156 us (9%)
  other arithmetic  138 us (8%)
  matrix products  21.4 us (1%)
    psum x1, waiting for transfers between devices, local(): lax.psum((grad_qkv, grad_proj, grad_up, grad_down, gain_one, gain_two), (...  931 us
    psum x1, blocking collectives, local(): lax.psum((grad_qkv, grad_proj, grad_up, grad_down, gain_one, gain_two), (...  329 us
    psum x1, waiting for transfers between devices, local(): lax.psum(grad_table.astype(jnp.bfloat16), 'lon').astype(jnp.float32)  125 us
    scatter-add x1, other arithmetic, attend_local(): jax.ops.segment_sum(table_terms.T, bias_index.reshape(-1), num_segments=p...  113 us
    gather x2, local copies, waits for them, and re-layouts, attend_local(): table = jnp.take(pos_bias, bias_index, axis=3)  111 us
  transfers between devices with their start and end apart: 10, of which 6 were waited for; matrix products, arithmetic and copies ran while one was open for 15% of the time, Pallas kernels for 0%

commit v1 on v0

v1 whole, which is shorter than its diff:
```python
import functools

import jax
import jax.numpy as jnp
import numpy as np
from jax import lax
from jax.experimental import pallas as pl
from jax.experimental.pallas import tpu as pltpu
from jax.sharding import PartitionSpec as P

HD = 32
EPSILON = 1e-05
EXCLUDED = -1e30
BF = jnp.bfloat16
F32 = jnp.float32
I32 = jnp.int32
VM = pltpu.CompilerParams(vmem_limit_bytes=48 * 1024 * 1024)


def shape(dims, kind):
    return jax.ShapeDtypeStruct(dims, kind)


def dot_nn(a, b):
    return lax.dot_general(a, b, (((1,), (0,)), ((), ())), preferred_element_type=F32)


def dot_nt(a, b):
    return lax.dot_general(a, b, (((1,), (1,)), ((), ())), preferred_element_type=F32)


def dot_tn(a, b):
    return lax.dot_general(a, b, (((0,), (0,)), ((), ())), preferred_element_type=F32)


def layer_stats(rows):
    mean = jnp.mean(rows, axis=-1, keepdims=True)
    centred = rows - mean
    inverse = lax.rsqrt(jnp.mean(centred * centred, axis=-1, keepdims=True) + EPSILON)
    return centred * inverse, inverse


def norm_backward(grad_normed, gain, normed, inverse):
    scaled = grad_normed * gain
    first = jnp.mean(scaled, axis=-1, keepdims=True)
    second = jnp.mean(scaled * normed, axis=-1, keepdims=True)
    return (scaled - first - normed * second) * inverse


def gelu_pair(pre):
    cdf = 0.5 * (1.0 + lax.erf(pre * 0.7071067811865476))
    pdf = 0.3989422804014327 * jnp.exp(-0.5 * pre * pre)
    return pre * cdf, cdf + pre * pdf


def to_quarters(field_ref, scratch):
    for level in range(8):
        for lat in range(6):
            rows = field_ref[((level + 1) % 8) * 6 + lat].astype(F32)
            quarter = (lat // 3) * 2
            start = quarter * 144 + level * 18 + (lat % 3) * 6
            scratch[start : start + 6, :] = rows[0:6]
            scratch[start + 144 : start + 150, :] = rows[6:12]


def to_windows(parts, scratch):
    for s in range(4):
        rows = parts[s][...].astype(F32)
        for w in range(4):
            scratch[w * 144 + s * 36 : w * 144 + s * 36 + 36, :] = rows[w * 36 : w * 36 + 36]


def split_kernel(field_ref, o0, o1, o2, o3, scratch):
    to_quarters(field_ref, scratch)
    for q, out in enumerate((o0, o1, o2, o3)):
        out[...] = scratch[q * 144 : q * 144 + 144, :].astype(BF)


def split(field):
    return pl.pallas_call(
        split_kernel,
        out_shape=tuple(shape((144, 192), BF) for _ in range(4)),
        scratch_shapes=[pltpu.VMEM((576, 192), F32)],
        compiler_params=VM,
        name="split",
    )(field)


def mlp_kernel(mid_ref, up_ref, gain_ref, fc1_ref, fc2_ref, part_ref, midq_ref, upq_ref, down_ref, upg_ref, mid_s, up_s):
    to_quarters(mid_ref, mid_s)
    to_quarters(up_ref, up_s)
    mid = mid_s[...]
    up = up_s[...].astype(BF)
    midq_ref[...] = mid.astype(BF)
    upq_ref[...] = up
    normed, _ = layer_stats(mid)
    lowered = (normed * gain_ref[...]).astype(BF)
    pre = dot_nn(lowered, fc1_ref[...])
    active, slopes = gelu_pair(pre)
    grad_pre = (dot_nt(up, fc2_ref[...]) * slopes).astype(BF)
    part_ref[...] = dot_nt(grad_pre, fc1_ref[...]).astype(BF)
    down_ref[...] = dot_tn(active.astype(BF), up).astype(BF)
    upg_ref[...] = dot_tn(lowered, grad_pre).astype(BF)


def mlp(mid, up, gain, fc1, fc2):
    return pl.pallas_call(
        mlp_kernel,
        out_shape=(
            shape((576, 192), BF),
            shape((576, 192), BF),
            shape((576, 192), BF),
            shape((384, 192), BF),
            shape((192, 384), BF),
        ),
        scratch_shapes=[pltpu.VMEM((576, 192), F32)] * 2,
        compiler_params=VM,
        name="mlp",
    )(mid, up, gain, fc1, fc2)


def middle_kernel(mid_ref, up_ref, own_ref, other_ref, gain_ref, o0, o1, o2, o3, gain_out):
    normed, inverse = layer_stats(mid_ref[...].astype(F32))
    grad = own_ref[...].astype(F32) + other_ref[...].astype(F32)
    gain_out[...] = jnp.sum(grad * normed, axis=0, keepdims=True)
    out = up_ref[...].astype(F32) + norm_backward(grad, gain_ref[...], normed, inverse)
    for q, o in enumerate((o0, o1, o2, o3)):
        o[...] = out[q * 144 : q * 144 + 144].astype(BF)


def middle(mid, up, own, other, gain):
    return pl.pallas_call(
        middle_kernel,
        out_shape=tuple(shape((144, 192), BF) for _ in range(4)) + (shape((1, 192), F32),),
        compiler_params=VM,
        name="middle",
    )(mid, up, own, other, gain)


def window_order():
    canon = np.arange(144).reshape(2, 2, 3, 2, 6).transpose(1, 3, 0, 2, 4).reshape(-1)
    order = np.zeros((144, 144), np.float32)
    order[np.arange(144), canon] = 1.0
    return order


def pack_tail(tail):
    spread = (lax.broadcasted_iota(I32, (16, 128), 1) & 15) == lax.broadcasted_iota(I32, (16, 128), 0)
    wide = dot_nn(tail, spread.astype(F32).astype(BF))
    here = (lax.broadcasted_iota(I32, (144, 128), 1) >> 4) == (lax.broadcasted_iota(I32, (144, 128), 0) & 7)
    wide = jnp.where(here, wide, 0.0).astype(BF)
    rows = (lax.broadcasted_iota(I32, (24, 144), 1) >> 3) == lax.broadcasted_iota(I32, (24, 144), 0)
    return dot_nn(rows.astype(F32).astype(BF), wide)


def gather_kernel(index_ref, order_ref, bias_ref, main_ref, tail_ref, lo_ref, hi_ref, table, tail_s):
    index = index_ref[...]
    order = order_ref[...]
    pieces = []
    for part in (index & 127, index >> 7):
        moved = dot_nt(dot_nn(order, part.astype(F32).astype(BF)).astype(BF), order)
        pieces.append((moved[:, 0:128].astype(I32), pack_tail(moved[:, 128:144].astype(BF)).astype(I32)))
    lo_ref[0:144, :] = pieces[0][0]
    lo_ref[144:168, :] = pieces[0][1]
    hi_ref[0:144, :] = pieces[1][0]
    hi_ref[144:168, :] = pieces[1][1]
    for r in range(12):
        for c in range(26):
            wide = min(128, 3312 - c * 128)
            table[r, c : c + 1, 0:wide] = bias_ref[r // 3, r % 3 : r % 3 + 1, c * 128 : c * 128 + wide]

    def look_up(r, rows, count):
        lo, hi = lo_ref[rows, :], hi_ref[rows, :]
        acc = jnp.zeros((count, 128), F32)
        for c in range(26):
            entry = jnp.broadcast_to(table[r, c : c + 1, :], (count, 128))
            got = jnp.take_along_axis(entry, lo, axis=1, mode="promise_in_bounds")
            acc = jnp.where(hi == c, got, acc)
        return acc

    def one(r, _):
        main_ref[r, 0:72, :] = look_up(r, slice(0, 72), 72)
        main_ref[r, 72:144, :] = look_up(r, slice(72, 144), 72)
        acc = look_up(r, slice(144, 168), 24)
        for s in range(8):
            moved = pltpu.roll(acc, 128 - 16 * s, 1) if s else acc
            tail_ref[r, pl.ds(s, 18, stride=8), :] = moved[0:18]
        return 0

    lax.fori_loop(0, 12, one, 0)


def gather(index, bias):
    return pl.pallas_call(
        gather_kernel,
        out_shape=(
            shape((12, 144, 128), F32),
            shape((12, 144, 128), F32),
            shape((168, 128), I32),
            shape((168, 128), I32),
        ),
        scratch_shapes=[pltpu.VMEM((12, 26, 128), F32), pltpu.VMEM((8, 128), F32)],
        compiler_params=VM,
        name="gather",
    )(index, jnp.asarray(window_order(), BF), bias)


def forward_kernel(x0, x1, x2, x3, gain_ref, qkv_ref, main_ref, tail_ref, code_ref,
                   low_ref, q_ref, k_ref, v_ref, prob_ref, att_ref, scratch):
    to_windows((x0, x1, x2, x3), scratch)
    normed, _ = layer_stats(scratch[...])
    low = (normed * gain_ref[...]).astype(BF)
    low_ref[...] = low
    for j, out in enumerate((q_ref, k_ref, v_ref)):
        out[...] = dot_nn(low, qkv_ref[j]).astype(BF)
    eye = lax.broadcasted_iota(I32, (144, 144), 0) == lax.broadcasted_iota(I32, (144, 144), 1)

    def window(w, _):
        rows = pl.ds(pl.multiple_of(w * 144, 16), 144)
        code = code_ref[w]
        label = code >> 1
        column = jnp.sum(jnp.where(eye, label, 0), axis=1, keepdims=True)
        allowed = eye | ((column == label) & ((code & 1) > 0))
        query, key, value = q_ref[rows, :], k_ref[rows, :], v_ref[rows, :]
        heads = []
        for h in range(3):
            cols = slice(h * HD, h * HD + HD)
            bias = jnp.concatenate([main_ref[w * 3 + h], tail_ref[w * 3 + h][:, 0:16]], axis=1)
            scores = dot_nt(query[:, cols], key[:, cols]) * (HD ** -0.5) + bias
            scores = jnp.where(allowed, scores, EXCLUDED)
            expo = jnp.exp(scores - jnp.max(scores, axis=-1, keepdims=True))
            prob = expo * (1.0 / jnp.sum(expo, axis=-1, keepdims=True))
            prob_ref[w * 3 + h] = prob
            heads.append(dot_nn(prob.astype(BF), value[:, cols]))
        att_ref[rows, :] = jnp.concatenate(heads, axis=1).astype(BF)
        return 0

    lax.fori_loop(0, 4, window, 0)


def forward(x, gain, qkv, main, tail, code):
    return pl.pallas_call(
        forward_kernel,
        out_shape=(
            shape((576, 192), BF),
            shape((576, 96), BF),
            shape((576, 96), BF),
            shape((576, 96), BF),
            shape((12, 144, 144), F32),
            shape((576, 96), BF),
        ),
        scratch_shapes=[pltpu.VMEM((576, 192), F32)],
        compiler_params=VM,
        name="forward",
    )(*x, gain, qkv, main, tail, code)


def backward_kernel(g0, g1, g2, g3, proj_ref, qkv_ref, low_ref, q_ref, k_ref, v_ref, prob_ref, att_ref,
                    part_ref, score_ref, gqkv_ref, gproj_ref, scratch, gatt, gcols):
    to_windows((g0, g1, g2, g3), scratch)
    grad = scratch[...].astype(BF)
    gproj_ref[...] = dot_tn(att_ref[...], grad).astype(BF)
    gatt[...] = dot_nt(grad, proj_ref[...]).astype(BF)

    def window(w, _):
        rows = pl.ds(pl.multiple_of(w * 144, 16), 144)
        query, key, value, above = q_ref[rows, :], k_ref[rows, :], v_ref[rows, :], gatt[rows, :]
        queries, keys, values = [], [], []
        for h in range(3):
            cols = slice(h * HD, h * HD + HD)
            prob = prob_ref[w * 3 + h]
            values.append(dot_tn(prob.astype(BF), above[:, cols]))
            grad_prob = dot_nt(above[:, cols], value[:, cols])
            score = prob * (grad_prob - jnp.sum(grad_prob * prob, axis=-1, keepdims=True))
            score_ref[w * 3 + h, 0:144, :] = score[:, 0:128]
            score_ref[w * 3 + h, 144:168, :] = pack_tail(score[:, 128:144].astype(BF))
            low_score = (score * (HD ** -0.5)).astype(BF)
            queries.append(dot_nn(low_score, key[:, cols]))
            keys.append(dot_tn(low_score, query[:, cols]))
        gcols[0, rows, :] = jnp.concatenate(queries, axis=1).astype(BF)
        gcols[1, rows, :] = jnp.concatenate(keys, axis=1).astype(BF)
        gcols[2, rows, :] = jnp.concatenate(values, axis=1).astype(BF)
        return 0

    lax.fori_loop(0, 4, window, 0)
    low = low_ref[...]
    total = None
    for j in range(3):
        cols = gcols[j]
        gqkv_ref[j] = dot_tn(low, cols).astype(BF)
        term = dot_nt(cols, qkv_ref[j])
        total = term if total is None else total + term
    scratch[...] = total
    for s in range(4):
        pieces = [scratch[w * 144 + s * 36 : w * 144 + s * 36 + 36, :] for w in range(4)]
        part_ref[s * 144 : s * 144 + 144, :] = jnp.concatenate(pieces, axis=0).astype(BF)


def backward(g, proj, qkv, low, q, k, v, prob, att):
    return pl.pallas_call(
        backward_kernel,
        out_shape=(
            shape((576, 192), BF),
            shape((12, 168, 128), F32),
            shape((3, 192, 96), BF),
            shape((96, 192), BF),
        ),
        scratch_shapes=[pltpu.VMEM((576, 192), F32), pltpu.VMEM((576, 96), BF), pltpu.VMEM((3, 576, 96), BF)],
        compiler_params=VM,
        name="backward",
    )(*g, proj, qkv, low, q, k, v, prob, att)


def scatter_kernel(score_ref, lo_ref, hi_ref, out_ref):
    out_ref[...] = jnp.zeros((192, 256), F32)
    place = lax.broadcasted_iota(I32, (16, 128), 0)
    entry = lax.broadcasted_iota(I32, (256, 128), 0)

    def step(i, _):
        left, right = [], []
        for j in range(18):
            row = pl.ds(i * 18 + j, 1)
            high, low = hi_ref[row, :], lo_ref[row, :]
            here = place == (high >> 1)
            right.append((entry == (low + (high & 1) * 128)).astype(F32).astype(BF))
            left.append(
                jnp.concatenate([jnp.where(here, score_ref[r, row, :], 0.0).astype(BF) for r in range(12)], axis=0)
            )
        out_ref[...] += dot_nt(jnp.concatenate(left, axis=1), jnp.concatenate(right, axis=1))
        return 0

    lax.fori_loop(0, 9, step, 0)


def scatter(score, lo, hi):
    return pl.pallas_call(
        scatter_kernel, out_shape=shape((192, 256), F32), compiler_params=VM, name="scatter"
    )(score, lo, hi)


def meet_kernel(own_ref, other_ref, x0, x1, x2, x3, o0, o1, o2, o3, gain_out):
    gain = jnp.zeros((1, 192), F32)
    for s, (x, o) in enumerate(zip((x0, x1, x2, x3), (o0, o1, o2, o3))):
        rows = slice(s * 144, s * 144 + 144)
        grad = own_ref[rows, :].astype(F32) + other_ref[rows, :].astype(F32)
        normed, _ = layer_stats(x[...].astype(F32))
        gain = gain + jnp.sum(grad * normed, axis=0, keepdims=True)
        o[...] = grad.astype(BF)
    gain_out[...] = gain


def meet(own, other, x):
    return pl.pallas_call(
        meet_kernel,
        out_shape=tuple(shape((144, 192), BF) for _ in range(4)) + (shape((1, 192), F32),),
        compiler_params=VM,
        name="meet",
    )(own, other, *x)


def finish_kernel(x0, x1, x2, x3, m0, m1, m2, m3, g0, g1, g2, g3, gain_ref, out_ref, scratch):
    for q, (x, m, g) in enumerate(zip((x0, x1, x2, x3), (m0, m1, m2, m3), (g0, g1, g2, g3))):
        normed, inverse = layer_stats(x[...].astype(F32))
        rows = m[...].astype(F32) + norm_backward(g[...].astype(F32), gain_ref[...], normed, inverse)
        for level in range(8):
            for lat in range(3):
                target = (((level + 1) % 8) * 6 + (q // 2) * 3 + lat) * 16 + (q % 2) * 6
                start = level * 18 + lat * 6
                scratch[target : target + 6, :] = rows[start : start + 6]
    for g in range(48):
        out_ref[g] = scratch[g * 16 : g * 16 + 12, :].astype(BF)


def finish(x, m, g, gain):
    return pl.pallas_call(
        finish_kernel,
        out_shape=shape((48, 12, 192), BF),
        scratch_shapes=[pltpu.VMEM((768, 192), F32)],
        compiler_params=VM,
        name="finish",
    )(*x, *m, *g, gain)


def pack_kernel(down_ref, upg_ref, gqkv_ref, gproj_ref, table_ref, one_ref, two_ref, out_ref):
    for j in range(3):
        out_ref[j * 192 : j * 192 + 192, :] = upg_ref[:, j * 128 : j * 128 + 128]
    out_ref[576:960, :] = down_ref[:, 0:128]
    out_ref[960:1152, :] = jnp.concatenate([down_ref[0:192, 128:192], down_ref[192:384, 128:192]], axis=1)
    out_ref[1152:1248, :] = gproj_ref[:, 0:128]
    out_ref[1248:1296, :] = jnp.concatenate([gproj_ref[0:48, 128:192], gproj_ref[48:96, 128:192]], axis=1)
    a, b, c = gqkv_ref[0], gqkv_ref[1], gqkv_ref[2]
    out_ref[1296:1488, :] = jnp.concatenate([a, c[:, 0:32]], axis=1)
    out_ref[1488:1680, :] = jnp.concatenate([b, c[:, 32:64]], axis=1)
    out_ref[1680:1728, :] = jnp.concatenate([c[i * 48 : i * 48 + 48, 64:96] for i in range(4)], axis=1)
    rows = []
    for r in range(12):
        pair = table_ref[r * 16 : r * 16 + 13, :]
        rows += [pair[:, 0:128], pair[:, 128:256]]
    none = jnp.zeros((1, 64), F32)
    rows += [one_ref[:, 0:128], jnp.concatenate([one_ref[:, 128:192], none], axis=1)]
    rows += [two_ref[:, 0:128], jnp.concatenate([two_ref[:, 128:192], none], axis=1)]
    rows += [jnp.zeros((4, 128), F32)]
    out_ref[1728:2048, :] = jnp.concatenate(rows, axis=0).astype(BF)


def pack(down, upg, gqkv, gproj, table, one, two):
    return pl.pallas_call(
        pack_kernel, out_shape=shape((2048, 128), BF), compiler_params=VM, name="pack"
    )(down, upg, gqkv, gproj, table, one, two)


def add_kernel(place_ref, got_ref, out_ref):
    bands = [jnp.sum(got_ref[a * 32 : a * 32 + 32].astype(F32), axis=0) for a in range(4)]
    total = bands[0] + bands[1] + bands[2] + bands[3]
    row = place_ref[0] * 16 + lax.broadcasted_iota(I32, (16, 128), 0)
    table = (row >= 1728) & (row < 2040)
    for a in range(4):
        out_ref[a * 32 : a * 32 + 32] = jnp.broadcast_to(jnp.where(table, bands[a], total).astype(BF)[None], (32, 16, 128))


def add(place, got):
    return pl.pallas_call(
        add_kernel,
        out_shape=shape((128, 16, 128), BF),
        in_specs=[pl.BlockSpec(memory_space=pltpu.SMEM), pl.BlockSpec(memory_space=pltpu.VMEM)],
        compiler_params=VM,
        name="add",
    )(place, got)


def unpack_kernel(weight_scale, table_scale, in_ref, qkv_ref, proj_ref, upg_ref, down_ref, gain_ref, table_ref):
    def rows(start, stop):
        return in_ref[start:stop, :].astype(F32) * weight_scale

    for j in range(3):
        upg_ref[:, j * 128 : j * 128 + 128] = rows(j * 192, j * 192 + 192)
    down_ref[:, 0:128] = rows(576, 960)
    tail = rows(960, 1152)
    down_ref[0:192, 128:192] = tail[:, 0:64]
    down_ref[192:384, 128:192] = tail[:, 64:128]
    proj_ref[:, 0:128] = rows(1152, 1248)
    tail = rows(1248, 1296)
    proj_ref[0:48, 128:192] = tail[:, 0:64]
    proj_ref[48:96, 128:192] = tail[:, 64:128]
    first, second, third = rows(1296, 1488), rows(1488, 1680), rows(1680, 1728)
    qkv_ref[0] = first[:, 0:96]
    qkv_ref[1] = second[:, 0:96]
    qkv_ref[2, :, 0:32] = first[:, 96:128]
    qkv_ref[2, :, 32:64] = second[:, 96:128]
    for i in range(4):
        qkv_ref[2, i * 48 : i * 48 + 48, 64:96] = third[:, i * 32 : i * 32 + 32]
    table = in_ref[1728:2048, :].astype(F32)
    for r in range(12):
        for half in range(2):
            piece = table[r * 26 + half * 13 : r * 26 + half * 13 + 13] * table_scale
            for a in range(13):
                start = a * 256 + half * 128
                wide = min(128, 3312 - start)
                table_ref[r // 3, r % 3 : r % 3 + 1, start : start + wide] = piece[a : a + 1, 0:wide]
    gain_ref[...] = table[312:320] * weight_scale


def unpack(weight_scale, table_scale, got):
    return pl.pallas_call(
        functools.partial(unpack_kernel, weight_scale, table_scale),
        out_shape=(
            shape((3, 192, 96), F32),
            shape((96, 192), F32),
            shape((192, 384), F32),
            shape((384, 192), F32),
            shape((8, 128), F32),
            shape((4, 3, 3312), F32),
        ),
        compiler_params=VM,
        name="unpack",
    )(got)


def moved(value, band, sector, half):
    sizes = [lax.axis_size(name) for name in ("lat", "lon", "tp")]
    pairs = []
    for a in range(sizes[0]):
        for b in range(sizes[1]):
            for c in range(sizes[2]):
                source = ((a + band) % sizes[0], (b + sector) % sizes[1], (c + half) % sizes[2])
                pairs.append(tuple((x * sizes[1] + y) * sizes[2] + z for x, y, z in (source, (a, b, c))))
    return lax.ppermute(value, ("lat", "lon", "tp"), pairs)


def shifted_parts(quarters):
    return (
        quarters[3],
        moved(quarters[2], 0, 1, 0),
        moved(quarters[1], 1, 0, 0),
        moved(quarters[0], 1, 1, 0),
    )


def local(
    inputs,
    residual_mid,
    grad_out,
    mask_ids,
    key_valid,
    bias_index,
    pos_bias,
    norm1_gain,
    qkv_weight,
    proj_weight,
    norm2_gain,
    fc1_weight,
    fc2_weight,
):
    levels, lat_cells, lon_cells, channels = inputs.shape
    cell_count = levels * lat_cells * lon_cells
    weight_scale = (cell_count * lax.axis_size("lat") * lax.axis_size("lon")) ** (-0.5)
    table_scale = (lon_cells * lax.axis_size("lon") // 12) ** (-0.5)
    gain1, gain2 = norm1_gain.reshape(1, -1), norm2_gain.reshape(1, -1)

    x = split(inputs.reshape(48, 12, 192))
    xw = shifted_parts(x)
    part2, mid, up, down, upg = mlp(
        residual_mid.reshape(48, 12, 192), grad_out.reshape(48, 12, 192), gain2, fc1_weight, fc2_weight
    )
    other2 = moved(part2, 0, 0, 1)
    main, tail, lo, hi = gather(bias_index, pos_bias.reshape(4, 3, 3312))
    code = mask_ids * 2 + (key_valid > 0).astype(jnp.int32)
    code = code.reshape(4, 2, 2, 3, 2, 6).transpose(0, 2, 4, 1, 3, 5).reshape(4, 1, 144)
    *gm, gain_two = middle(mid, up, part2, other2, gain2)
    gw = shifted_parts(gm)
    low, q, k, v, prob, att = forward(xw, gain1, qkv_weight, main, tail, code)
    part1, score, gqkv, gproj = backward(gw, proj_weight, qkv_weight, low, q, k, v, prob, att)
    other1 = moved(part1, 0, 0, 1)
    table = scatter(score, lo, hi)
    *g, gain_one = meet(part1, other1, xw)
    back = (moved(g[3], -1, -1, 0), moved(g[2], -1, 0, 0), moved(g[1], 0, -1, 0), g[0])
    sums = pack(down, upg, gqkv, gproj, table, gain_one, gain_two).reshape(128, 16, 128)
    place = (lax.axis_index("lat") * lax.axis_size("lon") + lax.axis_index("lon")).reshape(1)
    got = lax.all_to_all(sums, ("lat", "lon"), 0, 0)
    got = lax.all_to_all(add(place, got), ("lat", "lon"), 0, 0)
    qkv_out, proj_out, up_out, down_out, gains, table_out = unpack(
        weight_scale, table_scale, got.reshape(2048, 128)
    )
    result = finish(x, gm, back, gain1).reshape(levels, lat_cells, lon_cells, channels)
    share = channels // lax.axis_size("tp")
    start = lax.axis_index("tp") * share
    gains = gains[0:4].reshape(2, 256)[:, 0:channels]
    mine = lax.dynamic_slice_in_dim(gains, start, share, axis=1)
    return (result, qkv_out, proj_out, up_out, down_out, mine[0], mine[1], table_out[None])


def solution(mesh):
    return jax.shard_map(
        local,
        mesh=mesh,
        in_specs=(
            P(None, "lat", "lon", None),
            P(None, "lat", "lon", None),
            P(None, "lat", "lon", None),
            P(None, "lat", "lon"),
            P(None, "lat", "lon"),
            P(),
            P("lat", None, "tp", None),
            P(),
            P(None, None, "tp"),
            P("tp", None),
            P(),
            P(None, "tp"),
            P("tp", None),
        ),
        out_specs=(
            P(None, "lat", "lon", None),
            P(None, None, "tp"),
            P("tp", None),
            P(None, "tp"),
            P("tp", None),
            P("tp"),
            P("tp"),
            P("lat", None, "tp", None),
        ),
        check_vma=False,
    )
```

time: 1770 us -> 130 us (0.07)
  the two profiles are of different devices: /device:TPU:24 before, /device:TPU:1 now
where the time goes in v1:
time: 130 us
  Pallas kernels  43.4 us (33%)
  starting transfers between devices  42.5 us (33%)
  waiting for transfers between devices  35.4 us (27%)
  local copies, waits for them, and re-layouts  7.35 us (6%)
    ppermute x11, starting transfers between devices, moved(): return lax.ppermute(value, ('lat', 'lon', 'tp'), pairs)  27.7 us
    pallas_call x1, Pallas kernels, gather(): pl.pallas_call(gather_kernel, out_shape=(shape((12, 144, 128), F32), shap...  20.8 us
    all_to_all x1, waiting for transfers between devices, local(): got = lax.all_to_all(sums, ('lat', 'lon'), 0, 0)  20.2 us
    ppermute x11, waiting for transfers between devices, moved(): return lax.ppermute(value, ('lat', 'lon', 'tp'), pairs)  15.2 us
    all_to_all x1, starting transfers between devices, local(): got = lax.all_to_all(sums, ('lat', 'lon'), 0, 0)  8.33 us
    pallas_call x1, Pallas kernels, backward(): pl.pallas_call(backward_kernel, out_shape=(shape((576, 192), BF), shape((...  6.86 us
    unnamed x32, local copies, waits for them, and re-layouts  6.51 us
    all_to_all x1, starting transfers between devices, local(): got = lax.all_to_all(add(place, got), ('lat', 'lon'), 0, 0)  6.47 us
  transfers between devices with their start and end apart: 13, of which 4 were waited for; matrix products, arithmetic and copies ran while one was open for 1% of the time, Pallas kernels for 25%

profile of v1, /device:TPU:1, one launch (start us, length us, event | category | flops | bytes accessed | tf_op | source)
XLA Modules:
  0.0 129.6 jit_solution(4365136493098232516)
XLA Ops:
  0.7 1.1 copy.32
  1.7 0.0 copy-start.6
  1.8 1.0 copy.33
  2.8 0.0 copy-start.11
  2.8 0.0 copy-start.9
  2.8 1.1 copy.34.fc2_ref
  3.9 0.0 copy-start.5
  3.9 0.7 copy-done.5
  4.6 1.5 %mlp.1 = (bf16[576,192]{1,0:T(8,128)(2,1)S(1)}, bf16[576,192]{1,0:T(8,128)(2,1)S(1)}, bf16[576,192]{1,0:T(8,128)(2,1)S(1)}, bf16[384,192]{1,0:T(8,128)(2,1)S(1)}, bf16[192,384]{1,0:T(8,128)(2,1)S(1)}) custom-call(bf16[48,12,192]{2,1,0:T(8,128)(2,1)S(1)} %bitcast.24, bf16[48,12,192]{2,1,0:T(8,128)(2,1)S(1)} %bitcast.25, f32[1,192]{1,0:T(1,128)S(1)} %bitcast.30, ...), custom_call_target="tpu_custom_call" | custom-call | tf_op jit(solution)/shard_map/mlp/pallas_call | solution.py:107
  6.1 0.0 copy-start.2
  6.1 0.0 copy-start.3
  6.1 2.2 %collective-permute-start = (bf16[576,192]{1,0:T(8,128)(2,1)S(1)}, bf16[576,192]{1,0:T(8,128)(2,1)S(1)}, u32[]{:S(2)}, u32[]{:S(2)}) collective-permute-start(bf16[576,192]{1,0:T(8,128)(2,1)S(1)} %get-tuple-element.53.own_ref), channel_id=1, source_target_pairs={{1,0},{0,1},{3,2},{2,3},{5,4},{4,5},{7,6},{6,7},{9,8},{8,9},{11,10... | collective-permute-start | bytes 663560 | tf_op jit(solution)/shard_map/ppermute | solution.py:487
  8.3 0.1 copy.31
  8.4 0.1 split.1
  8.5 7.8 %collective-permute-start.4 = (bf16[144,192]{1,0:T(8,128)(2,1)S(1)}, bf16[144,192]{1,0:T(8,128)(2,1)S(1)}, u32[]{:S(2)}, u32[]{:S(2)}) collective-permute-start(bf16[144,192]{1,0:T(8,128)(2,1)S(1)} %get-tuple-element.49.x2), channel_id=1, source_target_pairs={{2,0},{3,1},{4,2},{5,3},{6,4},{7,5},{8,6},{9,7},{10,8},{11,9},{12,... | collective-permute-start | bytes 165896 | tf_op jit(solution)/shard_map/ppermute | solution.py:487
  16.4 1.2 collective-permute-start.5
  17.6 2.2 %collective-permute-start.6 = (bf16[144,192]{1,0:T(8,128)(2,1)S(1)}, bf16[144,192]{1,0:T(8,128)(2,1)S(1)}, u32[]{:S(2)}, u32[]{:S(2)}) collective-permute-start(bf16[144,192]{1,0:T(8,128)(2,1)S(1)} %get-tuple-element.47.x0), channel_id=1, source_target_pairs={{66,0},{67,1},{68,2},{69,3},{70,4},{71,5},{72,6},{73,7},{74,8},{75... | collective-permute-start | bytes 165896 | tf_op jit(solution)/shard_map/ppermute | solution.py:487
  19.8 0.6 middle.1
  20.4 2.9 %collective-permute-start.1 = (bf16[144,192]{1,0:T(8,128)(2,1)S(1)}, bf16[144,192]{1,0:T(8,128)(2,1)S(1)}, u32[]{:S(2)}, u32[]{:S(2)}) collective-permute-start(bf16[144,192]{1,0:T(8,128)(2,1)S(1)} %get-tuple-element.56.m2), channel_id=1, source_target_pairs={{2,0},{3,1},{4,2},{5,3},{6,4},{7,5},{8,6},{9,7},{10,8},{11,9},{12,... | collective-permute-start | bytes 165896 | tf_op jit(solution)/shard_map/ppermute | solution.py:487
  23.3 1.8 %collective-permute-start.2 = (bf16[144,192]{1,0:T(8,128)(2,1)S(1)}, bf16[144,192]{1,0:T(8,128)(2,1)S(1)}, u32[]{:S(2)}, u32[]{:S(2)}) collective-permute-start(bf16[144,192]{1,0:T(8,128)(2,1)S(1)} %get-tuple-element.55.m1), channel_id=1, source_target_pairs={{64,0},{65,1},{66,2},{67,3},{68,4},{69,5},{70,6},{71,7},{72,8},{73... | collective-permute-start | bytes 165896 | tf_op jit(solution)/shard_map/ppermute | solution.py:487
  25.2 2.7 %collective-permute-start.3 = (bf16[144,192]{1,0:T(8,128)(2,1)S(1)}, bf16[144,192]{1,0:T(8,128)(2,1)S(1)}, u32[]{:S(2)}, u32[]{:S(2)}) collective-permute-start(bf16[144,192]{1,0:T(8,128)(2,1)S(1)} %get-tuple-element.54.m0), channel_id=1, source_target_pairs={{66,0},{67,1},{68,2},{69,3},{70,4},{71,5},{72,6},{73,7},{74,8},{75... | collective-permute-start | bytes 165896 | tf_op jit(solution)/shard_map/ppermute | solution.py:487
  27.9 0.1 copy.43
  28.0 0.1 reshape.61
  28.1 0.1 reshape.68.code_ref
  28.2 20.8 %gather.1 = (f32[12,144,128]{2,1,0:T(8,128)S(1)}, f32[12,144,128]{2,1,0:T(8,128)S(1)}, s32[168,128]{1,0:T(8,128)S(1)}, s32[168,128]{1,0:T(8,128)S(1)}) custom-call(s32[144,144]{1,0:T(8,128)S(1)} %copy-done.2, bf16[144,144]{1,0:T(8,128)(2,1)S(1)} %copy-done.3, f32[4,3,3312]{2,1,0:T(4,128)S(1)} %bitcast.28), custom_call_target="tpu_custom_call" | custom-call | tf_op jit(solution)/shard_map/gather/pallas_call | solution.py:194
  49.1 4.7 %forward.1 = (bf16[576,192]{1,0:T(8,128)(2,1)S(1)}, bf16[576,96]{1,0:T(8,128)(2,1)S(1)}, bf16[576,96]{1,0:T(8,128)(2,1)S(1)}, bf16[576,96]{1,0:T(8,128)(2,1)S(1)...) custom-call(bf16[144,192]{1,0:T(8,128)(2,1)S(1)} %get-tuple-element.50.x0.x3, ...), custom_call_target="tpu_custom_call" | custom-call | tf_op jit(solution)/shard_map/forward/pallas_call | solution.py:242
  53.8 6.9 %backward.1 = (bf16[576,192]{1,0:T(8,128)(2,1)S(1)}, f32[12,168,128]{2,1,0:T(8,128)S(1)}, bf16[3,192,96]{2,1,0:T(8,128)(2,1)S(1)}, bf16[96,192]{1,0:T(8,128)(2,1)S(1)}) custom-call(bf16[144,192]{1,0:T(8,128)(2,1)S(1)} %get-tuple-element.57.g0.m3, bf16[144,192]{1,0:T(8,128)(2,1)S(1)} %collective-permute-done.1.g1, ...), custom_call_target="tpu_custom_call" | custom-call | tf_op jit(solution)/shard_map/backward/pallas_call | solution.py:300
  60.7 0.7 collective-permute-start.7
  61.3 5.1 %scatter.1.table_ref = f32[192,256]{1,0:T(8,128)S(1)} custom-call(f32[12,168,128]{2,1,0:T(8,128)S(1)} %get-tuple-element.75.score_ref, s32[168,128]{1,0:T(8,128)S(1)} %get-tuple-element.76.lo_ref, s32[168,128]{1,0:T(8,128)S(1)} %get-tuple-element.77.hi_ref), custom_call_target="tpu_custom_call" | custom-call | tf_op jit(solution)/shard_map/scatter/pallas_call | solution.py:336
  66.4 1.4 %collective-permute-done.7.other_ref = bf16[576,192]{1,0:T(8,128)(2,1)S(1)} collective-permute-done((bf16[576,192]{1,0:T(8,128)(2,1)S(1)}, bf16[576,192]{1,0:T(8,128)(2,1)S(1)}, u32[]{:S(2)}, u32[]{:S(2)}) %collective-permute-start.7) | collective-permute-done | bytes 221216 | tf_op jit(solution)/shard_map/ppermute | solution.py:487
  67.8 0.3 meet.1
  68.1 0.9 pack.1
  69.0 8.3 %all-to-all-start = ((bf16[128,16,128]{2,1,0:T(8,128)(2,1)}), bf16[128,16,128]{2,1,0:T(8,128)(2,1)S(1)}, u32[]{:S(2)}, u32[]{:S(2)}) async-start(bf16[128,16,128]{2,1,0:T(8,128)(2,1)} %bitcast.9), calls=%async_computation | async-start | bytes 1048576 | tf_op jit(solution)/shard_map/all_to_all | solution.py:539
  77.4 20.2 %all-to-all-done.got_ref = bf16[128,16,128]{2,1,0:T(8,128)(2,1)S(1)} async-done(((bf16[128,16,128]{2,1,0:T(8,128)(2,1)}), bf16[128,16,128]{2,1,0:T(8,128)(2,1)S(1)}, u32[]{:S(2)}, u32[]{:S(2)}) %all-to-all-start) | async-done | bytes 524320 | tf_op jit(solution)/shard_map/all_to_all | solution.py:539
  97.6 0.9 add.14
  98.5 6.5 %all-to-all-start.1 = ((bf16[128,16,128]{2,1,0:T(8,128)(2,1)}), bf16[128,16,128]{2,1,0:T(8,128)(2,1)S(1)}, u32[]{:S(2)}, u32[]{:S(2)}) async-start(bf16[128,16,128]{2,1,0:T(8,128)(2,1)} %add.14), calls=%async_computation.1 | async-start | bytes 1048576 | tf_op jit(solution)/shard_map/all_to_all | solution.py:540
  105.0 1.4 %collective-permute-start.10 = (bf16[144,192]{1,0:T(8,128)(2,1)S(1)}, bf16[144,192]{1,0:T(8,128)(2,1)S(1)}, u32[]{:S(2)}, u32[]{:S(2)}) collective-permute-start(bf16[144,192]{1,0:T(8,128)(2,1)S(1)} %get-tuple-element.69), channel_id=1, source_target_pairs={{62,0},{63,1},{0,2},{1,3},{2,4},{3,5},{4,6},{5,7},{6,8},{7,9},{8,1... | collective-permute-start | bytes 165896 | tf_op jit(solution)/shard_map/ppermute | solution.py:487
  106.4 4.4 %collective-permute-start.8 = (bf16[144,192]{1,0:T(8,128)(2,1)S(1)}, bf16[144,192]{1,0:T(8,128)(2,1)S(1)}, u32[]{:S(2)}, u32[]{:S(2)}) collective-permute-start(bf16[144,192]{1,0:T(8,128)(2,1)S(1)} %get-tuple-element.67), channel_id=1, source_target_pairs={{254,0},{255,1},{192,2},{193,3},{194,4},{195,5},{196,6},{197,7},{1... | collective-permute-start | bytes 165896 | tf_op jit(solution)/shard_map/ppermute | solution.py:487
  110.8 0.2 collective-permute-start.9
  111.0 11.8 %collective-permute-done.10.g2 = bf16[144,192]{1,0:T(8,128)(2,1)S(1)} collective-permute-done((bf16[144,192]{1,0:T(8,128)(2,1)S(1)}, bf16[144,192]{1,0:T(8,128)(2,1)S(1)}, u32[]{:S(2)}, u32[]{:S(2)}) %collective-permute-start.10) | collective-permute-done | bytes 55328 | tf_op jit(solution)/shard_map/ppermute | solution.py:487
  122.8 2.0 %collective-permute-done.8.g0 = bf16[144,192]{1,0:T(8,128)(2,1)S(1)} collective-permute-done((bf16[144,192]{1,0:T(8,128)(2,1)S(1)}, bf16[144,192]{1,0:T(8,128)(2,1)S(1)}, u32[]{:S(2)}, u32[]{:S(2)}) %collective-permute-start.8) | collective-permute-done | bytes 55328 | tf_op jit(solution)/shard_map/ppermute | solution.py:487
  124.8 0.6 finish.1
  125.5 0.9 copy.38
  126.4 1.0 unpack.1
  127.4 0.9 copy.39
  128.3 0.7 copy.40
  129.0 0.1 constant_dynamic-slice_fusion
  129.1 0.5 slice_bitcast_fusion
  (30 shorter events, 0.1 us)
Async XLA Ops:
  0.6 3.3 %copy-start.1 = (bf16[192,384]{1,0:T(8,128)(2,1)S(1)}, bf16[192,384]{1,0:T(8,128)(2,1)}, u32[]{:S(2)}) copy-start(bf16[192,384]{1,0:T(8,128)(2,1)} %fc1_ref.1) | copy-start | bytes 442372
  0.6 7.7 %copy-start.8 = (bf16[8,6,12,192]{3,0,2,1:T(8,128)(2,1)S(1)}, bf16[8,6,12,192]{3,0,2,1:T(8,128)(2,1)}, u32[]{:S(2)}) copy-start(bf16[8,6,12,192]{3,0,2,1:T(8,128)(2,1)} %param.14) | copy-start | bytes 663556
  1.7 18.1 %copy-start.6 = (f32[192]{0:T(256)S(1)}, f32[192]{0:T(256)}, u32[]{:S(2)}) copy-start(f32[192]{0:T(256)} %param.24) | copy-start | bytes 2308
  2.8 25.1 %copy-start.10 = (s32[8,6,12]{2,0,1:T(8,128)S(1)}, s32[8,6,12]{2,0,1:T(8,128)}, u32[]{:S(2)}) copy-start(s32[8,6,12]{2,0,1:T(8,128)} %param.17) | copy-start | bytes 6916
  2.8 25.1 %copy-start.11 = (s32[8,6,12]{2,0,1:T(8,128)S(1)}, s32[8,6,12]{2,0,1:T(8,128)}, u32[]{:S(2)}) copy-start(s32[8,6,12]{2,0,1:T(8,128)} %param.18) | copy-start | bytes 6916
  2.8 25.1 %copy-start.9 = (f32[1,4,3,3312]{3,1,2,0:T(4,128)S(1)}, f32[1,4,3,3312]{3,1,2,0:T(4,128)}, u32[]{:S(2)}) copy-start(f32[1,4,3,3312]{3,1,2,0:T(4,128)} %param.20) | copy-start | bytes 476932
  3.9 0.7 copy-start.5
  6.1 22.1 %copy-start.2 = (s32[144,144]{1,0:T(8,128)S(1)}, s32[144,144]{1,0:T(8,128)}, u32[]{:S(2)}) copy-start(s32[144,144]{1,0:T(8,128)} %index_ref.1) | copy-start | bytes 248836
  6.1 22.1 %copy-start.3 = (bf16[144,144]{1,0:T(8,128)(2,1)S(1)}, bf16[144,144]{1,0:T(8,128)(2,1)}, u32[]{:S(2)}) copy-start(bf16[144,144]{1,0:T(8,128)(2,1)} %constant.27.clone.order_ref) | copy-start | bytes 124420
  6.1 43.0 %copy-start = (bf16[3,192,96]{2,1,0:T(8,128)(2,1)S(1)}, bf16[3,192,96]{2,1,0:T(8,128)(2,1)}, u32[]{:S(2)}) copy-start(bf16[3,192,96]{2,1,0:T(8,128)(2,1)} %qkv_ref.3) | copy-start | bytes 331780
  6.1 43.0 %copy-start.7 = (f32[192]{0:T(256)S(1)}, f32[192]{0:T(256)}, u32[]{:S(2)}) copy-start(f32[192]{0:T(256)} %param.21) | copy-start | bytes 2308
  6.1 13.7 %collective-permute-start = (bf16[576,192]{1,0:T(8,128)(2,1)S(1)}, bf16[576,192]{1,0:T(8,128)(2,1)S(1)}, u32[]{:S(2)}, u32[]{:S(2)}) collective-permute-start(bf16[576,192]{1,0:T(8,128)(2,1)S(1)} %get-tuple-element.53.own_ref), channel_id=1, source_target_pairs={{1,0},{0,1},{3,2},{2,3},{5,4},{4,5},{7,6},{6,7},{9,8},{8,9},{11,10... | collective-permute-start | bytes 663560 | tf_op jit(solution)/shard_map/ppermute | solution.py:487
  8.5 16.6 %collective-permute-start.4 = (bf16[144,192]{1,0:T(8,128)(2,1)S(1)}, bf16[144,192]{1,0:T(8,128)(2,1)S(1)}, u32[]{:S(2)}, u32[]{:S(2)}) collective-permute-start(bf16[144,192]{1,0:T(8,128)(2,1)S(1)} %get-tuple-element.49.x2), channel_id=1, source_target_pairs={{2,0},{3,1},{4,2},{5,3},{6,4},{7,5},{8,6},{9,7},{10,8},{11,9},{12,... | collective-permute-start | bytes 165896 | tf_op jit(solution)/shard_map/ppermute | solution.py:487
  16.4 32.7 %collective-permute-start.5 = (bf16[144,192]{1,0:T(8,128)(2,1)S(1)}, bf16[144,192]{1,0:T(8,128)(2,1)S(1)}, u32[]{:S(2)}, u32[]{:S(2)}) collective-permute-start(bf16[144,192]{1,0:T(8,128)(2,1)S(1)} %get-tuple-element.48.x1), channel_id=1, source_target_pairs={{64,0},{65,1},{66,2},{67,3},{68,4},{69,5},{70,6},{71,7},{72,8},{73... | collective-permute-start | bytes 165896 | tf_op jit(solution)/shard_map/ppermute | solution.py:487
  17.6 31.4 %collective-permute-start.6 = (bf16[144,192]{1,0:T(8,128)(2,1)S(1)}, bf16[144,192]{1,0:T(8,128)(2,1)S(1)}, u32[]{:S(2)}, u32[]{:S(2)}) collective-permute-start(bf16[144,192]{1,0:T(8,128)(2,1)S(1)} %get-tuple-element.47.x0), channel_id=1, source_target_pairs={{66,0},{67,1},{68,2},{69,3},{70,4},{71,5},{72,6},{73,7},{74,8},{75... | collective-permute-start | bytes 165896 | tf_op jit(solution)/shard_map/ppermute | solution.py:487
  20.4 33.4 %copy-start.4 = (bf16[96,192]{1,0:T(8,128)(2,1)S(1)}, bf16[96,192]{1,0:T(8,128)(2,1)}, u32[]{:S(2)}) copy-start(bf16[96,192]{1,0:T(8,128)(2,1)} %proj_ref.1) | copy-start | bytes 110596
  20.4 33.3 %collective-permute-start.1 = (bf16[144,192]{1,0:T(8,128)(2,1)S(1)}, bf16[144,192]{1,0:T(8,128)(2,1)S(1)}, u32[]{:S(2)}, u32[]{:S(2)}) collective-permute-start(bf16[144,192]{1,0:T(8,128)(2,1)S(1)} %get-tuple-element.56.m2), channel_id=1, source_target_pairs={{2,0},{3,1},{4,2},{5,3},{6,4},{7,5},{8,6},{9,7},{10,8},{11,9},{12,... | collective-permute-start | bytes 165896 | tf_op jit(solution)/shard_map/ppermute | solution.py:487
  23.3 30.4 %collective-permute-start.2 = (bf16[144,192]{1,0:T(8,128)(2,1)S(1)}, bf16[144,192]{1,0:T(8,128)(2,1)S(1)}, u32[]{:S(2)}, u32[]{:S(2)}) collective-permute-start(bf16[144,192]{1,0:T(8,128)(2,1)S(1)} %get-tuple-element.55.m1), channel_id=1, source_target_pairs={{64,0},{65,1},{66,2},{67,3},{68,4},{69,5},{70,6},{71,7},{72,8},{73... | collective-permute-start | bytes 165896 | tf_op jit(solution)/shard_map/ppermute | solution.py:487
  25.2 28.6 %collective-permute-start.3 = (bf16[144,192]{1,0:T(8,128)(2,1)S(1)}, bf16[144,192]{1,0:T(8,128)(2,1)S(1)}, u32[]{:S(2)}, u32[]{:S(2)}) collective-permute-start(bf16[144,192]{1,0:T(8,128)(2,1)S(1)} %get-tuple-element.54.m0), channel_id=1, source_target_pairs={{66,0},{67,1},{68,2},{69,3},{70,4},{71,5},{72,6},{73,7},{74,8},{75... | collective-permute-start | bytes 165896 | tf_op jit(solution)/shard_map/ppermute | solution.py:487
  60.7 7.1 %collective-permute-start.7 = (bf16[576,192]{1,0:T(8,128)(2,1)S(1)}, bf16[576,192]{1,0:T(8,128)(2,1)S(1)}, u32[]{:S(2)}, u32[]{:S(2)}) collective-permute-start(bf16[576,192]{1,0:T(8,128)(2,1)S(1)} %get-tuple-element.66.own_ref), channel_id=1, source_target_pairs={{1,0},{0,1},{3,2},{2,3},{5,4},{4,5},{7,6},{6,7},{9,8},{8,9},{11,10... | collective-permute-start | bytes 663560 | tf_op jit(solution)/shard_map/ppermute | solution.py:487
  69.0 28.6 %all-to-all-start = ((bf16[128,16,128]{2,1,0:T(8,128)(2,1)}), bf16[128,16,128]{2,1,0:T(8,128)(2,1)S(1)}, u32[]{:S(2)}, u32[]{:S(2)}) async-start(bf16[128,16,128]{2,1,0:T(8,128)(2,1)} %bitcast.9), calls=%async_computation | async-start | bytes 1048576 | tf_op jit(solution)/shard_map/all_to_all | solution.py:539
  98.5 27.9 %all-to-all-start.1 = ((bf16[128,16,128]{2,1,0:T(8,128)(2,1)}), bf16[128,16,128]{2,1,0:T(8,128)(2,1)S(1)}, u32[]{:S(2)}, u32[]{:S(2)}) async-start(bf16[128,16,128]{2,1,0:T(8,128)(2,1)} %add.14), calls=%async_computation.1 | async-start | bytes 1048576 | tf_op jit(solution)/shard_map/all_to_all | solution.py:540
  105.0 17.8 %collective-permute-start.10 = (bf16[144,192]{1,0:T(8,128)(2,1)S(1)}, bf16[144,192]{1,0:T(8,128)(2,1)S(1)}, u32[]{:S(2)}, u32[]{:S(2)}) collective-permute-start(bf16[144,192]{1,0:T(8,128)(2,1)S(1)} %get-tuple-element.69), channel_id=1, source_target_pairs={{62,0},{63,1},{0,2},{1,3},{2,4},{3,5},{4,6},{5,7},{6,8},{7,9},{8,1... | collective-permute-start | bytes 165896 | tf_op jit(solution)/shard_map/ppermute | solution.py:487
  106.4 18.4 %collective-permute-start.8 = (bf16[144,192]{1,0:T(8,128)(2,1)S(1)}, bf16[144,192]{1,0:T(8,128)(2,1)S(1)}, u32[]{:S(2)}, u32[]{:S(2)}) collective-permute-start(bf16[144,192]{1,0:T(8,128)(2,1)S(1)} %get-tuple-element.67), channel_id=1, source_target_pairs={{254,0},{255,1},{192,2},{193,3},{194,4},{195,5},{196,6},{197,7},{1... | collective-permute-start | bytes 165896 | tf_op jit(solution)/shard_map/ppermute | solution.py:487
  110.8 14.1 %collective-permute-start.9 = (bf16[144,192]{1,0:T(8,128)(2,1)S(1)}, bf16[144,192]{1,0:T(8,128)(2,1)S(1)}, u32[]{:S(2)}, u32[]{:S(2)}) collective-permute-start(bf16[144,192]{1,0:T(8,128)(2,1)S(1)} %get-tuple-element.68), channel_id=1, source_target_pairs={{192,0},{193,1},{194,2},{195,3},{196,4},{197,5},{198,6},{199,7},{2... | collective-permute-start | bytes 165896 | tf_op jit(solution)/shard_map/ppermute | solution.py:487

commit v2 on v1

v2 whole, which is shorter than its diff:
```python
import functools

import jax
import jax.numpy as jnp
import numpy as np
from jax import lax
from jax.experimental import pallas as pl
from jax.experimental.pallas import tpu as pltpu
from jax.sharding import PartitionSpec as P

HD = 32
EPSILON = 1e-05
EXCLUDED = -1e30
BF = jnp.bfloat16
F32 = jnp.float32
I32 = jnp.int32
VMEM = pl.BlockSpec(memory_space=pltpu.VMEM)
VM = pltpu.CompilerParams(vmem_limit_bytes=48 * 1024 * 1024)


def cost(microseconds):
    return pl.CostEstimate(flops=0, bytes_accessed=int(microseconds * 3000000), transcendentals=0)


def shape(dims, kind):
    return jax.ShapeDtypeStruct(dims, kind)


def dot_nn(a, b):
    return lax.dot_general(a, b, (((1,), (0,)), ((), ())), preferred_element_type=F32)


def dot_nt(a, b):
    return lax.dot_general(a, b, (((1,), (1,)), ((), ())), preferred_element_type=F32)


def dot_tn(a, b):
    return lax.dot_general(a, b, (((0,), (0,)), ((), ())), preferred_element_type=F32)


def layer_stats(rows):
    mean = jnp.mean(rows, axis=-1, keepdims=True)
    centred = rows - mean
    inverse = lax.rsqrt(jnp.mean(centred * centred, axis=-1, keepdims=True) + EPSILON)
    return centred * inverse, inverse


def norm_backward(grad_normed, gain, normed, inverse):
    scaled = grad_normed * gain
    first = jnp.mean(scaled, axis=-1, keepdims=True)
    second = jnp.mean(scaled * normed, axis=-1, keepdims=True)
    return (scaled - first - normed * second) * inverse


def gelu_pair(pre):
    cdf = 0.5 * (1.0 + lax.erf(pre * 0.7071067811865476))
    pdf = 0.3989422804014327 * jnp.exp(-0.5 * pre * pre)
    return pre * cdf, cdf + pre * pdf


def to_quarters(field_ref, scratch):
    for lat in range(6):
        for half in range(2):
            rows = field_ref[lat, half * 6 : half * 6 + 6].astype(F32).reshape(48, 192)
            start = ((lat // 3) * 2 + half) * 144 + (lat % 3) * 48
            scratch[start : start + 48, :] = rows


def level_order():
    order = np.zeros((144, 144), np.float32)
    for w in range(4):
        for cell in range(18):
            for level in range(2):
                order[w * 36 + cell * 2 + level, cell * 8 + (2 * w + 1 + level) % 8] = 1.0
    return jnp.asarray(order, BF)


def to_windows(parts, order, scratch):
    for s in range(4):
        rows = dot_nn(order, parts[s][...])
        for w in range(4):
            scratch[w * 144 + s * 36 : w * 144 + s * 36 + 36, :] = rows[w * 36 : w * 36 + 36]


def head_kernel(x_ref, mid_ref, up_ref, gain_ref, fc1_ref, fc2_ref,
                o0, o1, o2, o3, part_ref, midq_ref, upq_ref, grads_ref, scratch, mid_s, up_s):
    to_quarters(x_ref, scratch)
    for q, out in enumerate((o0, o1, o2, o3)):
        out[...] = scratch[q * 144 : q * 144 + 144, :].astype(BF)
    to_quarters(mid_ref, mid_s)
    to_quarters(up_ref, up_s)
    mid = mid_s[...]
    up = up_s[...].astype(BF)
    midq_ref[...] = mid.astype(BF)
    upq_ref[...] = up
    normed, _ = layer_stats(mid)
    lowered = (normed * gain_ref[...]).astype(BF)
    pre = dot_nn(lowered, fc1_ref[...])
    active, slopes = gelu_pair(pre)
    grad_pre = (dot_nn(up, fc2_ref[...]) * slopes).astype(BF)
    part_ref[...] = dot_nt(grad_pre, fc1_ref[...]).astype(BF)
    for start, grads in ((0, dot_tn(lowered, grad_pre)), (576, dot_tn(up, active.astype(BF)))):
        for j in range(3):
            grads_ref[start + j * 192 : start + j * 192 + 192, :] = grads[:, j * 128 : j * 128 + 128].astype(BF)


def head(x, mid, up, gain, fc1, fc2):
    return pl.pallas_call(
        head_kernel,
        out_shape=tuple(shape((144, 192), BF) for _ in range(4))
        + (shape((576, 192), BF), shape((576, 192), BF), shape((576, 192), BF), shape((1152, 128), BF)),
        scratch_shapes=[pltpu.VMEM((576, 192), F32)] * 3,
        compiler_params=VM,
        cost_estimate=cost(3),
        name="head",
    )(x, mid, up, gain, fc1, fc2)


def middle_kernel(mid_ref, up_ref, own_ref, other_ref, gain_ref, after_ref, o0, o1, o2, o3, gain_out):
    normed, inverse = layer_stats(mid_ref[...].astype(F32))
    grad = own_ref[...].astype(F32) + other_ref[...].astype(F32)
    gain_out[...] = jnp.sum(grad * normed, axis=0, keepdims=True)
    out = up_ref[...].astype(F32) + norm_backward(grad, gain_ref[...], normed, inverse)
    for q, o in enumerate((o0, o1, o2, o3)):
        o[...] = out[q * 144 : q * 144 + 144].astype(BF)


def middle(mid, up, own, other, gain, after):
    return pl.pallas_call(
        middle_kernel,
        out_shape=tuple(shape((144, 192), BF) for _ in range(4)) + (shape((1, 192), F32),),
        in_specs=[VMEM] * 5 + [pl.BlockSpec(memory_space=pl.ANY)],
        compiler_params=VM,
        cost_estimate=cost(1),
        name="middle",
    )(mid, up, own, other, gain, after)


def window_order():
    canon = np.arange(144).reshape(2, 2, 3, 2, 6).transpose(1, 3, 2, 4, 0).reshape(-1)
    order = np.zeros((144, 144), np.float32)
    order[np.arange(144), canon] = 1.0
    return order


def pack_tail(tail):
    spread = (lax.broadcasted_iota(I32, (16, 128), 1) & 15) == lax.broadcasted_iota(I32, (16, 128), 0)
    wide = dot_nn(tail, spread.astype(F32).astype(BF))
    here = (lax.broadcasted_iota(I32, (144, 128), 1) >> 4) == (lax.broadcasted_iota(I32, (144, 128), 0) & 7)
    wide = jnp.where(here, wide, 0.0).astype(BF)
    rows = (lax.broadcasted_iota(I32, (24, 144), 1) >> 3) == lax.broadcasted_iota(I32, (24, 144), 0)
    return dot_nn(rows.astype(F32).astype(BF), wide)


def one_hot(low):
    return (lax.broadcasted_iota(I32, (256, 128), 0) == low).astype(F32).astype(BF)


def gather_kernel(index_ref, order_ref, bias_ref, main_ref, tail_ref, lo_ref, hi_ref, table, stage):
    index = index_ref[...]
    order = order_ref[...]
    pieces = []
    for part in (index & 127, index >> 7):
        moved = dot_nt(dot_nn(order, part.astype(F32).astype(BF)).astype(BF), order)
        pieces.append((moved[:, 0:128].astype(I32), pack_tail(moved[:, 128:144].astype(BF)).astype(I32)))
    for rows, low, high in ((slice(0, 144), pieces[0][0], pieces[1][0]), (slice(144, 168), pieces[0][1], pieces[1][1])):
        lo_ref[rows, :] = low + (high & 1) * 128
        hi_ref[rows, :] = high >> 1
    table[...] = jnp.zeros((160, 256), F32)
    for r in range(12):
        line = bias_ref[r % 3, r // 3 : r // 3 + 1, :]
        line = line - jnp.max(line, axis=1, keepdims=True)
        for c in range(13):
            wide = min(256, 3312 - c * 256)
            row = c * 8 + r if r < 8 else 104 + (c // 2) * 8 + (c % 2) * 4 + r - 8
            table[row : row + 1, 0:wide] = line[:, c * 256 : c * 256 + wide]
    upper = table[...].astype(BF)
    lower = (table[...] - upper.astype(F32)).astype(BF)
    terms = jnp.concatenate([upper, lower], axis=1)
    half = (lax.broadcasted_iota(I32, (8, 128), 0) >> 2)

    def step(i, _):
        for pair in range(9):
            hot = jnp.concatenate([one_hot(lo_ref[pl.ds(i * 18 + pair * 2 + j, 1), :]) for j in range(2)], axis=1)
            found = dot_nn(terms, jnp.concatenate([hot, hot], axis=0))
            for j in range(2):
                block = i * 18 + pair * 2 + j
                cols = slice(j * 128, j * 128 + 128)
                high = hi_ref[pl.ds(block, 1), :]
                first = jnp.zeros((8, 128), F32)
                for c in range(13):
                    first = jnp.where(high == c, found[c * 8 : c * 8 + 8, cols], first)
                second = jnp.zeros((8, 128), F32)
                shifted = high - half
                for c in range(7):
                    second = jnp.where(shifted == 2 * c, found[104 + c * 8 : 112 + c * 8, cols], second)
                start = pl.multiple_of(block * 16, 16)
                stage[pl.ds(start, 8), :] = first
                stage[pl.ds(start + 8, 8), :] = second + pltpu.roll(second, 4, 0)
        return 0

    lax.fori_loop(0, 9, step, 0)
    for r in range(12):
        main_ref[r] = stage[pl.ds(r, 144, stride=16), :]
        packed = stage[pl.ds(144 * 16 + r, 18, stride=16), :]
        for s in range(8):
            tail_ref[r, pl.ds(s, 18, stride=8), :] = pltpu.roll(packed, 128 - 16 * s, 1) if s else packed


def gather(index, bias):
    return pl.pallas_call(
        gather_kernel,
        out_shape=(
            shape((12, 144, 128), F32),
            shape((12, 144, 128), F32),
            shape((168, 128), I32),
            shape((168, 128), I32),
        ),
        scratch_shapes=[pltpu.VMEM((160, 256), F32), pltpu.VMEM((162 * 16, 128), F32)],
        compiler_params=VM,
        cost_estimate=cost(10),
        name="gather",
    )(index, jnp.asarray(window_order(), BF), bias)


def forward_kernel(x0, x1, x2, x3, order_ref, gain_ref, qkv_ref, main_ref, tail_ref, code_ref,
                   low_ref, q_ref, k_ref, v_ref, prob_ref, att_ref, scratch):
    to_windows((x0, x1, x2, x3), order_ref[...], scratch)
    normed, _ = layer_stats(scratch[...])
    low = (normed * gain_ref[...]).astype(BF)
    low_ref[...] = low
    for j, out in enumerate((q_ref, k_ref, v_ref)):
        out[...] = dot_nn(low, qkv_ref[j]).astype(BF)
    eye = lax.broadcasted_iota(I32, (144, 144), 0) == lax.broadcasted_iota(I32, (144, 144), 1)

    def window(w, _):
        rows = pl.ds(pl.multiple_of(w * 144, 16), 144)
        code = code_ref[w]
        label = code >> 1
        column = jnp.sum(jnp.where(eye, label, 0), axis=1, keepdims=True)
        allowed = eye | ((column == label) & ((code & 1) > 0))
        query, key, value = q_ref[rows, :], k_ref[rows, :], v_ref[rows, :]
        heads = []
        for h in range(3):
            cols = slice(h * HD, h * HD + HD)
            bias = jnp.concatenate([main_ref[w * 3 + h], tail_ref[w * 3 + h][:, 0:16]], axis=1)
            scores = dot_nt(query[:, cols], key[:, cols]) * (HD ** -0.5) + bias
            scores = jnp.where(allowed, scores, EXCLUDED)
            expo = jnp.exp(scores - jnp.max(scores, axis=-1, keepdims=True))
            prob = expo * (1.0 / jnp.sum(expo, axis=-1, keepdims=True))
            prob_ref[w * 3 + h] = prob
            heads.append(dot_nn(prob.astype(BF), value[:, cols]))
        att_ref[rows, :] = jnp.concatenate(heads, axis=1).astype(BF)
        return 0

    lax.fori_loop(0, 4, window, 0)


def forward(x, gain, qkv, main, tail, code):
    return pl.pallas_call(
        forward_kernel,
        out_shape=(
            shape((576, 192), BF),
            shape((576, 96), BF),
            shape((576, 96), BF),
            shape((576, 96), BF),
            shape((12, 144, 144), F32),
            shape((576, 96), BF),
        ),
        scratch_shapes=[pltpu.VMEM((576, 192), F32)],
        compiler_params=VM,
        cost_estimate=cost(5),
        name="forward",
    )(*x, level_order(), gain, qkv, main, tail, code)


def backward_kernel(g0, g1, g2, g3, order_ref, proj_ref, qkv_ref, low_ref, q_ref, k_ref, v_ref, prob_ref, att_ref,
                    part_ref, score_ref, grads_ref, scratch, gatt, gcols):
    to_windows((g0, g1, g2, g3), order_ref[...], scratch)
    grad = scratch[...].astype(BF)
    gproj = dot_tn(att_ref[...], grad).astype(BF)
    grads_ref[0:96, :] = gproj[:, 0:128]
    grads_ref[96:144, :] = jnp.concatenate([gproj[0:48, 128:192], gproj[48:96, 128:192]], axis=1)
    gatt[...] = dot_nt(grad, proj_ref[...]).astype(BF)

    def window(w, _):
        rows = pl.ds(pl.multiple_of(w * 144, 16), 144)
        query, key, value, above = q_ref[rows, :], k_ref[rows, :], v_ref[rows, :], gatt[rows, :]
        queries, keys, values = [], [], []
        for h in range(3):
            cols = slice(h * HD, h * HD + HD)
            prob = prob_ref[w * 3 + h]
            values.append(dot_tn(prob.astype(BF), above[:, cols]))
            grad_prob = dot_nt(above[:, cols], value[:, cols])
            score = prob * (grad_prob - jnp.sum(grad_prob * prob, axis=-1, keepdims=True))
            score_ref[w * 3 + h, 0:144, :] = score[:, 0:128]
            score_ref[w * 3 + h, 144:168, :] = pack_tail(score[:, 128:144].astype(BF))
            low_score = (score * (HD ** -0.5)).astype(BF)
            queries.append(dot_nn(low_score, key[:, cols]))
            keys.append(dot_tn(low_score, query[:, cols]))
        gcols[0, rows, :] = jnp.concatenate(queries, axis=1).astype(BF)
        gcols[1, rows, :] = jnp.concatenate(keys, axis=1).astype(BF)
        gcols[2, rows, :] = jnp.concatenate(values, axis=1).astype(BF)
        return 0

    lax.fori_loop(0, 4, window, 0)
    low = low_ref[...]
    total = None
    gqkv = []
    for j in range(3):
        cols = gcols[j]
        gqkv.append(dot_tn(low, cols).astype(BF))
        term = dot_nt(cols, qkv_ref[j])
        total = term if total is None else total + term
    a, b, c = gqkv
    grads_ref[144:336, :] = jnp.concatenate([a, c[:, 0:32]], axis=1)
    grads_ref[336:528, :] = jnp.concatenate([b, c[:, 32:64]], axis=1)
    grads_ref[528:576, :] = jnp.concatenate([c[i * 48 : i * 48 + 48, 64:96] for i in range(4)], axis=1)
    scratch[...] = total
    for s in range(4):
        pieces = [scratch[w * 144 + s * 36 : w * 144 + s * 36 + 36, :] for w in range(4)]
        piece = jnp.concatenate(pieces, axis=0).astype(BF)
        part_ref[s * 144 : s * 144 + 144, :] = dot_tn(order_ref[...], piece).astype(BF)


def backward(g, proj, qkv, low, q, k, v, prob, att):
    return pl.pallas_call(
        backward_kernel,
        out_shape=(
            shape((576, 192), BF),
            shape((12, 168, 128), F32),
            shape((576, 128), BF),
        ),
        scratch_shapes=[pltpu.VMEM((576, 192), F32), pltpu.VMEM((576, 96), BF), pltpu.VMEM((3, 576, 96), BF)],
        compiler_params=VM,
        cost_estimate=cost(7),
        name="backward",
    )(*g, level_order(), proj, qkv, low, q, k, v, prob, att)


def scatter_kernel(score_ref, lo_ref, hi_ref, out_ref):
    out_ref[...] = jnp.zeros((192, 256), F32)
    place = lax.broadcasted_iota(I32, (16, 128), 0)

    def step(i, _):
        left, right = [], []
        for j in range(18):
            row = pl.ds(i * 18 + j, 1)
            here = place == hi_ref[row, :]
            right.append(one_hot(lo_ref[row, :]))
            left.append(
                jnp.concatenate([jnp.where(here, score_ref[r, row, :], 0.0).astype(BF) for r in range(12)], axis=0)
            )
        out_ref[...] += dot_nt(jnp.concatenate(left, axis=1), jnp.concatenate(right, axis=1))
        return 0

    lax.fori_loop(0, 9, step, 0)


def scatter(score, lo, hi):
    return pl.pallas_call(
        scatter_kernel, out_shape=shape((192, 256), F32), compiler_params=VM, cost_estimate=cost(5), name="scatter"
    )(score, lo, hi)


def meet_kernel(own_ref, other_ref, x0, x1, x2, x3, grads_ref, two_ref, o0, o1, o2, o3, out_ref):
    gain = jnp.zeros((1, 192), F32)
    for s, (x, o) in enumerate(zip((x0, x1, x2, x3), (o0, o1, o2, o3))):
        rows = slice(s * 144, s * 144 + 144)
        grad = own_ref[rows, :].astype(F32) + other_ref[rows, :].astype(F32)
        normed, _ = layer_stats(x[...].astype(F32))
        gain = gain + jnp.sum(grad * normed, axis=0, keepdims=True)
        o[...] = grad.astype(BF)
    out_ref[0:576, :] = grads_ref[...]
    none = jnp.zeros((1, 64), F32)
    rows = []
    for line in (gain, two_ref[...]):
        rows += [line[:, 0:128], jnp.concatenate([line[:, 128:192], none], axis=1)]
    out_ref[576:592, :] = jnp.concatenate(rows + [jnp.zeros((12, 128), F32)], axis=0).astype(BF)


def meet(own, other, x, grads, two):
    return pl.pallas_call(
        meet_kernel,
        out_shape=tuple(shape((144, 192), BF) for _ in range(4)) + (shape((592, 128), BF),),
        compiler_params=VM,
        name="meet",
    )(own, other, *x, grads, two)


def finish_kernel(x0, x1, x2, x3, m0, m1, m2, m3, g0, g1, g2, g3, gain_ref, out_ref):
    for q, (x, m, g) in enumerate(zip((x0, x1, x2, x3), (m0, m1, m2, m3), (g0, g1, g2, g3))):
        normed, inverse = layer_stats(x[...].astype(F32))
        rows = m[...].astype(F32) + norm_backward(g[...].astype(F32), gain_ref[...], normed, inverse)
        for lat in range(3):
            piece = rows[lat * 48 : lat * 48 + 48].reshape(6, 8, 192)
            out_ref[(q // 2) * 3 + lat, (q % 2) * 6 : (q % 2) * 6 + 6] = piece.astype(BF)


def finish(x, m, g, gain):
    return pl.pallas_call(
        finish_kernel, out_shape=shape((6, 12, 8, 192), BF), compiler_params=VM, name="finish"
    )(*x, *m, *g, gain)


def both(own, other):
    return (own.astype(F32) + other.astype(F32)).astype(BF)


def pack_kernel(first_ref, first_other, second_ref, second_other, table_ref, out_ref):
    out_ref[0:1152, :] = both(first_ref[...], first_other[...])
    second = second_ref[...].astype(F32) + second_other[...].astype(F32)
    out_ref[1152:1728, :] = second[0:576].astype(BF)
    rows = []
    for r in range(12):
        pair = table_ref[r * 16 : r * 16 + 13, :]
        rows += [pair[:, 0:128], pair[:, 128:256]]
    out_ref[1728:2048, :] = jnp.concatenate(rows + [second[576:584]], axis=0).astype(BF)


def pack(first, first_other, second, second_other, table):
    return pl.pallas_call(
        pack_kernel, out_shape=shape((2048, 128), BF), compiler_params=VM, cost_estimate=cost(1), name="pack"
    )(first, first_other, second, second_other, table)


def add_kernel(got_ref, out_ref):
    total = got_ref[0].astype(F32)
    for i in range(1, 32):
        total = total + got_ref[i].astype(F32)
    out_ref[...] = jnp.broadcast_to(total.astype(BF)[None], (32, 64, 128))


def add(got):
    return pl.pallas_call(
        add_kernel, out_shape=shape((32, 64, 128), BF), compiler_params=VM, cost_estimate=cost(1), name="add"
    )(got)


def unpack_kernel(weight_scale, table_scale, in_ref, qkv_ref, proj_ref, upg_ref, down_ref, gain_ref, table_ref):
    def rows(start, stop):
        return in_ref[start:stop, :].astype(F32) * weight_scale

    for j in range(3):
        upg_ref[:, j * 128 : j * 128 + 128] = rows(j * 192, j * 192 + 192)
        down_ref[:, j * 128 : j * 128 + 128] = rows(576 + j * 192, 768 + j * 192)
    proj_ref[:, 0:128] = rows(1152, 1248)
    tail = rows(1248, 1296)
    proj_ref[0:48, 128:192] = tail[:, 0:64]
    proj_ref[48:96, 128:192] = tail[:, 64:128]
    first, second, third = rows(1296, 1488), rows(1488, 1680), rows(1680, 1728)
    qkv_ref[0] = first[:, 0:96]
    qkv_ref[1] = second[:, 0:96]
    qkv_ref[2, :, 0:32] = first[:, 96:128]
    qkv_ref[2, :, 32:64] = second[:, 96:128]
    for i in range(4):
        qkv_ref[2, i * 48 : i * 48 + 48, 64:96] = third[:, i * 32 : i * 32 + 32]
    table = in_ref[1728:2048, :].astype(F32)
    for r in range(12):
        for half in range(2):
            piece = table[r * 26 + half * 13 : r * 26 + half * 13 + 13] * table_scale
            for a in range(13):
                start = a * 256 + half * 128
                wide = min(128, 3312 - start)
                table_ref[r % 3, r // 3 : r // 3 + 1, start : start + wide] = piece[a : a + 1, 0:wide]
    gain_ref[...] = table[312:320] * weight_scale


def unpack(weight_scale, table_scale, got):
    return pl.pallas_call(
        functools.partial(unpack_kernel, weight_scale, table_scale),
        out_shape=(
            shape((3, 192, 96), F32),
            shape((96, 192), F32),
            shape((192, 384), F32),
            shape((192, 384), F32),
            shape((8, 128), F32),
            shape((3, 4, 3312), F32),
        ),
        compiler_params=VM,
        name="unpack",
    )(got)


def moved(value, band, sector, half):
    sizes = [lax.axis_size(name) for name in ("lat", "lon", "tp")]
    pairs = []
    for a in range(sizes[0]):
        for b in range(sizes[1]):
            for c in range(sizes[2]):
                source = ((a + band) % sizes[0], (b + sector) % sizes[1], (c + half) % sizes[2])
                pairs.append(tuple((x * sizes[1] + y) * sizes[2] + z for x, y, z in (source, (a, b, c))))
    return lax.ppermute(value, ("lat", "lon", "tp"), pairs)


def swapped(value, bit):
    pairs = [(a, a ^ bit) for a in range(lax.axis_size("lat"))]
    return lax.ppermute(value, "lat", pairs)


def shifted_parts(quarters):
    return (
        quarters[3],
        moved(quarters[2], 0, 1, 0),
        moved(quarters[1], 1, 0, 0),
        moved(quarters[0], 1, 1, 0),
    )


def local(
    inputs,
    residual_mid,
    grad_out,
    mask_ids,
    key_valid,
    bias_index,
    pos_bias,
    norm1_gain,
    qkv_weight,
    proj_weight,
    norm2_gain,
    fc1_weight,
    fc2_weight,
):
    levels, lat_cells, lon_cells, channels = inputs.shape
    cell_count = levels * lat_cells * lon_cells
    weight_scale = (cell_count * lax.axis_size("lat") * lax.axis_size("lon")) ** (-0.5)
    table_scale = (lon_cells * lax.axis_size("lon") // 12) ** (-0.5)
    gain1, gain2 = norm1_gain.reshape(1, -1), norm2_gain.reshape(1, -1)

    def turned(field):
        return field.transpose(1, 2, 0, 3)

    *x, part2, mid, up, first = head(
        turned(inputs), turned(residual_mid), turned(grad_out), gain2, fc1_weight, fc2_weight.T
    )
    other2 = moved(part2, 0, 0, 1)
    xw = shifted_parts(x)
    main, tail, lo, hi = gather(bias_index, pos_bias[0].transpose(1, 0, 2))
    code = mask_ids * 2 + (key_valid > 0).astype(jnp.int32)
    code = code.reshape(4, 2, 2, 3, 2, 6).transpose(0, 2, 4, 3, 5, 1).reshape(4, 1, 144)
    *gm, gain_two = middle(mid, up, part2, other2, gain2, lo)
    gw = shifted_parts(gm)
    first = both(first, swapped(first, 1))
    first_other = swapped(first, 2)
    low, q, k, v, prob, att = forward(xw, gain1, qkv_weight, main, tail, code)
    part1, score, grads = backward(gw, proj_weight, qkv_weight, low, q, k, v, prob, att)
    other1 = moved(part1, 0, 0, 1)
    table = scatter(score, lo, hi)
    *g, second = meet(part1, other1, xw, grads, gain_two)
    second = both(second, swapped(second, 1))
    second_other = swapped(second, 2)
    back = (moved(g[3], -1, -1, 0), moved(g[2], -1, 0, 0), moved(g[1], 0, -1, 0), g[0])
    sums = pack(first, first_other, second, second_other, table).reshape(32, 64, 128)
    got = lax.all_to_all(sums, "lon", 0, 0)
    got = lax.all_to_all(add(got), "lon", 0, 0)
    qkv_out, proj_out, up_out, down_out, gains, table_out = unpack(
        weight_scale, table_scale, got.reshape(2048, 128)
    )
    result = finish(x, gm, back, gain1).transpose(2, 0, 1, 3)
    share = channels // lax.axis_size("tp")
    start = lax.axis_index("tp") * share
    gains = gains[0:4].reshape(2, 256)[:, 0:channels]
    mine = lax.dynamic_slice_in_dim(gains, start, share, axis=1)
    return (result, qkv_out, proj_out, up_out, down_out.T, mine[0], mine[1], table_out.transpose(1, 0, 2)[None])


def solution(mesh):
    return jax.shard_map(
        local,
        mesh=mesh,
        in_specs=(
            P(None, "lat", "lon", None),
            P(None, "lat", "lon", None),
            P(None, "lat", "lon", None),
            P(None, "lat", "lon"),
            P(None, "lat", "lon"),
            P(),
            P("lat", None, "tp", None),
            P(),
            P(None, None, "tp"),
            P("tp", None),
            P(),
            P(None, "tp"),
            P("tp", None),
        ),
        out_specs=(
            P(None, "lat", "lon", None),
            P(None, None, "tp"),
            P("tp", None),
            P(None, "tp"),
            P("tp", None),
            P("tp"),
            P("tp"),
            P("lat", None, "tp", None),
        ),
        check_vma=False,
    )
```

time: 130 us -> 128 us (0.985)
  blocking collectives: 0 us -> 21.1 us
  Pallas kernels: 43.4 us -> 31.7 us
  starting transfers between devices: 42.5 us -> 33 us
  waiting for transfers between devices: 35.4 us -> 25.9 us
  local copies, waits for them, and re-layouts: 7.35 us -> 12.8 us
  other arithmetic: 0.01 us -> 1.7 us
    all_to_all x0 -> x1, blocking collectives: none -> 21.1 us  [local(): got = lax.all_to_all(sums, 'lon', 0, 0)]
    all_to_all x2 -> x1, waiting for transfers between devices: 20.2 us -> 0.01 us  [local(): got = lax.all_to_all(add(got), 'lon', 0, 0)]
    pallas_call x1, Pallas kernels: 20.8 us -> 8.87 us  [gather(): pl.pallas_call(gather_kernel, out_shape=(shape((12, 144, 128), F32), shap...]
    all_to_all x2 -> x1, starting transfers between devices: 14.8 us -> 5.89 us  [local(): got = lax.all_to_all(add(got), 'lon', 0, 0)]
    ppermute x11, starting transfers between devices: 27.7 us -> 21.8 us  [moved(): return lax.ppermute(value, ('lat', 'lon', 'tp'), pairs)]
    ppermute x11, waiting for transfers between devices: 15.2 us -> 20.7 us  [moved(): return lax.ppermute(value, ('lat', 'lon', 'tp'), pairs)]
    ppermute x0 -> x4, starting transfers between devices: none -> 5.24 us  [swapped(): return lax.ppermute(value, 'lat', pairs)]
    ppermute x0 -> x4, waiting for transfers between devices: none -> 5.22 us  [swapped(): return lax.ppermute(value, 'lat', pairs)]
  transfers between devices with their start and end apart: 13 -> 16, of which waited for: 4 -> 4; matrix products, arithmetic and copies ran while one was open for 1% -> 5% of each run, Pallas kernels for 25% -> 22%
where the time goes in v2:
time: 128 us; the launch traced here: 127 us
  starting transfers between devices  33 us (26%)
  Pallas kernels  31.7 us (25%)
  waiting for transfers between devices  25.9 us (20%)
  blocking collectives  21.1 us (16%)
  local copies, waits for them, and re-layouts  12.8 us (10%)
  other arithmetic  1.7 us (1%)
    ppermute x11, starting transfers between devices, moved(): return lax.ppermute(value, ('lat', 'lon', 'tp'), pairs)  21.8 us
    all_to_all x1, blocking collectives, local(): got = lax.all_to_all(sums, 'lon', 0, 0)  21.1 us
    ppermute x11, waiting for transfers between devices, moved(): return lax.ppermute(value, ('lat', 'lon', 'tp'), pairs)  20.7 us
    pallas_call x1, Pallas kernels, gather(): pl.pallas_call(gather_kernel, out_shape=(shape((12, 144, 128), F32), shap...  8.87 us
    unnamed x30, local copies, waits for them, and re-layouts  8.15 us
    pallas_call x1, Pallas kernels, backward(): pl.pallas_call(backward_kernel, out_shape=(shape((576, 192), BF), shape((...  7.32 us
    all_to_all x1, starting transfers between devices, local(): got = lax.all_to_all(add(got), 'lon', 0, 0)  5.89 us
    ppermute x4, starting transfers between devices, swapped(): return lax.ppermute(value, 'lat', pairs)  5.24 us
  transfers between devices with their start and end apart: 16, of which 4 were waited for; matrix products, arithmetic and copies ran while one was open for 5% of the time, Pallas kernels for 22%

profile of v2, /device:TPU:1, one launch (start us, length us, event | category | flops | bytes accessed | tf_op | source)
XLA Modules:
  0.0 127.0 jit_solution(5022005578208517555)
XLA Ops:
  0.6 0.0 copy-start.1
  0.7 1.0 copy-done.2
  1.7 1.0 copy-done.3
  2.6 1.0 copy-done.4
  3.6 0.9 copy-done.6
  4.5 0.9 copy-done.7
  5.4 0.7 copy-done.12
  6.1 1.4 %head.1 = (bf16[144,192]{1,0:T(8,128)(2,1)S(1)}, bf16[144,192]{1,0:T(8,128)(2,1)S(1)}, bf16[144,192]{1,0:T(8,128)(2,1)S(1)}, bf16[144,192]{1,0:T(8,128)(2,1)S(1)...) custom-call(bf16[6,12,8,192]{3,2,1,0:T(8,128)(2,1)S(1)} %bitcast.28,, ...), custom_call_target="tpu_custom_call" | custom-call | bytes 9000000 | tf_op jit(solution)/shard_map/head/pallas_call | solution.py:108
  7.5 2.2 %collective-permute-start = (bf16[576,192]{1,0:T(8,128)(2,1)S(1)}, bf16[576,192]{1,0:T(8,128)(2,1)S(1)}, u32[]{:S(2)}, u32[]{:S(2)}) collective-permute-start(bf16[576,192]{1,0:T(8,128)(2,1)S(1)} %get-tuple-element.51.own_ref), channel_id=1, source_target_pairs={{1,0},{0,1},{3,2},{2,3},{5,4},{4,5},{7,6},{6,7},{9,8},{8,9},{11,10... | collective-permute-start | bytes 663560 | tf_op jit(solution)/shard_map/ppermute | solution.py:493
  9.7 7.8 %collective-permute-start.4 = (bf16[144,192]{1,0:T(8,128)(2,1)S(1)}, bf16[144,192]{1,0:T(8,128)(2,1)S(1)}, u32[]{:S(2)}, u32[]{:S(2)}) collective-permute-start(bf16[144,192]{1,0:T(8,128)(2,1)S(1)} %get-tuple-element.47.x2), channel_id=1, source_target_pairs={{2,0},{3,1},{4,2},{5,3},{6,4},{7,5},{8,6},{9,7},{10,8},{11,9},{12,... | collective-permute-start | bytes 165896 | tf_op jit(solution)/shard_map/ppermute | solution.py:493
  17.4 1.2 collective-permute-start.5
  18.7 2.2 %collective-permute-start.6 = (bf16[144,192]{1,0:T(8,128)(2,1)S(1)}, bf16[144,192]{1,0:T(8,128)(2,1)S(1)}, u32[]{:S(2)}, u32[]{:S(2)}) collective-permute-start(bf16[144,192]{1,0:T(8,128)(2,1)S(1)} %get-tuple-element.45.x0), channel_id=1, source_target_pairs={{66,0},{67,1},{68,2},{69,3},{70,4},{71,5},{72,6},{73,7},{74,8},{75... | collective-permute-start | bytes 165896 | tf_op jit(solution)/shard_map/ppermute | solution.py:493
  20.9 1.1 collective-permute-start.11
  22.0 0.9 copy-done.5
  22.9 0.9 copy-done.8
  23.8 0.9 copy-done.9
  24.7 8.9 %gather.1 = (f32[12,144,128]{2,1,0:T(8,128)S(1)}, f32[12,144,128]{2,1,0:T(8,128)S(1)}, s32[168,128]{1,0:T(8,128)S(1)}, s32[168,128]{1,0:T(8,128)S(1)}) custom-call(s32[144,144]{1,0:T(8,128)S(1)} %copy-done.8, bf16[144,144]{1,0:T(8,128)(2,1)S(1)} %copy-done.9, f32[3,4,3312]{2,1,0:T(4,128)S(1)} %bitcast.31), custom_call_target="tpu_custom_call" | custom-call | bytes 30000000 | tf_op jit(solution)/shard_map/gather/pallas_call | solution.py:211
  33.6 0.6 middle.1
  34.1 0.3 collective-permute-start.1
  34.5 0.3 collective-permute-start.2
  34.7 0.6 collective-permute-start.3
  35.4 0.6 convert_add_fusion
  36.0 1.4 %reshape.39 = s32[4,2,2,3,2,6]{5,4,1,0,3,2:T(2,128)} reshape(s32[8,6,12]{2,0,1:T(8,128)} %convert_add_fusion) | data formatting | bytes 4608 | tf_op jit(solution)/shard_map/reshape | solution.py:541
  37.4 1.7 %copy.25 = s32[4,2,2,3,2,6]{0,1,5,3,4,2:T(2,128)} copy(s32[4,2,2,3,2,6]{5,4,1,0,3,2:T(2,128)} %reshape.39) | data formatting | bytes 4608 | tf_op jit(solution)/shard_map/reshape | solution.py:541
  39.1 1.0 copy.26.code_ref
  40.1 4.8 %forward.1 = (bf16[576,192]{1,0:T(8,128)(2,1)S(1)}, bf16[576,96]{1,0:T(8,128)(2,1)S(1)}, bf16[576,96]{1,0:T(8,128)(2,1)S(1)}, bf16[576,96]{1,0:T(8,128)(2,1)S(1)...) custom-call(bf16[144,192]{1,0:T(8,128)(2,1)S(1)} %get-tuple-element.48.x0.x3, ...), custom_call_target="tpu_custom_call" | custom-call | bytes 15000000 | tf_op jit(solution)/shard_map/forward/pallas_call | solution.py:260
  45.0 7.3 %backward.1 = (bf16[576,192]{1,0:T(8,128)(2,1)S(1)}, f32[12,168,128]{2,1,0:T(8,128)S(1)}, bf16[576,128]{1,0:T(8,128)(2,1)S(1)}) custom-call(bf16[144,192]{1,0:T(8,128)(2,1)S(1)} %get-tuple-element.56.g0.m3, bf16[144,192]{1,0:T(8,128)(2,1)S(1)} %collective-permute-done.1.g1, bf16[144,192]{1,0:T(8,128)(2,1)S(1)} %collective-permute-done.2.g2, ...), custom_call_target="tpu_custom_call" | custom-call | bytes 21000000 | tf_op jit(solution)/shard_map/backward/pallas_call | solution.py:327
  52.3 0.3 collective-permute-start.7
  52.6 8.3 %collective-permute-done.7.other_ref = bf16[576,192]{1,0:T(8,128)(2,1)S(1)} collective-permute-done((bf16[576,192]{1,0:T(8,128)(2,1)S(1)}, bf16[576,192]{1,0:T(8,128)(2,1)S(1)}, u32[]{:S(2)}, u32[]{:S(2)}) %collective-permute-start.7) | collective-permute-done | bytes 221216 | tf_op jit(solution)/shard_map/ppermute | solution.py:493
  60.9 0.3 meet.1
  61.2 1.0 collective-permute-start.13
  62.3 1.0 add_convert_fusion.first_ref
  63.3 2.7 %collective-permute-start.12 = (bf16[1152,128]{1,0:T(8,128)(2,1)S(1)}, bf16[1152,128]{1,0:T(8,128)(2,1)S(1)}, u32[]{:S(2)}, u32[]{:S(2)}) collective-permute-start(bf16[1152,128]{1,0:T(8,128)(2,1)S(1)} %add_convert_fusion.first_ref), channel_id=1, source_target_pairs={{0,128},{64,192},{128,0},{192,64},{1,129},{65,193},{129,1},{193,65... | collective-permute-start | bytes 884744 | tf_op jit(solution)/shard_map/ppermute | solution.py:498
  66.1 0.4 collective-permute-start.14
  66.5 5.0 %scatter.1.table_ref = f32[192,256]{1,0:T(8,128)S(1)} custom-call(f32[12,168,128]{2,1,0:T(8,128)S(1)} %get-tuple-element.74.score_ref, s32[168,128]{1,0:T(8,128)S(1)} %get-tuple-element.52.after_ref.lo_ref, s32[168,128]{1,0:T(8,128)S(1)} %get-tuple-element.75.hi_ref), custom_call_target="tpu_custom_call" | custom-call | bytes 15000000 | tf_op jit(solution)/shard_map/scatter/pallas_call | solution.py:361
  71.5 2.0 %collective-permute-done.12.first_other = bf16[1152,128]{1,0:T(8,128)(2,1)S(1)} collective-permute-done((bf16[1152,128]{1,0:T(8,128)(2,1)S(1)}, bf16[1152,128]{1,0:T(8,128)(2,1)S(1)}, u32[]{:S(2)}, u32[]{:S(2)}) %collective-permute-start.12) | collective-permute-done | bytes 294944 | tf_op jit(solution)/shard_map/ppermute | solution.py:498
  73.5 3.2 %collective-permute-done.14.second_other = bf16[592,128]{1,0:T(8,128)(2,1)S(1)} collective-permute-done((bf16[592,128]{1,0:T(8,128)(2,1)S(1)}, bf16[592,128]{1,0:T(8,128)(2,1)S(1)}, u32[]{:S(2)}, u32[]{:S(2)}) %collective-permute-start.14) | collective-permute-done | bytes 151584 | tf_op jit(solution)/shard_map/ppermute | solution.py:498
  76.8 0.1 pack.1
  76.9 21.1 %all_to_all.10.got_ref = bf16[32,64,128]{2,1,0:T(8,128)(2,1)S(1)} all-to-all(bf16[32,64,128]{2,1,0:T(8,128)(2,1)S(1)} %bitcast.26), channel_id=1, replica_groups=mesh['lat'=4,'lon'=32,'tp'=2] {'lon'}, dimensions={0} | all-to-all | bytes 1048576 | tf_op jit(solution)/shard_map/all_to_all | solution.py:555
  98.0 0.9 add.20
  98.9 5.9 %all-to-all-start.1 = ((bf16[32,64,128]{2,1,0:T(8,128)(2,1)}), bf16[32,64,128]{2,1,0:T(8,128)(2,1)S(1)}, u32[]{:S(2)}, u32[]{:S(2)}) async-start(bf16[32,64,128]{2,1,0:T(8,128)(2,1)} %add.20), calls=%async_computation.1 | async-start | bytes 1048576 | tf_op jit(solution)/shard_map/all_to_all | solution.py:556
  104.8 5.7 %collective-permute-start.8 = (bf16[144,192]{1,0:T(8,128)(2,1)S(1)}, bf16[144,192]{1,0:T(8,128)(2,1)S(1)}, u32[]{:S(2)}, u32[]{:S(2)}) collective-permute-start(bf16[144,192]{1,0:T(8,128)(2,1)S(1)} %get-tuple-element.68), channel_id=1, source_target_pairs={{254,0},{255,1},{192,2},{193,3},{194,4},{195,5},{196,6},{197,7},{1... | collective-permute-start | bytes 165896 | tf_op jit(solution)/shard_map/ppermute | solution.py:493
  110.5 1.2 collective-permute-start.10
  111.7 12.4 %collective-permute-done.8.g0 = bf16[144,192]{1,0:T(8,128)(2,1)S(1)} collective-permute-done((bf16[144,192]{1,0:T(8,128)(2,1)S(1)}, bf16[144,192]{1,0:T(8,128)(2,1)S(1)}, u32[]{:S(2)}, u32[]{:S(2)}) %collective-permute-start.8) | collective-permute-done | bytes 55328 | tf_op jit(solution)/shard_map/ppermute | solution.py:493
  124.1 1.2 finish.1
  125.3 1.1 unpack.1
  126.4 0.1 constant_dynamic-slice_fusion
  126.5 0.5 slice_bitcast_fusion
  (36 shorter events, 0.1 us)
Async XLA Ops:
  0.6 39.4 %copy-start.1 = (bf16[144,144]{1,0:T(8,128)(2,1)S(1)}, bf16[144,144]{1,0:T(8,128)(2,1)}, u32[]{:S(2)}) copy-start(bf16[144,144]{1,0:T(8,128)(2,1)} %constant.18.clone.order_ref) | copy-start | bytes 124420
  0.6 39.4 %copy-start = (bf16[3,192,96]{2,1,0:T(8,128)(2,1)S(1)}, bf16[3,192,96]{2,1,0:T(8,128)(2,1)}, u32[]{:S(2)}) copy-start(bf16[3,192,96]{2,1,0:T(8,128)(2,1)} %qkv_ref.3) | copy-start | bytes 331780
  0.7 1.0 copy-start.2
  1.7 1.0 copy-start.3
  2.6 1.0 copy-start.4
  3.6 0.9 copy-start.6
  4.5 0.9 copy-start.7
  5.4 0.7 copy-start.12
  6.1 29.3 %copy-start.13 = (s32[8,6,12]{2,0,1:T(8,128)S(1)}, s32[8,6,12]{2,0,1:T(8,128)}, u32[]{:S(2)}) copy-start(s32[8,6,12]{2,0,1:T(8,128)} %param.19) | copy-start | bytes 6916
  6.1 29.3 %copy-start.14 = (s32[8,6,12]{2,0,1:T(8,128)S(1)}, s32[8,6,12]{2,0,1:T(8,128)}, u32[]{:S(2)}) copy-start(s32[8,6,12]{2,0,1:T(8,128)} %param.20) | copy-start | bytes 6916
  6.1 34.0 %copy-start.11 = (f32[192]{0:T(256)S(1)}, f32[192]{0:T(256)}, u32[]{:S(2)}) copy-start(f32[192]{0:T(256)} %param.23) | copy-start | bytes 2308
  7.5 26.1 %collective-permute-start = (bf16[576,192]{1,0:T(8,128)(2,1)S(1)}, bf16[576,192]{1,0:T(8,128)(2,1)S(1)}, u32[]{:S(2)}, u32[]{:S(2)}) collective-permute-start(bf16[576,192]{1,0:T(8,128)(2,1)S(1)} %get-tuple-element.51.own_ref), channel_id=1, source_target_pairs={{1,0},{0,1},{3,2},{2,3},{5,4},{4,5},{7,6},{6,7},{9,8},{8,9},{11,10... | collective-permute-start | bytes 663560 | tf_op jit(solution)/shard_map/ppermute | solution.py:493
  9.7 24.8 %collective-permute-start.4 = (bf16[144,192]{1,0:T(8,128)(2,1)S(1)}, bf16[144,192]{1,0:T(8,128)(2,1)S(1)}, u32[]{:S(2)}, u32[]{:S(2)}) collective-permute-start(bf16[144,192]{1,0:T(8,128)(2,1)S(1)} %get-tuple-element.47.x2), channel_id=1, source_target_pairs={{2,0},{3,1},{4,2},{5,3},{6,4},{7,5},{8,6},{9,7},{10,8},{11,9},{12,... | collective-permute-start | bytes 165896 | tf_op jit(solution)/shard_map/ppermute | solution.py:493
  17.4 17.3 %collective-permute-start.5 = (bf16[144,192]{1,0:T(8,128)(2,1)S(1)}, bf16[144,192]{1,0:T(8,128)(2,1)S(1)}, u32[]{:S(2)}, u32[]{:S(2)}) collective-permute-start(bf16[144,192]{1,0:T(8,128)(2,1)S(1)} %get-tuple-element.46.x1), channel_id=1, source_target_pairs={{64,0},{65,1},{66,2},{67,3},{68,4},{69,5},{70,6},{71,7},{72,8},{73... | collective-permute-start | bytes 165896 | tf_op jit(solution)/shard_map/ppermute | solution.py:493
  18.7 21.4 %collective-permute-start.6 = (bf16[144,192]{1,0:T(8,128)(2,1)S(1)}, bf16[144,192]{1,0:T(8,128)(2,1)S(1)}, u32[]{:S(2)}, u32[]{:S(2)}) collective-permute-start(bf16[144,192]{1,0:T(8,128)(2,1)S(1)} %get-tuple-element.45.x0), channel_id=1, source_target_pairs={{66,0},{67,1},{68,2},{69,3},{70,4},{71,5},{72,6},{73,7},{74,8},{75... | collective-permute-start | bytes 165896 | tf_op jit(solution)/shard_map/ppermute | solution.py:493
  20.9 41.4 %collective-permute-start.11 = (bf16[1152,128]{1,0:T(8,128)(2,1)S(1)}, bf16[1152,128]{1,0:T(8,128)(2,1)}, u32[]{:S(2)}, u32[]{:S(2)}) collective-permute-start(bf16[1152,128]{1,0:T(8,128)(2,1)S(1)} %get-tuple-element.72), channel_id=1, source_target_pairs={{0,64},{64,0},{128,192},{192,128},{1,65},{65,1},{129,193},{193,129... | collective-permute-start | bytes 884744 | tf_op jit(solution)/shard_map/ppermute | solution.py:498
  22.0 0.9 copy-start.5
  22.9 0.9 copy-start.8
  23.8 0.9 copy-start.9
  33.6 11.4 %copy-start.10 = (bf16[96,192]{1,0:T(8,128)(2,1)S(1)}, bf16[96,192]{1,0:T(8,128)(2,1)}, u32[]{:S(2)}) copy-start(bf16[96,192]{1,0:T(8,128)(2,1)} %proj_ref.1) | copy-start | bytes 110596
  34.1 10.8 %collective-permute-start.1 = (bf16[144,192]{1,0:T(8,128)(2,1)S(1)}, bf16[144,192]{1,0:T(8,128)(2,1)S(1)}, u32[]{:S(2)}, u32[]{:S(2)}) collective-permute-start(bf16[144,192]{1,0:T(8,128)(2,1)S(1)} %get-tuple-element.55.m2), channel_id=1, source_target_pairs={{2,0},{3,1},{4,2},{5,3},{6,4},{7,5},{8,6},{9,7},{10,8},{11,9},{12,... | collective-permute-start | bytes 165896 | tf_op jit(solution)/shard_map/ppermute | solution.py:493
  34.5 10.5 %collective-permute-start.2 = (bf16[144,192]{1,0:T(8,128)(2,1)S(1)}, bf16[144,192]{1,0:T(8,128)(2,1)S(1)}, u32[]{:S(2)}, u32[]{:S(2)}) collective-permute-start(bf16[144,192]{1,0:T(8,128)(2,1)S(1)} %get-tuple-element.54.m1), channel_id=1, source_target_pairs={{64,0},{65,1},{66,2},{67,3},{68,4},{69,5},{70,6},{71,7},{72,8},{73... | collective-permute-start | bytes 165896 | tf_op jit(solution)/shard_map/ppermute | solution.py:493
  34.7 10.2 %collective-permute-start.3 = (bf16[144,192]{1,0:T(8,128)(2,1)S(1)}, bf16[144,192]{1,0:T(8,128)(2,1)S(1)}, u32[]{:S(2)}, u32[]{:S(2)}) collective-permute-start(bf16[144,192]{1,0:T(8,128)(2,1)S(1)} %get-tuple-element.53.m0), channel_id=1, source_target_pairs={{66,0},{67,1},{68,2},{69,3},{70,4},{71,5},{72,6},{73,7},{74,8},{75... | collective-permute-start | bytes 165896 | tf_op jit(solution)/shard_map/ppermute | solution.py:493
  52.3 8.6 %collective-permute-start.7 = (bf16[576,192]{1,0:T(8,128)(2,1)S(1)}, bf16[576,192]{1,0:T(8,128)(2,1)S(1)}, u32[]{:S(2)}, u32[]{:S(2)}) collective-permute-start(bf16[576,192]{1,0:T(8,128)(2,1)S(1)} %get-tuple-element.65.own_ref), channel_id=1, source_target_pairs={{1,0},{0,1},{3,2},{2,3},{5,4},{4,5},{7,6},{6,7},{9,8},{8,9},{11,10... | collective-permute-start | bytes 663560 | tf_op jit(solution)/shard_map/ppermute | solution.py:493
  61.2 4.8 %collective-permute-start.13 = (bf16[592,128]{1,0:T(8,128)(2,1)S(1)}, bf16[592,128]{1,0:T(8,128)(2,1)S(1)}, u32[]{:S(2)}, u32[]{:S(2)}) collective-permute-start(bf16[592,128]{1,0:T(8,128)(2,1)S(1)} %get-tuple-element.73), channel_id=1, source_target_pairs={{0,64},{64,0},{128,192},{192,128},{1,65},{65,1},{129,193},{193,129... | collective-permute-start | bytes 454664 | tf_op jit(solution)/shard_map/ppermute | solution.py:498
  63.3 10.2 %collective-permute-start.12 = (bf16[1152,128]{1,0:T(8,128)(2,1)S(1)}, bf16[1152,128]{1,0:T(8,128)(2,1)S(1)}, u32[]{:S(2)}, u32[]{:S(2)}) collective-permute-start(bf16[1152,128]{1,0:T(8,128)(2,1)S(1)} %add_convert_fusion.first_ref), channel_id=1, source_target_pairs={{0,128},{64,192},{128,0},{192,64},{1,129},{65,193},{129,1},{193,65... | collective-permute-start | bytes 884744 | tf_op jit(solution)/shard_map/ppermute | solution.py:498
  66.1 10.7 %collective-permute-start.14 = (bf16[592,128]{1,0:T(8,128)(2,1)S(1)}, bf16[592,128]{1,0:T(8,128)(2,1)S(1)}, u32[]{:S(2)}, u32[]{:S(2)}) collective-permute-start(bf16[592,128]{1,0:T(8,128)(2,1)S(1)} %add_convert_fusion.1.second_ref), channel_id=1, source_target_pairs={{0,128},{64,192},{128,0},{192,64},{1,129},{65,193},{129,1},{193,65... | collective-permute-start | bytes 454664 | tf_op jit(solution)/shard_map/ppermute | solution.py:498
  98.9 26.4 %all-to-all-start.1 = ((bf16[32,64,128]{2,1,0:T(8,128)(2,1)}), bf16[32,64,128]{2,1,0:T(8,128)(2,1)S(1)}, u32[]{:S(2)}, u32[]{:S(2)}) async-start(bf16[32,64,128]{2,1,0:T(8,128)(2,1)} %add.20), calls=%async_computation.1 | async-start | bytes 1048576 | tf_op jit(solution)/shard_map/all_to_all | solution.py:556
  104.8 19.3 %collective-permute-start.8 = (bf16[144,192]{1,0:T(8,128)(2,1)S(1)}, bf16[144,192]{1,0:T(8,128)(2,1)S(1)}, u32[]{:S(2)}, u32[]{:S(2)}) collective-permute-start(bf16[144,192]{1,0:T(8,128)(2,1)S(1)} %get-tuple-element.68), channel_id=1, source_target_pairs={{254,0},{255,1},{192,2},{193,3},{194,4},{195,5},{196,6},{197,7},{1... | collective-permute-start | bytes 165896 | tf_op jit(solution)/shard_map/ppermute | solution.py:493
  110.5 13.6 %collective-permute-start.9 = (bf16[144,192]{1,0:T(8,128)(2,1)S(1)}, bf16[144,192]{1,0:T(8,128)(2,1)S(1)}, u32[]{:S(2)}, u32[]{:S(2)}) collective-permute-start(bf16[144,192]{1,0:T(8,128)(2,1)S(1)} %get-tuple-element.69), channel_id=1, source_target_pairs={{192,0},{193,1},{194,2},{195,3},{196,4},{197,5},{198,6},{199,7},{2... | collective-permute-start | bytes 165896 | tf_op jit(solution)/shard_map/ppermute | solution.py:493
  110.5 13.6 %collective-permute-start.10 = (bf16[144,192]{1,0:T(8,128)(2,1)S(1)}, bf16[144,192]{1,0:T(8,128)(2,1)S(1)}, u32[]{:S(2)}, u32[]{:S(2)}) collective-permute-start(bf16[144,192]{1,0:T(8,128)(2,1)S(1)} %get-tuple-element.70), channel_id=1, source_target_pairs={{62,0},{63,1},{0,2},{1,3},{2,4},{3,5},{4,6},{5,7},{6,8},{7,9},{8,1... | collective-permute-start | bytes 165896 | tf_op jit(solution)/shard_map/ppermute | solution.py:493

commit v3 on v2

--- a/solution.py
+++ b/solution.py
@@ -15,11 +15,13 @@
 F32 = jnp.float32
 I32 = jnp.int32
 VMEM = pl.BlockSpec(memory_space=pltpu.VMEM)
-VM = pltpu.CompilerParams(vmem_limit_bytes=48 * 1024 * 1024)
+VM = pltpu.CompilerParams(vmem_limit_bytes=24 * 1024 * 1024)
+ALL = pltpu.CompilerParams(vmem_limit_bytes=63 * 1024 * 1024)
+ANY = pl.BlockSpec(memory_space=pl.ANY)
 
 
 def cost(microseconds):
-    return pl.CostEstimate(flops=0, bytes_accessed=int(microseconds * 3000000), transcendentals=0)
+    return pl.CostEstimate(flops=int(microseconds * 1e9), bytes_accessed=0, transcendentals=0)
 
 
 def shape(dims, kind):
@@ -75,65 +77,91 @@
     return jnp.asarray(order, BF)
 
 
-def to_windows(parts, order, scratch):
+def to_windows(parts, start, order, scratch):
     for s in range(4):
-        rows = dot_nn(order, parts[s][...])
+        rows = dot_nn(order, parts[s][start : start + 144, :])
         for w in range(4):
             scratch[w * 144 + s * 36 : w * 144 + s * 36 + 36, :] = rows[w * 36 : w * 36 + 36]
 
 
-def head_kernel(x_ref, mid_ref, up_ref, gain_ref, fc1_ref, fc2_ref,
-                o0, o1, o2, o3, part_ref, midq_ref, upq_ref, grads_ref, scratch, mid_s, up_s):
-    to_quarters(x_ref, scratch)
-    for q, out in enumerate((o0, o1, o2, o3)):
-        out[...] = scratch[q * 144 : q * 144 + 144, :].astype(BF)
+def head_kernel(mid_hbm, up_hbm, gain_hbm, fc1_hbm, fc2_hbm, part_hbm, grads_hbm,
+                mid_ref, up_ref, gain_ref, fc1_ref, fc2_ref, part_ref, grads_ref, mid_s, up_s, sem):
+    pairs = ((mid_hbm, mid_ref), (gain_hbm, gain_ref), (fc1_hbm, fc1_ref), (up_hbm, up_ref), (fc2_hbm, fc2_ref))
+    copies = [pltpu.make_async_copy(a, b, sem.at[i]) for i, (a, b) in enumerate(pairs)]
+    for copy in copies:
+        copy.start()
+    for copy in copies[:3]:
+        copy.wait()
     to_quarters(mid_ref, mid_s)
-    to_quarters(up_ref, up_s)
-    mid = mid_s[...]
-    up = up_s[...].astype(BF)
-    midq_ref[...] = mid.astype(BF)
-    upq_ref[...] = up
-    normed, _ = layer_stats(mid)
+    normed, _ = layer_stats(mid_s[...])
     lowered = (normed * gain_ref[...]).astype(BF)
     pre = dot_nn(lowered, fc1_ref[...])
     active, slopes = gelu_pair(pre)
+    for copy in copies[3:]:
+        copy.wait()
+    to_quarters(up_ref, up_s)
+    up = up_s[...].astype(BF)
     grad_pre = (dot_nn(up, fc2_ref[...]) * slopes).astype(BF)
     part_ref[...] = dot_nt(grad_pre, fc1_ref[...]).astype(BF)
+    part_copy = pltpu.make_async_copy(part_ref, part_hbm, sem.at[5])
+    part_copy.start()
     for start, grads in ((0, dot_tn(lowered, grad_pre)), (576, dot_tn(up, active.astype(BF)))):
         for j in range(3):
             grads_ref[start + j * 192 : start + j * 192 + 192, :] = grads[:, j * 128 : j * 128 + 128].astype(BF)
-
-
-def head(x, mid, up, gain, fc1, fc2):
+    grads_copy = pltpu.make_async_copy(grads_ref, grads_hbm, sem.at[6])
+    grads_copy.start()
+    part_copy.wait()
+    grads_copy.wait()
+
+
+def head(mid, up, gain, fc1, fc2):
     return pl.pallas_call(
         head_kernel,
-        out_shape=tuple(shape((144, 192), BF) for _ in range(4))
-        + (shape((576, 192), BF), shape((576, 192), BF), shape((576, 192), BF), shape((1152, 128), BF)),
-        scratch_shapes=[pltpu.VMEM((576, 192), F32)] * 3,
-        compiler_params=VM,
+        out_shape=(shape((576, 192), BF), shape((1152, 128), BF)),
+        in_specs=[ANY] * 5,
+        out_specs=(ANY, ANY),
+        scratch_shapes=[
+            pltpu.VMEM((6, 12, 8, 192), BF),
+            pltpu.VMEM((6, 12, 8, 192), BF),
+            pltpu.VMEM((1, 192), F32),
+            pltpu.VMEM((192, 384), BF),
+            pltpu.VMEM((192, 384), BF),
+            pltpu.VMEM((576, 192), BF),
+            pltpu.VMEM((1152, 128), BF),
+            pltpu.VMEM((576, 192), F32),
+            pltpu.VMEM((576, 192), F32),
+            pltpu.SemaphoreType.DMA((7,)),
+        ],
+        compiler_params=ALL,
         cost_estimate=cost(3),
         name="head",
-    )(x, mid, up, gain, fc1, fc2)
-
-
-def middle_kernel(mid_ref, up_ref, own_ref, other_ref, gain_ref, after_ref, o0, o1, o2, o3, gain_out):
-    normed, inverse = layer_stats(mid_ref[...].astype(F32))
+    )(mid, up, gain, fc1, fc2)
+
+
+def middle_kernel(x_ref, mid_ref, up_ref, own_ref, other_ref, gain_ref, after_ref,
+                  o0, o1, o2, o3, gain_out, x_s, mid_s, up_s):
+    to_quarters(x_ref, x_s)
+    to_quarters(mid_ref, mid_s)
+    to_quarters(up_ref, up_s)
+    normed, inverse = layer_stats(mid_s[...])
     grad = own_ref[...].astype(F32) + other_ref[...].astype(F32)
     gain_out[...] = jnp.sum(grad * normed, axis=0, keepdims=True)
-    out = up_ref[...].astype(F32) + norm_backward(grad, gain_ref[...], normed, inverse)
+    out = up_s[...] + norm_backward(grad, gain_ref[...], normed, inverse)
     for q, o in enumerate((o0, o1, o2, o3)):
-        o[...] = out[q * 144 : q * 144 + 144].astype(BF)
-
-
-def middle(mid, up, own, other, gain, after):
+        o[0:144, :] = x_s[q * 144 : q * 144 + 144, :].astype(BF)
+        o[144:288, :] = out[q * 144 : q * 144 + 144].astype(BF)
+
+
+def middle(x, mid, up, own, other, gain, after):
     return pl.pallas_call(
         middle_kernel,
-        out_shape=tuple(shape((144, 192), BF) for _ in range(4)) + (shape((1, 192), F32),),
-        in_specs=[VMEM] * 5 + [pl.BlockSpec(memory_space=pl.ANY)],
+        out_shape=tuple(shape((288, 192), BF) for _ in range(4)) + (shape((1, 192), F32),),
+        in_specs=[VMEM] * 6 + [ANY],
+        scratch_shapes=[pltpu.VMEM((576, 192), F32)] * 3,
         compiler_params=VM,
         cost_estimate=cost(1),
         name="middle",
-    )(mid, up, own, other, gain, after)
+    )(x, mid, up, own, other, gain, after)
 
 
 def window_order():
@@ -153,10 +181,38 @@
 
 
 def one_hot(low):
-    return (lax.broadcasted_iota(I32, (256, 128), 0) == low).astype(F32).astype(BF)
-
-
-def gather_kernel(index_ref, order_ref, bias_ref, main_ref, tail_ref, lo_ref, hi_ref, table, stage):
+    rows = lax.broadcasted_iota(I32, (256, 128), 0).astype(F32).astype(BF)
+    return jnp.where(rows == low.astype(F32).astype(BF), jnp.ones((), BF), jnp.zeros((), BF))
+
+
+def look_up(terms, lo_ref, hi_ref, stage, first_block, steps):
+    half = (lax.broadcasted_iota(I32, (8, 128), 0) >> 2)
+
+    def step(i, _):
+        for pair in range(9):
+            base = first_block + i * 18 + pair * 2
+            hot = jnp.concatenate([one_hot(lo_ref[pl.ds(base + j, 1), :]) for j in range(2)], axis=1)
+            found = dot_nn(terms, jnp.concatenate([hot, hot], axis=0))
+            for j in range(2):
+                cols = slice(j * 128, j * 128 + 128)
+                high = hi_ref[pl.ds(base + j, 1), :]
+                first = jnp.zeros((8, 128), F32)
+                for c in range(13):
+                    first = jnp.where(high == c, found[c * 8 : c * 8 + 8, cols], first)
+                second = jnp.zeros((8, 128), F32)
+                shifted = high - half
+                for c in range(7):
+                    second = jnp.where(shifted == 2 * c, found[104 + c * 8 : 112 + c * 8, cols], second)
+                start = pl.multiple_of((base + j - first_block) * 16, 16)
+                stage[pl.ds(start, 8), :] = first
+                stage[pl.ds(start + 8, 8), :] = second + pltpu.roll(second, 4, 0)
+        return 0
+
+    lax.fori_loop(0, steps, step, 0)
+
+
+def gather_first_kernel(index_ref, order_ref, bias_ref, ids_ref, valid_ref,
+                        stage, lo_ref, hi_ref, terms_ref, code_ref, table):
     index = index_ref[...]
     order = order_ref[...]
     pieces = []
@@ -175,57 +231,63 @@
             row = c * 8 + r if r < 8 else 104 + (c // 2) * 8 + (c % 2) * 4 + r - 8
             table[row : row + 1, 0:wide] = line[:, c * 256 : c * 256 + wide]
     upper = table[...].astype(BF)
-    lower = (table[...] - upper.astype(F32)).astype(BF)
-    terms = jnp.concatenate([upper, lower], axis=1)
-    half = (lax.broadcasted_iota(I32, (8, 128), 0) >> 2)
-
-    def step(i, _):
-        for pair in range(9):
-            hot = jnp.concatenate([one_hot(lo_ref[pl.ds(i * 18 + pair * 2 + j, 1), :]) for j in range(2)], axis=1)
-            found = dot_nn(terms, jnp.concatenate([hot, hot], axis=0))
-            for j in range(2):
-                block = i * 18 + pair * 2 + j
-                cols = slice(j * 128, j * 128 + 128)
-                high = hi_ref[pl.ds(block, 1), :]
-                first = jnp.zeros((8, 128), F32)
-                for c in range(13):
-                    first = jnp.where(high == c, found[c * 8 : c * 8 + 8, cols], first)
-                second = jnp.zeros((8, 128), F32)
-                shifted = high - half
-                for c in range(7):
-                    second = jnp.where(shifted == 2 * c, found[104 + c * 8 : 112 + c * 8, cols], second)
-                start = pl.multiple_of(block * 16, 16)
-                stage[pl.ds(start, 8), :] = first
-                stage[pl.ds(start + 8, 8), :] = second + pltpu.roll(second, 4, 0)
-        return 0
-
-    lax.fori_loop(0, 9, step, 0)
+    terms_ref[:, 0:256] = upper
+    terms_ref[:, 256:512] = (table[...] - upper.astype(F32)).astype(BF)
+    code = (ids_ref[...] * 2 + (valid_ref[...] > 0).astype(I32)).astype(F32).reshape(48, 12).astype(BF)
+    row = lax.broadcasted_iota(I32, (24, 48), 0)
+    column = lax.broadcasted_iota(I32, (24, 48), 1)
+    lines = []
+    for level in range(2):
+        pick = ((row >> 2) * 8 + (row & 3) * 2 + level) == column
+        picked = dot_nn(pick.astype(F32).astype(BF), code)
+        lines += [picked[lat * 4 : lat * 4 + 4] for lat in range(6)]
+    lines = jnp.concatenate(lines, axis=1)
+    code_ref[...] = dot_nt(lines.astype(BF), order)
+    look_up(terms_ref[...], lo_ref, hi_ref, stage, 0, 5)
+
+
+def gather_first(index, bias, ids, valid):
+    return pl.pallas_call(
+        gather_first_kernel,
+        out_shape=(
+            shape((90 * 16, 128), F32),
+            shape((168, 128), I32),
+            shape((168, 128), I32),
+            shape((160, 512), BF),
+            shape((4, 144), F32),
+        ),
+        scratch_shapes=[pltpu.VMEM((160, 256), F32)],
+        compiler_params=VM,
+        cost_estimate=cost(6),
+        name="gather_first",
+    )(index, jnp.asarray(window_order(), BF), bias, ids, valid)
+
+
+def gather_second_kernel(first_stage, lo_ref, hi_ref, terms_ref, after_ref, main_ref, tail_ref, stage):
+    look_up(terms_ref[...], lo_ref, hi_ref, stage, 90, 4)
     for r in range(12):
-        main_ref[r] = stage[pl.ds(r, 144, stride=16), :]
-        packed = stage[pl.ds(144 * 16 + r, 18, stride=16), :]
+        main_ref[r, 0:90, :] = first_stage[pl.ds(r, 90, stride=16), :]
+        main_ref[r, 90:144, :] = stage[pl.ds(r, 54, stride=16), :]
+        packed = stage[pl.ds(54 * 16 + r, 18, stride=16), :]
         for s in range(8):
             tail_ref[r, pl.ds(s, 18, stride=8), :] = pltpu.roll(packed, 128 - 16 * s, 1) if s else packed
 
 
-def gather(index, bias):
-    return pl.pallas_call(
-        gather_kernel,
-        out_shape=(
-            shape((12, 144, 128), F32),
-            shape((12, 144, 128), F32),
-            shape((168, 128), I32),
-            shape((168, 128), I32),
-        ),
-        scratch_shapes=[pltpu.VMEM((160, 256), F32), pltpu.VMEM((162 * 16, 128), F32)],
-        compiler_params=VM,
-        cost_estimate=cost(10),
-        name="gather",
-    )(index, jnp.asarray(window_order(), BF), bias)
+def gather_second(first_stage, lo, hi, terms, after):
+    return pl.pallas_call(
+        gather_second_kernel,
+        out_shape=(shape((12, 144, 128), F32), shape((12, 144, 128), F32)),
+        in_specs=[VMEM] * 4 + [ANY],
+        scratch_shapes=[pltpu.VMEM((72 * 16, 128), F32)],
+        compiler_params=VM,
+        cost_estimate=cost(4),
+        name="gather_second",
+    )(first_stage, lo, hi, terms, after)
 
 
 def forward_kernel(x0, x1, x2, x3, order_ref, gain_ref, qkv_ref, main_ref, tail_ref, code_ref,
                    low_ref, q_ref, k_ref, v_ref, prob_ref, att_ref, scratch):
-    to_windows((x0, x1, x2, x3), order_ref[...], scratch)
+    to_windows((x0, x1, x2, x3), 0, order_ref[...], scratch)
     normed, _ = layer_stats(scratch[...])
     low = (normed * gain_ref[...]).astype(BF)
     low_ref[...] = low
@@ -235,7 +297,7 @@
 
     def window(w, _):
         rows = pl.ds(pl.multiple_of(w * 144, 16), 144)
-        code = code_ref[w]
+        code = code_ref[pl.ds(w, 1), :].astype(I32)
         label = code >> 1
         column = jnp.sum(jnp.where(eye, label, 0), axis=1, keepdims=True)
         allowed = eye | ((column == label) & ((code & 1) > 0))
@@ -276,7 +338,7 @@
 
 def backward_kernel(g0, g1, g2, g3, order_ref, proj_ref, qkv_ref, low_ref, q_ref, k_ref, v_ref, prob_ref, att_ref,
                     part_ref, score_ref, grads_ref, scratch, gatt, gcols):
-    to_windows((g0, g1, g2, g3), order_ref[...], scratch)
+    to_windows((g0, g1, g2, g3), 144, order_ref[...], scratch)
     grad = scratch[...].astype(BF)
     gproj = dot_tn(att_ref[...], grad).astype(BF)
     grads_ref[0:96, :] = gproj[:, 0:128]
@@ -363,81 +425,87 @@
     )(score, lo, hi)
 
 
-def meet_kernel(own_ref, other_ref, x0, x1, x2, x3, grads_ref, two_ref, o0, o1, o2, o3, out_ref):
+def meet_kernel(own_ref, other_ref, x0, x1, x2, x3, first_ref, second_ref, table_ref, two_ref,
+                o0, o1, o2, o3, out_ref):
     gain = jnp.zeros((1, 192), F32)
     for s, (x, o) in enumerate(zip((x0, x1, x2, x3), (o0, o1, o2, o3))):
         rows = slice(s * 144, s * 144 + 144)
         grad = own_ref[rows, :].astype(F32) + other_ref[rows, :].astype(F32)
-        normed, _ = layer_stats(x[...].astype(F32))
+        normed, _ = layer_stats(x[0:144, :].astype(F32))
         gain = gain + jnp.sum(grad * normed, axis=0, keepdims=True)
         o[...] = grad.astype(BF)
-    out_ref[0:576, :] = grads_ref[...]
-    none = jnp.zeros((1, 64), F32)
-    rows = []
-    for line in (gain, two_ref[...]):
-        rows += [line[:, 0:128], jnp.concatenate([line[:, 128:192], none], axis=1)]
-    out_ref[576:592, :] = jnp.concatenate(rows + [jnp.zeros((12, 128), F32)], axis=0).astype(BF)
-
-
-def meet(own, other, x, grads, two):
-    return pl.pallas_call(
-        meet_kernel,
-        out_shape=tuple(shape((144, 192), BF) for _ in range(4)) + (shape((592, 128), BF),),
-        compiler_params=VM,
-        name="meet",
-    )(own, other, *x, grads, two)
-
-
-def finish_kernel(x0, x1, x2, x3, m0, m1, m2, m3, g0, g1, g2, g3, gain_ref, out_ref):
-    for q, (x, m, g) in enumerate(zip((x0, x1, x2, x3), (m0, m1, m2, m3), (g0, g1, g2, g3))):
-        normed, inverse = layer_stats(x[...].astype(F32))
-        rows = m[...].astype(F32) + norm_backward(g[...].astype(F32), gain_ref[...], normed, inverse)
-        for lat in range(3):
-            piece = rows[lat * 48 : lat * 48 + 48].reshape(6, 8, 192)
-            out_ref[(q // 2) * 3 + lat, (q % 2) * 6 : (q % 2) * 6 + 6] = piece.astype(BF)
-
-
-def finish(x, m, g, gain):
-    return pl.pallas_call(
-        finish_kernel, out_shape=shape((6, 12, 8, 192), BF), compiler_params=VM, name="finish"
-    )(*x, *m, *g, gain)
-
-
-def both(own, other):
-    return (own.astype(F32) + other.astype(F32)).astype(BF)
-
-
-def pack_kernel(first_ref, first_other, second_ref, second_other, table_ref, out_ref):
-    out_ref[0:1152, :] = both(first_ref[...], first_other[...])
-    second = second_ref[...].astype(F32) + second_other[...].astype(F32)
-    out_ref[1152:1728, :] = second[0:576].astype(BF)
+    out_ref[0:1152, :] = first_ref[...]
+    out_ref[1152:1728, :] = second_ref[...]
     rows = []
     for r in range(12):
         pair = table_ref[r * 16 : r * 16 + 13, :]
         rows += [pair[:, 0:128], pair[:, 128:256]]
-    out_ref[1728:2048, :] = jnp.concatenate(rows + [second[576:584]], axis=0).astype(BF)
-
-
-def pack(first, first_other, second, second_other, table):
-    return pl.pallas_call(
-        pack_kernel, out_shape=shape((2048, 128), BF), compiler_params=VM, cost_estimate=cost(1), name="pack"
-    )(first, first_other, second, second_other, table)
+    none = jnp.zeros((1, 64), F32)
+    for line in (gain, two_ref[...]):
+        rows += [line[:, 0:128], jnp.concatenate([line[:, 128:192], none], axis=1)]
+    rows += [jnp.zeros((4, 128), F32)]
+    out_ref[1728:2048, :] = jnp.concatenate(rows, axis=0).astype(BF)
+
+
+def meet(own, other, x, first, second, table, two):
+    return pl.pallas_call(
+        meet_kernel,
+        out_shape=tuple(shape((144, 192), BF) for _ in range(4)) + (shape((2048, 128), BF),),
+        compiler_params=VM,
+        cost_estimate=cost(1),
+        name="meet",
+    )(own, other, *x, first, second, table, two)
+
+
+def finish_kernel(x0, x1, x2, x3, g0, g1, g2, g3, gain_ref, out_ref):
+    for q, (x, g) in enumerate(zip((x0, x1, x2, x3), (g0, g1, g2, g3))):
+        normed, inverse = layer_stats(x[0:144, :].astype(F32))
+        rows = x[144:288, :].astype(F32) + norm_backward(g[...].astype(F32), gain_ref[...], normed, inverse)
+        for lat in range(3):
+            piece = rows[lat * 48 : lat * 48 + 48].reshape(6, 8, 192)
+            out_ref[(q // 2) * 3 + lat, (q % 2) * 6 : (q % 2) * 6 + 6] = piece.astype(BF)
+
+
+def finish(x, g, gain):
+    return pl.pallas_call(
+        finish_kernel, out_shape=shape((6, 12, 8, 192), BF), compiler_params=VM, cost_estimate=cost(1), name="finish"
+    )(*x, *g, gain)
 
 
 def add_kernel(got_ref, out_ref):
     total = got_ref[0].astype(F32)
     for i in range(1, 32):
         total = total + got_ref[i].astype(F32)
-    out_ref[...] = jnp.broadcast_to(total.astype(BF)[None], (32, 64, 128))
+    out_ref[...] = total.astype(BF)
 
 
 def add(got):
     return pl.pallas_call(
-        add_kernel, out_shape=shape((32, 64, 128), BF), compiler_params=VM, cost_estimate=cost(1), name="add"
+        add_kernel, out_shape=shape((64, 128), BF), compiler_params=VM, cost_estimate=cost(1), name="add"
     )(got)
 
 
-def unpack_kernel(weight_scale, table_scale, in_ref, qkv_ref, proj_ref, upg_ref, down_ref, gain_ref, table_ref):
+def spread_kernel(place_ref, own_ref, a_ref, b_ref, c_ref, out_ref):
+    own = own_ref[...].astype(F32)
+    total = own + a_ref[...].astype(F32) + b_ref[...].astype(F32) + c_ref[...].astype(F32)
+    row = place_ref[0] * 64 + lax.broadcasted_iota(I32, (64, 128), 0)
+    table = (row >= 1728) & (row < 2040)
+    out_ref[...] = jnp.broadcast_to(jnp.where(table, own, total).astype(BF)[None], (32, 64, 128))
+
+
+def spread(place, own, a, b, c):
+    return pl.pallas_call(
+        spread_kernel,
+        out_shape=shape((32, 64, 128), BF),
+        in_specs=[pl.BlockSpec(memory_space=pltpu.SMEM)] + [VMEM] * 4,
+        compiler_params=VM,
+        cost_estimate=cost(1),
+        name="spread",
+    )(place, own, a, b, c)
+
+
+def unpack_kernel(weight_scale, table_scale, half_ref, in_ref,
+                  qkv_ref, proj_ref, upg_ref, down_ref, one_ref, two_ref, table_ref):
     def rows(start, stop):
         return in_ref[start:stop, :].astype(F32) * weight_scale
 
@@ -463,10 +531,13 @@
                 start = a * 256 + half * 128
                 wide = min(128, 3312 - start)
                 table_ref[r % 3, r // 3 : r // 3 + 1, start : start + wide] = piece[a : a + 1, 0:wide]
-    gain_ref[...] = table[312:320] * weight_scale
-
-
-def unpack(weight_scale, table_scale, got):
+    for start, out in ((312, one_ref), (314, two_ref)):
+        line = table[start : start + 1]
+        upper = jnp.concatenate([line[:, 96:128], table[start + 1 : start + 2, 0:64]], axis=1)
+        out[...] = jnp.where(half_ref[0] == 0, line[:, 0:96], upper) * weight_scale
+
+
+def unpack(weight_scale, table_scale, half, got):
     return pl.pallas_call(
         functools.partial(unpack_kernel, weight_scale, table_scale),
         out_shape=(
@@ -474,12 +545,14 @@
             shape((96, 192), F32),
             shape((192, 384), F32),
             shape((192, 384), F32),
-            shape((8, 128), F32),
+            shape((1, 96), F32),
+            shape((1, 96), F32),
             shape((3, 4, 3312), F32),
         ),
+        in_specs=[pl.BlockSpec(memory_space=pltpu.SMEM), VMEM],
         compiler_params=VM,
         name="unpack",
-    )(got)
+    )(half, got)
 
 
 def moved(value, band, sector, half):
@@ -531,38 +604,39 @@
     def turned(field):
         return field.transpose(1, 2, 0, 3)
 
-    *x, part2, mid, up, first = head(
-        turned(inputs), turned(residual_mid), turned(grad_out), gain2, fc1_weight, fc2_weight.T
+    x_in, mid_in, up_in = turned(inputs), turned(residual_mid), turned(grad_out)
+    part2, first = head(mid_in, up_in, gain2, fc1_weight, fc2_weight.T)
+    other2 = moved(part2, 0, 0, 1)
+    stage, lo, hi, terms, code = gather_first(
+        bias_index, pos_bias[0].transpose(1, 0, 2), mask_ids.transpose(1, 0, 2), key_valid.transpose(1, 0, 2)
     )
-    other2 = moved(part2, 0, 0, 1)
+    *x, gain_two = middle(x_in, mid_in, up_in, part2, other2, gain2, lo)
     xw = shifted_parts(x)
-    main, tail, lo, hi = gather(bias_index, pos_bias[0].transpose(1, 0, 2))
-    code = mask_ids * 2 + (key_valid > 0).astype(jnp.int32)
-    code = code.reshape(4, 2, 2, 3, 2, 6).transpose(0, 2, 4, 3, 5, 1).reshape(4, 1, 144)
-    *gm, gain_two = middle(mid, up, part2, other2, gain2, lo)
-    gw = shifted_parts(gm)
-    first = both(first, swapped(first, 1))
-    first_other = swapped(first, 2)
+    main, tail = gather_second(stage, lo, hi, terms, gain_two)
     low, q, k, v, prob, att = forward(xw, gain1, qkv_weight, main, tail, code)
-    part1, score, grads = backward(gw, proj_weight, qkv_weight, low, q, k, v, prob, att)
+    part1, score, second = backward(xw, proj_weight, qkv_weight, low, q, k, v, prob, att)
     other1 = moved(part1, 0, 0, 1)
     table = scatter(score, lo, hi)
-    *g, second = meet(part1, other1, xw, grads, gain_two)
-    second = both(second, swapped(second, 1))
-    second_other = swapped(second, 2)
+    *g, sums = meet(part1, other1, xw, first, second, table, gain_two)
     back = (moved(g[3], -1, -1, 0), moved(g[2], -1, 0, 0), moved(g[1], 0, -1, 0), g[0])
-    sums = pack(first, first_other, second, second_other, table).reshape(32, 64, 128)
-    got = lax.all_to_all(sums, "lon", 0, 0)
-    got = lax.all_to_all(add(got), "lon", 0, 0)
-    qkv_out, proj_out, up_out, down_out, gains, table_out = unpack(
-        weight_scale, table_scale, got.reshape(2048, 128)
+    own = add(lax.all_to_all(sums.reshape(32, 64, 128), "lon", 0, 0))
+    place = lax.axis_index("lon").reshape(1)
+    totals = spread(place, own, swapped(own, 1), swapped(own, 2), swapped(own, 3))
+    got = lax.all_to_all(totals, "lon", 0, 0)
+    qkv_out, proj_out, up_out, down_out, one, two, table_out = unpack(
+        weight_scale, table_scale, lax.axis_index("tp").reshape(1), got.reshape(2048, 128)
     )
-    result = finish(x, gm, back, gain1).transpose(2, 0, 1, 3)
-    share = channels // lax.axis_size("tp")
-    start = lax.axis_index("tp") * share
-    gains = gains[0:4].reshape(2, 256)[:, 0:channels]
-    mine = lax.dynamic_slice_in_dim(gains, start, share, axis=1)
-    return (result, qkv_out, proj_out, up_out, down_out.T, mine[0], mine[1], table_out.transpose(1, 0, 2)[None])
+    result = finish(x, back, gain1).transpose(2, 0, 1, 3)
+    return (
+        result,
+        qkv_out,
+        proj_out,
+        up_out,
+        down_out.T,
+        one.reshape(channels // lax.axis_size("tp")),
+        two.reshape(channels // lax.axis_size("tp")),
+        table_out.transpose(1, 0, 2)[None],
+    )
 
 
 def solution(mesh):

time: 128 us -> 110 us (0.86)
  local copies, waits for them, and re-layouts: 12.8 us -> 0.07 us
  starting transfers between devices: 33 us -> 28.5 us
  other arithmetic: 1.7 us -> 0 us
    unnamed x30, local copies, waits for them, and re-layouts: 8.15 us -> 0.07 us
    reshape x4 -> x0, local copies, waits for them, and re-layouts: 4.09 us -> none  [the longest x3 4.08 us: local(): code.reshape(4, 2, 2, 3, 2, 6).transpose(0, 2, 4, 3, 5, 1)]
    ppermute x11 -> x8, starting transfers between devices: 21.8 us -> 19.5 us  [moved(): return lax.ppermute(value, ('lat', 'lon', 'tp'), pairs)]
    all_to_all x1, starting transfers between devices: 5.89 us -> 4.31 us  [local(): got = lax.all_to_all(totals, 'lon', 0, 0)]
    ppermute x11 -> x8, waiting for transfers between devices: 20.7 us -> 22.3 us  [moved(): return lax.ppermute(value, ('lat', 'lon', 'tp'), pairs)]
    ppermute x4 -> x3, waiting for transfers between devices: 5.22 us -> 3.86 us  [swapped(): return lax.ppermute(value, 'lat', pairs)]
    ppermute x4 -> x3, starting transfers between devices: 5.24 us -> 4.62 us  [swapped(): return lax.ppermute(value, 'lat', pairs)]
    pallas_call x5 -> x6, Pallas kernels: 11.8 us -> 11.9 us  [the longest x1 3.92 us: gather_first(): pl.pallas_call(gather_first_kernel, out_shape=(shape((90 * 16, 128), F32)...]
  transfers between devices with their start and end apart: 16 -> 12, of which waited for: 4 -> 7; matrix products, arithmetic and copies ran while one was open for 5% -> 0% of each run, Pallas kernels for 22% -> 12%
where the time goes in v3:
time: 110 us
  Pallas kernels  31.7 us (29%)
  starting transfers between devices  28.5 us (26%)
  waiting for transfers between devices  26.1 us (24%)
  blocking collectives  22.3 us (20%)
    all_to_all x1, blocking collectives, local(): own = add(lax.all_to_all(sums.reshape(32, 64, 128), 'lon', 0, 0))  22.3 us
    ppermute x8, waiting for transfers between devices, moved(): return lax.ppermute(value, ('lat', 'lon', 'tp'), pairs)  22.3 us
    ppermute x8, starting transfers between devices, moved(): return lax.ppermute(value, ('lat', 'lon', 'tp'), pairs)  19.5 us
    pallas_call x1, Pallas kernels, backward(): pl.pallas_call(backward_kernel, out_shape=(shape((576, 192), BF), shape((...  7.31 us
    pallas_call x1, Pallas kernels, scatter(): pl.pallas_call(scatter_kernel, out_shape=shape((192, 256), F32), compiler...  5.02 us
    pallas_call x1, Pallas kernels, forward(): pl.pallas_call(forward_kernel, out_shape=(shape((576, 192), BF), shape((5...  4.82 us
    ppermute x3, starting transfers between devices, swapped(): return lax.ppermute(value, 'lat', pairs)  4.62 us
    all_to_all x1, starting transfers between devices, local(): got = lax.all_to_all(totals, 'lon', 0, 0)  4.31 us
  transfers between devices with their start and end apart: 12, of which 7 were waited for; matrix products, arithmetic and copies ran while one was open for 0% of the time, Pallas kernels for 12%

profile of v3, /device:TPU:1, one launch (start us, length us, event | category | flops | bytes accessed | tf_op | source)
XLA Modules:
  0.0 109.5 jit_solution(11242232636460680621)
XLA Ops:
  0.7 0.0 copy-start.13
  0.7 3.4 %head.1 = (bf16[576,192]{1,0:T(8,128)(2,1)}, bf16[1152,128]{1,0:T(8,128)(2,1)}) custom-call(bf16[6,12,8,192]{3,2,1,0:T(8,128)(2,1)} %bitcast.25, bf16[6,12,8,192]{3,2,1,0:T(8,128)(2,1)} %bitcast.27, f32[1,192]{1,0:T(1,128)} %bitcast.32, bf16[192,384]{1,0:T(8,128)(2,1)} %fc1_hbm.1, bf16[192,384]{1,0:T(8,128)(2,1)} %bitcast.38), custom_call_target="tpu_custom_call" | custom-call | flops 3000000000 | tf_op jit(solution)/shard_map/head/pallas_call | solution.py:118
  4.1 2.2 %collective-permute-start = (bf16[576,192]{1,0:T(8,128)(2,1)}, bf16[576,192]{1,0:T(8,128)(2,1)S(1)}, u32[]{:S(2)}, u32[]{:S(2)}) collective-permute-start(bf16[576,192]{1,0:T(8,128)(2,1)} %get-tuple-element.43.own_ref), channel_id=1, source_target_pairs={{1,0},{0,1},{3,2},{2,3},{5,4},{4,5},{7,6},{6,7},{9,8},{8,9},{11,10... | collective-permute-start | bytes 663560 | tf_op jit(solution)/shard_map/ppermute | solution.py:566
  6.4 0.0 copy-done.4
  6.4 0.0 copy-done.13
  6.4 0.0 copy-start
  6.4 0.0 copy-start.1
  6.4 0.0 copy-start.2
  6.4 0.0 copy-start.10
  6.4 3.9 %gather_first.1 = (f32[1440,128]{1,0:T(8,128)S(1)}, s32[168,128]{1,0:T(8,128)S(1)}, s32[168,128]{1,0:T(8,128)S(1)}, bf16[160,512]{1,0:T(8,128)(2,1)S(1)}, f32[4,144]{1,0:T(4,128)S(1)}) custom-call(s32[144,144]{1,0:T(8,128)S(1)} %copy-done.5, bf16[144,144]{1,0:T(8,128)(2,1)S(1)} %copy-done.13, f32[3,4,3312]{2,1,0:T(4,128)S(1)} %bitcast.29, ...), custom_call_target="tpu_custom_call" | custom-call | flops 6000000000 | tf_op jit(solution)/shard_map/gather_first/pallas_call | solution.py:250
  10.4 1.8 %collective-permute-done.other_ref = bf16[576,192]{1,0:T(8,128)(2,1)S(1)} collective-permute-done((bf16[576,192]{1,0:T(8,128)(2,1)}, bf16[576,192]{1,0:T(8,128)(2,1)S(1)}, u32[]{:S(2)}, u32[]{:S(2)}) %collective-permute-start) | collective-permute-done | bytes 221216 | tf_op jit(solution)/shard_map/ppermute | solution.py:566
  12.2 0.0 copy-done.1
  12.2 0.6 middle.1
  12.8 8.8 %collective-permute-start.1 = (bf16[288,192]{1,0:T(8,128)(2,1)S(1)}, bf16[288,192]{1,0:T(8,128)(2,1)S(1)}, u32[]{:S(2)}, u32[]{:S(2)}) collective-permute-start(bf16[288,192]{1,0:T(8,128)(2,1)S(1)} %get-tuple-element.47.x2), channel_id=1, source_target_pairs={{2,0},{3,1},{4,2},{5,3},{6,4},{7,5},{8,6},{9,7},{10,8},{11,9},{12,... | collective-permute-start | bytes 331784 | tf_op jit(solution)/shard_map/ppermute | solution.py:566
  21.7 1.8 %collective-permute-start.2 = (bf16[288,192]{1,0:T(8,128)(2,1)S(1)}, bf16[288,192]{1,0:T(8,128)(2,1)S(1)}, u32[]{:S(2)}, u32[]{:S(2)}) collective-permute-start(bf16[288,192]{1,0:T(8,128)(2,1)S(1)} %get-tuple-element.46.x1), channel_id=1, source_target_pairs={{64,0},{65,1},{66,2},{67,3},{68,4},{69,5},{70,6},{71,7},{72,8},{73... | collective-permute-start | bytes 331784 | tf_op jit(solution)/shard_map/ppermute | solution.py:566
  23.5 1.9 %collective-permute-start.3 = (bf16[288,192]{1,0:T(8,128)(2,1)S(1)}, bf16[288,192]{1,0:T(8,128)(2,1)S(1)}, u32[]{:S(2)}, u32[]{:S(2)}) collective-permute-start(bf16[288,192]{1,0:T(8,128)(2,1)S(1)} %get-tuple-element.45.x0), channel_id=1, source_target_pairs={{66,0},{67,1},{68,2},{69,3},{70,4},{71,5},{72,6},{73,7},{74,8},{75... | collective-permute-start | bytes 331784 | tf_op jit(solution)/shard_map/ppermute | solution.py:566
  25.4 2.9 %gather_second.1 = (f32[12,144,128]{2,1,0:T(8,128)S(1)}, f32[12,144,128]{2,1,0:T(8,128)S(1)}) custom-call(f32[1440,128]{1,0:T(8,128)S(1)} %get-tuple-element.49.first_stage, s32[168,128]{1,0:T(8,128)S(1)} %get-tuple-element.44.after_ref.lo_ref, s32[168,128]{1,0:T(8,128)S(1)} %get-tuple-element.50.hi_ref, bf16[160,512]{1,0:T(8,128)(2,1)S(1)} %get-tuple-element.51.terms_ref, ...), custom_call_target="tpu_custom_call" | custom-call | flops 4000000000 | tf_op jit(solution)/shard_map/gather_second/pallas_call | solution.py:277
  28.3 0.0 collective-permute-done.1.x1.g1
  28.4 1.1 collective-permute-done.2.x2.g2
  29.4 2.2 %collective-permute-done.3.x3.g3 = bf16[288,192]{1,0:T(8,128)(2,1)S(1)} collective-permute-done((bf16[288,192]{1,0:T(8,128)(2,1)S(1)}, bf16[288,192]{1,0:T(8,128)(2,1)S(1)}, u32[]{:S(2)}, u32[]{:S(2)}) %collective-permute-start.3) | collective-permute-done | bytes 110624 | tf_op jit(solution)/shard_map/ppermute | solution.py:566
  31.6 0.0 copy-done.6
  31.6 0.0 copy-done.12
  31.6 0.0 copy-start.7
  31.6 4.8 %forward.1 = (bf16[576,192]{1,0:T(8,128)(2,1)S(1)}, bf16[576,96]{1,0:T(8,128)(2,1)S(1)}, bf16[576,96]{1,0:T(8,128)(2,1)S(1)}, bf16[576,96]{1,0:T(8,128)(2,1)S(1)...) custom-call(bf16[288,192]{1,0:T(8,128)(2,1)S(1)} %get-tuple-element.48.x0.g0.x3, ...), custom_call_target="tpu_custom_call" | custom-call | flops 5000000000 | tf_op jit(solution)/shard_map/forward/pallas_call | solution.py:322
  36.5 7.3 %backward.1 = (bf16[576,192]{1,0:T(8,128)(2,1)S(1)}, f32[12,168,128]{2,1,0:T(8,128)S(1)}, bf16[576,128]{1,0:T(8,128)(2,1)S(1)}) custom-call(bf16[288,192]{1,0:T(8,128)(2,1)S(1)} %get-tuple-element.48.x0.g0.x3, bf16[288,192]{1,0:T(8,128)(2,1)S(1)} %collective-permute-done.1.x1.g1, bf16[288,192]{1,0:T(8,128)(2,1)S(1)} %collective-permute-done.2.x2.g2, ...), custom_call_target="tpu_custom_call" | custom-call | flops 7000000000 | tf_op jit(solution)/shard_map/backward/pallas_call | solution.py:389
  43.8 0.5 collective-permute-start.4
  44.3 5.0 %scatter.1.table_ref = f32[192,256]{1,0:T(8,128)S(1)} custom-call(f32[12,168,128]{2,1,0:T(8,128)S(1)} %get-tuple-element.65.score_ref, s32[168,128]{1,0:T(8,128)S(1)} %get-tuple-element.44.after_ref.lo_ref, s32[168,128]{1,0:T(8,128)S(1)} %get-tuple-element.50.hi_ref), custom_call_target="tpu_custom_call" | custom-call | flops 5000000000 | tf_op jit(solution)/shard_map/scatter/pallas_call | solution.py:423
  49.3 2.3 %collective-permute-done.4.other_ref = bf16[576,192]{1,0:T(8,128)(2,1)S(1)} collective-permute-done((bf16[576,192]{1,0:T(8,128)(2,1)S(1)}, bf16[576,192]{1,0:T(8,128)(2,1)S(1)}, u32[]{:S(2)}, u32[]{:S(2)}) %collective-permute-start.4) | collective-permute-done | bytes 221216 | tf_op jit(solution)/shard_map/ppermute | solution.py:566
  51.5 0.4 meet.1
  51.9 22.3 %all_to_all.10.got_ref = bf16[32,64,128]{2,1,0:T(8,128)(2,1)S(1)} all-to-all(bf16[32,64,128]{2,1,0:T(8,128)(2,1)S(1)} %bitcast.23), channel_id=1, replica_groups=mesh['lat'=4,'lon'=32,'tp'=2] {'lon'}, dimensions={0} | all-to-all | bytes 1048576 | tf_op jit(solution)/shard_map/all_to_all | solution.py:622
  74.2 0.1 add.1.own_ref
  74.3 4.4 %collective-permute-start.10 = (bf16[64,128]{1,0:T(8,128)(2,1)S(1)}, bf16[64,128]{1,0:T(8,128)(2,1)S(1)}, u32[]{:S(2)}, u32[]{:S(2)}) collective-permute-start(bf16[64,128]{1,0:T(8,128)(2,1)S(1)} %add.1.own_ref), channel_id=1, source_target_pairs={{0,192},{64,128},{128,64},{192,0},{1,193},{65,129},{129,65},{193,1... | collective-permute-start | bytes 49160 | tf_op jit(solution)/shard_map/ppermute | solution.py:571
  78.7 0.0 collective-permute-start.8
  78.7 0.2 collective-permute-start.9
  78.9 1.2 %collective-permute-done.10.c_ref = bf16[64,128]{1,0:T(8,128)(2,1)S(1)} collective-permute-done((bf16[64,128]{1,0:T(8,128)(2,1)S(1)}, bf16[64,128]{1,0:T(8,128)(2,1)S(1)}, u32[]{:S(2)}, u32[]{:S(2)}) %collective-permute-start.10) | collective-permute-done | bytes 16416 | tf_op jit(solution)/shard_map/ppermute | solution.py:571
  80.1 0.0 collective-permute-done.8.a_ref
  80.1 2.7 %collective-permute-done.9.b_ref = bf16[64,128]{1,0:T(8,128)(2,1)S(1)} collective-permute-done((bf16[64,128]{1,0:T(8,128)(2,1)S(1)}, bf16[64,128]{1,0:T(8,128)(2,1)S(1)}, u32[]{:S(2)}, u32[]{:S(2)}) %collective-permute-start.9) | collective-permute-done | bytes 16416 | tf_op jit(solution)/shard_map/ppermute | solution.py:571
  82.8 0.9 spread.1
  83.6 4.3 %all-to-all-start.1 = ((bf16[32,64,128]{2,1,0:T(8,128)(2,1)}), bf16[32,64,128]{2,1,0:T(8,128)(2,1)S(1)}, u32[]{:S(2)}, u32[]{:S(2)}) async-start(bf16[32,64,128]{2,1,0:T(8,128)(2,1)} %spread.1), calls=%async_computation.1 | async-start | bytes 1048576 | tf_op jit(solution)/shard_map/all_to_all | solution.py:625
  88.0 3.1 %collective-permute-start.5 = (bf16[144,192]{1,0:T(8,128)(2,1)S(1)}, bf16[144,192]{1,0:T(8,128)(2,1)S(1)}, u32[]{:S(2)}, u32[]{:S(2)}) collective-permute-start(bf16[144,192]{1,0:T(8,128)(2,1)S(1)} %get-tuple-element.66), channel_id=1, source_target_pairs={{254,0},{255,1},{192,2},{193,3},{194,4},{195,5},{196,6},{197,7},{1... | collective-permute-start | bytes 165896 | tf_op jit(solution)/shard_map/ppermute | solution.py:566
  91.0 0.0 collective-permute-start.6
  91.0 1.2 %collective-permute-start.7 = (bf16[144,192]{1,0:T(8,128)(2,1)S(1)}, bf16[144,192]{1,0:T(8,128)(2,1)S(1)}, u32[]{:S(2)}, u32[]{:S(2)}) collective-permute-start(bf16[144,192]{1,0:T(8,128)(2,1)S(1)} %get-tuple-element.68), channel_id=1, source_target_pairs={{62,0},{63,1},{0,2},{1,3},{2,4},{3,5},{4,6},{5,7},{6,8},{7,9},{8,1... | collective-permute-start | bytes 165896 | tf_op jit(solution)/shard_map/ppermute | solution.py:566
  92.2 15.0 %collective-permute-done.5.g0 = bf16[144,192]{1,0:T(8,128)(2,1)S(1)} collective-permute-done((bf16[144,192]{1,0:T(8,128)(2,1)S(1)}, bf16[144,192]{1,0:T(8,128)(2,1)S(1)}, u32[]{:S(2)}, u32[]{:S(2)}) %collective-permute-start.5) | collective-permute-done | bytes 55328 | tf_op jit(solution)/shard_map/ppermute | solution.py:566
  107.2 0.0 collective-permute-done.6.g1
  107.2 0.0 collective-permute-done.7.g2
  107.2 1.2 %finish.1 = bf16[6,12,8,192]{3,2,1,0:T(8,128)(2,1)} custom-call(bf16[288,192]{1,0:T(8,128)(2,1)S(1)} %get-tuple-element.45.x0, bf16[288,192]{1,0:T(8,128)(2,1)S(1)} %get-tuple-element.46.x1, bf16[288,192]{1,0:T(8,128)(2,1)S(1)} %get-tuple-element.47.x2, bf16[288,192]{1,0:T(8,128)(2,1)S(1)} %get-tuple-element.48.x0.g0.x3, ...), custom_call_target="tpu_custom_call" | custom-call | flops 1000000000 | tf_op jit(solution)/shard_map/finish/pallas_call | solution.py:470
  108.4 0.0 all-to-all-done.1
  108.4 1.1 %unpack.1 = (f32[3,192,96]{2,1,0:T(8,128)}, f32[96,192]{1,0:T(8,128)}, f32[192,384]{1,0:T(8,128)}, f32[192,384]{1,0:T(8,128)}, f32[1,96]{1,0:T(1,128)}, /*index=5*/f32[1,96]{1,0:T(1,128)}, f32[3,4,3312]{2,1,0:T(4,128)}) custom-call(s32[1]{0:T(128)} %bitcast.11.half_ref, bf16[2048,128]{1,0:T(8,128)(2,1)S(1)} %bitcast.22), custom_call_target="tpu_custom_call" | custom-call | tf_op jit(solution)/shard_map/unpack/pallas_call | solution.py:541
  (19 shorter events, 0.0 us)
Async XLA Ops:
  0.6 5.7 %copy-start.4 = (f32[1,4,3,3312]{3,1,2,0:T(4,128)S(1)}, f32[1,4,3,3312]{3,1,2,0:T(4,128)}, u32[]{:S(2)}) copy-start(f32[1,4,3,3312]{3,1,2,0:T(4,128)} %param.22) | copy-start | bytes 476932
  0.6 5.7 %copy-start.5 = (s32[144,144]{1,0:T(8,128)S(1)}, s32[144,144]{1,0:T(8,128)}, u32[]{:S(2)}) copy-start(s32[144,144]{1,0:T(8,128)} %index_ref.1) | copy-start | bytes 248836
  0.7 5.7 %copy-start.8 = (s32[8,6,12]{2,0,1:T(8,128)S(1)}, s32[8,6,12]{2,0,1:T(8,128)}, u32[]{:S(2)}) copy-start(s32[8,6,12]{2,0,1:T(8,128)} %param.19) | copy-start | bytes 6916
  0.7 5.7 %copy-start.9 = (s32[8,6,12]{2,0,1:T(8,128)S(1)}, s32[8,6,12]{2,0,1:T(8,128)}, u32[]{:S(2)}) copy-start(s32[8,6,12]{2,0,1:T(8,128)} %param.20) | copy-start | bytes 6916
  0.7 5.7 %copy-start.13 = (bf16[144,144]{1,0:T(8,128)(2,1)S(1)}, bf16[144,144]{1,0:T(8,128)(2,1)}, u32[]{:S(2)}) copy-start(bf16[144,144]{1,0:T(8,128)(2,1)} %constant.12.clone.order_ref) | copy-start | bytes 124420
  4.1 8.0 %collective-permute-start = (bf16[576,192]{1,0:T(8,128)(2,1)}, bf16[576,192]{1,0:T(8,128)(2,1)S(1)}, u32[]{:S(2)}, u32[]{:S(2)}) collective-permute-start(bf16[576,192]{1,0:T(8,128)(2,1)} %get-tuple-element.43.own_ref), channel_id=1, source_target_pairs={{1,0},{0,1},{3,2},{2,3},{5,4},{4,5},{7,6},{6,7},{9,8},{8,9},{11,10... | collective-permute-start | bytes 663560 | tf_op jit(solution)/shard_map/ppermute | solution.py:566
  6.4 5.8 %copy-start = (bf16[8,6,12,192]{3,0,2,1:T(8,128)(2,1)S(1)}, bf16[8,6,12,192]{3,0,2,1:T(8,128)(2,1)}, u32[]{:S(2)}) copy-start(bf16[8,6,12,192]{3,0,2,1:T(8,128)(2,1)} %param.16) | copy-start | bytes 663556
  6.4 5.8 %copy-start.1 = (bf16[8,6,12,192]{3,0,2,1:T(8,128)(2,1)S(1)}, bf16[8,6,12,192]{3,0,2,1:T(8,128)(2,1)}, u32[]{:S(2)}) copy-start(bf16[8,6,12,192]{3,0,2,1:T(8,128)(2,1)} %param.17) | copy-start | bytes 663556
  6.4 5.8 %copy-start.2 = (bf16[8,6,12,192]{3,0,2,1:T(8,128)(2,1)S(1)}, bf16[8,6,12,192]{3,0,2,1:T(8,128)(2,1)}, u32[]{:S(2)}) copy-start(bf16[8,6,12,192]{3,0,2,1:T(8,128)(2,1)} %param.18) | copy-start | bytes 663556
  6.4 5.8 %copy-start.3 = (bf16[576,192]{1,0:T(8,128)(2,1)S(1)}, bf16[576,192]{1,0:T(8,128)(2,1)}, u32[]{:S(2)}) copy-start(bf16[576,192]{1,0:T(8,128)(2,1)} %get-tuple-element.43.own_ref) | copy-start | bytes 663556
  6.4 5.8 %copy-start.10 = (f32[192]{0:T(256)S(1)}, f32[192]{0:T(256)}, u32[]{:S(2)}) copy-start(f32[192]{0:T(256)} %param.26) | copy-start | bytes 2308
  12.8 15.5 %collective-permute-start.1 = (bf16[288,192]{1,0:T(8,128)(2,1)S(1)}, bf16[288,192]{1,0:T(8,128)(2,1)S(1)}, u32[]{:S(2)}, u32[]{:S(2)}) collective-permute-start(bf16[288,192]{1,0:T(8,128)(2,1)S(1)} %get-tuple-element.47.x2), channel_id=1, source_target_pairs={{2,0},{3,1},{4,2},{5,3},{6,4},{7,5},{8,6},{9,7},{10,8},{11,9},{12,... | collective-permute-start | bytes 331784 | tf_op jit(solution)/shard_map/ppermute | solution.py:566
  21.7 7.8 %collective-permute-start.2 = (bf16[288,192]{1,0:T(8,128)(2,1)S(1)}, bf16[288,192]{1,0:T(8,128)(2,1)S(1)}, u32[]{:S(2)}, u32[]{:S(2)}) collective-permute-start(bf16[288,192]{1,0:T(8,128)(2,1)S(1)} %get-tuple-element.46.x1), channel_id=1, source_target_pairs={{64,0},{65,1},{66,2},{67,3},{68,4},{69,5},{70,6},{71,7},{72,8},{73... | collective-permute-start | bytes 331784 | tf_op jit(solution)/shard_map/ppermute | solution.py:566
  23.5 8.1 %collective-permute-start.3 = (bf16[288,192]{1,0:T(8,128)(2,1)S(1)}, bf16[288,192]{1,0:T(8,128)(2,1)S(1)}, u32[]{:S(2)}, u32[]{:S(2)}) collective-permute-start(bf16[288,192]{1,0:T(8,128)(2,1)S(1)} %get-tuple-element.45.x0), channel_id=1, source_target_pairs={{66,0},{67,1},{68,2},{69,3},{70,4},{71,5},{72,6},{73,7},{74,8},{75... | collective-permute-start | bytes 331784 | tf_op jit(solution)/shard_map/ppermute | solution.py:566
  25.4 6.2 %copy-start.6 = (bf16[3,192,96]{2,1,0:T(8,128)(2,1)S(1)}, bf16[3,192,96]{2,1,0:T(8,128)(2,1)}, u32[]{:S(2)}) copy-start(bf16[3,192,96]{2,1,0:T(8,128)(2,1)} %qkv_ref.3) | copy-start | bytes 331780
  25.4 6.2 %copy-start.11 = (f32[192]{0:T(256)S(1)}, f32[192]{0:T(256)}, u32[]{:S(2)}) copy-start(f32[192]{0:T(256)} %param.23) | copy-start | bytes 2308
  25.4 6.2 %copy-start.12 = (bf16[144,144]{1,0:T(8,128)(2,1)S(1)}, bf16[144,144]{1,0:T(8,128)(2,1)}, u32[]{:S(2)}) copy-start(bf16[144,144]{1,0:T(8,128)(2,1)} %constant.13.clone.order_ref) | copy-start | bytes 124420
  31.6 4.8 %copy-start.7 = (bf16[96,192]{1,0:T(8,128)(2,1)S(1)}, bf16[96,192]{1,0:T(8,128)(2,1)}, u32[]{:S(2)}) copy-start(bf16[96,192]{1,0:T(8,128)(2,1)} %proj_ref.1) | copy-start | bytes 110596
  43.8 7.8 %collective-permute-start.4 = (bf16[576,192]{1,0:T(8,128)(2,1)S(1)}, bf16[576,192]{1,0:T(8,128)(2,1)S(1)}, u32[]{:S(2)}, u32[]{:S(2)}) collective-permute-start(bf16[576,192]{1,0:T(8,128)(2,1)S(1)} %get-tuple-element.62.own_ref), channel_id=1, source_target_pairs={{1,0},{0,1},{3,2},{2,3},{5,4},{4,5},{7,6},{6,7},{9,8},{8,9},{11,10... | collective-permute-start | bytes 663560 | tf_op jit(solution)/shard_map/ppermute | solution.py:566
  44.3 7.3 %copy-start.14 = (bf16[1152,128]{1,0:T(8,128)(2,1)S(1)}, bf16[1152,128]{1,0:T(8,128)(2,1)}, u32[]{:S(2)}) copy-start(bf16[1152,128]{1,0:T(8,128)(2,1)} %get-tuple-element.63.first_ref) | copy-start | bytes 884740
  74.3 5.8 %collective-permute-start.10 = (bf16[64,128]{1,0:T(8,128)(2,1)S(1)}, bf16[64,128]{1,0:T(8,128)(2,1)S(1)}, u32[]{:S(2)}, u32[]{:S(2)}) collective-permute-start(bf16[64,128]{1,0:T(8,128)(2,1)S(1)} %add.1.own_ref), channel_id=1, source_target_pairs={{0,192},{64,128},{128,64},{192,0},{1,193},{65,129},{129,65},{193,1... | collective-permute-start | bytes 49160 | tf_op jit(solution)/shard_map/ppermute | solution.py:571
  78.7 1.4 %collective-permute-start.8 = (bf16[64,128]{1,0:T(8,128)(2,1)S(1)}, bf16[64,128]{1,0:T(8,128)(2,1)S(1)}, u32[]{:S(2)}, u32[]{:S(2)}) collective-permute-start(bf16[64,128]{1,0:T(8,128)(2,1)S(1)} %add.1.own_ref), channel_id=1, source_target_pairs={{0,64},{64,0},{128,192},{192,128},{1,65},{65,1},{129,193},{193,129... | collective-permute-start | bytes 49160 | tf_op jit(solution)/shard_map/ppermute | solution.py:571
  78.7 4.1 %collective-permute-start.9 = (bf16[64,128]{1,0:T(8,128)(2,1)S(1)}, bf16[64,128]{1,0:T(8,128)(2,1)S(1)}, u32[]{:S(2)}, u32[]{:S(2)}) collective-permute-start(bf16[64,128]{1,0:T(8,128)(2,1)S(1)} %add.1.own_ref), channel_id=1, source_target_pairs={{0,128},{64,192},{128,0},{192,64},{1,129},{65,193},{129,1},{193,65... | collective-permute-start | bytes 49160 | tf_op jit(solution)/shard_map/ppermute | solution.py:571
  83.6 24.8 %all-to-all-start.1 = ((bf16[32,64,128]{2,1,0:T(8,128)(2,1)}), bf16[32,64,128]{2,1,0:T(8,128)(2,1)S(1)}, u32[]{:S(2)}, u32[]{:S(2)}) async-start(bf16[32,64,128]{2,1,0:T(8,128)(2,1)} %spread.1), calls=%async_computation.1 | async-start | bytes 1048576 | tf_op jit(solution)/shard_map/all_to_all | solution.py:625
  88.0 19.2 %collective-permute-start.5 = (bf16[144,192]{1,0:T(8,128)(2,1)S(1)}, bf16[144,192]{1,0:T(8,128)(2,1)S(1)}, u32[]{:S(2)}, u32[]{:S(2)}) collective-permute-start(bf16[144,192]{1,0:T(8,128)(2,1)S(1)} %get-tuple-element.66), channel_id=1, source_target_pairs={{254,0},{255,1},{192,2},{193,3},{194,4},{195,5},{196,6},{197,7},{1... | collective-permute-start | bytes 165896 | tf_op jit(solution)/shard_map/ppermute | solution.py:566
  91.0 16.1 %collective-permute-start.6 = (bf16[144,192]{1,0:T(8,128)(2,1)S(1)}, bf16[144,192]{1,0:T(8,128)(2,1)S(1)}, u32[]{:S(2)}, u32[]{:S(2)}) collective-permute-start(bf16[144,192]{1,0:T(8,128)(2,1)S(1)} %get-tuple-element.67), channel_id=1, source_target_pairs={{192,0},{193,1},{194,2},{195,3},{196,4},{197,5},{198,6},{199,7},{2... | collective-permute-start | bytes 165896 | tf_op jit(solution)/shard_map/ppermute | solution.py:566
  91.0 16.1 %collective-permute-start.7 = (bf16[144,192]{1,0:T(8,128)(2,1)S(1)}, bf16[144,192]{1,0:T(8,128)(2,1)S(1)}, u32[]{:S(2)}, u32[]{:S(2)}) collective-permute-start(bf16[144,192]{1,0:T(8,128)(2,1)S(1)} %get-tuple-element.68), channel_id=1, source_target_pairs={{62,0},{63,1},{0,2},{1,3},{2,4},{3,5},{4,6},{5,7},{6,8},{7,9},{8,1... | collective-permute-start | bytes 165896 | tf_op jit(solution)/shard_map/ppermute | solution.py:566

commit v4 on v3

--- a/solution.py
+++ b/solution.py
@@ -77,16 +77,23 @@
     return jnp.asarray(order, BF)
 
 
-def to_windows(parts, start, order, scratch):
+def to_windows(parts, order, scratch):
     for s in range(4):
-        rows = dot_nn(order, parts[s][start : start + 144, :])
+        rows = dot_nn(order, parts[s][...])
         for w in range(4):
             scratch[w * 144 + s * 36 : w * 144 + s * 36 + 36, :] = rows[w * 36 : w * 36 + 36]
 
 
-def head_kernel(mid_hbm, up_hbm, gain_hbm, fc1_hbm, fc2_hbm, part_hbm, grads_hbm,
-                mid_ref, up_ref, gain_ref, fc1_ref, fc2_ref, part_ref, grads_ref, mid_s, up_s, sem):
-    pairs = ((mid_hbm, mid_ref), (gain_hbm, gain_ref), (fc1_hbm, fc1_ref), (up_hbm, up_ref), (fc2_hbm, fc2_ref))
+def head_kernel(x_hbm, mid_hbm, up_hbm, gain_hbm, fc1_hbm, fc2_hbm, o0, o1, o2, o3, part_hbm, grads_hbm,
+                x_ref, mid_ref, up_ref, gain_ref, fc1_ref, fc2_ref, xq_ref, part_ref, grads_ref, x_s, mid_s, up_s, sem):
+    pairs = (
+        (mid_hbm, mid_ref),
+        (gain_hbm, gain_ref),
+        (fc1_hbm, fc1_ref),
+        (up_hbm, up_ref),
+        (fc2_hbm, fc2_ref),
+        (x_hbm, x_ref),
+    )
     copies = [pltpu.make_async_copy(a, b, sem.at[i]) for i, (a, b) in enumerate(pairs)]
     for copy in copies:
         copy.start()
@@ -99,48 +106,55 @@
     active, slopes = gelu_pair(pre)
     for copy in copies[3:]:
         copy.wait()
+    to_quarters(x_ref, x_s)
+    writes = []
+    for q, out in enumerate((o0, o1, o2, o3)):
+        xq_ref[q] = x_s[q * 144 : q * 144 + 144, :].astype(BF)
+        writes.append(pltpu.make_async_copy(xq_ref.at[q], out, sem.at[8 + q]))
+        writes[-1].start()
     to_quarters(up_ref, up_s)
     up = up_s[...].astype(BF)
     grad_pre = (dot_nn(up, fc2_ref[...]) * slopes).astype(BF)
     part_ref[...] = dot_nt(grad_pre, fc1_ref[...]).astype(BF)
-    part_copy = pltpu.make_async_copy(part_ref, part_hbm, sem.at[5])
-    part_copy.start()
+    writes.append(pltpu.make_async_copy(part_ref, part_hbm, sem.at[6]))
+    writes[-1].start()
     for start, grads in ((0, dot_tn(lowered, grad_pre)), (576, dot_tn(up, active.astype(BF)))):
         for j in range(3):
             grads_ref[start + j * 192 : start + j * 192 + 192, :] = grads[:, j * 128 : j * 128 + 128].astype(BF)
-    grads_copy = pltpu.make_async_copy(grads_ref, grads_hbm, sem.at[6])
-    grads_copy.start()
-    part_copy.wait()
-    grads_copy.wait()
-
-
-def head(mid, up, gain, fc1, fc2):
+    writes.append(pltpu.make_async_copy(grads_ref, grads_hbm, sem.at[7]))
+    writes[-1].start()
+    for write in writes:
+        write.wait()
+
+
+def head(x, mid, up, gain, fc1, fc2):
     return pl.pallas_call(
         head_kernel,
-        out_shape=(shape((576, 192), BF), shape((1152, 128), BF)),
-        in_specs=[ANY] * 5,
-        out_specs=(ANY, ANY),
+        out_shape=tuple(shape((144, 192), BF) for _ in range(4)) + (shape((576, 192), BF), shape((1152, 128), BF)),
+        in_specs=[ANY] * 6,
+        out_specs=tuple(ANY for _ in range(6)),
         scratch_shapes=[
+            pltpu.VMEM((6, 12, 8, 192), BF),
             pltpu.VMEM((6, 12, 8, 192), BF),
             pltpu.VMEM((6, 12, 8, 192), BF),
             pltpu.VMEM((1, 192), F32),
             pltpu.VMEM((192, 384), BF),
             pltpu.VMEM((192, 384), BF),
+            pltpu.VMEM((4, 144, 192), BF),
             pltpu.VMEM((576, 192), BF),
             pltpu.VMEM((1152, 128), BF),
             pltpu.VMEM((576, 192), F32),
             pltpu.VMEM((576, 192), F32),
-            pltpu.SemaphoreType.DMA((7,)),
+            pltpu.VMEM((576, 192), F32),
+            pltpu.SemaphoreType.DMA((12,)),
         ],
         compiler_params=ALL,
         cost_estimate=cost(3),
         name="head",
-    )(mid, up, gain, fc1, fc2)
-
-
-def middle_kernel(x_ref, mid_ref, up_ref, own_ref, other_ref, gain_ref, after_ref,
-                  o0, o1, o2, o3, gain_out, x_s, mid_s, up_s):
-    to_quarters(x_ref, x_s)
+    )(x, mid, up, gain, fc1, fc2)
+
+
+def middle_kernel(mid_ref, up_ref, own_ref, other_ref, gain_ref, after_ref, o0, o1, o2, o3, gain_out, mid_s, up_s):
     to_quarters(mid_ref, mid_s)
     to_quarters(up_ref, up_s)
     normed, inverse = layer_stats(mid_s[...])
@@ -148,20 +162,19 @@
     gain_out[...] = jnp.sum(grad * normed, axis=0, keepdims=True)
     out = up_s[...] + norm_backward(grad, gain_ref[...], normed, inverse)
     for q, o in enumerate((o0, o1, o2, o3)):
-        o[0:144, :] = x_s[q * 144 : q * 144 + 144, :].astype(BF)
-        o[144:288, :] = out[q * 144 : q * 144 + 144].astype(BF)
-
-
-def middle(x, mid, up, own, other, gain, after):
+        o[...] = out[q * 144 : q * 144 + 144].astype(BF)
+
+
+def middle(mid, up, own, other, gain, after):
     return pl.pallas_call(
         middle_kernel,
-        out_shape=tuple(shape((288, 192), BF) for _ in range(4)) + (shape((1, 192), F32),),
-        in_specs=[VMEM] * 6 + [ANY],
-        scratch_shapes=[pltpu.VMEM((576, 192), F32)] * 3,
+        out_shape=tuple(shape((144, 192), BF) for _ in range(4)) + (shape((1, 192), F32),),
+        in_specs=[VMEM] * 5 + [ANY],
+        scratch_shapes=[pltpu.VMEM((576, 192), F32)] * 2,
         compiler_params=VM,
         cost_estimate=cost(1),
         name="middle",
-    )(x, mid, up, own, other, gain, after)
+    )(mid, up, own, other, gain, after)
 
 
 def window_order():
@@ -208,7 +221,7 @@
                 stage[pl.ds(start + 8, 8), :] = second + pltpu.roll(second, 4, 0)
         return 0
 
-    lax.fori_loop(0, steps, step, 0)
+    lax.fori_loop(0, steps, step, 0, unroll=True)
 
 
 def gather_first_kernel(index_ref, order_ref, bias_ref, ids_ref, valid_ref,
@@ -287,7 +300,7 @@
 
 def forward_kernel(x0, x1, x2, x3, order_ref, gain_ref, qkv_ref, main_ref, tail_ref, code_ref,
                    low_ref, q_ref, k_ref, v_ref, prob_ref, att_ref, scratch):
-    to_windows((x0, x1, x2, x3), 0, order_ref[...], scratch)
+    to_windows((x0, x1, x2, x3), order_ref[...], scratch)
     normed, _ = layer_stats(scratch[...])
     low = (normed * gain_ref[...]).astype(BF)
     low_ref[...] = low
@@ -315,7 +328,7 @@
         att_ref[rows, :] = jnp.concatenate(heads, axis=1).astype(BF)
         return 0
 
-    lax.fori_loop(0, 4, window, 0)
+    lax.fori_loop(0, 4, window, 0, unroll=True)
 
 
 def forward(x, gain, qkv, main, tail, code):
@@ -338,7 +351,7 @@
 
 def backward_kernel(g0, g1, g2, g3, order_ref, proj_ref, qkv_ref, low_ref, q_ref, k_ref, v_ref, prob_ref, att_ref,
                     part_ref, score_ref, grads_ref, scratch, gatt, gcols):
-    to_windows((g0, g1, g2, g3), 144, order_ref[...], scratch)
+    to_windows((g0, g1, g2, g3), order_ref[...], scratch)
     grad = scratch[...].astype(BF)
     gproj = dot_tn(att_ref[...], grad).astype(BF)
     grads_ref[0:96, :] = gproj[:, 0:128]
@@ -365,7 +378,7 @@
         gcols[2, rows, :] = jnp.concatenate(values, axis=1).astype(BF)
         return 0
 
-    lax.fori_loop(0, 4, window, 0)
+    lax.fori_loop(0, 4, window, 0, unroll=True)
     low = low_ref[...]
     total = None
     gqkv = []
@@ -416,7 +429,7 @@
         out_ref[...] += dot_nt(jnp.concatenate(left, axis=1), jnp.concatenate(right, axis=1))
         return 0
 
-    lax.fori_loop(0, 9, step, 0)
+    lax.fori_loop(0, 9, step, 0, unroll=True)
 
 
 def scatter(score, lo, hi):
@@ -431,7 +444,7 @@
     for s, (x, o) in enumerate(zip((x0, x1, x2, x3), (o0, o1, o2, o3))):
         rows = slice(s * 144, s * 144 + 144)
         grad = own_ref[rows, :].astype(F32) + other_ref[rows, :].astype(F32)
-        normed, _ = layer_stats(x[0:144, :].astype(F32))
+        normed, _ = layer_stats(x[...].astype(F32))
         gain = gain + jnp.sum(grad * normed, axis=0, keepdims=True)
         o[...] = grad.astype(BF)
     out_ref[0:1152, :] = first_ref[...]
@@ -457,35 +470,40 @@
     )(own, other, *x, first, second, table, two)
 
 
-def finish_kernel(x0, x1, x2, x3, g0, g1, g2, g3, gain_ref, out_ref):
-    for q, (x, g) in enumerate(zip((x0, x1, x2, x3), (g0, g1, g2, g3))):
-        normed, inverse = layer_stats(x[0:144, :].astype(F32))
-        rows = x[144:288, :].astype(F32) + norm_backward(g[...].astype(F32), gain_ref[...], normed, inverse)
+def finish_kernel(x0, x1, x2, x3, m0, m1, m2, m3, g0, g1, g2, g3, gain_ref, out_ref):
+    for q, (x, m, g) in enumerate(zip((x0, x1, x2, x3), (m0, m1, m2, m3), (g0, g1, g2, g3))):
+        normed, inverse = layer_stats(x[...].astype(F32))
+        rows = m[...].astype(F32) + norm_backward(g[...].astype(F32), gain_ref[...], normed, inverse)
         for lat in range(3):
             piece = rows[lat * 48 : lat * 48 + 48].reshape(6, 8, 192)
             out_ref[(q // 2) * 3 + lat, (q % 2) * 6 : (q % 2) * 6 + 6] = piece.astype(BF)
 
 
-def finish(x, g, gain):
+def finish(x, m, g, gain):
     return pl.pallas_call(
         finish_kernel, out_shape=shape((6, 12, 8, 192), BF), compiler_params=VM, cost_estimate=cost(1), name="finish"
-    )(*x, *g, gain)
-
-
-def add_kernel(got_ref, out_ref):
+    )(*x, *m, *g, gain)
+
+
+def add_kernel(got_ref, b0, b1, b2, out_ref):
     total = got_ref[0].astype(F32)
     for i in range(1, 32):
         total = total + got_ref[i].astype(F32)
     out_ref[...] = total.astype(BF)
 
 
-def add(got):
-    return pl.pallas_call(
-        add_kernel, out_shape=shape((64, 128), BF), compiler_params=VM, cost_estimate=cost(1), name="add"
-    )(got)
-
-
-def spread_kernel(place_ref, own_ref, a_ref, b_ref, c_ref, out_ref):
+def add(got, after):
+    return pl.pallas_call(
+        add_kernel,
+        out_shape=shape((64, 128), BF),
+        in_specs=[VMEM] + [ANY] * 3,
+        compiler_params=VM,
+        cost_estimate=cost(1),
+        name="add",
+    )(got, *after)
+
+
+def spread_kernel(place_ref, own_ref, a_ref, b_ref, c_ref, after_ref, out_ref):
     own = own_ref[...].astype(F32)
     total = own + a_ref[...].astype(F32) + b_ref[...].astype(F32) + c_ref[...].astype(F32)
     row = place_ref[0] * 64 + lax.broadcasted_iota(I32, (64, 128), 0)
@@ -493,15 +511,15 @@
     out_ref[...] = jnp.broadcast_to(jnp.where(table, own, total).astype(BF)[None], (32, 64, 128))
 
 
-def spread(place, own, a, b, c):
+def spread(place, own, a, b, c, after):
     return pl.pallas_call(
         spread_kernel,
         out_shape=shape((32, 64, 128), BF),
-        in_specs=[pl.BlockSpec(memory_space=pltpu.SMEM)] + [VMEM] * 4,
+        in_specs=[pl.BlockSpec(memory_space=pltpu.SMEM)] + [VMEM] * 4 + [ANY],
         compiler_params=VM,
         cost_estimate=cost(1),
         name="spread",
-    )(place, own, a, b, c)
+    )(place, own, a, b, c, after)
 
 
 def unpack_kernel(weight_scale, table_scale, half_ref, in_ref,
@@ -605,30 +623,31 @@
         return field.transpose(1, 2, 0, 3)
 
     x_in, mid_in, up_in = turned(inputs), turned(residual_mid), turned(grad_out)
-    part2, first = head(mid_in, up_in, gain2, fc1_weight, fc2_weight.T)
+    *x, part2, first = head(x_in, mid_in, up_in, gain2, fc1_weight, fc2_weight.T)
     other2 = moved(part2, 0, 0, 1)
+    xw = shifted_parts(x)
     stage, lo, hi, terms, code = gather_first(
         bias_index, pos_bias[0].transpose(1, 0, 2), mask_ids.transpose(1, 0, 2), key_valid.transpose(1, 0, 2)
     )
-    *x, gain_two = middle(x_in, mid_in, up_in, part2, other2, gain2, lo)
-    xw = shifted_parts(x)
+    *gm, gain_two = middle(mid_in, up_in, part2, other2, gain2, lo)
+    gw = shifted_parts(gm)
     main, tail = gather_second(stage, lo, hi, terms, gain_two)
     low, q, k, v, prob, att = forward(xw, gain1, qkv_weight, main, tail, code)
-    part1, score, second = backward(xw, proj_weight, qkv_weight, low, q, k, v, prob, att)
+    part1, score, second = backward(gw, proj_weight, qkv_weight, low, q, k, v, prob, att)
     other1 = moved(part1, 0, 0, 1)
     table = scatter(score, lo, hi)
     *g, sums = meet(part1, other1, xw, first, second, table, gain_two)
     back = (moved(g[3], -1, -1, 0), moved(g[2], -1, 0, 0), moved(g[1], 0, -1, 0), g[0])
-    own = add(lax.all_to_all(sums.reshape(32, 64, 128), "lon", 0, 0))
+    own = add(lax.all_to_all(sums.reshape(32, 64, 128), "lon", 0, 0), back[:3])
+    result = finish(x, gm, back, gain1)
     place = lax.axis_index("lon").reshape(1)
-    totals = spread(place, own, swapped(own, 1), swapped(own, 2), swapped(own, 3))
+    totals = spread(place, own, swapped(own, 1), swapped(own, 2), swapped(own, 3), result)
     got = lax.all_to_all(totals, "lon", 0, 0)
     qkv_out, proj_out, up_out, down_out, one, two, table_out = unpack(
         weight_scale, table_scale, lax.axis_index("tp").reshape(1), got.reshape(2048, 128)
     )
-    result = finish(x, back, gain1).transpose(2, 0, 1, 3)
     return (
-        result,
+        result.transpose(2, 0, 1, 3),
         qkv_out,
         proj_out,
         up_out,

time: 110 us -> 107 us (0.973)
  blocking collectives: 22.3 us -> 0 us
  starting transfers between devices: 28.5 us -> 41.3 us
  waiting for transfers between devices: 26.1 us -> 36.8 us
  Pallas kernels: 31.7 us -> 26.5 us
    all_to_all x1 -> x0, blocking collectives: 22.3 us -> none  [local(): own = add(lax.all_to_all(sums.reshape(32, 64, 128), 'lon', 0, 0))]
    all_to_all x1, waiting for transfers between devices: 0.01 us -> 16.6 us  [local(): got = lax.all_to_all(totals, 'lon', 0, 0)]
    all_to_all x0 -> x1, starting transfers between devices: none -> 6.79 us  [local(): own = add(lax.all_to_all(sums.reshape(32, 64, 128), 'lon', 0, 0), back[:3])]
    ppermute x8 -> x11, starting transfers between devices: 19.5 us -> 24.2 us  [moved(): return lax.ppermute(value, ('lat', 'lon', 'tp'), pairs)]
    ppermute x3, waiting for transfers between devices: 3.86 us -> 0.64 us  [swapped(): return lax.ppermute(value, 'lat', pairs)]
    ppermute x8 -> x11, waiting for transfers between devices: 22.3 us -> 19.6 us  [moved(): return lax.ppermute(value, ('lat', 'lon', 'tp'), pairs)]
    pallas_call x1, Pallas kernels: 4.82 us -> 2.97 us  [forward(): pl.pallas_call(forward_kernel, out_shape=(shape((576, 192), BF), shape((5...]
    pallas_call x1, Pallas kernels: 5.02 us -> 3.58 us  [scatter(): pl.pallas_call(scatter_kernel, out_shape=shape((192, 256), F32), compiler...]
  transfers between devices with their start and end apart: 12 -> 16, of which waited for: 7 -> 6; matrix products, arithmetic and copies ran while one was open for 0% -> 0% of each run, Pallas kernels for 12% -> 13%
where the time goes in v4:
time: 107 us
  starting transfers between devices  41.3 us (39%)
  waiting for transfers between devices  36.8 us (34%)
  Pallas kernels  26.5 us (25%)
    ppermute x11, starting transfers between devices, moved(): return lax.ppermute(value, ('lat', 'lon', 'tp'), pairs)  24.2 us
    ppermute x11, waiting for transfers between devices, moved(): return lax.ppermute(value, ('lat', 'lon', 'tp'), pairs)  19.6 us
    all_to_all x1, waiting for transfers between devices, local(): got = lax.all_to_all(totals, 'lon', 0, 0)  16.6 us
    all_to_all x1, starting transfers between devices, local(): own = add(lax.all_to_all(sums.reshape(32, 64, 128), 'lon', 0, 0), back[:3])  6.79 us
    pallas_call x1, Pallas kernels, backward(): pl.pallas_call(backward_kernel, out_shape=(shape((576, 192), BF), shape((...  6.07 us
    all_to_all x1, starting transfers between devices, local(): got = lax.all_to_all(totals, 'lon', 0, 0)  5.18 us
    ppermute x3, starting transfers between devices, swapped(): return lax.ppermute(value, 'lat', pairs)  5.17 us
    pallas_call x1, Pallas kernels, head(): pl.pallas_call(head_kernel, out_shape=tuple((shape((144, 192), BF) for _...  3.62 us
  transfers between devices with their start and end apart: 16, of which 6 were waited for; matrix products, arithmetic and copies ran while one was open for 0% of the time, Pallas kernels for 13%

profile of v4, /device:TPU:1, one launch (start us, length us, event | category | flops | bytes accessed | tf_op | source)
XLA Modules:
  0.0 106.5 jit_solution(9690688179525658191)
XLA Ops:
  0.7 0.0 copy-start.16
  0.7 3.6 %head.1 = (bf16[144,192]{1,0:T(8,128)(2,1)}, bf16[144,192]{1,0:T(8,128)(2,1)}, bf16[144,192]{1,0:T(8,128)(2,1)}, bf16[144,192]{1,0:T(8,128)(2,1)}, bf16[576,192]{1,0:T(8,128)(2,1)}, /*index=5*/bf16[1152,128]{1,0:T(8,128)(2,1)}) custom-call(bf16[6,12,8,192]{3,2,1,0:T(8,128)(2,1)} %bitcast.35, bf16[6,12,8,192]{3,2,1,0:T(8,128)(2,1)} %bitcast.23, ...), custom_call_target="tpu_custom_call" | custom-call | flops 3000000000 | tf_op jit(solution)/shard_map/head/pallas_call | solution.py:131
  4.3 2.2 %collective-permute-start = (bf16[576,192]{1,0:T(8,128)(2,1)}, bf16[576,192]{1,0:T(8,128)(2,1)S(1)}, u32[]{:S(2)}, u32[]{:S(2)}) collective-permute-start(bf16[576,192]{1,0:T(8,128)(2,1)} %get-tuple-element.51.own_ref), channel_id=1, source_target_pairs={{1,0},{0,1},{3,2},{2,3},{5,4},{4,5},{7,6},{6,7},{9,8},{8,9},{11,10... | collective-permute-start | bytes 663560 | tf_op jit(solution)/shard_map/ppermute | solution.py:584
  6.5 7.8 %collective-permute-start.4 = (bf16[144,192]{1,0:T(8,128)(2,1)}, bf16[144,192]{1,0:T(8,128)(2,1)S(1)}, u32[]{:S(2)}, u32[]{:S(2)}) collective-permute-start(bf16[144,192]{1,0:T(8,128)(2,1)} %get-tuple-element.49.x2), channel_id=1, source_target_pairs={{2,0},{3,1},{4,2},{5,3},{6,4},{7,5},{8,6},{9,7},{10,8},{11,9},{12,... | collective-permute-start | bytes 165896 | tf_op jit(solution)/shard_map/ppermute | solution.py:584
  14.3 1.2 %collective-permute-start.5 = (bf16[144,192]{1,0:T(8,128)(2,1)}, bf16[144,192]{1,0:T(8,128)(2,1)S(1)}, u32[]{:S(2)}, u32[]{:S(2)}) collective-permute-start(bf16[144,192]{1,0:T(8,128)(2,1)} %get-tuple-element.48.x1), channel_id=1, source_target_pairs={{64,0},{65,1},{66,2},{67,3},{68,4},{69,5},{70,6},{71,7},{72,8},{73... | collective-permute-start | bytes 165896 | tf_op jit(solution)/shard_map/ppermute | solution.py:584
  15.5 2.2 %collective-permute-start.6 = (bf16[144,192]{1,0:T(8,128)(2,1)}, bf16[144,192]{1,0:T(8,128)(2,1)S(1)}, u32[]{:S(2)}, u32[]{:S(2)}) collective-permute-start(bf16[144,192]{1,0:T(8,128)(2,1)} %get-tuple-element.47.x0), channel_id=1, source_target_pairs={{66,0},{67,1},{68,2},{69,3},{70,4},{71,5},{72,6},{73,7},{74,8},{75... | collective-permute-start | bytes 165896 | tf_op jit(solution)/shard_map/ppermute | solution.py:584
  17.8 0.0 copy-start
  17.8 0.0 copy-start.1
  17.8 0.0 copy-start.2
  17.8 0.0 copy-start.12
  17.8 3.0 %gather_first.1 = (f32[1440,128]{1,0:T(8,128)S(1)}, s32[168,128]{1,0:T(8,128)S(1)}, s32[168,128]{1,0:T(8,128)S(1)}, bf16[160,512]{1,0:T(8,128)(2,1)S(1)}, f32[4,144]{1,0:T(4,128)S(1)}) custom-call(s32[144,144]{1,0:T(8,128)S(1)} %copy-done.4, bf16[144,144]{1,0:T(8,128)(2,1)S(1)} %copy-done.16, f32[3,4,3312]{2,1,0:T(4,128)S(1)} %bitcast.27, ...), custom_call_target="tpu_custom_call" | custom-call | flops 6000000000 | tf_op jit(solution)/shard_map/gather_first/pallas_call | solution.py:263
  20.8 0.0 collective-permute-done.other_ref
  20.9 0.6 middle.1
  21.5 0.3 collective-permute-start.1
  21.8 1.8 %collective-permute-start.2 = (bf16[144,192]{1,0:T(8,128)(2,1)S(1)}, bf16[144,192]{1,0:T(8,128)(2,1)S(1)}, u32[]{:S(2)}, u32[]{:S(2)}) collective-permute-start(bf16[144,192]{1,0:T(8,128)(2,1)S(1)} %get-tuple-element.54.m1), channel_id=1, source_target_pairs={{64,0},{65,1},{66,2},{67,3},{68,4},{69,5},{70,6},{71,7},{72,8},{73... | collective-permute-start | bytes 165896 | tf_op jit(solution)/shard_map/ppermute | solution.py:584
  23.6 2.1 %gather_second.1 = (f32[12,144,128]{2,1,0:T(8,128)S(1)}, f32[12,144,128]{2,1,0:T(8,128)S(1)}) custom-call(f32[1440,128]{1,0:T(8,128)S(1)} %get-tuple-element.57.first_stage, s32[168,128]{1,0:T(8,128)S(1)} %get-tuple-element.52.after_ref.lo_ref, s32[168,128]{1,0:T(8,128)S(1)} %get-tuple-element.58.hi_ref, bf16[160,512]{1,0:T(8,128)(2,1)S(1)} %get-tuple-element.59.terms_ref, ...), custom_call_target="tpu_custom_call" | custom-call | flops 4000000000 | tf_op jit(solution)/shard_map/gather_second/pallas_call | solution.py:290
  25.8 0.0 collective-permute-done.4.x1
  25.8 3.0 %collective-permute-start.3 = (bf16[144,192]{1,0:T(8,128)(2,1)S(1)}, bf16[144,192]{1,0:T(8,128)(2,1)S(1)}, u32[]{:S(2)}, u32[]{:S(2)}) collective-permute-start(bf16[144,192]{1,0:T(8,128)(2,1)S(1)} %get-tuple-element.53.m0), channel_id=1, source_target_pairs={{66,0},{67,1},{68,2},{69,3},{70,4},{71,5},{72,6},{73,7},{74,8},{75... | collective-permute-start | bytes 165896 | tf_op jit(solution)/shard_map/ppermute | solution.py:584
  28.7 0.0 collective-permute-done.5.x2
  28.7 0.0 collective-permute-done.6.x3
  28.8 0.0 copy-start.9
  28.8 3.0 %forward.1 = (bf16[576,192]{1,0:T(8,128)(2,1)S(1)}, bf16[576,96]{1,0:T(8,128)(2,1)S(1)}, bf16[576,96]{1,0:T(8,128)(2,1)S(1)}, bf16[576,96]{1,0:T(8,128)(2,1)S(1)...) custom-call(bf16[144,192]{1,0:T(8,128)(2,1)S(1)} %copy-done.18, ...), custom_call_target="tpu_custom_call" | custom-call | flops 5000000000 | tf_op jit(solution)/shard_map/forward/pallas_call | solution.py:335
  31.8 0.0 collective-permute-done.1.g1
  31.8 0.0 collective-permute-done.2.g2
  31.8 0.8 collective-permute-done.3.g3
  32.6 6.1 %backward.1 = (bf16[576,192]{1,0:T(8,128)(2,1)S(1)}, f32[12,168,128]{2,1,0:T(8,128)S(1)}, bf16[576,128]{1,0:T(8,128)(2,1)S(1)}) custom-call(bf16[144,192]{1,0:T(8,128)(2,1)S(1)} %get-tuple-element.56.g0.m3, bf16[144,192]{1,0:T(8,128)(2,1)S(1)} %collective-permute-done.1.g1, bf16[144,192]{1,0:T(8,128)(2,1)S(1)} %collective-permute-done.2.g2, ...), custom_call_target="tpu_custom_call" | custom-call | flops 7000000000 | tf_op jit(solution)/shard_map/backward/pallas_call | solution.py:402
  38.6 1.0 collective-permute-start.7
  39.7 3.6 %scatter.1.table_ref = f32[192,256]{1,0:T(8,128)S(1)} custom-call(f32[12,168,128]{2,1,0:T(8,128)S(1)} %get-tuple-element.73.score_ref, s32[168,128]{1,0:T(8,128)S(1)} %get-tuple-element.52.after_ref.lo_ref, s32[168,128]{1,0:T(8,128)S(1)} %get-tuple-element.58.hi_ref), custom_call_target="tpu_custom_call" | custom-call | flops 5000000000 | tf_op jit(solution)/shard_map/scatter/pallas_call | solution.py:436
  43.3 3.1 %collective-permute-done.7.other_ref = bf16[576,192]{1,0:T(8,128)(2,1)S(1)} collective-permute-done((bf16[576,192]{1,0:T(8,128)(2,1)S(1)}, bf16[576,192]{1,0:T(8,128)(2,1)S(1)}, u32[]{:S(2)}, u32[]{:S(2)}) %collective-permute-start.7) | collective-permute-done | bytes 221216 | tf_op jit(solution)/shard_map/ppermute | solution.py:584
  46.3 1.2 %meet.1 = (bf16[144,192]{1,0:T(8,128)(2,1)S(1)}, bf16[144,192]{1,0:T(8,128)(2,1)S(1)}, bf16[144,192]{1,0:T(8,128)(2,1)S(1)}, bf16[144,192]{1,0:T(8,128)(2,1)S(1)}, bf16[2048,128]{1,0:T(8,128)(2,1)}) custom-call(bf16[576,192]{1,0:T(8,128)(2,1)S(1)} %get-tuple-element.70.own_ref, bf16[576,192]{1,0:T(8,128)(2,1)S(1)} %collective-permute-done.7.other_ref, ...), custom_call_target="tpu_custom_call" | custom-call | flops 1000000000 | tf_op jit(solution)/shard_map/meet/pallas_call | solution.py:464
  47.5 6.8 %all-to-all-start = ((bf16[32,64,128]{2,1,0:T(8,128)(2,1)}), bf16[32,64,128]{2,1,0:T(8,128)(2,1)S(1)}, u32[]{:S(2)}, u32[]{:S(2)}) async-start(bf16[32,64,128]{2,1,0:T(8,128)(2,1)} %bitcast.13), calls=%async_computation | async-start | bytes 1048576 | tf_op jit(solution)/shard_map/all_to_all | solution.py:641
  54.3 1.3 %collective-permute-start.10 = (bf16[144,192]{1,0:T(8,128)(2,1)S(1)}, bf16[144,192]{1,0:T(8,128)(2,1)S(1)}, u32[]{:S(2)}, u32[]{:S(2)}) collective-permute-start(bf16[144,192]{1,0:T(8,128)(2,1)S(1)} %get-tuple-element.76), channel_id=1, source_target_pairs={{62,0},{63,1},{0,2},{1,3},{2,4},{3,5},{4,6},{5,7},{6,8},{7,9},{8,1... | collective-permute-start | bytes 165896 | tf_op jit(solution)/shard_map/ppermute | solution.py:584
  55.6 2.6 %collective-permute-start.8 = (bf16[144,192]{1,0:T(8,128)(2,1)S(1)}, bf16[144,192]{1,0:T(8,128)(2,1)S(1)}, u32[]{:S(2)}, u32[]{:S(2)}) collective-permute-start(bf16[144,192]{1,0:T(8,128)(2,1)S(1)} %get-tuple-element.74), channel_id=1, source_target_pairs={{254,0},{255,1},{192,2},{193,3},{194,4},{195,5},{196,6},{197,7},{1... | collective-permute-start | bytes 165896 | tf_op jit(solution)/shard_map/ppermute | solution.py:584
  58.2 0.7 collective-permute-start.9
  59.0 12.8 %collective-permute-done.10.g2.b2 = bf16[144,192]{1,0:T(8,128)(2,1)S(1)} collective-permute-done((bf16[144,192]{1,0:T(8,128)(2,1)S(1)}, bf16[144,192]{1,0:T(8,128)(2,1)S(1)}, u32[]{:S(2)}, u32[]{:S(2)}) %collective-permute-start.10) | collective-permute-done | bytes 55328 | tf_op jit(solution)/shard_map/ppermute | solution.py:584
  71.8 2.9 %collective-permute-done.8.g0.b0 = bf16[144,192]{1,0:T(8,128)(2,1)S(1)} collective-permute-done((bf16[144,192]{1,0:T(8,128)(2,1)S(1)}, bf16[144,192]{1,0:T(8,128)(2,1)S(1)}, u32[]{:S(2)}, u32[]{:S(2)}) %collective-permute-start.8) | collective-permute-done | bytes 55328 | tf_op jit(solution)/shard_map/ppermute | solution.py:584
  74.7 0.1 add.1.own_ref
  74.8 1.9 %collective-permute-start.11 = (bf16[64,128]{1,0:T(8,128)(2,1)S(1)}, bf16[64,128]{1,0:T(8,128)(2,1)S(1)}, u32[]{:S(2)}, u32[]{:S(2)}) collective-permute-start(bf16[64,128]{1,0:T(8,128)(2,1)S(1)} %add.1.own_ref), channel_id=1, source_target_pairs={{0,64},{64,0},{128,192},{192,128},{1,65},{65,1},{129,193},{193,129... | collective-permute-start | bytes 49160 | tf_op jit(solution)/shard_map/ppermute | solution.py:589
  76.7 0.5 collective-permute-start.12
  77.2 2.8 %collective-permute-start.13 = (bf16[64,128]{1,0:T(8,128)(2,1)S(1)}, bf16[64,128]{1,0:T(8,128)(2,1)S(1)}, u32[]{:S(2)}, u32[]{:S(2)}) collective-permute-start(bf16[64,128]{1,0:T(8,128)(2,1)S(1)} %add.1.own_ref), channel_id=1, source_target_pairs={{0,192},{64,128},{128,64},{192,0},{1,193},{65,129},{129,65},{193,1... | collective-permute-start | bytes 49160 | tf_op jit(solution)/shard_map/ppermute | solution.py:589
  80.0 1.2 %finish.1.after_ref = bf16[6,12,8,192]{3,2,1,0:T(8,128)(2,1)} custom-call(bf16[144,192]{1,0:T(8,128)(2,1)S(1)} %copy-done.6, bf16[144,192]{1,0:T(8,128)(2,1)S(1)} %copy-done.7, bf16[144,192]{1,0:T(8,128)(2,1)S(1)} %copy-done.8, bf16[144,192]{1,0:T(8,128)(2,1)S(1)} %copy-done.18, bf16[144,192]{1,0:T(8,128)(2,1)S(1)} %get-tuple-element.53.m0, ...), custom_call_target="tpu_custom_call" | custom-call | flops 1000000000 | tf_op jit(solution)/shard_map/finish/pallas_call | solution.py:483
  81.2 0.0 collective-permute-done.11.a_ref
  81.2 0.6 collective-permute-done.13.c_ref
  81.9 1.0 copy-done.14
  82.8 0.9 spread.1
  83.7 5.2 %all-to-all-start.1 = ((bf16[32,64,128]{2,1,0:T(8,128)(2,1)}), bf16[32,64,128]{2,1,0:T(8,128)(2,1)S(1)}, u32[]{:S(2)}, u32[]{:S(2)}) async-start(bf16[32,64,128]{2,1,0:T(8,128)(2,1)} %spread.1), calls=%async_computation.1 | async-start | bytes 1048576 | tf_op jit(solution)/shard_map/all_to_all | solution.py:645
  88.9 16.6 %all-to-all-done.1 = bf16[32,64,128]{2,1,0:T(8,128)(2,1)S(1)} async-done(((bf16[32,64,128]{2,1,0:T(8,128)(2,1)}), bf16[32,64,128]{2,1,0:T(8,128)(2,1)S(1)}, u32[]{:S(2)}, u32[]{:S(2)}) %all-to-all-start.1) | async-done | bytes 524320 | tf_op jit(solution)/shard_map/all_to_all | solution.py:645
  105.4 1.1 %unpack.1 = (f32[3,192,96]{2,1,0:T(8,128)}, f32[96,192]{1,0:T(8,128)}, f32[192,384]{1,0:T(8,128)}, f32[192,384]{1,0:T(8,128)}, f32[1,96]{1,0:T(1,128)}, /*index=5*/f32[1,96]{1,0:T(1,128)}, f32[3,4,3312]{2,1,0:T(4,128)}) custom-call(s32[1]{0:T(128)} %bitcast.11.half_ref, bf16[2048,128]{1,0:T(8,128)(2,1)S(1)} %bitcast.22), custom_call_target="tpu_custom_call" | custom-call | tf_op jit(solution)/shard_map/unpack/pallas_call | solution.py:559
  (34 shorter events, 0.1 us)
Async XLA Ops:
  0.6 17.1 %copy-start.3 = (f32[1,4,3,3312]{3,1,2,0:T(4,128)S(1)}, f32[1,4,3,3312]{3,1,2,0:T(4,128)}, u32[]{:S(2)}) copy-start(f32[1,4,3,3312]{3,1,2,0:T(4,128)} %param.22) | copy-start | bytes 476932
  0.6 17.1 %copy-start.4 = (s32[144,144]{1,0:T(8,128)S(1)}, s32[144,144]{1,0:T(8,128)}, u32[]{:S(2)}) copy-start(s32[144,144]{1,0:T(8,128)} %index_ref.1) | copy-start | bytes 248836
  0.7 17.1 %copy-start.10 = (s32[8,6,12]{2,0,1:T(8,128)S(1)}, s32[8,6,12]{2,0,1:T(8,128)}, u32[]{:S(2)}) copy-start(s32[8,6,12]{2,0,1:T(8,128)} %param.19) | copy-start | bytes 6916
  0.7 17.1 %copy-start.11 = (s32[8,6,12]{2,0,1:T(8,128)S(1)}, s32[8,6,12]{2,0,1:T(8,128)}, u32[]{:S(2)}) copy-start(s32[8,6,12]{2,0,1:T(8,128)} %param.20) | copy-start | bytes 6916
  0.7 17.1 %copy-start.16 = (bf16[144,144]{1,0:T(8,128)(2,1)S(1)}, bf16[144,144]{1,0:T(8,128)(2,1)}, u32[]{:S(2)}) copy-start(bf16[144,144]{1,0:T(8,128)(2,1)} %constant.12.clone.order_ref) | copy-start | bytes 124420
  4.3 16.5 %collective-permute-start = (bf16[576,192]{1,0:T(8,128)(2,1)}, bf16[576,192]{1,0:T(8,128)(2,1)S(1)}, u32[]{:S(2)}, u32[]{:S(2)}) collective-permute-start(bf16[576,192]{1,0:T(8,128)(2,1)} %get-tuple-element.51.own_ref), channel_id=1, source_target_pairs={{1,0},{0,1},{3,2},{2,3},{5,4},{4,5},{7,6},{6,7},{9,8},{8,9},{11,10... | collective-permute-start | bytes 663560 | tf_op jit(solution)/shard_map/ppermute | solution.py:584
  6.5 19.2 %collective-permute-start.4 = (bf16[144,192]{1,0:T(8,128)(2,1)}, bf16[144,192]{1,0:T(8,128)(2,1)S(1)}, u32[]{:S(2)}, u32[]{:S(2)}) collective-permute-start(bf16[144,192]{1,0:T(8,128)(2,1)} %get-tuple-element.49.x2), channel_id=1, source_target_pairs={{2,0},{3,1},{4,2},{5,3},{6,4},{7,5},{8,6},{9,7},{10,8},{11,9},{12,... | collective-permute-start | bytes 165896 | tf_op jit(solution)/shard_map/ppermute | solution.py:584
  14.3 14.5 %collective-permute-start.5 = (bf16[144,192]{1,0:T(8,128)(2,1)}, bf16[144,192]{1,0:T(8,128)(2,1)S(1)}, u32[]{:S(2)}, u32[]{:S(2)}) collective-permute-start(bf16[144,192]{1,0:T(8,128)(2,1)} %get-tuple-element.48.x1), channel_id=1, source_target_pairs={{64,0},{65,1},{66,2},{67,3},{68,4},{69,5},{70,6},{71,7},{72,8},{73... | collective-permute-start | bytes 165896 | tf_op jit(solution)/shard_map/ppermute | solution.py:584
  15.5 13.2 %collective-permute-start.6 = (bf16[144,192]{1,0:T(8,128)(2,1)}, bf16[144,192]{1,0:T(8,128)(2,1)S(1)}, u32[]{:S(2)}, u32[]{:S(2)}) collective-permute-start(bf16[144,192]{1,0:T(8,128)(2,1)} %get-tuple-element.47.x0), channel_id=1, source_target_pairs={{66,0},{67,1},{68,2},{69,3},{70,4},{71,5},{72,6},{73,7},{74,8},{75... | collective-permute-start | bytes 165896 | tf_op jit(solution)/shard_map/ppermute | solution.py:584
  17.8 3.1 %copy-start = (bf16[8,6,12,192]{3,0,2,1:T(8,128)(2,1)S(1)}, bf16[8,6,12,192]{3,0,2,1:T(8,128)(2,1)}, u32[]{:S(2)}) copy-start(bf16[8,6,12,192]{3,0,2,1:T(8,128)(2,1)} %param.17) | copy-start | bytes 663556
  17.8 3.1 %copy-start.1 = (bf16[8,6,12,192]{3,0,2,1:T(8,128)(2,1)S(1)}, bf16[8,6,12,192]{3,0,2,1:T(8,128)(2,1)}, u32[]{:S(2)}) copy-start(bf16[8,6,12,192]{3,0,2,1:T(8,128)(2,1)} %param.18) | copy-start | bytes 663556
  17.8 3.1 %copy-start.2 = (bf16[576,192]{1,0:T(8,128)(2,1)S(1)}, bf16[576,192]{1,0:T(8,128)(2,1)}, u32[]{:S(2)}) copy-start(bf16[576,192]{1,0:T(8,128)(2,1)} %get-tuple-element.51.own_ref) | copy-start | bytes 663556
  17.8 3.1 %copy-start.12 = (f32[192]{0:T(256)S(1)}, f32[192]{0:T(256)}, u32[]{:S(2)}) copy-start(f32[192]{0:T(256)} %param.26) | copy-start | bytes 2308
  21.5 10.3 %collective-permute-start.1 = (bf16[144,192]{1,0:T(8,128)(2,1)S(1)}, bf16[144,192]{1,0:T(8,128)(2,1)S(1)}, u32[]{:S(2)}, u32[]{:S(2)}) collective-permute-start(bf16[144,192]{1,0:T(8,128)(2,1)S(1)} %get-tuple-element.55.m2), channel_id=1, source_target_pairs={{2,0},{3,1},{4,2},{5,3},{6,4},{7,5},{8,6},{9,7},{10,8},{11,9},{12,... | collective-permute-start | bytes 165896 | tf_op jit(solution)/shard_map/ppermute | solution.py:584
  21.8 10.0 %collective-permute-start.2 = (bf16[144,192]{1,0:T(8,128)(2,1)S(1)}, bf16[144,192]{1,0:T(8,128)(2,1)S(1)}, u32[]{:S(2)}, u32[]{:S(2)}) collective-permute-start(bf16[144,192]{1,0:T(8,128)(2,1)S(1)} %get-tuple-element.54.m1), channel_id=1, source_target_pairs={{64,0},{65,1},{66,2},{67,3},{68,4},{69,5},{70,6},{71,7},{72,8},{73... | collective-permute-start | bytes 165896 | tf_op jit(solution)/shard_map/ppermute | solution.py:584
  23.6 5.2 %copy-start.5 = (bf16[3,192,96]{2,1,0:T(8,128)(2,1)S(1)}, bf16[3,192,96]{2,1,0:T(8,128)(2,1)}, u32[]{:S(2)}) copy-start(bf16[3,192,96]{2,1,0:T(8,128)(2,1)} %qkv_ref.3) | copy-start | bytes 331780
  23.6 5.2 %copy-start.13 = (f32[192]{0:T(256)S(1)}, f32[192]{0:T(256)}, u32[]{:S(2)}) copy-start(f32[192]{0:T(256)} %param.23) | copy-start | bytes 2308
  23.6 5.2 %copy-start.15 = (bf16[144,144]{1,0:T(8,128)(2,1)S(1)}, bf16[144,144]{1,0:T(8,128)(2,1)}, u32[]{:S(2)}) copy-start(bf16[144,144]{1,0:T(8,128)(2,1)} %constant.13.clone.order_ref) | copy-start | bytes 124420
  23.6 5.2 %copy-start.18 = (bf16[144,192]{1,0:T(8,128)(2,1)S(1)}, bf16[144,192]{1,0:T(8,128)(2,1)}, u32[]{:S(2)}) copy-start(bf16[144,192]{1,0:T(8,128)(2,1)} %get-tuple-element.50.x0.x3) | copy-start | bytes 165892
  25.8 6.8 %collective-permute-start.3 = (bf16[144,192]{1,0:T(8,128)(2,1)S(1)}, bf16[144,192]{1,0:T(8,128)(2,1)S(1)}, u32[]{:S(2)}, u32[]{:S(2)}) collective-permute-start(bf16[144,192]{1,0:T(8,128)(2,1)S(1)} %get-tuple-element.53.m0), channel_id=1, source_target_pairs={{66,0},{67,1},{68,2},{69,3},{70,4},{71,5},{72,6},{73,7},{74,8},{75... | collective-permute-start | bytes 165896 | tf_op jit(solution)/shard_map/ppermute | solution.py:584
  28.8 3.8 %copy-start.9 = (bf16[96,192]{1,0:T(8,128)(2,1)S(1)}, bf16[96,192]{1,0:T(8,128)(2,1)}, u32[]{:S(2)}) copy-start(bf16[96,192]{1,0:T(8,128)(2,1)} %proj_ref.1) | copy-start | bytes 110596
  38.6 7.7 %collective-permute-start.7 = (bf16[576,192]{1,0:T(8,128)(2,1)S(1)}, bf16[576,192]{1,0:T(8,128)(2,1)S(1)}, u32[]{:S(2)}, u32[]{:S(2)}) collective-permute-start(bf16[576,192]{1,0:T(8,128)(2,1)S(1)} %get-tuple-element.70.own_ref), channel_id=1, source_target_pairs={{1,0},{0,1},{3,2},{2,3},{5,4},{4,5},{7,6},{6,7},{9,8},{8,9},{11,10... | collective-permute-start | bytes 663560 | tf_op jit(solution)/shard_map/ppermute | solution.py:584
  39.7 6.7 %copy-start.17 = (bf16[1152,128]{1,0:T(8,128)(2,1)S(1)}, bf16[1152,128]{1,0:T(8,128)(2,1)}, u32[]{:S(2)}) copy-start(bf16[1152,128]{1,0:T(8,128)(2,1)} %get-tuple-element.71.first_ref) | copy-start | bytes 884740
  47.5 27.2 %all-to-all-start = ((bf16[32,64,128]{2,1,0:T(8,128)(2,1)}), bf16[32,64,128]{2,1,0:T(8,128)(2,1)S(1)}, u32[]{:S(2)}, u32[]{:S(2)}) async-start(bf16[32,64,128]{2,1,0:T(8,128)(2,1)} %bitcast.13), calls=%async_computation | async-start | bytes 1048576 | tf_op jit(solution)/shard_map/all_to_all | solution.py:641
  54.3 17.5 %collective-permute-start.10 = (bf16[144,192]{1,0:T(8,128)(2,1)S(1)}, bf16[144,192]{1,0:T(8,128)(2,1)S(1)}, u32[]{:S(2)}, u32[]{:S(2)}) collective-permute-start(bf16[144,192]{1,0:T(8,128)(2,1)S(1)} %get-tuple-element.76), channel_id=1, source_target_pairs={{62,0},{63,1},{0,2},{1,3},{2,4},{3,5},{4,6},{5,7},{6,8},{7,9},{8,1... | collective-permute-start | bytes 165896 | tf_op jit(solution)/shard_map/ppermute | solution.py:584
  55.6 19.1 %collective-permute-start.8 = (bf16[144,192]{1,0:T(8,128)(2,1)S(1)}, bf16[144,192]{1,0:T(8,128)(2,1)S(1)}, u32[]{:S(2)}, u32[]{:S(2)}) collective-permute-start(bf16[144,192]{1,0:T(8,128)(2,1)S(1)} %get-tuple-element.74), channel_id=1, source_target_pairs={{254,0},{255,1},{192,2},{193,3},{194,4},{195,5},{196,6},{197,7},{1... | collective-permute-start | bytes 165896 | tf_op jit(solution)/shard_map/ppermute | solution.py:584
  58.2 16.4 %collective-permute-start.9 = (bf16[144,192]{1,0:T(8,128)(2,1)S(1)}, bf16[144,192]{1,0:T(8,128)(2,1)S(1)}, u32[]{:S(2)}, u32[]{:S(2)}) collective-permute-start(bf16[144,192]{1,0:T(8,128)(2,1)S(1)} %get-tuple-element.75), channel_id=1, source_target_pairs={{192,0},{193,1},{194,2},{195,3},{196,4},{197,5},{198,6},{199,7},{2... | collective-permute-start | bytes 165896 | tf_op jit(solution)/shard_map/ppermute | solution.py:584
  59.0 21.0 %copy-start.6 = (bf16[144,192]{1,0:T(8,128)(2,1)S(1)}, bf16[144,192]{1,0:T(8,128)(2,1)}, u32[]{:S(2)}) copy-start(bf16[144,192]{1,0:T(8,128)(2,1)} %get-tuple-element.47.x0) | copy-start | bytes 165892
  59.0 21.0 %copy-start.7 = (bf16[144,192]{1,0:T(8,128)(2,1)S(1)}, bf16[144,192]{1,0:T(8,128)(2,1)}, u32[]{:S(2)}) copy-start(bf16[144,192]{1,0:T(8,128)(2,1)} %get-tuple-element.48.x1) | copy-start | bytes 165892
  59.0 21.0 %copy-start.8 = (bf16[144,192]{1,0:T(8,128)(2,1)S(1)}, bf16[144,192]{1,0:T(8,128)(2,1)}, u32[]{:S(2)}) copy-start(bf16[144,192]{1,0:T(8,128)(2,1)} %get-tuple-element.49.x2) | copy-start | bytes 165892
  74.8 6.4 %collective-permute-start.11 = (bf16[64,128]{1,0:T(8,128)(2,1)S(1)}, bf16[64,128]{1,0:T(8,128)(2,1)S(1)}, u32[]{:S(2)}, u32[]{:S(2)}) collective-permute-start(bf16[64,128]{1,0:T(8,128)(2,1)S(1)} %add.1.own_ref), channel_id=1, source_target_pairs={{0,64},{64,0},{128,192},{192,128},{1,65},{65,1},{129,193},{193,129... | collective-permute-start | bytes 49160 | tf_op jit(solution)/shard_map/ppermute | solution.py:589
  76.7 4.5 %collective-permute-start.12 = (bf16[64,128]{1,0:T(8,128)(2,1)S(1)}, bf16[64,128]{1,0:T(8,128)(2,1)S(1)}, u32[]{:S(2)}, u32[]{:S(2)}) collective-permute-start(bf16[64,128]{1,0:T(8,128)(2,1)S(1)} %add.1.own_ref), channel_id=1, source_target_pairs={{0,128},{64,192},{128,0},{192,64},{1,129},{65,193},{129,1},{193,65... | collective-permute-start | bytes 49160 | tf_op jit(solution)/shard_map/ppermute | solution.py:589
  77.2 4.7 %collective-permute-start.13 = (bf16[64,128]{1,0:T(8,128)(2,1)S(1)}, bf16[64,128]{1,0:T(8,128)(2,1)S(1)}, u32[]{:S(2)}, u32[]{:S(2)}) collective-permute-start(bf16[64,128]{1,0:T(8,128)(2,1)S(1)} %add.1.own_ref), channel_id=1, source_target_pairs={{0,192},{64,128},{128,64},{192,0},{1,193},{65,129},{129,65},{193,1... | collective-permute-start | bytes 49160 | tf_op jit(solution)/shard_map/ppermute | solution.py:589
  81.9 1.0 copy-start.14
  83.7 21.8 %all-to-all-start.1 = ((bf16[32,64,128]{2,1,0:T(8,128)(2,1)}), bf16[32,64,128]{2,1,0:T(8,128)(2,1)S(1)}, u32[]{:S(2)}, u32[]{:S(2)}) async-start(bf16[32,64,128]{2,1,0:T(8,128)(2,1)} %spread.1), calls=%async_computation.1 | async-start | bytes 1048576 | tf_op jit(solution)/shard_map/all_to_all | solution.py:645

commit v5 on v4

--- a/solution.py
+++ b/solution.py
@@ -17,6 +17,7 @@
 VMEM = pl.BlockSpec(memory_space=pltpu.VMEM)
 VM = pltpu.CompilerParams(vmem_limit_bytes=24 * 1024 * 1024)
 ALL = pltpu.CompilerParams(vmem_limit_bytes=63 * 1024 * 1024)
+SMEM = pl.BlockSpec(memory_space=pltpu.SMEM)
 ANY = pl.BlockSpec(memory_space=pl.ANY)
 
 
@@ -349,13 +350,11 @@
     )(*x, level_order(), gain, qkv, main, tail, code)
 
 
-def backward_kernel(g0, g1, g2, g3, order_ref, proj_ref, qkv_ref, low_ref, q_ref, k_ref, v_ref, prob_ref, att_ref,
-                    part_ref, score_ref, grads_ref, scratch, gatt, gcols):
+def backward_kernel(g0, g1, g2, g3, order_ref, proj_ref, qkv_ref, q_ref, k_ref, v_ref, prob_ref,
+                    part_ref, score_ref, gcols, grad_ref, scratch, gatt):
     to_windows((g0, g1, g2, g3), order_ref[...], scratch)
     grad = scratch[...].astype(BF)
-    gproj = dot_tn(att_ref[...], grad).astype(BF)
-    grads_ref[0:96, :] = gproj[:, 0:128]
-    grads_ref[96:144, :] = jnp.concatenate([gproj[0:48, 128:192], gproj[48:96, 128:192]], axis=1)
+    grad_ref[...] = grad
     gatt[...] = dot_nt(grad, proj_ref[...]).astype(BF)
 
     def window(w, _):
@@ -368,8 +367,7 @@
             values.append(dot_tn(prob.astype(BF), above[:, cols]))
             grad_prob = dot_nt(above[:, cols], value[:, cols])
             score = prob * (grad_prob - jnp.sum(grad_prob * prob, axis=-1, keepdims=True))
-            score_ref[w * 3 + h, 0:144, :] = score[:, 0:128]
-            score_ref[w * 3 + h, 144:168, :] = pack_tail(score[:, 128:144].astype(BF))
+            score_ref[w * 3 + h] = score
             low_score = (score * (HD ** -0.5)).astype(BF)
             queries.append(dot_nn(low_score, key[:, cols]))
             keys.append(dot_tn(low_score, query[:, cols]))
@@ -379,18 +377,10 @@
         return 0
 
     lax.fori_loop(0, 4, window, 0, unroll=True)
-    low = low_ref[...]
     total = None
-    gqkv = []
     for j in range(3):
-        cols = gcols[j]
-        gqkv.append(dot_tn(low, cols).astype(BF))
-        term = dot_nt(cols, qkv_ref[j])
+        term = dot_nt(gcols[j], qkv_ref[j])
         total = term if total is None else total + term
-    a, b, c = gqkv
-    grads_ref[144:336, :] = jnp.concatenate([a, c[:, 0:32]], axis=1)
-    grads_ref[336:528, :] = jnp.concatenate([b, c[:, 32:64]], axis=1)
-    grads_ref[528:576, :] = jnp.concatenate([c[i * 48 : i * 48 + 48, 64:96] for i in range(4)], axis=1)
     scratch[...] = total
     for s in range(4):
         pieces = [scratch[w * 144 + s * 36 : w * 144 + s * 36 + 36, :] for w in range(4)]
@@ -398,55 +388,64 @@
         part_ref[s * 144 : s * 144 + 144, :] = dot_tn(order_ref[...], piece).astype(BF)
 
 
-def backward(g, proj, qkv, low, q, k, v, prob, att):
+def backward(g, proj, qkv, q, k, v, prob):
     return pl.pallas_call(
         backward_kernel,
         out_shape=(
             shape((576, 192), BF),
-            shape((12, 168, 128), F32),
-            shape((576, 128), BF),
+            shape((12, 144, 144), F32),
+            shape((3, 576, 96), BF),
+            shape((576, 192), BF),
         ),
-        scratch_shapes=[pltpu.VMEM((576, 192), F32), pltpu.VMEM((576, 96), BF), pltpu.VMEM((3, 576, 96), BF)],
+        scratch_shapes=[pltpu.VMEM((576, 192), F32), pltpu.VMEM((576, 96), BF)],
         compiler_params=VM,
         cost_estimate=cost(7),
         name="backward",
-    )(*g, level_order(), proj, qkv, low, q, k, v, prob, att)
-
-
-def scatter_kernel(score_ref, lo_ref, hi_ref, out_ref):
+    )(*g, level_order(), proj, qkv, q, k, v, prob)
+
+
+def scatter_kernel(score_ref, lo_ref, hi_ref, low_ref, gcols, att_ref, grad_ref, out_ref, grads_ref, tails):
     out_ref[...] = jnp.zeros((192, 256), F32)
     place = lax.broadcasted_iota(I32, (16, 128), 0)
-
-    def step(i, _):
+    for r in range(12):
+        tails[r] = pack_tail(score_ref[r, :, 128:144].astype(BF))
+    for i in range(9):
         left, right = [], []
         for j in range(18):
-            row = pl.ds(i * 18 + j, 1)
+            row = slice(i * 18 + j, i * 18 + j + 1)
             here = place == hi_ref[row, :]
             right.append(one_hot(lo_ref[row, :]))
-            left.append(
-                jnp.concatenate([jnp.where(here, score_ref[r, row, :], 0.0).astype(BF) for r in range(12)], axis=0)
-            )
+            lines = [score_ref[r, row, 0:128] if i < 8 else tails[r, j : j + 1, :] for r in range(12)]
+            left.append(jnp.concatenate([jnp.where(here, line, 0.0).astype(BF) for line in lines], axis=0))
         out_ref[...] += dot_nt(jnp.concatenate(left, axis=1), jnp.concatenate(right, axis=1))
-        return 0
-
-    lax.fori_loop(0, 9, step, 0, unroll=True)
-
-
-def scatter(score, lo, hi):
-    return pl.pallas_call(
-        scatter_kernel, out_shape=shape((192, 256), F32), compiler_params=VM, cost_estimate=cost(5), name="scatter"
-    )(score, lo, hi)
-
-
-def meet_kernel(own_ref, other_ref, x0, x1, x2, x3, first_ref, second_ref, table_ref, two_ref,
-                o0, o1, o2, o3, out_ref):
+    gproj = dot_tn(att_ref[...], grad_ref[...]).astype(BF)
+    grads_ref[0:96, :] = gproj[:, 0:128]
+    grads_ref[96:144, :] = jnp.concatenate([gproj[0:48, 128:192], gproj[48:96, 128:192]], axis=1)
+    low = low_ref[...]
+    a, b, c = [dot_tn(low, gcols[j]).astype(BF) for j in range(3)]
+    grads_ref[144:336, :] = jnp.concatenate([a, c[:, 0:32]], axis=1)
+    grads_ref[336:528, :] = jnp.concatenate([b, c[:, 32:64]], axis=1)
+    grads_ref[528:576, :] = jnp.concatenate([c[i * 48 : i * 48 + 48, 64:96] for i in range(4)], axis=1)
+
+
+def scatter(score, lo, hi, low, gcols, att, grad):
+    return pl.pallas_call(
+        scatter_kernel,
+        out_shape=(shape((192, 256), F32), shape((576, 128), BF)),
+        scratch_shapes=[pltpu.VMEM((12, 24, 128), F32)],
+        compiler_params=VM,
+        cost_estimate=cost(5),
+        name="scatter",
+    )(score, lo, hi, low, gcols, att, grad)
+
+
+def meet_kernel(place_ref, own_ref, other_ref, x0, x1, x2, x3, first_ref, second_ref, table_ref, two_ref, out_ref):
     gain = jnp.zeros((1, 192), F32)
-    for s, (x, o) in enumerate(zip((x0, x1, x2, x3), (o0, o1, o2, o3))):
+    for s, x in enumerate((x0, x1, x2, x3)):
         rows = slice(s * 144, s * 144 + 144)
         grad = own_ref[rows, :].astype(F32) + other_ref[rows, :].astype(F32)
         normed, _ = layer_stats(x[...].astype(F32))
         gain = gain + jnp.sum(grad * normed, axis=0, keepdims=True)
-        o[...] = grad.astype(BF)
     out_ref[0:1152, :] = first_ref[...]
     out_ref[1152:1728, :] = second_ref[...]
     rows = []
@@ -460,20 +459,22 @@
     out_ref[1728:2048, :] = jnp.concatenate(rows, axis=0).astype(BF)
 
 
-def meet(own, other, x, first, second, table, two):
+def meet(place, own, other, x, first, second, table, two):
     return pl.pallas_call(
         meet_kernel,
-        out_shape=tuple(shape((144, 192), BF) for _ in range(4)) + (shape((2048, 128), BF),),
+        out_shape=shape((2048, 128), BF),
+        in_specs=[SMEM] + [VMEM] * 10,
         compiler_params=VM,
         cost_estimate=cost(1),
         name="meet",
-    )(own, other, *x, first, second, table, two)
-
-
-def finish_kernel(x0, x1, x2, x3, m0, m1, m2, m3, g0, g1, g2, g3, gain_ref, out_ref):
+    )(place, own, other, *x, first, second, table, two)
+
+
+def finish_kernel(x0, x1, x2, x3, m0, m1, m2, m3, g0, g1, g2, g3, gain_ref, out_ref, token_ref):
+    token_ref[...] = jnp.zeros((8, 128), F32)
     for q, (x, m, g) in enumerate(zip((x0, x1, x2, x3), (m0, m1, m2, m3), (g0, g1, g2, g3))):
         normed, inverse = layer_stats(x[...].astype(F32))
-        rows = m[...].astype(F32) + norm_backward(g[...].astype(F32), gain_ref[...], normed, inverse)
+        rows = m[...].astype(F32) + norm_backward(g[0:144, :].astype(F32), gain_ref[...], normed, inverse)
         for lat in range(3):
             piece = rows[lat * 48 : lat * 48 + 48].reshape(6, 8, 192)
             out_ref[(q // 2) * 3 + lat, (q % 2) * 6 : (q % 2) * 6 + 6] = piece.astype(BF)
@@ -481,31 +482,39 @@
 
 def finish(x, m, g, gain):
     return pl.pallas_call(
-        finish_kernel, out_shape=shape((6, 12, 8, 192), BF), compiler_params=VM, cost_estimate=cost(1), name="finish"
+        finish_kernel,
+        out_shape=(shape((6, 12, 8, 192), BF), shape((8, 128), F32)),
+        compiler_params=VM,
+        cost_estimate=cost(1),
+        name="finish",
     )(*x, *m, *g, gain)
 
 
-def add_kernel(got_ref, b0, b1, b2, out_ref):
+def add_kernel(got_ref, own_ref, other_ref, out_ref, g0, g1, g2, g3):
     total = got_ref[0].astype(F32)
     for i in range(1, 32):
         total = total + got_ref[i].astype(F32)
     out_ref[...] = total.astype(BF)
-
-
-def add(got, after):
+    for s, out in enumerate((g0, g1, g2, g3)):
+        rows = slice(s * 144, s * 144 + 144)
+        out[0:144, :] = (own_ref[rows, :].astype(F32) + other_ref[rows, :].astype(F32)).astype(BF)
+    g2[144:208, :] = jnp.concatenate([total, jnp.zeros((64, 64), F32)], axis=1).astype(BF)
+
+
+def add(got, own, other):
+    quarter = shape((144, 192), BF)
     return pl.pallas_call(
         add_kernel,
-        out_shape=shape((64, 128), BF),
-        in_specs=[VMEM] + [ANY] * 3,
+        out_shape=(shape((64, 128), BF), quarter, quarter, shape((208, 192), BF), quarter),
         compiler_params=VM,
         cost_estimate=cost(1),
         name="add",
-    )(got, *after)
+    )(got, own, other)
 
 
 def spread_kernel(place_ref, own_ref, a_ref, b_ref, c_ref, after_ref, out_ref):
     own = own_ref[...].astype(F32)
-    total = own + a_ref[...].astype(F32) + b_ref[...].astype(F32) + c_ref[...].astype(F32)
+    total = own + a_ref[144:208, 0:128].astype(F32) + b_ref[...].astype(F32) + c_ref[...].astype(F32)
     row = place_ref[0] * 64 + lax.broadcasted_iota(I32, (64, 128), 0)
     table = (row >= 1728) & (row < 2040)
     out_ref[...] = jnp.broadcast_to(jnp.where(table, own, total).astype(BF)[None], (32, 64, 128))
@@ -515,14 +524,14 @@
     return pl.pallas_call(
         spread_kernel,
         out_shape=shape((32, 64, 128), BF),
-        in_specs=[pl.BlockSpec(memory_space=pltpu.SMEM)] + [VMEM] * 4 + [ANY],
+        in_specs=[SMEM] + [VMEM] * 4 + [ANY],
         compiler_params=VM,
         cost_estimate=cost(1),
         name="spread",
     )(place, own, a, b, c, after)
 
 
-def unpack_kernel(weight_scale, table_scale, half_ref, in_ref,
+def unpack_kernel(weight_scale, table_scale, place_ref, in_ref,
                   qkv_ref, proj_ref, upg_ref, down_ref, one_ref, two_ref, table_ref):
     def rows(start, stop):
         return in_ref[start:stop, :].astype(F32) * weight_scale
@@ -552,10 +561,10 @@
     for start, out in ((312, one_ref), (314, two_ref)):
         line = table[start : start + 1]
         upper = jnp.concatenate([line[:, 96:128], table[start + 1 : start + 2, 0:64]], axis=1)
-        out[...] = jnp.where(half_ref[0] == 0, line[:, 0:96], upper) * weight_scale
-
-
-def unpack(weight_scale, table_scale, half, got):
+        out[...] = jnp.where(place_ref[1] == 0, line[:, 0:96], upper) * weight_scale
+
+
+def unpack(weight_scale, table_scale, place, got):
     return pl.pallas_call(
         functools.partial(unpack_kernel, weight_scale, table_scale),
         out_shape=(
@@ -567,10 +576,10 @@
             shape((1, 96), F32),
             shape((3, 4, 3312), F32),
         ),
-        in_specs=[pl.BlockSpec(memory_space=pltpu.SMEM), VMEM],
+        in_specs=[SMEM, VMEM],
         compiler_params=VM,
         name="unpack",
-    )(half, got)
+    )(place, got)
 
 
 def moved(value, band, sector, half):
@@ -582,11 +591,6 @@
                 source = ((a + band) % sizes[0], (b + sector) % sizes[1], (c + half) % sizes[2])
                 pairs.append(tuple((x * sizes[1] + y) * sizes[2] + z for x, y, z in (source, (a, b, c))))
     return lax.ppermute(value, ("lat", "lon", "tp"), pairs)
-
-
-def swapped(value, bit):
-    pairs = [(a, a ^ bit) for a in range(lax.axis_size("lat"))]
-    return lax.ppermute(value, "lat", pairs)
 
 
 def shifted_parts(quarters):
@@ -633,18 +637,19 @@
     gw = shifted_parts(gm)
     main, tail = gather_second(stage, lo, hi, terms, gain_two)
     low, q, k, v, prob, att = forward(xw, gain1, qkv_weight, main, tail, code)
-    part1, score, second = backward(gw, proj_weight, qkv_weight, low, q, k, v, prob, att)
+    part1, score, gcols, grad = backward(gw, proj_weight, qkv_weight, q, k, v, prob)
     other1 = moved(part1, 0, 0, 1)
-    table = scatter(score, lo, hi)
-    *g, sums = meet(part1, other1, xw, first, second, table, gain_two)
-    back = (moved(g[3], -1, -1, 0), moved(g[2], -1, 0, 0), moved(g[1], 0, -1, 0), g[0])
-    own = add(lax.all_to_all(sums.reshape(32, 64, 128), "lon", 0, 0), back[:3])
-    result = finish(x, gm, back, gain1)
-    place = lax.axis_index("lon").reshape(1)
-    totals = spread(place, own, swapped(own, 1), swapped(own, 2), swapped(own, 3), result)
+    table, second = scatter(score, lo, hi, low, gcols, att, grad)
+    place = jnp.stack([lax.axis_index("lon"), lax.axis_index("tp")])
+    sums = meet(place, part1, other1, xw, first, second, table, gain_two)
+    own, g0, g1, g2, g3 = add(lax.all_to_all(sums.reshape(32, 64, 128), "lon", 0, 0), part1, other1)
+    next_band = moved(g2, -1, 0, 0)
+    back = (moved(g3, -1, -1, 0), next_band, moved(g1, 0, -1, 0), g0)
+    result, token = finish(x, gm, back, gain1)
+    totals = spread(place, own, next_band, moved(own, -2, 0, 0), moved(own, -3, 0, 0), token)
     got = lax.all_to_all(totals, "lon", 0, 0)
     qkv_out, proj_out, up_out, down_out, one, two, table_out = unpack(
-        weight_scale, table_scale, lax.axis_index("tp").reshape(1), got.reshape(2048, 128)
+        weight_scale, table_scale, place, got.reshape(2048, 128)
     )
     return (
         result.transpose(2, 0, 1, 3),

time: 107 us -> 106 us (level)
  blocking collectives: 0 us -> 44.2 us
  waiting for transfers between devices: 36.8 us -> 6.56 us
  starting transfers between devices: 41.3 us -> 26.8 us
    all_to_all x0 -> x2, blocking collectives: none -> 44.2 us  [the longest x1 23.5 us: local(): lax.all_to_all(sums.reshape(32, 64, 128), 'lon', 0, 0)]
    all_to_all x2 -> x0, waiting for transfers between devices: 16.6 us -> none  [the longest x1 16.6 us: local(): got = lax.all_to_all(totals, 'lon', 0, 0)]
    ppermute x11 -> x13, waiting for transfers between devices: 19.6 us -> 6.56 us  [moved(): return lax.ppermute(value, ('lat', 'lon', 'tp'), pairs)]
    all_to_all x2 -> x0, starting transfers between devices: 12 us -> none  [the longest x1 6.79 us: local(): own = add(lax.all_to_all(sums.reshape(32, 64, 128), 'lon', 0, 0), back[:3])]
    ppermute x3 -> x0, starting transfers between devices: 5.17 us -> none  [swapped(): return lax.ppermute(value, 'lat', pairs)]
    ppermute x11 -> x13, starting transfers between devices: 24.2 us -> 26.8 us  [moved(): return lax.ppermute(value, ('lat', 'lon', 'tp'), pairs)]
    pallas_call x4, Pallas kernels: 6.09 us -> 7.55 us  [the longest x1 5.25 us: scatter(): pl.pallas_call(scatter_kernel, out_shape=(shape((192, 256), F32), shape((...]
  transfers between devices with their start and end apart: 16 -> 13, of which waited for: 6 -> 4; matrix products, arithmetic and copies ran while one was open for 0% -> 0% of each run, Pallas kernels for 13% -> 14%
where the time goes in v5:
time: 106 us
  blocking collectives  44.2 us (42%)
  Pallas kernels  27.5 us (26%)
  starting transfers between devices  26.8 us (25%)
  waiting for transfers between devices  6.56 us (6%)
    ppermute x13, starting transfers between devices, moved(): return lax.ppermute(value, ('lat', 'lon', 'tp'), pairs)  26.8 us
    all_to_all x1, blocking collectives, local(): lax.all_to_all(sums.reshape(32, 64, 128), 'lon', 0, 0)  23.5 us
    all_to_all x1, blocking collectives, local(): got = lax.all_to_all(totals, 'lon', 0, 0)  20.8 us
    ppermute x13, waiting for transfers between devices, moved(): return lax.ppermute(value, ('lat', 'lon', 'tp'), pairs)  6.56 us
    pallas_call x1, Pallas kernels, backward(): pl.pallas_call(backward_kernel, out_shape=(shape((576, 192), BF), shape((...  5.33 us
    pallas_call x1, Pallas kernels, scatter(): pl.pallas_call(scatter_kernel, out_shape=(shape((192, 256), F32), shape((...  5.25 us
    pallas_call x1, Pallas kernels, head(): pl.pallas_call(head_kernel, out_shape=tuple((shape((144, 192), BF) for _...  3.62 us
    pallas_call x1, Pallas kernels, forward(): pl.pallas_call(forward_kernel, out_shape=(shape((576, 192), BF), shape((5...  3.01 us
  transfers between devices with their start and end apart: 13, of which 4 were waited for; matrix products, arithmetic and copies ran while one was open for 0% of the time, Pallas kernels for 14%

profile of v5, /device:TPU:1, one launch (start us, length us, event | category | flops | bytes accessed | tf_op | source)
XLA Modules:
  0.0 106.1 jit_solution(3759150392987824529)
XLA Ops:
  0.7 0.0 copy-start.15
  0.7 3.6 %head.1 = (bf16[144,192]{1,0:T(8,128)(2,1)}, bf16[144,192]{1,0:T(8,128)(2,1)}, bf16[144,192]{1,0:T(8,128)(2,1)}, bf16[144,192]{1,0:T(8,128)(2,1)}, bf16[576,192]{1,0:T(8,128)(2,1)}, /*index=5*/bf16[1152,128]{1,0:T(8,128)(2,1)}) custom-call(bf16[6,12,8,192]{3,2,1,0:T(8,128)(2,1)} %bitcast.35, bf16[6,12,8,192]{3,2,1,0:T(8,128)(2,1)} %bitcast.24, ...), custom_call_target="tpu_custom_call" | custom-call | flops 3000000000 | tf_op jit(solution)/shard_map/head/pallas_call | solution.py:132
  4.3 2.2 %collective-permute-start = (bf16[576,192]{1,0:T(8,128)(2,1)}, bf16[576,192]{1,0:T(8,128)(2,1)S(1)}, u32[]{:S(2)}, u32[]{:S(2)}) collective-permute-start(bf16[576,192]{1,0:T(8,128)(2,1)} %get-tuple-element.56.own_ref), channel_id=1, source_target_pairs={{1,0},{0,1},{3,2},{2,3},{5,4},{4,5},{7,6},{6,7},{9,8},{8,9},{11,10... | collective-permute-start | bytes 663560 | tf_op jit(solution)/shard_map/ppermute | solution.py:593
  6.5 7.8 %collective-permute-start.4 = (bf16[144,192]{1,0:T(8,128)(2,1)}, bf16[144,192]{1,0:T(8,128)(2,1)S(1)}, u32[]{:S(2)}, u32[]{:S(2)}) collective-permute-start(bf16[144,192]{1,0:T(8,128)(2,1)} %get-tuple-element.54.x2), channel_id=1, source_target_pairs={{2,0},{3,1},{4,2},{5,3},{6,4},{7,5},{8,6},{9,7},{10,8},{11,9},{12,... | collective-permute-start | bytes 165896 | tf_op jit(solution)/shard_map/ppermute | solution.py:593
  14.3 1.2 %collective-permute-start.5 = (bf16[144,192]{1,0:T(8,128)(2,1)}, bf16[144,192]{1,0:T(8,128)(2,1)S(1)}, u32[]{:S(2)}, u32[]{:S(2)}) collective-permute-start(bf16[144,192]{1,0:T(8,128)(2,1)} %get-tuple-element.53.x1), channel_id=1, source_target_pairs={{64,0},{65,1},{66,2},{67,3},{68,4},{69,5},{70,6},{71,7},{72,8},{73... | collective-permute-start | bytes 165896 | tf_op jit(solution)/shard_map/ppermute | solution.py:593
  15.5 2.2 %collective-permute-start.6 = (bf16[144,192]{1,0:T(8,128)(2,1)}, bf16[144,192]{1,0:T(8,128)(2,1)S(1)}, u32[]{:S(2)}, u32[]{:S(2)}) collective-permute-start(bf16[144,192]{1,0:T(8,128)(2,1)} %get-tuple-element.52.x0), channel_id=1, source_target_pairs={{66,0},{67,1},{68,2},{69,3},{70,4},{71,5},{72,6},{73,7},{74,8},{75... | collective-permute-start | bytes 165896 | tf_op jit(solution)/shard_map/ppermute | solution.py:593
  17.8 0.0 copy-done.10
  17.8 0.0 copy-start
  17.8 0.0 copy-start.1
  17.8 0.0 copy-start.2
  17.8 0.0 copy-start.12
  17.8 3.0 %gather_first.1 = (f32[1440,128]{1,0:T(8,128)S(1)}, s32[168,128]{1,0:T(8,128)S(1)}, s32[168,128]{1,0:T(8,128)S(1)}, bf16[160,512]{1,0:T(8,128)(2,1)S(1)}, f32[4,144]{1,0:T(4,128)S(1)}) custom-call(s32[144,144]{1,0:T(8,128)S(1)} %copy-done.4, bf16[144,144]{1,0:T(8,128)(2,1)S(1)} %copy-done.15, f32[3,4,3312]{2,1,0:T(4,128)S(1)} %bitcast.28, ...), custom_call_target="tpu_custom_call" | custom-call | flops 6000000000 | tf_op jit(solution)/shard_map/gather_first/pallas_call | solution.py:264
  20.8 0.1 pad_add_fusion.place_ref
  20.9 0.0 collective-permute-done.other_ref
  20.9 0.6 middle.1
  21.5 0.3 collective-permute-start.1
  21.9 1.7 %collective-permute-start.2 = (bf16[144,192]{1,0:T(8,128)(2,1)S(1)}, bf16[144,192]{1,0:T(8,128)(2,1)S(1)}, u32[]{:S(2)}, u32[]{:S(2)}) collective-permute-start(bf16[144,192]{1,0:T(8,128)(2,1)S(1)} %get-tuple-element.59.m1), channel_id=1, source_target_pairs={{64,0},{65,1},{66,2},{67,3},{68,4},{69,5},{70,6},{71,7},{72,8},{73... | collective-permute-start | bytes 165896 | tf_op jit(solution)/shard_map/ppermute | solution.py:593
  23.6 2.1 %gather_second.1 = (f32[12,144,128]{2,1,0:T(8,128)S(1)}, f32[12,144,128]{2,1,0:T(8,128)S(1)}) custom-call(f32[1440,128]{1,0:T(8,128)S(1)} %get-tuple-element.62.first_stage, s32[168,128]{1,0:T(8,128)S(1)} %get-tuple-element.57.after_ref.lo_ref, s32[168,128]{1,0:T(8,128)S(1)} %get-tuple-element.63.hi_ref, bf16[160,512]{1,0:T(8,128)(2,1)S(1)} %get-tuple-element.64.terms_ref, ...), custom_call_target="tpu_custom_call" | custom-call | flops 4000000000 | tf_op jit(solution)/shard_map/gather_second/pallas_call | solution.py:291
  25.8 0.0 collective-permute-done.4.x1
  25.8 3.0 %collective-permute-start.3 = (bf16[144,192]{1,0:T(8,128)(2,1)S(1)}, bf16[144,192]{1,0:T(8,128)(2,1)S(1)}, u32[]{:S(2)}, u32[]{:S(2)}) collective-permute-start(bf16[144,192]{1,0:T(8,128)(2,1)S(1)} %get-tuple-element.58.m0), channel_id=1, source_target_pairs={{66,0},{67,1},{68,2},{69,3},{70,4},{71,5},{72,6},{73,7},{74,8},{75... | collective-permute-start | bytes 165896 | tf_op jit(solution)/shard_map/ppermute | solution.py:593
  28.7 0.0 collective-permute-done.5.x2
  28.8 0.0 collective-permute-done.6.x3
  28.8 0.0 copy-start.9
  28.8 3.0 %forward.1 = (bf16[576,192]{1,0:T(8,128)(2,1)S(1)}, bf16[576,96]{1,0:T(8,128)(2,1)S(1)}, bf16[576,96]{1,0:T(8,128)(2,1)S(1)}, bf16[576,96]{1,0:T(8,128)(2,1)S(1)...) custom-call(bf16[144,192]{1,0:T(8,128)(2,1)S(1)} %copy-done.17, ...), custom_call_target="tpu_custom_call" | custom-call | flops 5000000000 | tf_op jit(solution)/shard_map/forward/pallas_call | solution.py:336
  31.8 0.0 collective-permute-done.1.g1
  31.8 0.0 collective-permute-done.2.g2
  31.8 0.7 collective-permute-done.3.g3
  32.6 5.3 %backward.1 = (bf16[576,192]{1,0:T(8,128)(2,1)S(1)}, f32[12,144,144]{2,1,0:T(8,128)S(1)}, bf16[3,576,96]{2,1,0:T(8,128)(2,1)S(1)}, bf16[576,192]{1,0:T(8,128)(2,1)S(1)}) custom-call(bf16[144,192]{1,0:T(8,128)(2,1)S(1)} %get-tuple-element.61.g0.m3, bf16[144,192]{1,0:T(8,128)(2,1)S(1)} %collective-permute-done.1.g1, ...), custom_call_target="tpu_custom_call" | custom-call | flops 7000000000 | tf_op jit(solution)/shard_map/backward/pallas_call | solution.py:392
  37.9 1.0 collective-permute-start.7
  39.0 5.2 %scatter.1 = (f32[192,256]{1,0:T(8,128)S(1)}, bf16[576,128]{1,0:T(8,128)(2,1)S(1)}) custom-call(f32[12,144,144]{2,1,0:T(8,128)S(1)} %get-tuple-element.75.score_ref, s32[168,128]{1,0:T(8,128)S(1)} %get-tuple-element.57.after_ref.lo_ref, s32[168,128]{1,0:T(8,128)S(1)} %get-tuple-element.63.hi_ref, bf16[576,192]{1,0:T(8,128)(2,1)S(1)} %get-tuple-element.76.low_ref, ...), custom_call_target="tpu_custom_call" | custom-call | flops 5000000000 | tf_op jit(solution)/shard_map/scatter/pallas_call | solution.py:432
  44.2 1.3 %collective-permute-done.7.other_ref = bf16[576,192]{1,0:T(8,128)(2,1)S(1)} collective-permute-done((bf16[576,192]{1,0:T(8,128)(2,1)S(1)}, bf16[576,192]{1,0:T(8,128)(2,1)S(1)}, u32[]{:S(2)}, u32[]{:S(2)}) %collective-permute-start.7) | collective-permute-done | bytes 221216 | tf_op jit(solution)/shard_map/ppermute | solution.py:593
  45.6 0.9 meet.1
  46.5 23.5 %all_to_all.10.got_ref = bf16[32,64,128]{2,1,0:T(8,128)(2,1)S(1)} all-to-all(bf16[32,64,128]{2,1,0:T(8,128)(2,1)S(1)} %bitcast.23), channel_id=1, replica_groups=mesh['lat'=4,'lon'=32,'tp'=2] {'lon'}, dimensions={0} | all-to-all | bytes 1048576 | tf_op jit(solution)/shard_map/all_to_all | solution.py:645
  70.0 0.1 add.3
  70.1 2.6 %collective-permute-start.9 = (bf16[208,192]{1,0:T(8,128)(2,1)S(1)}, bf16[208,192]{1,0:T(8,128)(2,1)S(1)}, u32[]{:S(2)}, u32[]{:S(2)}) collective-permute-start(bf16[208,192]{1,0:T(8,128)(2,1)S(1)} %get-tuple-element.83), channel_id=1, source_target_pairs={{192,0},{193,1},{194,2},{195,3},{196,4},{197,5},{198,6},{199,7},{2... | collective-permute-start | bytes 239624 | tf_op jit(solution)/shard_map/ppermute | solution.py:593
  72.7 1.2 %collective-permute-start.10 = (bf16[144,192]{1,0:T(8,128)(2,1)S(1)}, bf16[144,192]{1,0:T(8,128)(2,1)S(1)}, u32[]{:S(2)}, u32[]{:S(2)}) collective-permute-start(bf16[144,192]{1,0:T(8,128)(2,1)S(1)} %get-tuple-element.84), channel_id=1, source_target_pairs={{62,0},{63,1},{0,2},{1,3},{2,4},{3,5},{4,6},{5,7},{6,8},{7,9},{8,1... | collective-permute-start | bytes 165896 | tf_op jit(solution)/shard_map/ppermute | solution.py:593
  73.9 1.4 %collective-permute-start.8 = (bf16[144,192]{1,0:T(8,128)(2,1)S(1)}, bf16[144,192]{1,0:T(8,128)(2,1)S(1)}, u32[]{:S(2)}, u32[]{:S(2)}) collective-permute-start(bf16[144,192]{1,0:T(8,128)(2,1)S(1)} %get-tuple-element.82), channel_id=1, source_target_pairs={{254,0},{255,1},{192,2},{193,3},{194,4},{195,5},{196,6},{197,7},{1... | collective-permute-start | bytes 165896 | tf_op jit(solution)/shard_map/ppermute | solution.py:593
  75.3 1.5 %collective-permute-start.11 = (bf16[64,128]{1,0:T(8,128)(2,1)S(1)}, bf16[64,128]{1,0:T(8,128)(2,1)S(1)}, u32[]{:S(2)}, u32[]{:S(2)}) collective-permute-start(bf16[64,128]{1,0:T(8,128)(2,1)S(1)} %get-tuple-element.87.own_ref), channel_id=1, source_target_pairs={{128,0},{129,1},{130,2},{131,3},{132,4},{133,5},{134,6},{135,7},{1... | collective-permute-start | bytes 49160 | tf_op jit(solution)/shard_map/ppermute | solution.py:593
  76.8 0.6 collective-permute-start.12
  77.3 2.8 %collective-permute-done.10.g2 = bf16[144,192]{1,0:T(8,128)(2,1)S(1)} collective-permute-done((bf16[144,192]{1,0:T(8,128)(2,1)S(1)}, bf16[144,192]{1,0:T(8,128)(2,1)S(1)}, u32[]{:S(2)}, u32[]{:S(2)}) %collective-permute-start.10) | collective-permute-done | bytes 55328 | tf_op jit(solution)/shard_map/ppermute | solution.py:593
  80.2 1.7 %collective-permute-done.8.g0 = bf16[144,192]{1,0:T(8,128)(2,1)S(1)} collective-permute-done((bf16[144,192]{1,0:T(8,128)(2,1)S(1)}, bf16[144,192]{1,0:T(8,128)(2,1)S(1)}, u32[]{:S(2)}, u32[]{:S(2)}) %collective-permute-start.8) | collective-permute-done | bytes 55328 | tf_op jit(solution)/shard_map/ppermute | solution.py:593
  81.8 0.0 collective-permute-done.9.g1.a_ref
  81.8 1.2 %finish.1 = (bf16[6,12,8,192]{3,2,1,0:T(8,128)(2,1)}, f32[8,128]{1,0:T(8,128)S(1)}) custom-call(bf16[144,192]{1,0:T(8,128)(2,1)S(1)} %copy-done.6, bf16[144,192]{1,0:T(8,128)(2,1)S(1)} %copy-done.7, bf16[144,192]{1,0:T(8,128)(2,1)S(1)} %copy-done.8, bf16[144,192]{1,0:T(8,128)(2,1)S(1)} %copy-done.17, bf16[144,192]{1,0:T(8,128)(2,1)S(1)} %get-tuple-element.58.m0, ...), custom_call_target="tpu_custom_call" | custom-call | flops 1000000000 | tf_op jit(solution)/shard_map/finish/pallas_call | solution.py:484
  83.1 0.0 collective-permute-done.11.b_ref
  83.1 0.0 collective-permute-done.12.c_ref
  83.1 0.6 spread.1
  83.7 20.8 %all_to_all.11 = bf16[32,64,128]{2,1,0:T(8,128)(2,1)S(1)} all-to-all(bf16[32,64,128]{2,1,0:T(8,128)(2,1)S(1)} %spread.1), channel_id=1, replica_groups=mesh['lat'=4,'lon'=32,'tp'=2] {'lon'}, dimensions={0} | all-to-all | bytes 1048576 | tf_op jit(solution)/shard_map/all_to_all | solution.py:650
  104.4 1.6 %unpack.1 = (f32[3,192,96]{2,1,0:T(8,128)}, f32[96,192]{1,0:T(8,128)}, f32[192,384]{1,0:T(8,128)}, f32[192,384]{1,0:T(8,128)}, f32[1,96]{1,0:T(1,128)}, /*index=5*/f32[1,96]{1,0:T(1,128)}, f32[3,4,3312]{2,1,0:T(4,128)}) custom-call(s32[2]{0:T(128)S(1)} %pad_add_fusion.place_ref, bf16[2048,128]{1,0:T(8,128)(2,1)S(1)} %bitcast.22), custom_call_target="tpu_custom_call" | custom-call | tf_op jit(solution)/shard_map/unpack/pallas_call | solution.py:568
  (29 shorter events, 0.1 us)
Async XLA Ops:
  0.6 17.1 %copy-start.3 = (f32[1,4,3,3312]{3,1,2,0:T(4,128)S(1)}, f32[1,4,3,3312]{3,1,2,0:T(4,128)}, u32[]{:S(2)}) copy-start(f32[1,4,3,3312]{3,1,2,0:T(4,128)} %param.22) | copy-start | bytes 476932
  0.6 17.1 %copy-start.4 = (s32[144,144]{1,0:T(8,128)S(1)}, s32[144,144]{1,0:T(8,128)}, u32[]{:S(2)}) copy-start(s32[144,144]{1,0:T(8,128)} %index_ref.1) | copy-start | bytes 248836
  0.7 17.1 %copy-start.10 = (s32[8,6,12]{2,0,1:T(8,128)S(1)}, s32[8,6,12]{2,0,1:T(8,128)}, u32[]{:S(2)}) copy-start(s32[8,6,12]{2,0,1:T(8,128)} %param.19) | copy-start | bytes 6916
  0.7 17.1 %copy-start.11 = (s32[8,6,12]{2,0,1:T(8,128)S(1)}, s32[8,6,12]{2,0,1:T(8,128)}, u32[]{:S(2)}) copy-start(s32[8,6,12]{2,0,1:T(8,128)} %param.20) | copy-start | bytes 6916
  0.7 17.1 %copy-start.15 = (bf16[144,144]{1,0:T(8,128)(2,1)S(1)}, bf16[144,144]{1,0:T(8,128)(2,1)}, u32[]{:S(2)}) copy-start(bf16[144,144]{1,0:T(8,128)(2,1)} %constant.12.clone.order_ref) | copy-start | bytes 124420
  4.3 16.6 %collective-permute-start = (bf16[576,192]{1,0:T(8,128)(2,1)}, bf16[576,192]{1,0:T(8,128)(2,1)S(1)}, u32[]{:S(2)}, u32[]{:S(2)}) collective-permute-start(bf16[576,192]{1,0:T(8,128)(2,1)} %get-tuple-element.56.own_ref), channel_id=1, source_target_pairs={{1,0},{0,1},{3,2},{2,3},{5,4},{4,5},{7,6},{6,7},{9,8},{8,9},{11,10... | collective-permute-start | bytes 663560 | tf_op jit(solution)/shard_map/ppermute | solution.py:593
  6.5 19.2 %collective-permute-start.4 = (bf16[144,192]{1,0:T(8,128)(2,1)}, bf16[144,192]{1,0:T(8,128)(2,1)S(1)}, u32[]{:S(2)}, u32[]{:S(2)}) collective-permute-start(bf16[144,192]{1,0:T(8,128)(2,1)} %get-tuple-element.54.x2), channel_id=1, source_target_pairs={{2,0},{3,1},{4,2},{5,3},{6,4},{7,5},{8,6},{9,7},{10,8},{11,9},{12,... | collective-permute-start | bytes 165896 | tf_op jit(solution)/shard_map/ppermute | solution.py:593
  14.3 14.5 %collective-permute-start.5 = (bf16[144,192]{1,0:T(8,128)(2,1)}, bf16[144,192]{1,0:T(8,128)(2,1)S(1)}, u32[]{:S(2)}, u32[]{:S(2)}) collective-permute-start(bf16[144,192]{1,0:T(8,128)(2,1)} %get-tuple-element.53.x1), channel_id=1, source_target_pairs={{64,0},{65,1},{66,2},{67,3},{68,4},{69,5},{70,6},{71,7},{72,8},{73... | collective-permute-start | bytes 165896 | tf_op jit(solution)/shard_map/ppermute | solution.py:593
  15.5 13.2 %collective-permute-start.6 = (bf16[144,192]{1,0:T(8,128)(2,1)}, bf16[144,192]{1,0:T(8,128)(2,1)S(1)}, u32[]{:S(2)}, u32[]{:S(2)}) collective-permute-start(bf16[144,192]{1,0:T(8,128)(2,1)} %get-tuple-element.52.x0), channel_id=1, source_target_pairs={{66,0},{67,1},{68,2},{69,3},{70,4},{71,5},{72,6},{73,7},{74,8},{75... | collective-permute-start | bytes 165896 | tf_op jit(solution)/shard_map/ppermute | solution.py:593
  17.8 3.1 %copy-start = (bf16[8,6,12,192]{3,0,2,1:T(8,128)(2,1)S(1)}, bf16[8,6,12,192]{3,0,2,1:T(8,128)(2,1)}, u32[]{:S(2)}) copy-start(bf16[8,6,12,192]{3,0,2,1:T(8,128)(2,1)} %param.17) | copy-start | bytes 663556
  17.8 3.1 %copy-start.1 = (bf16[8,6,12,192]{3,0,2,1:T(8,128)(2,1)S(1)}, bf16[8,6,12,192]{3,0,2,1:T(8,128)(2,1)}, u32[]{:S(2)}) copy-start(bf16[8,6,12,192]{3,0,2,1:T(8,128)(2,1)} %param.18) | copy-start | bytes 663556
  17.8 3.1 %copy-start.2 = (bf16[576,192]{1,0:T(8,128)(2,1)S(1)}, bf16[576,192]{1,0:T(8,128)(2,1)}, u32[]{:S(2)}) copy-start(bf16[576,192]{1,0:T(8,128)(2,1)} %get-tuple-element.56.own_ref) | copy-start | bytes 663556
  17.8 3.1 %copy-start.12 = (f32[192]{0:T(256)S(1)}, f32[192]{0:T(256)}, u32[]{:S(2)}) copy-start(f32[192]{0:T(256)} %param.26) | copy-start | bytes 2308
  21.5 10.3 %collective-permute-start.1 = (bf16[144,192]{1,0:T(8,128)(2,1)S(1)}, bf16[144,192]{1,0:T(8,128)(2,1)S(1)}, u32[]{:S(2)}, u32[]{:S(2)}) collective-permute-start(bf16[144,192]{1,0:T(8,128)(2,1)S(1)} %get-tuple-element.60.m2), channel_id=1, source_target_pairs={{2,0},{3,1},{4,2},{5,3},{6,4},{7,5},{8,6},{9,7},{10,8},{11,9},{12,... | collective-permute-start | bytes 165896 | tf_op jit(solution)/shard_map/ppermute | solution.py:593
  21.9 10.0 %collective-permute-start.2 = (bf16[144,192]{1,0:T(8,128)(2,1)S(1)}, bf16[144,192]{1,0:T(8,128)(2,1)S(1)}, u32[]{:S(2)}, u32[]{:S(2)}) collective-permute-start(bf16[144,192]{1,0:T(8,128)(2,1)S(1)} %get-tuple-element.59.m1), channel_id=1, source_target_pairs={{64,0},{65,1},{66,2},{67,3},{68,4},{69,5},{70,6},{71,7},{72,8},{73... | collective-permute-start | bytes 165896 | tf_op jit(solution)/shard_map/ppermute | solution.py:593
  23.6 5.2 %copy-start.5 = (bf16[3,192,96]{2,1,0:T(8,128)(2,1)S(1)}, bf16[3,192,96]{2,1,0:T(8,128)(2,1)}, u32[]{:S(2)}) copy-start(bf16[3,192,96]{2,1,0:T(8,128)(2,1)} %qkv_ref.3) | copy-start | bytes 331780
  23.6 5.2 %copy-start.13 = (f32[192]{0:T(256)S(1)}, f32[192]{0:T(256)}, u32[]{:S(2)}) copy-start(f32[192]{0:T(256)} %param.23) | copy-start | bytes 2308
  23.6 5.2 %copy-start.14 = (bf16[144,144]{1,0:T(8,128)(2,1)S(1)}, bf16[144,144]{1,0:T(8,128)(2,1)}, u32[]{:S(2)}) copy-start(bf16[144,144]{1,0:T(8,128)(2,1)} %constant.13.clone.order_ref) | copy-start | bytes 124420
  23.6 5.2 %copy-start.17 = (bf16[144,192]{1,0:T(8,128)(2,1)S(1)}, bf16[144,192]{1,0:T(8,128)(2,1)}, u32[]{:S(2)}) copy-start(bf16[144,192]{1,0:T(8,128)(2,1)} %get-tuple-element.55.x0.x3) | copy-start | bytes 165892
  25.8 6.8 %collective-permute-start.3 = (bf16[144,192]{1,0:T(8,128)(2,1)S(1)}, bf16[144,192]{1,0:T(8,128)(2,1)S(1)}, u32[]{:S(2)}, u32[]{:S(2)}) collective-permute-start(bf16[144,192]{1,0:T(8,128)(2,1)S(1)} %get-tuple-element.58.m0), channel_id=1, source_target_pairs={{66,0},{67,1},{68,2},{69,3},{70,4},{71,5},{72,6},{73,7},{74,8},{75... | collective-permute-start | bytes 165896 | tf_op jit(solution)/shard_map/ppermute | solution.py:593
  28.8 3.8 %copy-start.9 = (bf16[96,192]{1,0:T(8,128)(2,1)S(1)}, bf16[96,192]{1,0:T(8,128)(2,1)}, u32[]{:S(2)}) copy-start(bf16[96,192]{1,0:T(8,128)(2,1)} %proj_ref.1) | copy-start | bytes 110596
  37.9 7.6 %collective-permute-start.7 = (bf16[576,192]{1,0:T(8,128)(2,1)S(1)}, bf16[576,192]{1,0:T(8,128)(2,1)S(1)}, u32[]{:S(2)}, u32[]{:S(2)}) collective-permute-start(bf16[576,192]{1,0:T(8,128)(2,1)S(1)} %get-tuple-element.73.own_ref), channel_id=1, source_target_pairs={{1,0},{0,1},{3,2},{2,3},{5,4},{4,5},{7,6},{6,7},{9,8},{8,9},{11,10... | collective-permute-start | bytes 663560 | tf_op jit(solution)/shard_map/ppermute | solution.py:593
  38.9 6.6 %copy-start.16 = (bf16[1152,128]{1,0:T(8,128)(2,1)S(1)}, bf16[1152,128]{1,0:T(8,128)(2,1)}, u32[]{:S(2)}) copy-start(bf16[1152,128]{1,0:T(8,128)(2,1)} %get-tuple-element.74.first_ref) | copy-start | bytes 884740
  69.9 11.9 %copy-start.6 = (bf16[144,192]{1,0:T(8,128)(2,1)S(1)}, bf16[144,192]{1,0:T(8,128)(2,1)}, u32[]{:S(2)}) copy-start(bf16[144,192]{1,0:T(8,128)(2,1)} %get-tuple-element.52.x0) | copy-start | bytes 165892
  69.9 11.9 %copy-start.7 = (bf16[144,192]{1,0:T(8,128)(2,1)S(1)}, bf16[144,192]{1,0:T(8,128)(2,1)}, u32[]{:S(2)}) copy-start(bf16[144,192]{1,0:T(8,128)(2,1)} %get-tuple-element.53.x1) | copy-start | bytes 165892
  69.9 11.9 %copy-start.8 = (bf16[144,192]{1,0:T(8,128)(2,1)S(1)}, bf16[144,192]{1,0:T(8,128)(2,1)}, u32[]{:S(2)}) copy-start(bf16[144,192]{1,0:T(8,128)(2,1)} %get-tuple-element.54.x2) | copy-start | bytes 165892
  70.1 11.7 %collective-permute-start.9 = (bf16[208,192]{1,0:T(8,128)(2,1)S(1)}, bf16[208,192]{1,0:T(8,128)(2,1)S(1)}, u32[]{:S(2)}, u32[]{:S(2)}) collective-permute-start(bf16[208,192]{1,0:T(8,128)(2,1)S(1)} %get-tuple-element.83), channel_id=1, source_target_pairs={{192,0},{193,1},{194,2},{195,3},{196,4},{197,5},{198,6},{199,7},{2... | collective-permute-start | bytes 239624 | tf_op jit(solution)/shard_map/ppermute | solution.py:593
  72.7 7.4 %collective-permute-start.10 = (bf16[144,192]{1,0:T(8,128)(2,1)S(1)}, bf16[144,192]{1,0:T(8,128)(2,1)S(1)}, u32[]{:S(2)}, u32[]{:S(2)}) collective-permute-start(bf16[144,192]{1,0:T(8,128)(2,1)S(1)} %get-tuple-element.84), channel_id=1, source_target_pairs={{62,0},{63,1},{0,2},{1,3},{2,4},{3,5},{4,6},{5,7},{6,8},{7,9},{8,1... | collective-permute-start | bytes 165896 | tf_op jit(solution)/shard_map/ppermute | solution.py:593
  73.9 7.9 %collective-permute-start.8 = (bf16[144,192]{1,0:T(8,128)(2,1)S(1)}, bf16[144,192]{1,0:T(8,128)(2,1)S(1)}, u32[]{:S(2)}, u32[]{:S(2)}) collective-permute-start(bf16[144,192]{1,0:T(8,128)(2,1)S(1)} %get-tuple-element.82), channel_id=1, source_target_pairs={{254,0},{255,1},{192,2},{193,3},{194,4},{195,5},{196,6},{197,7},{1... | collective-permute-start | bytes 165896 | tf_op jit(solution)/shard_map/ppermute | solution.py:593
  75.3 7.8 %collective-permute-start.11 = (bf16[64,128]{1,0:T(8,128)(2,1)S(1)}, bf16[64,128]{1,0:T(8,128)(2,1)S(1)}, u32[]{:S(2)}, u32[]{:S(2)}) collective-permute-start(bf16[64,128]{1,0:T(8,128)(2,1)S(1)} %get-tuple-element.87.own_ref), channel_id=1, source_target_pairs={{128,0},{129,1},{130,2},{131,3},{132,4},{133,5},{134,6},{135,7},{1... | collective-permute-start | bytes 49160 | tf_op jit(solution)/shard_map/ppermute | solution.py:593
  76.8 6.3 %collective-permute-start.12 = (bf16[64,128]{1,0:T(8,128)(2,1)S(1)}, bf16[64,128]{1,0:T(8,128)(2,1)S(1)}, u32[]{:S(2)}, u32[]{:S(2)}) collective-permute-start(bf16[64,128]{1,0:T(8,128)(2,1)S(1)} %get-tuple-element.87.own_ref), channel_id=1, source_target_pairs={{64,0},{65,1},{66,2},{67,3},{68,4},{69,5},{70,6},{71,7},{72,8},{73... | collective-permute-start | bytes 49160 | tf_op jit(solution)/shard_map/ppermute | solution.py:593

commit v6 on v5

--- a/solution.py
+++ b/solution.py
@@ -29,6 +29,10 @@
     return jax.ShapeDtypeStruct(dims, kind)
 
 
+def both(own, other):
+    return (own.astype(F32) + other.astype(F32)).astype(BF)
+
+
 def dot_nn(a, b):
     return lax.dot_general(a, b, (((1,), (0,)), ((), ())), preferred_element_type=F32)
 
@@ -78,14 +82,18 @@
     return jnp.asarray(order, BF)
 
 
+def window_parts(own, band, sector):
+    return (own[...], sector[0:144, :], band[0:144, :], sector[144:288, :])
+
+
 def to_windows(parts, order, scratch):
     for s in range(4):
-        rows = dot_nn(order, parts[s][...])
+        rows = dot_nn(order, parts[s])
         for w in range(4):
             scratch[w * 144 + s * 36 : w * 144 + s * 36 + 36, :] = rows[w * 36 : w * 36 + 36]
 
 
-def head_kernel(x_hbm, mid_hbm, up_hbm, gain_hbm, fc1_hbm, fc2_hbm, o0, o1, o2, o3, part_hbm, grads_hbm,
+def head_kernel(place_ref, x_hbm, mid_hbm, up_hbm, gain_hbm, fc1_hbm, fc2_hbm, o10, o2, o3, part_hbm, keep_hbm, send_hbm,
                 x_ref, mid_ref, up_ref, gain_ref, fc1_ref, fc2_ref, xq_ref, part_ref, grads_ref, x_s, mid_s, up_s, sem):
     pairs = (
         (mid_hbm, mid_ref),
@@ -108,10 +116,11 @@
     for copy in copies[3:]:
         copy.wait()
     to_quarters(x_ref, x_s)
+    for place, q in enumerate((1, 0, 2, 3)):
+        xq_ref[place * 144 : place * 144 + 144, :] = x_s[q * 144 : q * 144 + 144, :].astype(BF)
     writes = []
-    for q, out in enumerate((o0, o1, o2, o3)):
-        xq_ref[q] = x_s[q * 144 : q * 144 + 144, :].astype(BF)
-        writes.append(pltpu.make_async_copy(xq_ref.at[q], out, sem.at[8 + q]))
+    for i, (start, size, out) in enumerate(((0, 288, o10), (288, 144, o2), (432, 144, o3))):
+        writes.append(pltpu.make_async_copy(xq_ref.at[pl.ds(start, size)], out, sem.at[9 + i]))
         writes[-1].start()
     to_quarters(up_ref, up_s)
     up = up_s[...].astype(BF)
@@ -122,17 +131,27 @@
     for start, grads in ((0, dot_tn(lowered, grad_pre)), (576, dot_tn(up, active.astype(BF)))):
         for j in range(3):
             grads_ref[start + j * 192 : start + j * 192 + 192, :] = grads[:, j * 128 : j * 128 + 128].astype(BF)
-    writes.append(pltpu.make_async_copy(grads_ref, grads_hbm, sem.at[7]))
-    writes[-1].start()
+    core = place_ref[2]
+    for i, (half, out) in enumerate(((core, keep_hbm), (1 - core, send_hbm))):
+        piece = grads_ref.at[pl.ds(pl.multiple_of(half * 576, 16), 576)]
+        writes.append(pltpu.make_async_copy(piece, out, sem.at[7 + i]))
+        writes[-1].start()
     for write in writes:
         write.wait()
 
 
-def head(x, mid, up, gain, fc1, fc2):
+def head(place, x, mid, up, gain, fc1, fc2):
     return pl.pallas_call(
         head_kernel,
-        out_shape=tuple(shape((144, 192), BF) for _ in range(4)) + (shape((576, 192), BF), shape((1152, 128), BF)),
-        in_specs=[ANY] * 6,
+        out_shape=(
+            shape((288, 192), BF),
+            shape((144, 192), BF),
+            shape((144, 192), BF),
+            shape((576, 192), BF),
+            shape((576, 128), BF),
+            shape((576, 128), BF),
+        ),
+        in_specs=[SMEM] + [ANY] * 6,
         out_specs=tuple(ANY for _ in range(6)),
         scratch_shapes=[
             pltpu.VMEM((6, 12, 8, 192), BF),
@@ -141,7 +160,7 @@
             pltpu.VMEM((1, 192), F32),
             pltpu.VMEM((192, 384), BF),
             pltpu.VMEM((192, 384), BF),
-            pltpu.VMEM((4, 144, 192), BF),
+            pltpu.VMEM((576, 192), BF),
             pltpu.VMEM((576, 192), BF),
             pltpu.VMEM((1152, 128), BF),
             pltpu.VMEM((576, 192), F32),
@@ -152,30 +171,52 @@
         compiler_params=ALL,
         cost_estimate=cost(3),
         name="head",
-    )(x, mid, up, gain, fc1, fc2)
-
-
-def middle_kernel(mid_ref, up_ref, own_ref, other_ref, gain_ref, after_ref, o0, o1, o2, o3, gain_out, mid_s, up_s):
+    )(place, x, mid, up, gain, fc1, fc2)
+
+
+def middle_kernel(mid_ref, up_ref, own_ref, other_ref, gain_ref, x2_ref, band_ref, after_ref,
+                  o10, o2, o3, x_out, gain_out, mid_s, up_s):
     to_quarters(mid_ref, mid_s)
     to_quarters(up_ref, up_s)
     normed, inverse = layer_stats(mid_s[...])
     grad = own_ref[...].astype(F32) + other_ref[...].astype(F32)
     gain_out[...] = jnp.sum(grad * normed, axis=0, keepdims=True)
-    out = up_s[...] + norm_backward(grad, gain_ref[...], normed, inverse)
-    for q, o in enumerate((o0, o1, o2, o3)):
-        o[...] = out[q * 144 : q * 144 + 144].astype(BF)
-
-
-def middle(mid, up, own, other, gain, after):
+    out = (up_s[...] + norm_backward(grad, gain_ref[...], normed, inverse)).astype(BF)
+    o10[0:144, :] = out[144:288]
+    o10[144:288, :] = out[0:144]
+    o2[...] = out[288:432]
+    o3[...] = out[432:576]
+    x_out[0:144, :] = x2_ref[...]
+    x_out[144:288, :] = band_ref[144:288, :]
+
+
+def middle(mid, up, own, other, gain, x2, band, after):
     return pl.pallas_call(
         middle_kernel,
-        out_shape=tuple(shape((144, 192), BF) for _ in range(4)) + (shape((1, 192), F32),),
-        in_specs=[VMEM] * 5 + [ANY],
+        out_shape=(
+            shape((288, 192), BF),
+            shape((144, 192), BF),
+            shape((144, 192), BF),
+            shape((288, 192), BF),
+            shape((1, 192), F32),
+        ),
+        in_specs=[VMEM] * 7 + [ANY],
         scratch_shapes=[pltpu.VMEM((576, 192), F32)] * 2,
         compiler_params=VM,
         cost_estimate=cost(1),
         name="middle",
-    )(mid, up, own, other, gain, after)
+    )(mid, up, own, other, gain, x2, band, after)
+
+
+def join_kernel(first_ref, band_ref, out_ref):
+    out_ref[0:144, :] = first_ref[...]
+    out_ref[144:288, :] = band_ref[144:288, :]
+
+
+def join(first, band):
+    return pl.pallas_call(
+        join_kernel, out_shape=shape((288, 192), BF), compiler_params=VM, cost_estimate=cost(0.1), name="join"
+    )(first, band)
 
 
 def window_order():
@@ -257,14 +298,14 @@
         lines += [picked[lat * 4 : lat * 4 + 4] for lat in range(6)]
     lines = jnp.concatenate(lines, axis=1)
     code_ref[...] = dot_nt(lines.astype(BF), order)
-    look_up(terms_ref[...], lo_ref, hi_ref, stage, 0, 5)
+    look_up(terms_ref[...], lo_ref, hi_ref, stage, 0, 7)
 
 
 def gather_first(index, bias, ids, valid):
     return pl.pallas_call(
         gather_first_kernel,
         out_shape=(
-            shape((90 * 16, 128), F32),
+            shape((126 * 16, 128), F32),
             shape((168, 128), I32),
             shape((168, 128), I32),
             shape((160, 512), BF),
@@ -278,11 +319,11 @@
 
 
 def gather_second_kernel(first_stage, lo_ref, hi_ref, terms_ref, after_ref, main_ref, tail_ref, stage):
-    look_up(terms_ref[...], lo_ref, hi_ref, stage, 90, 4)
+    look_up(terms_ref[...], lo_ref, hi_ref, stage, 126, 2)
     for r in range(12):
-        main_ref[r, 0:90, :] = first_stage[pl.ds(r, 90, stride=16), :]
-        main_ref[r, 90:144, :] = stage[pl.ds(r, 54, stride=16), :]
-        packed = stage[pl.ds(54 * 16 + r, 18, stride=16), :]
+        main_ref[r, 0:126, :] = first_stage[pl.ds(r, 126, stride=16), :]
+        main_ref[r, 126:144, :] = stage[pl.ds(r, 18, stride=16), :]
+        packed = stage[pl.ds(18 * 16 + r, 18, stride=16), :]
         for s in range(8):
             tail_ref[r, pl.ds(s, 18, stride=8), :] = pltpu.roll(packed, 128 - 16 * s, 1) if s else packed
 
@@ -292,16 +333,16 @@
         gather_second_kernel,
         out_shape=(shape((12, 144, 128), F32), shape((12, 144, 128), F32)),
         in_specs=[VMEM] * 4 + [ANY],
-        scratch_shapes=[pltpu.VMEM((72 * 16, 128), F32)],
+        scratch_shapes=[pltpu.VMEM((36 * 16, 128), F32)],
         compiler_params=VM,
         cost_estimate=cost(4),
         name="gather_second",
     )(first_stage, lo, hi, terms, after)
 
 
-def forward_kernel(x0, x1, x2, x3, order_ref, gain_ref, qkv_ref, main_ref, tail_ref, code_ref,
+def forward_kernel(own_ref, band_ref, sector_ref, order_ref, gain_ref, qkv_ref, main_ref, tail_ref, code_ref,
                    low_ref, q_ref, k_ref, v_ref, prob_ref, att_ref, scratch):
-    to_windows((x0, x1, x2, x3), order_ref[...], scratch)
+    to_windows(window_parts(own_ref, band_ref, sector_ref), order_ref[...], scratch)
     normed, _ = layer_stats(scratch[...])
     low = (normed * gain_ref[...]).astype(BF)
     low_ref[...] = low
@@ -350,9 +391,9 @@
     )(*x, level_order(), gain, qkv, main, tail, code)
 
 
-def backward_kernel(g0, g1, g2, g3, order_ref, proj_ref, qkv_ref, q_ref, k_ref, v_ref, prob_ref,
+def backward_kernel(own_ref, band_ref, sector_ref, order_ref, proj_ref, qkv_ref, q_ref, k_ref, v_ref, prob_ref,
                     part_ref, score_ref, gcols, grad_ref, scratch, gatt):
-    to_windows((g0, g1, g2, g3), order_ref[...], scratch)
+    to_windows(window_parts(own_ref, band_ref, sector_ref), order_ref[...], scratch)
     grad = scratch[...].astype(BF)
     grad_ref[...] = grad
     gatt[...] = dot_nt(grad, proj_ref[...]).astype(BF)
@@ -404,7 +445,8 @@
     )(*g, level_order(), proj, qkv, q, k, v, prob)
 
 
-def scatter_kernel(score_ref, lo_ref, hi_ref, low_ref, gcols, att_ref, grad_ref, out_ref, grads_ref, tails):
+def scatter_kernel(place_ref, score_ref, lo_ref, hi_ref, low_ref, gcols, att_ref, grad_ref,
+                   out_ref, keep_ref, send_ref, grads_ref, tails):
     out_ref[...] = jnp.zeros((192, 256), F32)
     place = lax.broadcasted_iota(I32, (16, 128), 0)
     for r in range(12):
@@ -426,28 +468,33 @@
     grads_ref[144:336, :] = jnp.concatenate([a, c[:, 0:32]], axis=1)
     grads_ref[336:528, :] = jnp.concatenate([b, c[:, 32:64]], axis=1)
     grads_ref[528:576, :] = jnp.concatenate([c[i * 48 : i * 48 + 48, 64:96] for i in range(4)], axis=1)
-
-
-def scatter(score, lo, hi, low, gcols, att, grad):
+    core = place_ref[2]
+    keep_ref[...] = grads_ref[pl.ds(pl.multiple_of(core * 288, 16), 288), :]
+    send_ref[...] = grads_ref[pl.ds(pl.multiple_of((1 - core) * 288, 16), 288), :]
+
+
+def scatter(place, score, lo, hi, low, gcols, att, grad):
     return pl.pallas_call(
         scatter_kernel,
-        out_shape=(shape((192, 256), F32), shape((576, 128), BF)),
-        scratch_shapes=[pltpu.VMEM((12, 24, 128), F32)],
+        out_shape=(shape((192, 256), F32), shape((288, 128), BF), shape((288, 128), BF)),
+        in_specs=[SMEM] + [VMEM] * 7,
+        scratch_shapes=[pltpu.VMEM((576, 128), BF), pltpu.VMEM((12, 24, 128), F32)],
         compiler_params=VM,
         cost_estimate=cost(5),
         name="scatter",
-    )(score, lo, hi, low, gcols, att, grad)
-
-
-def meet_kernel(place_ref, own_ref, other_ref, x0, x1, x2, x3, first_ref, second_ref, table_ref, two_ref, out_ref):
+    )(place, score, lo, hi, low, gcols, att, grad)
+
+
+def meet_kernel(own_ref, other_ref, x_own, x_band, x_sector, first_ref, first_other, second_ref, second_other,
+                table_ref, two_ref, out_ref):
     gain = jnp.zeros((1, 192), F32)
-    for s, x in enumerate((x0, x1, x2, x3)):
+    for s, x in enumerate(window_parts(x_own, x_band, x_sector)):
         rows = slice(s * 144, s * 144 + 144)
         grad = own_ref[rows, :].astype(F32) + other_ref[rows, :].astype(F32)
-        normed, _ = layer_stats(x[...].astype(F32))
+        normed, _ = layer_stats(x.astype(F32))
         gain = gain + jnp.sum(grad * normed, axis=0, keepdims=True)
-    out_ref[0:1152, :] = first_ref[...]
-    out_ref[1152:1728, :] = second_ref[...]
+    out_ref[0:576, :] = both(first_ref[...], first_other[...])
+    out_ref[576:864, :] = both(second_ref[...], second_other[...])
     rows = []
     for r in range(12):
         pair = table_ref[r * 16 : r * 16 + 13, :]
@@ -455,26 +502,27 @@
     none = jnp.zeros((1, 64), F32)
     for line in (gain, two_ref[...]):
         rows += [line[:, 0:128], jnp.concatenate([line[:, 128:192], none], axis=1)]
-    rows += [jnp.zeros((4, 128), F32)]
-    out_ref[1728:2048, :] = jnp.concatenate(rows, axis=0).astype(BF)
-
-
-def meet(place, own, other, x, first, second, table, two):
+    rows += [jnp.zeros((100, 128), F32)]
+    out_ref[864:1280, :] = jnp.concatenate(rows, axis=0).astype(BF)
+
+
+def meet(own, other, x, first, first_other, second, second_other, table, two):
     return pl.pallas_call(
         meet_kernel,
-        out_shape=shape((2048, 128), BF),
-        in_specs=[SMEM] + [VMEM] * 10,
+        out_shape=shape((1280, 128), BF),
         compiler_params=VM,
         cost_estimate=cost(1),
         name="meet",
-    )(place, own, other, *x, first, second, table, two)
-
-
-def finish_kernel(x0, x1, x2, x3, m0, m1, m2, m3, g0, g1, g2, g3, gain_ref, out_ref, token_ref):
+    )(own, other, *x, first, first_other, second, second_other, table, two)
+
+
+def finish_kernel(x10, x2, x3, m10, m2, m3, g0, g1, g2, g3, gain_ref, out_ref, token_ref):
     token_ref[...] = jnp.zeros((8, 128), F32)
-    for q, (x, m, g) in enumerate(zip((x0, x1, x2, x3), (m0, m1, m2, m3), (g0, g1, g2, g3))):
-        normed, inverse = layer_stats(x[...].astype(F32))
-        rows = m[...].astype(F32) + norm_backward(g[0:144, :].astype(F32), gain_ref[...], normed, inverse)
+    xs = (x10[144:288, :], x10[0:144, :], x2[...], x3[...])
+    ms = (m10[144:288, :], m10[0:144, :], m2[...], m3[...])
+    for q, (x, m, g) in enumerate(zip(xs, ms, (g0, g1, g2, g3))):
+        normed, inverse = layer_stats(x.astype(F32))
+        rows = m.astype(F32) + norm_backward(g[...].astype(F32), gain_ref[...], normed, inverse)
         for lat in range(3):
             piece = rows[lat * 48 : lat * 48 + 48].reshape(6, 8, 192)
             out_ref[(q // 2) * 3 + lat, (q % 2) * 6 : (q % 2) * 6 + 6] = piece.astype(BF)
@@ -497,60 +545,57 @@
     out_ref[...] = total.astype(BF)
     for s, out in enumerate((g0, g1, g2, g3)):
         rows = slice(s * 144, s * 144 + 144)
-        out[0:144, :] = (own_ref[rows, :].astype(F32) + other_ref[rows, :].astype(F32)).astype(BF)
-    g2[144:208, :] = jnp.concatenate([total, jnp.zeros((64, 64), F32)], axis=1).astype(BF)
+        out[...] = both(own_ref[rows, :], other_ref[rows, :])
 
 
 def add(got, own, other):
-    quarter = shape((144, 192), BF)
     return pl.pallas_call(
         add_kernel,
-        out_shape=(shape((64, 128), BF), quarter, quarter, shape((208, 192), BF), quarter),
+        out_shape=(shape((40, 128), BF),) + tuple(shape((144, 192), BF) for _ in range(4)),
         compiler_params=VM,
         cost_estimate=cost(1),
         name="add",
     )(got, own, other)
 
 
-def spread_kernel(place_ref, own_ref, a_ref, b_ref, c_ref, after_ref, out_ref):
+def spread_kernel(place_ref, own_ref, other_ref, after_ref, out_ref):
     own = own_ref[...].astype(F32)
-    total = own + a_ref[144:208, 0:128].astype(F32) + b_ref[...].astype(F32) + c_ref[...].astype(F32)
-    row = place_ref[0] * 64 + lax.broadcasted_iota(I32, (64, 128), 0)
-    table = (row >= 1728) & (row < 2040)
-    out_ref[...] = jnp.broadcast_to(jnp.where(table, own, total).astype(BF)[None], (32, 64, 128))
-
-
-def spread(place, own, a, b, c, after):
+    row = place_ref[0] * 40 + lax.broadcasted_iota(I32, (40, 128), 0)
+    table = (row >= 864) & (row < 1176)
+    total = own + jnp.where(table, 0.0, other_ref[...].astype(F32))
+    out_ref[...] = jnp.broadcast_to(total.astype(BF)[None], (32, 40, 128))
+
+
+def spread(place, own, other, after):
     return pl.pallas_call(
         spread_kernel,
-        out_shape=shape((32, 64, 128), BF),
-        in_specs=[SMEM] + [VMEM] * 4 + [ANY],
+        out_shape=shape((32, 40, 128), BF),
+        in_specs=[SMEM] + [VMEM] * 2 + [ANY],
         compiler_params=VM,
         cost_estimate=cost(1),
         name="spread",
-    )(place, own, a, b, c, after)
-
-
-def unpack_kernel(weight_scale, table_scale, place_ref, in_ref,
+    )(place, own, other, after)
+
+
+def unpack_kernel(weight_scale, table_scale, place_ref, own_ref, other_ref,
                   qkv_ref, proj_ref, upg_ref, down_ref, one_ref, two_ref, table_ref):
-    def rows(start, stop):
-        return in_ref[start:stop, :].astype(F32) * weight_scale
-
+    swap = place_ref[2] == 1
+    own, other = own_ref[0:864, :].astype(F32) * weight_scale, other_ref[0:864, :].astype(F32) * weight_scale
+    lower, upper = jnp.where(swap, other, own), jnp.where(swap, own, other)
     for j in range(3):
-        upg_ref[:, j * 128 : j * 128 + 128] = rows(j * 192, j * 192 + 192)
-        down_ref[:, j * 128 : j * 128 + 128] = rows(576 + j * 192, 768 + j * 192)
-    proj_ref[:, 0:128] = rows(1152, 1248)
-    tail = rows(1248, 1296)
-    proj_ref[0:48, 128:192] = tail[:, 0:64]
-    proj_ref[48:96, 128:192] = tail[:, 64:128]
-    first, second, third = rows(1296, 1488), rows(1488, 1680), rows(1680, 1728)
-    qkv_ref[0] = first[:, 0:96]
-    qkv_ref[1] = second[:, 0:96]
-    qkv_ref[2, :, 0:32] = first[:, 96:128]
-    qkv_ref[2, :, 32:64] = second[:, 96:128]
+        upg_ref[:, j * 128 : j * 128 + 128] = lower[j * 192 : j * 192 + 192]
+        down_ref[:, j * 128 : j * 128 + 128] = upper[j * 192 : j * 192 + 192]
+    second = jnp.concatenate([lower[576:864], upper[576:864]], axis=0)
+    proj_ref[:, 0:128] = second[0:96]
+    proj_ref[0:48, 128:192] = second[96:144, 0:64]
+    proj_ref[48:96, 128:192] = second[96:144, 64:128]
+    qkv_ref[0] = second[144:336, 0:96]
+    qkv_ref[1] = second[336:528, 0:96]
+    qkv_ref[2, :, 0:32] = second[144:336, 96:128]
+    qkv_ref[2, :, 32:64] = second[336:528, 96:128]
     for i in range(4):
-        qkv_ref[2, i * 48 : i * 48 + 48, 64:96] = third[:, i * 32 : i * 32 + 32]
-    table = in_ref[1728:2048, :].astype(F32)
+        qkv_ref[2, i * 48 : i * 48 + 48, 64:96] = second[528:576, i * 32 : i * 32 + 32]
+    table = own_ref[864:1184, :].astype(F32)
     for r in range(12):
         for half in range(2):
             piece = table[r * 26 + half * 13 : r * 26 + half * 13 + 13] * table_scale
@@ -558,13 +603,14 @@
                 start = a * 256 + half * 128
                 wide = min(128, 3312 - start)
                 table_ref[r % 3, r // 3 : r // 3 + 1, start : start + wide] = piece[a : a + 1, 0:wide]
-    for start, out in ((312, one_ref), (314, two_ref)):
-        line = table[start : start + 1]
-        upper = jnp.concatenate([line[:, 96:128], table[start + 1 : start + 2, 0:64]], axis=1)
-        out[...] = jnp.where(place_ref[1] == 0, line[:, 0:96], upper) * weight_scale
-
-
-def unpack(weight_scale, table_scale, place, got):
+    gains = table[304:320] + other_ref[1168:1184, :].astype(F32)
+    for start, out in ((8, one_ref), (10, two_ref)):
+        line = gains[start : start + 1]
+        later = jnp.concatenate([line[:, 96:128], gains[start + 1 : start + 2, 0:64]], axis=1)
+        out[...] = jnp.where(place_ref[1] == 0, line[:, 0:96], later) * weight_scale
+
+
+def unpack(weight_scale, table_scale, place, got, other):
     return pl.pallas_call(
         functools.partial(unpack_kernel, weight_scale, table_scale),
         out_shape=(
@@ -576,10 +622,10 @@
             shape((1, 96), F32),
             shape((3, 4, 3312), F32),
         ),
-        in_specs=[SMEM, VMEM],
+        in_specs=[SMEM, VMEM, VMEM],
         compiler_params=VM,
         name="unpack",
-    )(place, got)
+    )(place, got, other)
 
 
 def moved(value, band, sector, half):
@@ -593,13 +639,8 @@
     return lax.ppermute(value, ("lat", "lon", "tp"), pairs)
 
 
-def shifted_parts(quarters):
-    return (
-        quarters[3],
-        moved(quarters[2], 0, 1, 0),
-        moved(quarters[1], 1, 0, 0),
-        moved(quarters[0], 1, 1, 0),
-    )
+def other_core(value):
+    return lax.ppermute(value, "lat", [(a, a ^ 1) for a in range(lax.axis_size("lat"))])
 
 
 def local(
@@ -627,29 +668,34 @@
         return field.transpose(1, 2, 0, 3)
 
     x_in, mid_in, up_in = turned(inputs), turned(residual_mid), turned(grad_out)
-    *x, part2, first = head(x_in, mid_in, up_in, gain2, fc1_weight, fc2_weight.T)
+    place = jnp.stack([lax.axis_index("lon"), lax.axis_index("tp"), lax.axis_index("lat") % 2])
+    x10, x2, x3, part2, first, first_send = head(place, x_in, mid_in, up_in, gain2, fc1_weight, fc2_weight.T)
     other2 = moved(part2, 0, 0, 1)
-    xw = shifted_parts(x)
+    x_band = moved(x10, 1, 0, 0)
     stage, lo, hi, terms, code = gather_first(
         bias_index, pos_bias[0].transpose(1, 0, 2), mask_ids.transpose(1, 0, 2), key_valid.transpose(1, 0, 2)
     )
-    *gm, gain_two = middle(mid_in, up_in, part2, other2, gain2, lo)
-    gw = shifted_parts(gm)
+    m10, m2, m3, x_next, gain_two = middle(mid_in, up_in, part2, other2, gain2, x2, x_band, lo)
+    m_band = moved(m10, 1, 0, 0)
+    x_sector = moved(x_next, 0, 1, 0)
     main, tail = gather_second(stage, lo, hi, terms, gain_two)
+    m_sector = moved(join(m2, m_band), 0, 1, 0)
+    xw = (x3, x_band, x_sector)
     low, q, k, v, prob, att = forward(xw, gain1, qkv_weight, main, tail, code)
-    part1, score, gcols, grad = backward(gw, proj_weight, qkv_weight, q, k, v, prob)
+    part1, score, gcols, grad = backward((m3, m_band, m_sector), proj_weight, qkv_weight, q, k, v, prob)
     other1 = moved(part1, 0, 0, 1)
-    table, second = scatter(score, lo, hi, low, gcols, att, grad)
-    place = jnp.stack([lax.axis_index("lon"), lax.axis_index("tp")])
-    sums = meet(place, part1, other1, xw, first, second, table, gain_two)
-    own, g0, g1, g2, g3 = add(lax.all_to_all(sums.reshape(32, 64, 128), "lon", 0, 0), part1, other1)
-    next_band = moved(g2, -1, 0, 0)
-    back = (moved(g3, -1, -1, 0), next_band, moved(g1, 0, -1, 0), g0)
-    result, token = finish(x, gm, back, gain1)
-    totals = spread(place, own, next_band, moved(own, -2, 0, 0), moved(own, -3, 0, 0), token)
-    got = lax.all_to_all(totals, "lon", 0, 0)
+    table, second, second_send = scatter(place, score, lo, hi, low, gcols, att, grad)
+    sums = meet(
+        part1, other1, xw, first, other_core(first_send), second, other_core(second_send), table, gain_two
+    )
+    own, g0, g1, g2, g3 = add(lax.all_to_all(sums.reshape(32, 40, 128), "lon", 0, 0), part1, other1)
+    across = moved(own, 2, 0, 0)
+    back = (moved(g3, -1, -1, 0), moved(g2, -1, 0, 0), moved(g1, 0, -1, 0), g0)
+    result, token = finish((x10, x2, x3), (m10, m2, m3), back, gain1)
+    totals = spread(place, own, across, token)
+    got = lax.all_to_all(totals, "lon", 0, 0).reshape(1280, 128)
     qkv_out, proj_out, up_out, down_out, one, two, table_out = unpack(
-        weight_scale, table_scale, place, got.reshape(2048, 128)
+        weight_scale, table_scale, place, got, other_core(got)
     )
     return (
         result.transpose(2, 0, 1, 3),

time: 106 us -> 105 us (level)
  waiting for transfers between devices: 6.56 us -> 17.5 us
  blocking collectives: 44.2 us -> 33.3 us
  starting transfers between devices: 26.8 us -> 23.5 us
    all_to_all x2, blocking collectives: 44.2 us -> 33.3 us  [the longest x1 18.4 us: local(): lax.all_to_all(sums.reshape(32, 40, 128), 'lon', 0, 0)]
    ppermute x13 -> x10, starting transfers between devices: 26.8 us -> 16.6 us  [moved(): return lax.ppermute(value, ('lat', 'lon', 'tp'), pairs)]
    ppermute x13 -> x10, waiting for transfers between devices: 6.56 us -> 15 us  [moved(): return lax.ppermute(value, ('lat', 'lon', 'tp'), pairs)]
    ppermute x0 -> x3, starting transfers between devices: none -> 6.89 us  [other_core(): lax.ppermute(value, 'lat', [(a, a ^ 1) for a in range(lax.axis_size('lat'...]
    ppermute x0 -> x3, waiting for transfers between devices: none -> 2.5 us  [other_core(): lax.ppermute(value, 'lat', [(a, a ^ 1) for a in range(lax.axis_size('lat'...]
    pallas_call x6 -> x7, Pallas kernels: 8.86 us -> 9.87 us  [the longest x1 4.37 us: head(): pl.pallas_call(head_kernel, out_shape=(shape((288, 192), BF), shape((144,...]
  transfers between devices with their start and end apart: 13 -> 13, of which waited for: 4 -> 8; matrix products, arithmetic and copies ran while one was open for 0% -> 0% of each run, Pallas kernels for 14% -> 20%
where the time goes in v6:
time: 105 us; the launch traced here: 104 us
  blocking collectives  33.3 us (32%)
  Pallas kernels  28.4 us (27%)
  starting transfers between devices  23.5 us (22%)
  waiting for transfers between devices  17.5 us (17%)
    all_to_all x1, blocking collectives, local(): lax.all_to_all(sums.reshape(32, 40, 128), 'lon', 0, 0)  18.4 us
    ppermute x10, starting transfers between devices, moved(): return lax.ppermute(value, ('lat', 'lon', 'tp'), pairs)  16.6 us
    ppermute x10, waiting for transfers between devices, moved(): return lax.ppermute(value, ('lat', 'lon', 'tp'), pairs)  15 us
    all_to_all x1, blocking collectives, local(): got = lax.all_to_all(totals, 'lon', 0, 0).reshape(1280, 128)  14.9 us
    ppermute x3, starting transfers between devices, other_core(): lax.ppermute(value, 'lat', [(a, a ^ 1) for a in range(lax.axis_size('lat'...  6.89 us
    pallas_call x1, Pallas kernels, scatter(): pl.pallas_call(scatter_kernel, out_shape=(shape((192, 256), F32), shape((...  5.81 us
    pallas_call x1, Pallas kernels, backward(): pl.pallas_call(backward_kernel, out_shape=(shape((576, 192), BF), shape((...  5.35 us
    pallas_call x1, Pallas kernels, head(): pl.pallas_call(head_kernel, out_shape=(shape((288, 192), BF), shape((144,...  4.37 us
  transfers between devices with their start and end apart: 13, of which 8 were waited for; matrix products, arithmetic and copies ran while one was open for 0% of the time, Pallas kernels for 20%

profile of v6, /device:TPU:1, one launch (start us, length us, event | category | flops | bytes accessed | tf_op | source)
XLA Modules:
  0.0 104.3 jit_solution(13565169660695877050)
XLA Ops:
  0.6 0.6 pad_add_fusion.place_ref
  1.3 0.0 copy-start.14
  1.3 4.4 %head.1 = (bf16[288,192]{1,0:T(8,128)(2,1)}, bf16[144,192]{1,0:T(8,128)(2,1)}, bf16[144,192]{1,0:T(8,128)(2,1)}, bf16[576,192]{1,0:T(8,128)(2,1)}, bf16[576,128]{1,0:T(8,128)(2,1)}, /*index=5*/bf16[576,128]{1,0:T(8,128)(2,1)}) custom-call(s32[3]{0:T(128)} %pad_add_fusion.place_ref, bf16[6,12,8,192]{3,2,1,0:T(8,128)(2,1)} %bitcast.37, ...), custom_call_target="tpu_custom_call" | custom-call | flops 3000000000 | tf_op jit(solution)/shard_map/head/pallas_call | solution.py:144
  5.7 3.3 %collective-permute-start.6 = (bf16[576,128]{1,0:T(8,128)(2,1)}, bf16[576,128]{1,0:T(8,128)(2,1)S(1)}, u32[]{:S(2)}, u32[]{:S(2)}) collective-permute-start(bf16[576,128]{1,0:T(8,128)(2,1)} %get-tuple-element.75), channel_id=1, source_target_pairs={{0,64},{64,0},{128,192},{192,128},{1,65},{65,1},{129,193},{193,129... | collective-permute-start | bytes 442376 | tf_op jit(solution)/shard_map/ppermute | solution.py:643
  9.0 0.1 collective-permute-start.1
  9.1 0.0 collective-permute-start
  9.2 0.0 copy-start.1
  9.2 0.0 copy-start.2
  9.2 0.0 copy-start.11
  9.2 0.0 copy-start.17
  9.2 3.8 %gather_first.1 = (f32[2016,128]{1,0:T(8,128)S(1)}, s32[168,128]{1,0:T(8,128)S(1)}, s32[168,128]{1,0:T(8,128)S(1)}, bf16[160,512]{1,0:T(8,128)(2,1)S(1)}, f32[4,144]{1,0:T(4,128)S(1)}) custom-call(s32[144,144]{1,0:T(8,128)S(1)} %copy-done.5, bf16[144,144]{1,0:T(8,128)(2,1)S(1)} %copy-done.14, f32[3,4,3312]{2,1,0:T(4,128)S(1)} %bitcast.30, ...), custom_call_target="tpu_custom_call" | custom-call | flops 6000000000 | tf_op jit(solution)/shard_map/gather_first/pallas_call | solution.py:305
  13.0 3.9 %collective-permute-done.1.band_ref.x_band = bf16[288,192]{1,0:T(8,128)(2,1)S(1)} collective-permute-done((bf16[288,192]{1,0:T(8,128)(2,1)}, bf16[288,192]{1,0:T(8,128)(2,1)S(1)}, u32[]{:S(2)}, u32[]{:S(2)}) %collective-permute-start.1) | collective-permute-done | bytes 110624 | tf_op jit(solution)/shard_map/ppermute | solution.py:639
  16.9 0.9 collective-permute-done.other_ref
  17.8 0.0 copy-done.1
  17.8 0.6 middle.1
  18.5 4.8 %collective-permute-start.4 = (bf16[288,192]{1,0:T(8,128)(2,1)S(1)}, bf16[288,192]{1,0:T(8,128)(2,1)S(1)}, u32[]{:S(2)}, u32[]{:S(2)}) collective-permute-start(bf16[288,192]{1,0:T(8,128)(2,1)S(1)} %get-tuple-element.61), channel_id=1, source_target_pairs={{2,0},{3,1},{4,2},{5,3},{6,4},{7,5},{8,6},{9,7},{10,8},{11,9},{12,... | collective-permute-start | bytes 331784 | tf_op jit(solution)/shard_map/ppermute | solution.py:639
  23.3 4.1 %collective-permute-start.2 = (bf16[288,192]{1,0:T(8,128)(2,1)S(1)}, bf16[288,192]{1,0:T(8,128)(2,1)S(1)}, u32[]{:S(2)}, u32[]{:S(2)}) collective-permute-start(bf16[288,192]{1,0:T(8,128)(2,1)S(1)} %get-tuple-element.58.m10), channel_id=1, source_target_pairs={{64,0},{65,1},{66,2},{67,3},{68,4},{69,5},{70,6},{71,7},{72,8},{73... | collective-permute-start | bytes 331784 | tf_op jit(solution)/shard_map/ppermute | solution.py:639
  27.4 1.4 %gather_second.1 = (f32[12,144,128]{2,1,0:T(8,128)S(1)}, f32[12,144,128]{2,1,0:T(8,128)S(1)}) custom-call(f32[2016,128]{1,0:T(8,128)S(1)} %get-tuple-element.62.first_stage, s32[168,128]{1,0:T(8,128)S(1)} %get-tuple-element.57.after_ref.lo_ref, s32[168,128]{1,0:T(8,128)S(1)} %get-tuple-element.63.hi_ref, bf16[160,512]{1,0:T(8,128)(2,1)S(1)} %get-tuple-element.64.terms_ref, ...), custom_call_target="tpu_custom_call" | custom-call | flops 4000000000 | tf_op jit(solution)/shard_map/gather_second/pallas_call | solution.py:332
  28.8 4.2 %collective-permute-done.2.band_ref = bf16[288,192]{1,0:T(8,128)(2,1)S(1)} collective-permute-done((bf16[288,192]{1,0:T(8,128)(2,1)S(1)}, bf16[288,192]{1,0:T(8,128)(2,1)S(1)}, u32[]{:S(2)}, u32[]{:S(2)}) %collective-permute-start.2) | collective-permute-done | bytes 110624 | tf_op jit(solution)/shard_map/ppermute | solution.py:639
  33.0 1.1 %collective-permute-start.3 = (bf16[288,192]{1,0:T(8,128)(2,1)S(1)}, bf16[288,192]{1,0:T(8,128)(2,1)S(1)}, u32[]{:S(2)}, u32[]{:S(2)}) collective-permute-start(bf16[288,192]{1,0:T(8,128)(2,1)S(1)} %join.1), channel_id=1, source_target_pairs={{2,0},{3,1},{4,2},{5,3},{6,4},{7,5},{8,6},{9,7},{10,8},{11,9},{12,... | collective-permute-start | bytes 331784 | tf_op jit(solution)/shard_map/ppermute | solution.py:639
  34.1 0.0 collective-permute-done.4.sector_ref.x_sector
  34.1 0.0 copy-start.8
  34.1 3.0 %forward.1 = (bf16[576,192]{1,0:T(8,128)(2,1)S(1)}, bf16[576,96]{1,0:T(8,128)(2,1)S(1)}, bf16[576,96]{1,0:T(8,128)(2,1)S(1)}, bf16[576,96]{1,0:T(8,128)(2,1)S(1)...) custom-call(bf16[144,192]{1,0:T(8,128)(2,1)S(1)} %copy-done.16, ...), custom_call_target="tpu_custom_call" | custom-call | flops 5000000000 | tf_op jit(solution)/shard_map/forward/pallas_call | solution.py:377
  37.1 0.1 collective-permute-done.3.sector_ref
  37.2 5.3 %backward.1 = (bf16[576,192]{1,0:T(8,128)(2,1)S(1)}, f32[12,144,144]{2,1,0:T(8,128)S(1)}, bf16[3,576,96]{2,1,0:T(8,128)(2,1)S(1)}, bf16[576,192]{1,0:T(8,128)(2,1)S(1)}) custom-call(bf16[144,192]{1,0:T(8,128)(2,1)S(1)} %get-tuple-element.60.own_ref.m3, bf16[288,192]{1,0:T(8,128)(2,1)S(1)} %collective-permute-done.2.band_ref, ...), custom_call_target="tpu_custom_call" | custom-call | flops 7000000000 | tf_op jit(solution)/shard_map/backward/pallas_call | solution.py:433
  42.6 0.5 collective-permute-start.5
  43.1 5.8 %scatter.1 = (f32[192,256]{1,0:T(8,128)S(1)}, bf16[288,128]{1,0:T(8,128)(2,1)S(1)}, bf16[288,128]{1,0:T(8,128)(2,1)S(1)}) custom-call(s32[3]{0:T(128)S(1)} %copy-done, f32[12,144,144]{2,1,0:T(8,128)S(1)} %get-tuple-element.76.score_ref, s32[168,128]{1,0:T(8,128)S(1)} %get-tuple-element.57.after_ref.lo_ref, s32[168,128]{1,0:T(8,128)S(1)} %get-tuple-element.63.hi_ref, ...), custom_call_target="tpu_custom_call" | custom-call | flops 5000000000 | tf_op jit(solution)/shard_map/scatter/pallas_call | solution.py:477
  49.0 0.1 collective-permute-start.7
  49.1 0.0 collective-permute-done.6.first_other
  49.1 1.2 %collective-permute-done.7.second_other = bf16[288,128]{1,0:T(8,128)(2,1)S(1)} collective-permute-done((bf16[288,128]{1,0:T(8,128)(2,1)S(1)}, bf16[288,128]{1,0:T(8,128)(2,1)S(1)}, u32[]{:S(2)}, u32[]{:S(2)}) %collective-permute-start.7) | collective-permute-done | bytes 73760 | tf_op jit(solution)/shard_map/ppermute | solution.py:643
  50.3 0.0 collective-permute-done.5.other_ref
  50.3 0.4 meet.1
  50.8 18.4 %all_to_all.10.got_ref = bf16[32,40,128]{2,1,0:T(8,128)(2,1)S(1)} all-to-all(bf16[32,40,128]{2,1,0:T(8,128)(2,1)S(1)} %bitcast.25), channel_id=1, replica_groups=mesh['lat'=4,'lon'=32,'tp'=2] {'lon'}, dimensions={0} | all-to-all | bytes 655360 | tf_op jit(solution)/shard_map/all_to_all | solution.py:691
  69.2 0.1 add.10
  69.3 3.9 %collective-permute-start.8 = (bf16[144,192]{1,0:T(8,128)(2,1)S(1)}, bf16[144,192]{1,0:T(8,128)(2,1)S(1)}, u32[]{:S(2)}, u32[]{:S(2)}) collective-permute-start(bf16[144,192]{1,0:T(8,128)(2,1)S(1)} %get-tuple-element.84), channel_id=1, source_target_pairs={{254,0},{255,1},{192,2},{193,3},{194,4},{195,5},{196,6},{197,7},{1... | collective-permute-start | bytes 165896 | tf_op jit(solution)/shard_map/ppermute | solution.py:639
  73.2 0.5 collective-permute-start.9
  73.7 0.7 collective-permute-start.10
  74.4 0.9 collective-permute-start.11
  75.3 1.2 %collective-permute-done.8.g0 = bf16[144,192]{1,0:T(8,128)(2,1)S(1)} collective-permute-done((bf16[144,192]{1,0:T(8,128)(2,1)S(1)}, bf16[144,192]{1,0:T(8,128)(2,1)S(1)}, u32[]{:S(2)}, u32[]{:S(2)}) %collective-permute-start.8) | collective-permute-done | bytes 55328 | tf_op jit(solution)/shard_map/ppermute | solution.py:639
  76.5 0.0 collective-permute-done.9.g1
  76.5 4.7 %collective-permute-done.10.g2 = bf16[144,192]{1,0:T(8,128)(2,1)S(1)} collective-permute-done((bf16[144,192]{1,0:T(8,128)(2,1)S(1)}, bf16[144,192]{1,0:T(8,128)(2,1)S(1)}, u32[]{:S(2)}, u32[]{:S(2)}) %collective-permute-start.10) | collective-permute-done | bytes 55328 | tf_op jit(solution)/shard_map/ppermute | solution.py:639
  81.2 1.2 %finish.1 = (bf16[6,12,8,192]{3,2,1,0:T(8,128)(2,1)}, f32[8,128]{1,0:T(8,128)S(1)}) custom-call(bf16[288,192]{1,0:T(8,128)(2,1)S(1)} %copy-done.7, bf16[144,192]{1,0:T(8,128)(2,1)S(1)} %copy-done.17, bf16[144,192]{1,0:T(8,128)(2,1)S(1)} %copy-done.16, bf16[288,192]{1,0:T(8,128)(2,1)S(1)} %get-tuple-element.58.m10, ...), custom_call_target="tpu_custom_call" | custom-call | flops 1000000000 | tf_op jit(solution)/shard_map/finish/pallas_call | solution.py:532
  82.5 0.0 collective-permute-done.11.other_ref
  82.5 0.6 spread.1
  83.0 14.9 %all_to_all.11 = bf16[32,40,128]{2,1,0:T(8,128)(2,1)S(1)} all-to-all(bf16[32,40,128]{2,1,0:T(8,128)(2,1)S(1)} %spread.1), channel_id=1, replica_groups=mesh['lat'=4,'lon'=32,'tp'=2] {'lon'}, dimensions={0} | all-to-all | bytes 655360 | tf_op jit(solution)/shard_map/all_to_all | solution.py:696
  97.9 3.5 %collective-permute-start.12 = (bf16[1280,128]{1,0:T(8,128)(2,1)S(1)}, bf16[1280,128]{1,0:T(8,128)(2,1)S(1)}, u32[]{:S(2)}, u32[]{:S(2)}) collective-permute-start(bf16[1280,128]{1,0:T(8,128)(2,1)S(1)} %bitcast.23), channel_id=1, source_target_pairs={{0,64},{64,0},{128,192},{192,128},{1,65},{65,1},{129,193},{193,129... | collective-permute-start | bytes 983048 | tf_op jit(solution)/shard_map/ppermute | solution.py:643
  101.4 1.3 %collective-permute-done.12.other_ref = bf16[1280,128]{1,0:T(8,128)(2,1)S(1)} collective-permute-done((bf16[1280,128]{1,0:T(8,128)(2,1)S(1)}, bf16[1280,128]{1,0:T(8,128)(2,1)S(1)}, u32[]{:S(2)}, u32[]{:S(2)}) %collective-permute-start.12) | collective-permute-done | bytes 327712 | tf_op jit(solution)/shard_map/ppermute | solution.py:643
  102.6 1.7 %unpack.1 = (f32[3,192,96]{2,1,0:T(8,128)}, f32[96,192]{1,0:T(8,128)}, f32[192,384]{1,0:T(8,128)}, f32[192,384]{1,0:T(8,128)}, f32[1,96]{1,0:T(1,128)}, /*index=5*/f32[1,96]{1,0:T(1,128)}, f32[3,4,3312]{2,1,0:T(4,128)}) custom-call(s32[3]{0:T(128)S(1)} %copy-done, bf16[1280,128]{1,0:T(8,128)(2,1)S(1)} %bitcast.24, ...), custom_call_target="tpu_custom_call" | custom-call | tf_op jit(solution)/shard_map/unpack/pallas_call | solution.py:614
  (30 shorter events, 0.1 us)
Async XLA Ops:
  1.3 7.8 %copy-start.4 = (f32[1,4,3,3312]{3,1,2,0:T(4,128)S(1)}, f32[1,4,3,3312]{3,1,2,0:T(4,128)}, u32[]{:S(2)}) copy-start(f32[1,4,3,3312]{3,1,2,0:T(4,128)} %param.22) | copy-start | bytes 476932
  1.3 7.8 %copy-start.5 = (s32[144,144]{1,0:T(8,128)S(1)}, s32[144,144]{1,0:T(8,128)}, u32[]{:S(2)}) copy-start(s32[144,144]{1,0:T(8,128)} %index_ref.1) | copy-start | bytes 248836
  1.3 7.8 %copy-start.9 = (s32[8,6,12]{2,0,1:T(8,128)S(1)}, s32[8,6,12]{2,0,1:T(8,128)}, u32[]{:S(2)}) copy-start(s32[8,6,12]{2,0,1:T(8,128)} %param.19) | copy-start | bytes 6916
  1.3 7.8 %copy-start.10 = (s32[8,6,12]{2,0,1:T(8,128)S(1)}, s32[8,6,12]{2,0,1:T(8,128)}, u32[]{:S(2)}) copy-start(s32[8,6,12]{2,0,1:T(8,128)} %param.20) | copy-start | bytes 6916
  1.3 7.8 %copy-start.14 = (bf16[144,144]{1,0:T(8,128)(2,1)S(1)}, bf16[144,144]{1,0:T(8,128)(2,1)}, u32[]{:S(2)}) copy-start(bf16[144,144]{1,0:T(8,128)(2,1)} %constant.31.clone.order_ref) | copy-start | bytes 124420
  5.7 43.4 %collective-permute-start.6 = (bf16[576,128]{1,0:T(8,128)(2,1)}, bf16[576,128]{1,0:T(8,128)(2,1)S(1)}, u32[]{:S(2)}, u32[]{:S(2)}) collective-permute-start(bf16[576,128]{1,0:T(8,128)(2,1)} %get-tuple-element.75), channel_id=1, source_target_pairs={{0,64},{64,0},{128,192},{192,128},{1,65},{65,1},{129,193},{193,129... | collective-permute-start | bytes 442376 | tf_op jit(solution)/shard_map/ppermute | solution.py:643
  9.0 7.9 %collective-permute-start.1 = (bf16[288,192]{1,0:T(8,128)(2,1)}, bf16[288,192]{1,0:T(8,128)(2,1)S(1)}, u32[]{:S(2)}, u32[]{:S(2)}) collective-permute-start(bf16[288,192]{1,0:T(8,128)(2,1)} %get-tuple-element.53.x10), channel_id=1, source_target_pairs={{64,0},{65,1},{66,2},{67,3},{68,4},{69,5},{70,6},{71,7},{72,8},{73... | collective-permute-start | bytes 331784 | tf_op jit(solution)/shard_map/ppermute | solution.py:639
  9.1 8.7 %collective-permute-start = (bf16[576,192]{1,0:T(8,128)(2,1)}, bf16[576,192]{1,0:T(8,128)(2,1)S(1)}, u32[]{:S(2)}, u32[]{:S(2)}) collective-permute-start(bf16[576,192]{1,0:T(8,128)(2,1)} %get-tuple-element.56.own_ref), channel_id=1, source_target_pairs={{1,0},{0,1},{3,2},{2,3},{5,4},{4,5},{7,6},{6,7},{9,8},{8,9},{11,10... | collective-permute-start | bytes 663560 | tf_op jit(solution)/shard_map/ppermute | solution.py:639
  9.2 8.7 %copy-start.1 = (bf16[8,6,12,192]{3,0,2,1:T(8,128)(2,1)S(1)}, bf16[8,6,12,192]{3,0,2,1:T(8,128)(2,1)}, u32[]{:S(2)}) copy-start(bf16[8,6,12,192]{3,0,2,1:T(8,128)(2,1)} %param.17) | copy-start | bytes 663556
  9.2 8.7 %copy-start.2 = (bf16[8,6,12,192]{3,0,2,1:T(8,128)(2,1)S(1)}, bf16[8,6,12,192]{3,0,2,1:T(8,128)(2,1)}, u32[]{:S(2)}) copy-start(bf16[8,6,12,192]{3,0,2,1:T(8,128)(2,1)} %param.18) | copy-start | bytes 663556
  9.2 8.6 %copy-start.3 = (bf16[576,192]{1,0:T(8,128)(2,1)S(1)}, bf16[576,192]{1,0:T(8,128)(2,1)}, u32[]{:S(2)}) copy-start(bf16[576,192]{1,0:T(8,128)(2,1)} %get-tuple-element.56.own_ref) | copy-start | bytes 663556
  9.2 8.6 %copy-start.11 = (f32[192]{0:T(256)S(1)}, f32[192]{0:T(256)}, u32[]{:S(2)}) copy-start(f32[192]{0:T(256)} %param.26) | copy-start | bytes 2308
  9.2 8.6 %copy-start.17 = (bf16[144,192]{1,0:T(8,128)(2,1)S(1)}, bf16[144,192]{1,0:T(8,128)(2,1)}, u32[]{:S(2)}) copy-start(bf16[144,192]{1,0:T(8,128)(2,1)} %get-tuple-element.54.x2_ref.x2) | copy-start | bytes 165892
  18.5 15.6 %collective-permute-start.4 = (bf16[288,192]{1,0:T(8,128)(2,1)S(1)}, bf16[288,192]{1,0:T(8,128)(2,1)S(1)}, u32[]{:S(2)}, u32[]{:S(2)}) collective-permute-start(bf16[288,192]{1,0:T(8,128)(2,1)S(1)} %get-tuple-element.61), channel_id=1, source_target_pairs={{2,0},{3,1},{4,2},{5,3},{6,4},{7,5},{8,6},{9,7},{10,8},{11,9},{12,... | collective-permute-start | bytes 331784 | tf_op jit(solution)/shard_map/ppermute | solution.py:639
  23.3 9.7 %collective-permute-start.2 = (bf16[288,192]{1,0:T(8,128)(2,1)S(1)}, bf16[288,192]{1,0:T(8,128)(2,1)S(1)}, u32[]{:S(2)}, u32[]{:S(2)}) collective-permute-start(bf16[288,192]{1,0:T(8,128)(2,1)S(1)} %get-tuple-element.58.m10), channel_id=1, source_target_pairs={{64,0},{65,1},{66,2},{67,3},{68,4},{69,5},{70,6},{71,7},{72,8},{73... | collective-permute-start | bytes 331784 | tf_op jit(solution)/shard_map/ppermute | solution.py:639
  27.4 6.7 %copy-start.6 = (bf16[3,192,96]{2,1,0:T(8,128)(2,1)S(1)}, bf16[3,192,96]{2,1,0:T(8,128)(2,1)}, u32[]{:S(2)}) copy-start(bf16[3,192,96]{2,1,0:T(8,128)(2,1)} %qkv_ref.3) | copy-start | bytes 331780
  27.4 6.7 %copy-start.12 = (f32[192]{0:T(256)S(1)}, f32[192]{0:T(256)}, u32[]{:S(2)}) copy-start(f32[192]{0:T(256)} %param.23) | copy-start | bytes 2308
  27.4 6.7 %copy-start.13 = (bf16[144,144]{1,0:T(8,128)(2,1)S(1)}, bf16[144,144]{1,0:T(8,128)(2,1)}, u32[]{:S(2)}) copy-start(bf16[144,144]{1,0:T(8,128)(2,1)} %constant.32.clone.order_ref) | copy-start | bytes 124420
  27.4 6.8 %copy-start.16 = (bf16[144,192]{1,0:T(8,128)(2,1)S(1)}, bf16[144,192]{1,0:T(8,128)(2,1)}, u32[]{:S(2)}) copy-start(bf16[144,192]{1,0:T(8,128)(2,1)} %get-tuple-element.55.own_ref.x_own.x3) | copy-start | bytes 165892
  33.0 4.3 %collective-permute-start.3 = (bf16[288,192]{1,0:T(8,128)(2,1)S(1)}, bf16[288,192]{1,0:T(8,128)(2,1)S(1)}, u32[]{:S(2)}, u32[]{:S(2)}) collective-permute-start(bf16[288,192]{1,0:T(8,128)(2,1)S(1)} %join.1), channel_id=1, source_target_pairs={{2,0},{3,1},{4,2},{5,3},{6,4},{7,5},{8,6},{9,7},{10,8},{11,9},{12,... | collective-permute-start | bytes 331784 | tf_op jit(solution)/shard_map/ppermute | solution.py:639
  34.1 3.1 %copy-start.8 = (bf16[96,192]{1,0:T(8,128)(2,1)S(1)}, bf16[96,192]{1,0:T(8,128)(2,1)}, u32[]{:S(2)}) copy-start(bf16[96,192]{1,0:T(8,128)(2,1)} %proj_ref.1) | copy-start | bytes 110596
  37.2 5.9 %copy-start = (s32[3]{0:T(128)S(1)}, s32[3]{0:T(128)}, u32[]{:S(2)}) copy-start(s32[3]{0:T(128)} %pad_add_fusion.place_ref) | copy-start | bytes 40
  42.6 7.7 %collective-permute-start.5 = (bf16[576,192]{1,0:T(8,128)(2,1)S(1)}, bf16[576,192]{1,0:T(8,128)(2,1)S(1)}, u32[]{:S(2)}, u32[]{:S(2)}) collective-permute-start(bf16[576,192]{1,0:T(8,128)(2,1)S(1)} %get-tuple-element.73.own_ref), channel_id=1, source_target_pairs={{1,0},{0,1},{3,2},{2,3},{5,4},{4,5},{7,6},{6,7},{9,8},{8,9},{11,10... | collective-permute-start | bytes 663560 | tf_op jit(solution)/shard_map/ppermute | solution.py:639
  43.1 7.2 %copy-start.15 = (bf16[576,128]{1,0:T(8,128)(2,1)S(1)}, bf16[576,128]{1,0:T(8,128)(2,1)}, u32[]{:S(2)}) copy-start(bf16[576,128]{1,0:T(8,128)(2,1)} %get-tuple-element.74.first_ref) | copy-start | bytes 442372
  49.0 1.4 %collective-permute-start.7 = (bf16[288,128]{1,0:T(8,128)(2,1)S(1)}, bf16[288,128]{1,0:T(8,128)(2,1)S(1)}, u32[]{:S(2)}, u32[]{:S(2)}) collective-permute-start(bf16[288,128]{1,0:T(8,128)(2,1)S(1)} %get-tuple-element.82), channel_id=1, source_target_pairs={{0,64},{64,0},{128,192},{192,128},{1,65},{65,1},{129,193},{193,129... | collective-permute-start | bytes 221192 | tf_op jit(solution)/shard_map/ppermute | solution.py:643
  69.2 12.0 %copy-start.7 = (bf16[288,192]{1,0:T(8,128)(2,1)S(1)}, bf16[288,192]{1,0:T(8,128)(2,1)}, u32[]{:S(2)}) copy-start(bf16[288,192]{1,0:T(8,128)(2,1)} %get-tuple-element.53.x10) | copy-start | bytes 331780
  69.3 7.2 %collective-permute-start.8 = (bf16[144,192]{1,0:T(8,128)(2,1)S(1)}, bf16[144,192]{1,0:T(8,128)(2,1)S(1)}, u32[]{:S(2)}, u32[]{:S(2)}) collective-permute-start(bf16[144,192]{1,0:T(8,128)(2,1)S(1)} %get-tuple-element.84), channel_id=1, source_target_pairs={{254,0},{255,1},{192,2},{193,3},{194,4},{195,5},{196,6},{197,7},{1... | collective-permute-start | bytes 165896 | tf_op jit(solution)/shard_map/ppermute | solution.py:639
  73.2 3.3 %collective-permute-start.9 = (bf16[144,192]{1,0:T(8,128)(2,1)S(1)}, bf16[144,192]{1,0:T(8,128)(2,1)S(1)}, u32[]{:S(2)}, u32[]{:S(2)}) collective-permute-start(bf16[144,192]{1,0:T(8,128)(2,1)S(1)} %get-tuple-element.85), channel_id=1, source_target_pairs={{192,0},{193,1},{194,2},{195,3},{196,4},{197,5},{198,6},{199,7},{2... | collective-permute-start | bytes 165896 | tf_op jit(solution)/shard_map/ppermute | solution.py:639
  73.7 7.5 %collective-permute-start.10 = (bf16[144,192]{1,0:T(8,128)(2,1)S(1)}, bf16[144,192]{1,0:T(8,128)(2,1)S(1)}, u32[]{:S(2)}, u32[]{:S(2)}) collective-permute-start(bf16[144,192]{1,0:T(8,128)(2,1)S(1)} %get-tuple-element.86), channel_id=1, source_target_pairs={{62,0},{63,1},{0,2},{1,3},{2,4},{3,5},{4,6},{5,7},{6,8},{7,9},{8,1... | collective-permute-start | bytes 165896 | tf_op jit(solution)/shard_map/ppermute | solution.py:639
  74.4 8.1 %collective-permute-start.11 = (bf16[40,128]{1,0:T(8,128)(2,1)S(1)}, bf16[40,128]{1,0:T(8,128)(2,1)S(1)}, u32[]{:S(2)}, u32[]{:S(2)}) collective-permute-start(bf16[40,128]{1,0:T(8,128)(2,1)S(1)} %get-tuple-element.89.own_ref), channel_id=1, source_target_pairs={{128,0},{129,1},{130,2},{131,3},{132,4},{133,5},{134,6},{135,7},{1... | collective-permute-start | bytes 30728 | tf_op jit(solution)/shard_map/ppermute | solution.py:639
  97.9 4.7 %collective-permute-start.12 = (bf16[1280,128]{1,0:T(8,128)(2,1)S(1)}, bf16[1280,128]{1,0:T(8,128)(2,1)S(1)}, u32[]{:S(2)}, u32[]{:S(2)}) collective-permute-start(bf16[1280,128]{1,0:T(8,128)(2,1)S(1)} %bitcast.23), channel_id=1, source_target_pairs={{0,64},{64,0},{128,192},{192,128},{1,65},{65,1},{129,193},{193,129... | collective-permute-start | bytes 983048 | tf_op jit(solution)/shard_map/ppermute | solution.py:643

commit v7 on v5

--- a/solution.py
+++ b/solution.py
@@ -29,6 +29,10 @@
     return jax.ShapeDtypeStruct(dims, kind)
 
 
+def both(own, other):
+    return (own.astype(F32) + other.astype(F32)).astype(BF)
+
+
 def dot_nn(a, b):
     return lax.dot_general(a, b, (((1,), (0,)), ((), ())), preferred_element_type=F32)
 
@@ -85,7 +89,7 @@
             scratch[w * 144 + s * 36 : w * 144 + s * 36 + 36, :] = rows[w * 36 : w * 36 + 36]
 
 
-def head_kernel(x_hbm, mid_hbm, up_hbm, gain_hbm, fc1_hbm, fc2_hbm, o0, o1, o2, o3, part_hbm, grads_hbm,
+def head_kernel(x_hbm, mid_hbm, up_hbm, gain_hbm, fc1_hbm, fc2_hbm, o0, o1, o2, o3, part_hbm, keep_hbm, send_hbm,
                 x_ref, mid_ref, up_ref, gain_ref, fc1_ref, fc2_ref, xq_ref, part_ref, grads_ref, x_s, mid_s, up_s, sem):
     pairs = (
         (mid_hbm, mid_ref),
@@ -122,8 +126,11 @@
     for start, grads in ((0, dot_tn(lowered, grad_pre)), (576, dot_tn(up, active.astype(BF)))):
         for j in range(3):
             grads_ref[start + j * 192 : start + j * 192 + 192, :] = grads[:, j * 128 : j * 128 + 128].astype(BF)
-    writes.append(pltpu.make_async_copy(grads_ref, grads_hbm, sem.at[7]))
-    writes[-1].start()
+    core = lax.rem(lax.axis_index("lat"), 2)
+    for i, (half, out) in enumerate(((core, keep_hbm), (1 - core, send_hbm))):
+        piece = grads_ref.at[pl.ds(pl.multiple_of(half * 576, 16), 576)]
+        writes.append(pltpu.make_async_copy(piece, out, sem.at[12 + i]))
+        writes[-1].start()
     for write in writes:
         write.wait()
 
@@ -131,9 +138,10 @@
 def head(x, mid, up, gain, fc1, fc2):
     return pl.pallas_call(
         head_kernel,
-        out_shape=tuple(shape((144, 192), BF) for _ in range(4)) + (shape((576, 192), BF), shape((1152, 128), BF)),
+        out_shape=tuple(shape((144, 192), BF) for _ in range(4))
+        + (shape((576, 192), BF), shape((576, 128), BF), shape((576, 128), BF)),
         in_specs=[ANY] * 6,
-        out_specs=tuple(ANY for _ in range(6)),
+        out_specs=tuple(ANY for _ in range(7)),
         scratch_shapes=[
             pltpu.VMEM((6, 12, 8, 192), BF),
             pltpu.VMEM((6, 12, 8, 192), BF),
@@ -147,7 +155,7 @@
             pltpu.VMEM((576, 192), F32),
             pltpu.VMEM((576, 192), F32),
             pltpu.VMEM((576, 192), F32),
-            pltpu.SemaphoreType.DMA((12,)),
+            pltpu.SemaphoreType.DMA((14,)),
         ],
         compiler_params=ALL,
         cost_estimate=cost(3),
@@ -272,12 +280,12 @@
         ),
         scratch_shapes=[pltpu.VMEM((160, 256), F32)],
         compiler_params=VM,
-        cost_estimate=cost(6),
+        cost_estimate=cost(0.5),
         name="gather_first",
     )(index, jnp.asarray(window_order(), BF), bias, ids, valid)
 
 
-def gather_second_kernel(first_stage, lo_ref, hi_ref, terms_ref, after_ref, main_ref, tail_ref, stage):
+def gather_second_kernel(first_stage, lo_ref, hi_ref, terms_ref, a0, a1, a2, a3, main_ref, tail_ref, stage):
     look_up(terms_ref[...], lo_ref, hi_ref, stage, 90, 4)
     for r in range(12):
         main_ref[r, 0:90, :] = first_stage[pl.ds(r, 90, stride=16), :]
@@ -291,12 +299,12 @@
     return pl.pallas_call(
         gather_second_kernel,
         out_shape=(shape((12, 144, 128), F32), shape((12, 144, 128), F32)),
-        in_specs=[VMEM] * 4 + [ANY],
+        in_specs=[VMEM] * 4 + [ANY] * 4,
         scratch_shapes=[pltpu.VMEM((72 * 16, 128), F32)],
         compiler_params=VM,
         cost_estimate=cost(4),
         name="gather_second",
-    )(first_stage, lo, hi, terms, after)
+    )(first_stage, lo, hi, terms, *after)
 
 
 def forward_kernel(x0, x1, x2, x3, order_ref, gain_ref, qkv_ref, main_ref, tail_ref, code_ref,
@@ -404,7 +412,8 @@
     )(*g, level_order(), proj, qkv, q, k, v, prob)
 
 
-def scatter_kernel(score_ref, lo_ref, hi_ref, low_ref, gcols, att_ref, grad_ref, out_ref, grads_ref, tails):
+def scatter_kernel(score_ref, lo_ref, hi_ref, low_ref, gcols, att_ref, grad_ref,
+                   out_ref, keep_ref, send_ref, grads_ref, tails):
     out_ref[...] = jnp.zeros((192, 256), F32)
     place = lax.broadcasted_iota(I32, (16, 128), 0)
     for r in range(12):
@@ -426,28 +435,32 @@
     grads_ref[144:336, :] = jnp.concatenate([a, c[:, 0:32]], axis=1)
     grads_ref[336:528, :] = jnp.concatenate([b, c[:, 32:64]], axis=1)
     grads_ref[528:576, :] = jnp.concatenate([c[i * 48 : i * 48 + 48, 64:96] for i in range(4)], axis=1)
+    core = lax.rem(lax.axis_index("lat"), 2)
+    keep_ref[...] = grads_ref[pl.ds(pl.multiple_of(core * 288, 16), 288), :]
+    send_ref[...] = grads_ref[pl.ds(pl.multiple_of((1 - core) * 288, 16), 288), :]
 
 
 def scatter(score, lo, hi, low, gcols, att, grad):
     return pl.pallas_call(
         scatter_kernel,
-        out_shape=(shape((192, 256), F32), shape((576, 128), BF)),
-        scratch_shapes=[pltpu.VMEM((12, 24, 128), F32)],
+        out_shape=(shape((192, 256), F32), shape((288, 128), BF), shape((288, 128), BF)),
+        scratch_shapes=[pltpu.VMEM((576, 128), BF), pltpu.VMEM((12, 24, 128), F32)],
         compiler_params=VM,
         cost_estimate=cost(5),
         name="scatter",
     )(score, lo, hi, low, gcols, att, grad)
 
 
-def meet_kernel(place_ref, own_ref, other_ref, x0, x1, x2, x3, first_ref, second_ref, table_ref, two_ref, out_ref):
+def meet_kernel(own_ref, other_ref, x0, x1, x2, x3, first_ref, first_other, second_ref, second_other,
+                table_ref, two_ref, out_ref):
     gain = jnp.zeros((1, 192), F32)
     for s, x in enumerate((x0, x1, x2, x3)):
         rows = slice(s * 144, s * 144 + 144)
         grad = own_ref[rows, :].astype(F32) + other_ref[rows, :].astype(F32)
         normed, _ = layer_stats(x[...].astype(F32))
         gain = gain + jnp.sum(grad * normed, axis=0, keepdims=True)
-    out_ref[0:1152, :] = first_ref[...]
-    out_ref[1152:1728, :] = second_ref[...]
+    out_ref[0:576, :] = both(first_ref[...], first_other[...])
+    out_ref[576:864, :] = both(second_ref[...], second_other[...])
     rows = []
     for r in range(12):
         pair = table_ref[r * 16 : r * 16 + 13, :]
@@ -455,102 +468,100 @@
     none = jnp.zeros((1, 64), F32)
     for line in (gain, two_ref[...]):
         rows += [line[:, 0:128], jnp.concatenate([line[:, 128:192], none], axis=1)]
-    rows += [jnp.zeros((4, 128), F32)]
-    out_ref[1728:2048, :] = jnp.concatenate(rows, axis=0).astype(BF)
-
-
-def meet(place, own, other, x, first, second, table, two):
+    rows += [jnp.zeros((100, 128), F32)]
+    out_ref[864:1280, :] = jnp.concatenate(rows, axis=0).astype(BF)
+
+
+def meet(own, other, x, first, first_other, second, second_other, table, two):
     return pl.pallas_call(
         meet_kernel,
-        out_shape=shape((2048, 128), BF),
-        in_specs=[SMEM] + [VMEM] * 10,
+        out_shape=shape((1280, 128), BF),
         compiler_params=VM,
         cost_estimate=cost(1),
         name="meet",
-    )(place, own, other, *x, first, second, table, two)
-
-
-def finish_kernel(x0, x1, x2, x3, m0, m1, m2, m3, g0, g1, g2, g3, gain_ref, out_ref, token_ref):
-    token_ref[...] = jnp.zeros((8, 128), F32)
-    for q, (x, m, g) in enumerate(zip((x0, x1, x2, x3), (m0, m1, m2, m3), (g0, g1, g2, g3))):
+    )(own, other, *x, first, first_other, second, second_other, table, two)
+
+
+def finish_kernel(x0, x1, x2, x3, m0, m1, m2, m3, g_own, band, sector, gain_ref, after_ref, out_ref):
+    gs = (sector[144:288, :], band[0:144, :], sector[0:144, :], g_own[...])
+    for q, (x, m, g) in enumerate(zip((x0, x1, x2, x3), (m0, m1, m2, m3), gs)):
         normed, inverse = layer_stats(x[...].astype(F32))
-        rows = m[...].astype(F32) + norm_backward(g[0:144, :].astype(F32), gain_ref[...], normed, inverse)
+        rows = m[...].astype(F32) + norm_backward(g.astype(F32), gain_ref[...], normed, inverse)
         for lat in range(3):
             piece = rows[lat * 48 : lat * 48 + 48].reshape(6, 8, 192)
             out_ref[(q // 2) * 3 + lat, (q % 2) * 6 : (q % 2) * 6 + 6] = piece.astype(BF)
 
 
-def finish(x, m, g, gain):
+def finish(x, m, g, gain, after):
     return pl.pallas_call(
         finish_kernel,
-        out_shape=(shape((6, 12, 8, 192), BF), shape((8, 128), F32)),
+        out_shape=shape((6, 12, 8, 192), BF),
+        in_specs=[VMEM] * 12 + [ANY],
         compiler_params=VM,
         cost_estimate=cost(1),
         name="finish",
-    )(*x, *m, *g, gain)
-
-
-def add_kernel(got_ref, own_ref, other_ref, out_ref, g0, g1, g2, g3):
+    )(*x, *m, *g, gain, after)
+
+
+def add_kernel(got_ref, own_ref, other_ref, out_ref, g0, g1, g23):
     total = got_ref[0].astype(F32)
     for i in range(1, 32):
         total = total + got_ref[i].astype(F32)
     out_ref[...] = total.astype(BF)
-    for s, out in enumerate((g0, g1, g2, g3)):
-        rows = slice(s * 144, s * 144 + 144)
-        out[0:144, :] = (own_ref[rows, :].astype(F32) + other_ref[rows, :].astype(F32)).astype(BF)
-    g2[144:208, :] = jnp.concatenate([total, jnp.zeros((64, 64), F32)], axis=1).astype(BF)
+    g0[...] = both(own_ref[0:144, :], other_ref[0:144, :])
+    g1[...] = both(own_ref[144:288, :], other_ref[144:288, :])
+    g23[...] = both(own_ref[288:576, :], other_ref[288:576, :])
 
 
 def add(got, own, other):
-    quarter = shape((144, 192), BF)
     return pl.pallas_call(
         add_kernel,
-        out_shape=(shape((64, 128), BF), quarter, quarter, shape((208, 192), BF), quarter),
+        out_shape=(shape((40, 128), BF), shape((144, 192), BF), shape((144, 192), BF), shape((288, 192), BF)),
         compiler_params=VM,
         cost_estimate=cost(1),
         name="add",
     )(got, own, other)
 
 
-def spread_kernel(place_ref, own_ref, a_ref, b_ref, c_ref, after_ref, out_ref):
+def spread_kernel(own_ref, other_ref, g1, band, out_ref, next_ref):
     own = own_ref[...].astype(F32)
-    total = own + a_ref[144:208, 0:128].astype(F32) + b_ref[...].astype(F32) + c_ref[...].astype(F32)
-    row = place_ref[0] * 64 + lax.broadcasted_iota(I32, (64, 128), 0)
-    table = (row >= 1728) & (row < 2040)
-    out_ref[...] = jnp.broadcast_to(jnp.where(table, own, total).astype(BF)[None], (32, 64, 128))
-
-
-def spread(place, own, a, b, c, after):
+    row = lax.axis_index("lon") * 40 + lax.broadcasted_iota(I32, (40, 128), 0)
+    table = (row >= 864) & (row < 1176)
+    total = own + jnp.where(table, 0.0, other_ref[...].astype(F32))
+    out_ref[...] = jnp.broadcast_to(total.astype(BF)[None], (32, 40, 128))
+    next_ref[0:144, :] = g1[...]
+    next_ref[144:288, :] = band[144:288, :]
+
+
+def spread(own, other, g1, band):
     return pl.pallas_call(
         spread_kernel,
-        out_shape=shape((32, 64, 128), BF),
-        in_specs=[SMEM] + [VMEM] * 4 + [ANY],
+        out_shape=(shape((32, 40, 128), BF), shape((288, 192), BF)),
         compiler_params=VM,
         cost_estimate=cost(1),
         name="spread",
-    )(place, own, a, b, c, after)
-
-
-def unpack_kernel(weight_scale, table_scale, place_ref, in_ref,
+    )(own, other, g1, band)
+
+
+def unpack_kernel(weight_scale, table_scale, own_ref, other_ref,
                   qkv_ref, proj_ref, upg_ref, down_ref, one_ref, two_ref, table_ref):
-    def rows(start, stop):
-        return in_ref[start:stop, :].astype(F32) * weight_scale
-
+    swap = lax.rem(lax.axis_index("lat"), 2) == 1
+    own, other = own_ref[0:864, :].astype(F32) * weight_scale, other_ref[0:864, :].astype(F32) * weight_scale
+    lower, upper = jnp.where(swap, other, own), jnp.where(swap, own, other)
     for j in range(3):
-        upg_ref[:, j * 128 : j * 128 + 128] = rows(j * 192, j * 192 + 192)
-        down_ref[:, j * 128 : j * 128 + 128] = rows(576 + j * 192, 768 + j * 192)
-    proj_ref[:, 0:128] = rows(1152, 1248)
-    tail = rows(1248, 1296)
-    proj_ref[0:48, 128:192] = tail[:, 0:64]
-    proj_ref[48:96, 128:192] = tail[:, 64:128]
-    first, second, third = rows(1296, 1488), rows(1488, 1680), rows(1680, 1728)
-    qkv_ref[0] = first[:, 0:96]
-    qkv_ref[1] = second[:, 0:96]
-    qkv_ref[2, :, 0:32] = first[:, 96:128]
-    qkv_ref[2, :, 32:64] = second[:, 96:128]
+        upg_ref[:, j * 128 : j * 128 + 128] = lower[j * 192 : j * 192 + 192]
+        down_ref[:, j * 128 : j * 128 + 128] = upper[j * 192 : j * 192 + 192]
+    second = jnp.concatenate([lower[576:864], upper[576:864]], axis=0)
+    proj_ref[:, 0:128] = second[0:96]
+    proj_ref[0:48, 128:192] = second[96:144, 0:64]
+    proj_ref[48:96, 128:192] = second[96:144, 64:128]
+    qkv_ref[0] = second[144:336, 0:96]
+    qkv_ref[1] = second[336:528, 0:96]
+    qkv_ref[2, :, 0:32] = second[144:336, 96:128]
+    qkv_ref[2, :, 32:64] = second[336:528, 96:128]
     for i in range(4):
-        qkv_ref[2, i * 48 : i * 48 + 48, 64:96] = third[:, i * 32 : i * 32 + 32]
-    table = in_ref[1728:2048, :].astype(F32)
+        qkv_ref[2, i * 48 : i * 48 + 48, 64:96] = second[528:576, i * 32 : i * 32 + 32]
+    table = own_ref[864:1184, :].astype(F32)
     for r in range(12):
         for half in range(2):
             piece = table[r * 26 + half * 13 : r * 26 + half * 13 + 13] * table_scale
@@ -558,13 +569,14 @@
                 start = a * 256 + half * 128
                 wide = min(128, 3312 - start)
                 table_ref[r % 3, r // 3 : r // 3 + 1, start : start + wide] = piece[a : a + 1, 0:wide]
-    for start, out in ((312, one_ref), (314, two_ref)):
-        line = table[start : start + 1]
-        upper = jnp.concatenate([line[:, 96:128], table[start + 1 : start + 2, 0:64]], axis=1)
-        out[...] = jnp.where(place_ref[1] == 0, line[:, 0:96], upper) * weight_scale
-
-
-def unpack(weight_scale, table_scale, place, got):
+    gains = table[304:320] + other_ref[1168:1184, :].astype(F32)
+    for start, out in ((8, one_ref), (10, two_ref)):
+        line = gains[start : start + 1]
+        later = jnp.concatenate([line[:, 96:128], gains[start + 1 : start + 2, 0:64]], axis=1)
+        out[...] = jnp.where(lax.axis_index("tp") == 0, line[:, 0:96], later) * weight_scale
+
+
+def unpack(weight_scale, table_scale, got, other):
     return pl.pallas_call(
         functools.partial(unpack_kernel, weight_scale, table_scale),
         out_shape=(
@@ -576,10 +588,9 @@
             shape((1, 96), F32),
             shape((3, 4, 3312), F32),
         ),
-        in_specs=[SMEM, VMEM],
         compiler_params=VM,
         name="unpack",
-    )(place, got)
+    )(got, other)
 
 
 def moved(value, band, sector, half):
@@ -600,6 +611,10 @@
         moved(quarters[1], 1, 0, 0),
         moved(quarters[0], 1, 1, 0),
     )
+
+
+def other_core(value):
+    return lax.ppermute(value, "lat", [(a, a ^ 1) for a in range(lax.axis_size("lat"))])
 
 
 def local(
@@ -627,7 +642,7 @@
         return field.transpose(1, 2, 0, 3)
 
     x_in, mid_in, up_in = turned(inputs), turned(residual_mid), turned(grad_out)
-    *x, part2, first = head(x_in, mid_in, up_in, gain2, fc1_weight, fc2_weight.T)
+    *x, part2, first, first_send = head(x_in, mid_in, up_in, gain2, fc1_weight, fc2_weight.T)
     other2 = moved(part2, 0, 0, 1)
     xw = shifted_parts(x)
     stage, lo, hi, terms, code = gather_first(
@@ -635,22 +650,23 @@
     )
     *gm, gain_two = middle(mid_in, up_in, part2, other2, gain2, lo)
     gw = shifted_parts(gm)
-    main, tail = gather_second(stage, lo, hi, terms, gain_two)
+    main, tail = gather_second(stage, lo, hi, terms, (gain_two, *xw[1:]))
     low, q, k, v, prob, att = forward(xw, gain1, qkv_weight, main, tail, code)
     part1, score, gcols, grad = backward(gw, proj_weight, qkv_weight, q, k, v, prob)
     other1 = moved(part1, 0, 0, 1)
-    table, second = scatter(score, lo, hi, low, gcols, att, grad)
-    place = jnp.stack([lax.axis_index("lon"), lax.axis_index("tp")])
-    sums = meet(place, part1, other1, xw, first, second, table, gain_two)
-    own, g0, g1, g2, g3 = add(lax.all_to_all(sums.reshape(32, 64, 128), "lon", 0, 0), part1, other1)
-    next_band = moved(g2, -1, 0, 0)
-    back = (moved(g3, -1, -1, 0), next_band, moved(g1, 0, -1, 0), g0)
-    result, token = finish(x, gm, back, gain1)
-    totals = spread(place, own, next_band, moved(own, -2, 0, 0), moved(own, -3, 0, 0), token)
-    got = lax.all_to_all(totals, "lon", 0, 0)
+    table, second, second_send = scatter(score, lo, hi, low, gcols, att, grad)
+    sums = meet(
+        part1, other1, xw, first, other_core(first_send), second, other_core(second_send), table, gain_two
+    )
+    own, g0, g1, g23 = add(lax.all_to_all(sums.reshape(32, 40, 128), "lon", 0, 0), part1, other1)
+    g_band = moved(g23, -1, 0, 0)
+    totals, g_next = spread(own, moved(own, 2, 0, 0), g1, g_band)
+    got = lax.all_to_all(totals, "lon", 0, 0).reshape(1280, 128)
+    g_sector = moved(g_next, 0, -1, 0)
     qkv_out, proj_out, up_out, down_out, one, two, table_out = unpack(
-        weight_scale, table_scale, place, got.reshape(2048, 128)
+        weight_scale, table_scale, got, other_core(got)
     )
+    result = finish(x, gm, (g0, g_band, g_sector), gain1, one)
     return (
         result.transpose(2, 0, 1, 3),
         qkv_out,

time: 106 us -> 101 us (0.953)
  blocking collectives: 44.2 us -> 32.9 us
  waiting for transfers between devices: 6.56 us -> 11.5 us
  starting transfers between devices: 26.8 us -> 28.9 us
  Pallas kernels: 27.5 us -> 26 us
    all_to_all x2, blocking collectives: 44.2 us -> 32.9 us  [the longest x1 16.5 us: local(): lax.all_to_all(sums.reshape(32, 40, 128), 'lon', 0, 0)]
    ppermute x0 -> x3, starting transfers between devices: none -> 6.39 us  [other_core(): lax.ppermute(value, 'lat', [(a, a ^ 1) for a in range(lax.axis_size('lat'...]
    ppermute x13 -> x11, starting transfers between devices: 26.8 us -> 22.6 us  [moved(): return lax.ppermute(value, ('lat', 'lon', 'tp'), pairs)]
    ppermute x13 -> x11, waiting for transfers between devices: 6.56 us -> 9.36 us  [moved(): return lax.ppermute(value, ('lat', 'lon', 'tp'), pairs)]
    ppermute x0 -> x3, waiting for transfers between devices: none -> 2.16 us  [other_core(): lax.ppermute(value, 'lat', [(a, a ^ 1) for a in range(lax.axis_size('lat'...]
    pallas_call x4, Pallas kernels: 2.9 us -> 1.83 us  [the longest x1 1.24 us: finish(): pl.pallas_call(finish_kernel, out_shape=shape((6, 12, 8, 192), BF), in_sp...]
  transfers between devices with their start and end apart: 13 -> 14, of which waited for: 4 -> 4; matrix products, arithmetic and copies ran while one was open for 0% -> 0% of each run, Pallas kernels for 14% -> 20%
where the time goes in v7:
time: 101 us
  blocking collectives  32.9 us (33%)
  starting transfers between devices  28.9 us (29%)
  Pallas kernels  26 us (26%)
  waiting for transfers between devices  11.5 us (11%)
    ppermute x11, starting transfers between devices, moved(): return lax.ppermute(value, ('lat', 'lon', 'tp'), pairs)  22.6 us
    all_to_all x1, blocking collectives, local(): lax.all_to_all(sums.reshape(32, 40, 128), 'lon', 0, 0)  16.5 us
    all_to_all x1, blocking collectives, local(): got = lax.all_to_all(totals, 'lon', 0, 0).reshape(1280, 128)  16.4 us
    ppermute x11, waiting for transfers between devices, moved(): return lax.ppermute(value, ('lat', 'lon', 'tp'), pairs)  9.36 us
    ppermute x3, starting transfers between devices, other_core(): lax.ppermute(value, 'lat', [(a, a ^ 1) for a in range(lax.axis_size('lat'...  6.39 us
    pallas_call x1, Pallas kernels, backward(): pl.pallas_call(backward_kernel, out_shape=(shape((576, 192), BF), shape((...  5.33 us
    pallas_call x1, Pallas kernels, scatter(): pl.pallas_call(scatter_kernel, out_shape=(shape((192, 256), F32), shape((...  5.29 us
    pallas_call x1, Pallas kernels, head(): pl.pallas_call(head_kernel, out_shape=tuple((shape((144, 192), BF) for _...  3.63 us
  transfers between devices with their start and end apart: 14, of which 4 were waited for; matrix products, arithmetic and copies ran while one was open for 0% of the time, Pallas kernels for 20%

profile of v7, /device:TPU:1, one launch (start us, length us, event | category | flops | bytes accessed | tf_op | source)
XLA Modules:
  0.0 101.0 jit_solution(18396596046286263097)
XLA Ops:
  0.7 0.0 copy-start.16
  0.7 3.6 %head.1 = (bf16[144,192]{1,0:T(8,128)(2,1)}, bf16[144,192]{1,0:T(8,128)(2,1)}, bf16[144,192]{1,0:T(8,128)(2,1)}, bf16[144,192]{1,0:T(8,128)(2,1)}, bf16[576,192]...) custom-call(bf16[6,12,8,192]{3,2,1,0:T(8,128)(2,1)} %bitcast.35, ...), custom_call_target="tpu_custom_call" | custom-call | flops 3000000000 | tf_op jit(solution)/shard_map/head/pallas_call | solution.py:139
  4.3 0.0 copy-start
  4.3 0.0 copy-start.1
  4.4 0.0 copy-start.2
  4.4 0.0 copy-start.12
  4.4 2.2 %collective-permute-start = (bf16[576,192]{1,0:T(8,128)(2,1)}, bf16[576,192]{1,0:T(8,128)(2,1)S(1)}, u32[]{:S(2)}, u32[]{:S(2)}) collective-permute-start(bf16[576,192]{1,0:T(8,128)(2,1)} %get-tuple-element.57.own_ref), channel_id=1, source_target_pairs={{1,0},{0,1},{3,2},{2,3},{5,4},{4,5},{7,6},{6,7},{9,8},{8,9},{11,10... | collective-permute-start | bytes 663560 | tf_op jit(solution)/shard_map/ppermute | solution.py:604
  6.6 8.6 %collective-permute-start.6 = (bf16[144,192]{1,0:T(8,128)(2,1)}, bf16[144,192]{1,0:T(8,128)(2,1)S(1)}, u32[]{:S(2)}, u32[]{:S(2)}) collective-permute-start(bf16[144,192]{1,0:T(8,128)(2,1)} %get-tuple-element.53.x0), channel_id=1, source_target_pairs={{66,0},{67,1},{68,2},{69,3},{70,4},{71,5},{72,6},{73,7},{74,8},{75... | collective-permute-start | bytes 165896 | tf_op jit(solution)/shard_map/ppermute | solution.py:604
  15.2 1.9 %collective-permute-start.5 = (bf16[144,192]{1,0:T(8,128)(2,1)}, bf16[144,192]{1,0:T(8,128)(2,1)S(1)}, u32[]{:S(2)}, u32[]{:S(2)}) collective-permute-start(bf16[144,192]{1,0:T(8,128)(2,1)} %get-tuple-element.54.x1), channel_id=1, source_target_pairs={{64,0},{65,1},{66,2},{67,3},{68,4},{69,5},{70,6},{71,7},{72,8},{73... | collective-permute-start | bytes 165896 | tf_op jit(solution)/shard_map/ppermute | solution.py:604
  17.1 0.6 collective-permute-start.4
  17.6 1.4 %collective-permute-start.8 = (bf16[576,128]{1,0:T(8,128)(2,1)}, bf16[576,128]{1,0:T(8,128)(2,1)S(1)}, u32[]{:S(2)}, u32[]{:S(2)}) collective-permute-start(bf16[576,128]{1,0:T(8,128)(2,1)} %get-tuple-element.76), channel_id=1, source_target_pairs={{0,64},{64,0},{128,192},{192,128},{1,65},{65,1},{129,193},{193,129... | collective-permute-start | bytes 442376 | tf_op jit(solution)/shard_map/ppermute | solution.py:617
  19.1 3.0 %gather_first.1 = (f32[1440,128]{1,0:T(8,128)S(1)}, s32[168,128]{1,0:T(8,128)S(1)}, s32[168,128]{1,0:T(8,128)S(1)}, bf16[160,512]{1,0:T(8,128)(2,1)S(1)}, f32[4,144]{1,0:T(4,128)S(1)}) custom-call(s32[144,144]{1,0:T(8,128)S(1)} %copy-done.4, bf16[144,144]{1,0:T(8,128)(2,1)S(1)} %copy-done.16, f32[3,4,3312]{2,1,0:T(4,128)S(1)} %bitcast.27, ...), custom_call_target="tpu_custom_call" | custom-call | flops 500000000 | tf_op jit(solution)/shard_map/gather_first/pallas_call | solution.py:272
  22.1 0.0 collective-permute-done.other_ref
  22.1 0.6 middle.1
  22.7 0.6 collective-permute-start.3
  23.3 0.0 collective-permute-done.6.a3.x3
  23.3 1.6 %collective-permute-start.2 = (bf16[144,192]{1,0:T(8,128)(2,1)S(1)}, bf16[144,192]{1,0:T(8,128)(2,1)S(1)}, u32[]{:S(2)}, u32[]{:S(2)}) collective-permute-start(bf16[144,192]{1,0:T(8,128)(2,1)S(1)} %get-tuple-element.60.m1), channel_id=1, source_target_pairs={{64,0},{65,1},{66,2},{67,3},{68,4},{69,5},{70,6},{71,7},{72,8},{73... | collective-permute-start | bytes 165896 | tf_op jit(solution)/shard_map/ppermute | solution.py:604
  24.9 0.0 collective-permute-done.5.a2.x2
  24.9 1.4 %collective-permute-start.1 = (bf16[144,192]{1,0:T(8,128)(2,1)S(1)}, bf16[144,192]{1,0:T(8,128)(2,1)S(1)}, u32[]{:S(2)}, u32[]{:S(2)}) collective-permute-start(bf16[144,192]{1,0:T(8,128)(2,1)S(1)} %get-tuple-element.61.m2), channel_id=1, source_target_pairs={{2,0},{3,1},{4,2},{5,3},{6,4},{7,5},{8,6},{9,7},{10,8},{11,9},{12,... | collective-permute-start | bytes 165896 | tf_op jit(solution)/shard_map/ppermute | solution.py:604
  26.3 0.0 collective-permute-done.4.a1.x1
  26.3 0.0 copy-start.18
  26.3 2.2 %gather_second.1 = (f32[12,144,128]{2,1,0:T(8,128)S(1)}, f32[12,144,128]{2,1,0:T(8,128)S(1)}) custom-call(f32[1440,128]{1,0:T(8,128)S(1)} %get-tuple-element.63.first_stage, s32[168,128]{1,0:T(8,128)S(1)} %get-tuple-element.58.after_ref.lo_ref, s32[168,128]{1,0:T(8,128)S(1)} %get-tuple-element.64.hi_ref, bf16[160,512]{1,0:T(8,128)(2,1)S(1)} %get-tuple-element.65.terms_ref, ...), custom_call_target="tpu_custom_call" | custom-call | flops 4000000000 | tf_op jit(solution)/shard_map/gather_second/pallas_call | solution.py:299
  28.5 0.0 copy-start.9
  28.5 3.0 %forward.1 = (bf16[576,192]{1,0:T(8,128)(2,1)S(1)}, bf16[576,96]{1,0:T(8,128)(2,1)S(1)}, bf16[576,96]{1,0:T(8,128)(2,1)S(1)}, bf16[576,96]{1,0:T(8,128)(2,1)S(1)...) custom-call(bf16[144,192]{1,0:T(8,128)(2,1)S(1)} %copy-done.18, ...), custom_call_target="tpu_custom_call" | custom-call | flops 5000000000 | tf_op jit(solution)/shard_map/forward/pallas_call | solution.py:344
  31.5 0.0 collective-permute-done.1.g1
  31.6 5.3 %backward.1 = (bf16[576,192]{1,0:T(8,128)(2,1)S(1)}, f32[12,144,144]{2,1,0:T(8,128)S(1)}, bf16[3,576,96]{2,1,0:T(8,128)(2,1)S(1)}, bf16[576,192]{1,0:T(8,128)(2,1)S(1)}) custom-call(bf16[144,192]{1,0:T(8,128)(2,1)S(1)} %get-tuple-element.62.g0.m3, bf16[144,192]{1,0:T(8,128)(2,1)S(1)} %collective-permute-done.1.g1, ...), custom_call_target="tpu_custom_call" | custom-call | flops 7000000000 | tf_op jit(solution)/shard_map/backward/pallas_call | solution.py:400
  36.9 0.5 collective-permute-start.7
  37.4 5.3 %scatter.1 = (f32[192,256]{1,0:T(8,128)S(1)}, bf16[288,128]{1,0:T(8,128)(2,1)S(1)}, bf16[288,128]{1,0:T(8,128)(2,1)S(1)}) custom-call(f32[12,144,144]{2,1,0:T(8,128)S(1)} %get-tuple-element.77.score_ref, s32[168,128]{1,0:T(8,128)S(1)} %get-tuple-element.58.after_ref.lo_ref, s32[168,128]{1,0:T(8,128)S(1)} %get-tuple-element.64.hi_ref, ...), custom_call_target="tpu_custom_call" | custom-call | flops 5000000000 | tf_op jit(solution)/shard_map/scatter/pallas_call | solution.py:444
  42.7 2.6 %collective-permute-start.9 = (bf16[288,128]{1,0:T(8,128)(2,1)S(1)}, bf16[288,128]{1,0:T(8,128)(2,1)S(1)}, u32[]{:S(2)}, u32[]{:S(2)}) collective-permute-start(bf16[288,128]{1,0:T(8,128)(2,1)S(1)} %get-tuple-element.83), channel_id=1, source_target_pairs={{0,64},{64,0},{128,192},{192,128},{1,65},{65,1},{129,193},{193,129... | collective-permute-start | bytes 221192 | tf_op jit(solution)/shard_map/ppermute | solution.py:617
  45.2 0.0 collective-permute-done.8.first_other
  45.2 0.9 collective-permute-done.9.second_other
  46.1 0.0 collective-permute-done.7.other_ref
  46.1 0.4 meet.1
  46.6 16.5 %all_to_all.10.got_ref = bf16[32,40,128]{2,1,0:T(8,128)(2,1)S(1)} all-to-all(bf16[32,40,128]{2,1,0:T(8,128)(2,1)S(1)} %bitcast.22), channel_id=1, replica_groups=mesh['lat'=4,'lon'=32,'tp'=2] {'lon'}, dimensions={0} | all-to-all | bytes 655360 | tf_op jit(solution)/shard_map/all_to_all | solution.py:661
  63.1 0.1 add.1
  63.2 3.5 %collective-permute-start.10 = (bf16[288,192]{1,0:T(8,128)(2,1)S(1)}, bf16[288,192]{1,0:T(8,128)(2,1)S(1)}, u32[]{:S(2)}, u32[]{:S(2)}) collective-permute-start(bf16[288,192]{1,0:T(8,128)(2,1)S(1)} %get-tuple-element.86), channel_id=1, source_target_pairs={{192,0},{193,1},{194,2},{195,3},{196,4},{197,5},{198,6},{199,7},{2... | collective-permute-start | bytes 331784 | tf_op jit(solution)/shard_map/ppermute | solution.py:604
  66.7 1.8 %collective-permute-start.11 = (bf16[40,128]{1,0:T(8,128)(2,1)S(1)}, bf16[40,128]{1,0:T(8,128)(2,1)S(1)}, u32[]{:S(2)}, u32[]{:S(2)}) collective-permute-start(bf16[40,128]{1,0:T(8,128)(2,1)S(1)} %get-tuple-element.87.own_ref), channel_id=1, source_target_pairs={{128,0},{129,1},{130,2},{131,3},{132,4},{133,5},{134,6},{135,7},{1... | collective-permute-start | bytes 30728 | tf_op jit(solution)/shard_map/ppermute | solution.py:604
  68.5 2.9 %collective-permute-done.11.other_ref = bf16[40,128]{1,0:T(8,128)(2,1)S(1)} collective-permute-done((bf16[40,128]{1,0:T(8,128)(2,1)S(1)}, bf16[40,128]{1,0:T(8,128)(2,1)S(1)}, u32[]{:S(2)}, u32[]{:S(2)}) %collective-permute-start.11) | collective-permute-done | bytes 10272 | tf_op jit(solution)/shard_map/ppermute | solution.py:604
  71.4 0.0 collective-permute-done.10.band
  71.5 16.4 %all_to_all.11 = bf16[32,40,128]{2,1,0:T(8,128)(2,1)S(1)} all-to-all(bf16[32,40,128]{2,1,0:T(8,128)(2,1)S(1)} %get-tuple-element.90), channel_id=1, replica_groups=mesh['lat'=4,'lon'=32,'tp'=2] {'lon'}, dimensions={0} | all-to-all | bytes 655360 | tf_op jit(solution)/shard_map/all_to_all | solution.py:664
  87.9 2.4 %collective-permute-start.13 = (bf16[1280,128]{1,0:T(8,128)(2,1)S(1)}, bf16[1280,128]{1,0:T(8,128)(2,1)S(1)}, u32[]{:S(2)}, u32[]{:S(2)}) collective-permute-start(bf16[1280,128]{1,0:T(8,128)(2,1)S(1)} %bitcast.20), channel_id=1, source_target_pairs={{0,64},{64,0},{128,192},{192,128},{1,65},{65,1},{129,193},{193,129... | collective-permute-start | bytes 983048 | tf_op jit(solution)/shard_map/ppermute | solution.py:617
  90.3 0.0 collective-permute-start.12
  90.3 1.3 %collective-permute-done.13.other_ref = bf16[1280,128]{1,0:T(8,128)(2,1)S(1)} collective-permute-done((bf16[1280,128]{1,0:T(8,128)(2,1)S(1)}, bf16[1280,128]{1,0:T(8,128)(2,1)S(1)}, u32[]{:S(2)}, u32[]{:S(2)}) %collective-permute-start.13) | collective-permute-done | bytes 327712 | tf_op jit(solution)/shard_map/ppermute | solution.py:617
  91.6 1.1 %unpack.1 = (f32[3,192,96]{2,1,0:T(8,128)}, f32[96,192]{1,0:T(8,128)}, f32[192,384]{1,0:T(8,128)}, f32[192,384]{1,0:T(8,128)}, f32[1,96]{1,0:T(1,128)}, /*index=5*/f32[1,96]{1,0:T(1,128)}, f32[3,4,3312]{2,1,0:T(4,128)}) custom-call(bf16[1280,128]{1,0:T(8,128)(2,1)S(1)} %bitcast.21, bf16[1280,128]{1,0:T(8,128)(2,1)S(1)} %collective-permute-done.13.other_ref), custom_call_target="tpu_custom_call" | custom-call | tf_op jit(solution)/shard_map/unpack/pallas_call | solution.py:580
  92.7 6.4 %collective-permute-done.12.sector = bf16[288,192]{1,0:T(8,128)(2,1)S(1)} collective-permute-done((bf16[288,192]{1,0:T(8,128)(2,1)S(1)}, bf16[288,192]{1,0:T(8,128)(2,1)S(1)}, u32[]{:S(2)}, u32[]{:S(2)}) %collective-permute-start.12) | collective-permute-done | bytes 110624 | tf_op jit(solution)/shard_map/ppermute | solution.py:604
  99.1 0.0 copy-start.14
  99.1 0.6 copy-done.14
  99.8 1.2 %finish.1 = bf16[6,12,8,192]{3,2,1,0:T(8,128)(2,1)} custom-call(bf16[144,192]{1,0:T(8,128)(2,1)S(1)} %copy-done.6, bf16[144,192]{1,0:T(8,128)(2,1)S(1)} %copy-done.7, bf16[144,192]{1,0:T(8,128)(2,1)S(1)} %copy-done.8, bf16[144,192]{1,0:T(8,128)(2,1)S(1)} %copy-done.18, bf16[144,192]{1,0:T(8,128)(2,1)S(1)} %get-tuple-element.59.m0, ...), custom_call_target="tpu_custom_call" | custom-call | flops 1000000000 | tf_op jit(solution)/shard_map/finish/pallas_call | solution.py:496
  (32 shorter events, 0.1 us)
Async XLA Ops:
  0.6 18.4 %copy-start.3 = (f32[1,4,3,3312]{3,1,2,0:T(4,128)S(1)}, f32[1,4,3,3312]{3,1,2,0:T(4,128)}, u32[]{:S(2)}) copy-start(f32[1,4,3,3312]{3,1,2,0:T(4,128)} %param.22) | copy-start | bytes 476932
  0.6 18.4 %copy-start.4 = (s32[144,144]{1,0:T(8,128)S(1)}, s32[144,144]{1,0:T(8,128)}, u32[]{:S(2)}) copy-start(s32[144,144]{1,0:T(8,128)} %index_ref.1) | copy-start | bytes 248836
  0.7 18.4 %copy-start.10 = (s32[8,6,12]{2,0,1:T(8,128)S(1)}, s32[8,6,12]{2,0,1:T(8,128)}, u32[]{:S(2)}) copy-start(s32[8,6,12]{2,0,1:T(8,128)} %param.19) | copy-start | bytes 6916
  0.7 18.4 %copy-start.11 = (s32[8,6,12]{2,0,1:T(8,128)S(1)}, s32[8,6,12]{2,0,1:T(8,128)}, u32[]{:S(2)}) copy-start(s32[8,6,12]{2,0,1:T(8,128)} %param.20) | copy-start | bytes 6916
  0.7 18.4 %copy-start.16 = (bf16[144,144]{1,0:T(8,128)(2,1)S(1)}, bf16[144,144]{1,0:T(8,128)(2,1)}, u32[]{:S(2)}) copy-start(bf16[144,144]{1,0:T(8,128)(2,1)} %constant.4.clone.order_ref) | copy-start | bytes 124420
  4.3 17.8 %copy-start = (bf16[8,6,12,192]{3,0,2,1:T(8,128)(2,1)S(1)}, bf16[8,6,12,192]{3,0,2,1:T(8,128)(2,1)}, u32[]{:S(2)}) copy-start(bf16[8,6,12,192]{3,0,2,1:T(8,128)(2,1)} %param.17) | copy-start | bytes 663556
  4.3 17.8 %copy-start.1 = (bf16[8,6,12,192]{3,0,2,1:T(8,128)(2,1)S(1)}, bf16[8,6,12,192]{3,0,2,1:T(8,128)(2,1)}, u32[]{:S(2)}) copy-start(bf16[8,6,12,192]{3,0,2,1:T(8,128)(2,1)} %param.18) | copy-start | bytes 663556
  4.4 17.7 %copy-start.2 = (bf16[576,192]{1,0:T(8,128)(2,1)S(1)}, bf16[576,192]{1,0:T(8,128)(2,1)}, u32[]{:S(2)}) copy-start(bf16[576,192]{1,0:T(8,128)(2,1)} %get-tuple-element.57.own_ref) | copy-start | bytes 663556
  4.4 17.7 %copy-start.12 = (f32[192]{0:T(256)S(1)}, f32[192]{0:T(256)}, u32[]{:S(2)}) copy-start(f32[192]{0:T(256)} %param.26) | copy-start | bytes 2308
  4.4 17.7 %collective-permute-start = (bf16[576,192]{1,0:T(8,128)(2,1)}, bf16[576,192]{1,0:T(8,128)(2,1)S(1)}, u32[]{:S(2)}, u32[]{:S(2)}) collective-permute-start(bf16[576,192]{1,0:T(8,128)(2,1)} %get-tuple-element.57.own_ref), channel_id=1, source_target_pairs={{1,0},{0,1},{3,2},{2,3},{5,4},{4,5},{7,6},{6,7},{9,8},{8,9},{11,10... | collective-permute-start | bytes 663560 | tf_op jit(solution)/shard_map/ppermute | solution.py:604
  6.6 16.7 %collective-permute-start.6 = (bf16[144,192]{1,0:T(8,128)(2,1)}, bf16[144,192]{1,0:T(8,128)(2,1)S(1)}, u32[]{:S(2)}, u32[]{:S(2)}) collective-permute-start(bf16[144,192]{1,0:T(8,128)(2,1)} %get-tuple-element.53.x0), channel_id=1, source_target_pairs={{66,0},{67,1},{68,2},{69,3},{70,4},{71,5},{72,6},{73,7},{74,8},{75... | collective-permute-start | bytes 165896 | tf_op jit(solution)/shard_map/ppermute | solution.py:604
  15.2 9.7 %collective-permute-start.5 = (bf16[144,192]{1,0:T(8,128)(2,1)}, bf16[144,192]{1,0:T(8,128)(2,1)S(1)}, u32[]{:S(2)}, u32[]{:S(2)}) collective-permute-start(bf16[144,192]{1,0:T(8,128)(2,1)} %get-tuple-element.54.x1), channel_id=1, source_target_pairs={{64,0},{65,1},{66,2},{67,3},{68,4},{69,5},{70,6},{71,7},{72,8},{73... | collective-permute-start | bytes 165896 | tf_op jit(solution)/shard_map/ppermute | solution.py:604
  17.1 9.2 %collective-permute-start.4 = (bf16[144,192]{1,0:T(8,128)(2,1)}, bf16[144,192]{1,0:T(8,128)(2,1)S(1)}, u32[]{:S(2)}, u32[]{:S(2)}) collective-permute-start(bf16[144,192]{1,0:T(8,128)(2,1)} %get-tuple-element.55.x2), channel_id=1, source_target_pairs={{2,0},{3,1},{4,2},{5,3},{6,4},{7,5},{8,6},{9,7},{10,8},{11,9},{12,... | collective-permute-start | bytes 165896 | tf_op jit(solution)/shard_map/ppermute | solution.py:604
  17.6 27.6 %collective-permute-start.8 = (bf16[576,128]{1,0:T(8,128)(2,1)}, bf16[576,128]{1,0:T(8,128)(2,1)S(1)}, u32[]{:S(2)}, u32[]{:S(2)}) collective-permute-start(bf16[576,128]{1,0:T(8,128)(2,1)} %get-tuple-element.76), channel_id=1, source_target_pairs={{0,64},{64,0},{128,192},{192,128},{1,65},{65,1},{129,193},{193,129... | collective-permute-start | bytes 442376 | tf_op jit(solution)/shard_map/ppermute | solution.py:617
  22.7 8.8 %collective-permute-start.3 = (bf16[144,192]{1,0:T(8,128)(2,1)S(1)}, bf16[144,192]{1,0:T(8,128)(2,1)S(1)}, u32[]{:S(2)}, u32[]{:S(2)}) collective-permute-start(bf16[144,192]{1,0:T(8,128)(2,1)S(1)} %get-tuple-element.59.m0), channel_id=1, source_target_pairs={{66,0},{67,1},{68,2},{69,3},{70,4},{71,5},{72,6},{73,7},{74,8},{75... | collective-permute-start | bytes 165896 | tf_op jit(solution)/shard_map/ppermute | solution.py:604
  23.3 8.3 %collective-permute-start.2 = (bf16[144,192]{1,0:T(8,128)(2,1)S(1)}, bf16[144,192]{1,0:T(8,128)(2,1)S(1)}, u32[]{:S(2)}, u32[]{:S(2)}) collective-permute-start(bf16[144,192]{1,0:T(8,128)(2,1)S(1)} %get-tuple-element.60.m1), channel_id=1, source_target_pairs={{64,0},{65,1},{66,2},{67,3},{68,4},{69,5},{70,6},{71,7},{72,8},{73... | collective-permute-start | bytes 165896 | tf_op jit(solution)/shard_map/ppermute | solution.py:604
  24.9 6.7 %collective-permute-start.1 = (bf16[144,192]{1,0:T(8,128)(2,1)S(1)}, bf16[144,192]{1,0:T(8,128)(2,1)S(1)}, u32[]{:S(2)}, u32[]{:S(2)}) collective-permute-start(bf16[144,192]{1,0:T(8,128)(2,1)S(1)} %get-tuple-element.61.m2), channel_id=1, source_target_pairs={{2,0},{3,1},{4,2},{5,3},{6,4},{7,5},{8,6},{9,7},{10,8},{11,9},{12,... | collective-permute-start | bytes 165896 | tf_op jit(solution)/shard_map/ppermute | solution.py:604
  26.3 2.2 %copy-start.5 = (bf16[3,192,96]{2,1,0:T(8,128)(2,1)S(1)}, bf16[3,192,96]{2,1,0:T(8,128)(2,1)}, u32[]{:S(2)}) copy-start(bf16[3,192,96]{2,1,0:T(8,128)(2,1)} %qkv_ref.3) | copy-start | bytes 331780
  26.3 2.2 %copy-start.13 = (f32[192]{0:T(256)S(1)}, f32[192]{0:T(256)}, u32[]{:S(2)}) copy-start(f32[192]{0:T(256)} %param.23) | copy-start | bytes 2308
  26.3 2.3 %copy-start.15 = (bf16[144,144]{1,0:T(8,128)(2,1)S(1)}, bf16[144,144]{1,0:T(8,128)(2,1)}, u32[]{:S(2)}) copy-start(bf16[144,144]{1,0:T(8,128)(2,1)} %constant.5.clone.order_ref) | copy-start | bytes 124420
  26.3 2.3 %copy-start.18 = (bf16[144,192]{1,0:T(8,128)(2,1)S(1)}, bf16[144,192]{1,0:T(8,128)(2,1)}, u32[]{:S(2)}) copy-start(bf16[144,192]{1,0:T(8,128)(2,1)} %get-tuple-element.56.x0.x3) | copy-start | bytes 165892
  28.5 3.0 %copy-start.9 = (bf16[96,192]{1,0:T(8,128)(2,1)S(1)}, bf16[96,192]{1,0:T(8,128)(2,1)}, u32[]{:S(2)}) copy-start(bf16[96,192]{1,0:T(8,128)(2,1)} %proj_ref.1) | copy-start | bytes 110596
  36.9 9.2 %collective-permute-start.7 = (bf16[576,192]{1,0:T(8,128)(2,1)S(1)}, bf16[576,192]{1,0:T(8,128)(2,1)S(1)}, u32[]{:S(2)}, u32[]{:S(2)}) collective-permute-start(bf16[576,192]{1,0:T(8,128)(2,1)S(1)} %get-tuple-element.74.own_ref), channel_id=1, source_target_pairs={{1,0},{0,1},{3,2},{2,3},{5,4},{4,5},{7,6},{6,7},{9,8},{8,9},{11,10... | collective-permute-start | bytes 663560 | tf_op jit(solution)/shard_map/ppermute | solution.py:604
  37.4 8.8 %copy-start.17 = (bf16[576,128]{1,0:T(8,128)(2,1)S(1)}, bf16[576,128]{1,0:T(8,128)(2,1)}, u32[]{:S(2)}) copy-start(bf16[576,128]{1,0:T(8,128)(2,1)} %get-tuple-element.75.first_ref) | copy-start | bytes 442372
  42.7 3.5 %collective-permute-start.9 = (bf16[288,128]{1,0:T(8,128)(2,1)S(1)}, bf16[288,128]{1,0:T(8,128)(2,1)S(1)}, u32[]{:S(2)}, u32[]{:S(2)}) collective-permute-start(bf16[288,128]{1,0:T(8,128)(2,1)S(1)} %get-tuple-element.83), channel_id=1, source_target_pairs={{0,64},{64,0},{128,192},{192,128},{1,65},{65,1},{129,193},{193,129... | collective-permute-start | bytes 221192 | tf_op jit(solution)/shard_map/ppermute | solution.py:617
  63.2 8.2 %collective-permute-start.10 = (bf16[288,192]{1,0:T(8,128)(2,1)S(1)}, bf16[288,192]{1,0:T(8,128)(2,1)S(1)}, u32[]{:S(2)}, u32[]{:S(2)}) collective-permute-start(bf16[288,192]{1,0:T(8,128)(2,1)S(1)} %get-tuple-element.86), channel_id=1, source_target_pairs={{192,0},{193,1},{194,2},{195,3},{196,4},{197,5},{198,6},{199,7},{2... | collective-permute-start | bytes 331784 | tf_op jit(solution)/shard_map/ppermute | solution.py:604
  66.7 4.7 %collective-permute-start.11 = (bf16[40,128]{1,0:T(8,128)(2,1)S(1)}, bf16[40,128]{1,0:T(8,128)(2,1)S(1)}, u32[]{:S(2)}, u32[]{:S(2)}) collective-permute-start(bf16[40,128]{1,0:T(8,128)(2,1)S(1)} %get-tuple-element.87.own_ref), channel_id=1, source_target_pairs={{128,0},{129,1},{130,2},{131,3},{132,4},{133,5},{134,6},{135,7},{1... | collective-permute-start | bytes 30728 | tf_op jit(solution)/shard_map/ppermute | solution.py:604
  71.4 27.7 %copy-start.6 = (bf16[144,192]{1,0:T(8,128)(2,1)S(1)}, bf16[144,192]{1,0:T(8,128)(2,1)}, u32[]{:S(2)}) copy-start(bf16[144,192]{1,0:T(8,128)(2,1)} %get-tuple-element.53.x0) | copy-start | bytes 165892
  71.4 27.7 %copy-start.7 = (bf16[144,192]{1,0:T(8,128)(2,1)S(1)}, bf16[144,192]{1,0:T(8,128)(2,1)}, u32[]{:S(2)}) copy-start(bf16[144,192]{1,0:T(8,128)(2,1)} %get-tuple-element.54.x1) | copy-start | bytes 165892
  71.4 27.7 %copy-start.8 = (bf16[144,192]{1,0:T(8,128)(2,1)S(1)}, bf16[144,192]{1,0:T(8,128)(2,1)}, u32[]{:S(2)}) copy-start(bf16[144,192]{1,0:T(8,128)(2,1)} %get-tuple-element.55.x2) | copy-start | bytes 165892
  87.9 3.7 %collective-permute-start.13 = (bf16[1280,128]{1,0:T(8,128)(2,1)S(1)}, bf16[1280,128]{1,0:T(8,128)(2,1)S(1)}, u32[]{:S(2)}, u32[]{:S(2)}) collective-permute-start(bf16[1280,128]{1,0:T(8,128)(2,1)S(1)} %bitcast.20), channel_id=1, source_target_pairs={{0,64},{64,0},{128,192},{192,128},{1,65},{65,1},{129,193},{193,129... | collective-permute-start | bytes 983048 | tf_op jit(solution)/shard_map/ppermute | solution.py:617
  90.3 8.8 %collective-permute-start.12 = (bf16[288,192]{1,0:T(8,128)(2,1)S(1)}, bf16[288,192]{1,0:T(8,128)(2,1)S(1)}, u32[]{:S(2)}, u32[]{:S(2)}) collective-permute-start(bf16[288,192]{1,0:T(8,128)(2,1)S(1)} %get-tuple-element.89), channel_id=1, source_target_pairs={{62,0},{63,1},{0,2},{1,3},{2,4},{3,5},{4,6},{5,7},{6,8},{7,9},{8,1... | collective-permute-start | bytes 331784 | tf_op jit(solution)/shard_map/ppermute | solution.py:604
  99.1 0.7 copy-start.14

commit v8 on v7

--- a/solution.py
+++ b/solution.py
@@ -452,13 +452,14 @@
 
 
 def meet_kernel(own_ref, other_ref, x0, x1, x2, x3, first_ref, first_other, second_ref, second_other,
-                table_ref, two_ref, out_ref):
+                table_ref, two_ref, out_ref, g0, g1, g2, g3):
     gain = jnp.zeros((1, 192), F32)
     for s, x in enumerate((x0, x1, x2, x3)):
         rows = slice(s * 144, s * 144 + 144)
         grad = own_ref[rows, :].astype(F32) + other_ref[rows, :].astype(F32)
         normed, _ = layer_stats(x[...].astype(F32))
         gain = gain + jnp.sum(grad * normed, axis=0, keepdims=True)
+        (g0, g1, g2, g3)[s][...] = grad.astype(BF)
     out_ref[0:576, :] = both(first_ref[...], first_other[...])
     out_ref[576:864, :] = both(second_ref[...], second_other[...])
     rows = []
@@ -475,72 +476,68 @@
 def meet(own, other, x, first, first_other, second, second_other, table, two):
     return pl.pallas_call(
         meet_kernel,
-        out_shape=shape((1280, 128), BF),
+        out_shape=(
+            shape((1280, 128), BF),
+            shape((144, 192), BF),
+            shape((144, 192), BF),
+            shape((144, 192), BF),
+            shape((144, 192), BF),
+        ),
         compiler_params=VM,
         cost_estimate=cost(1),
         name="meet",
     )(own, other, *x, first, first_other, second, second_other, table, two)
 
 
-def finish_kernel(x0, x1, x2, x3, m0, m1, m2, m3, g_own, band, sector, gain_ref, after_ref, out_ref):
-    gs = (sector[144:288, :], band[0:144, :], sector[0:144, :], g_own[...])
-    for q, (x, m, g) in enumerate(zip((x0, x1, x2, x3), (m0, m1, m2, m3), gs)):
+def finish_kernel(x0, x1, x2, x3, m0, m1, m2, m3, g0, g1, g2, g3, gain_ref, out_ref):
+    for q, (x, m, g) in enumerate(zip((x0, x1, x2, x3), (m0, m1, m2, m3), (g0, g1, g2, g3))):
         normed, inverse = layer_stats(x[...].astype(F32))
-        rows = m[...].astype(F32) + norm_backward(g.astype(F32), gain_ref[...], normed, inverse)
+        rows = m[...].astype(F32) + norm_backward(g[...].astype(F32), gain_ref[...], normed, inverse)
         for lat in range(3):
             piece = rows[lat * 48 : lat * 48 + 48].reshape(6, 8, 192)
             out_ref[(q // 2) * 3 + lat, (q % 2) * 6 : (q % 2) * 6 + 6] = piece.astype(BF)
 
 
-def finish(x, m, g, gain, after):
+def finish(x, m, g, gain):
     return pl.pallas_call(
         finish_kernel,
         out_shape=shape((6, 12, 8, 192), BF),
-        in_specs=[VMEM] * 12 + [ANY],
         compiler_params=VM,
         cost_estimate=cost(1),
         name="finish",
-    )(*x, *m, *g, gain, after)
-
-
-def add_kernel(got_ref, own_ref, other_ref, out_ref, g0, g1, g23):
+    )(*x, *m, *g, gain)
+
+
+def add_kernel(got_ref, b0, b1, b2, out_ref):
     total = got_ref[0].astype(F32)
     for i in range(1, 32):
         total = total + got_ref[i].astype(F32)
     out_ref[...] = total.astype(BF)
-    g0[...] = both(own_ref[0:144, :], other_ref[0:144, :])
-    g1[...] = both(own_ref[144:288, :], other_ref[144:288, :])
-    g23[...] = both(own_ref[288:576, :], other_ref[288:576, :])
-
-
-def add(got, own, other):
+
+
+def add(got, after):
     return pl.pallas_call(
         add_kernel,
-        out_shape=(shape((40, 128), BF), shape((144, 192), BF), shape((144, 192), BF), shape((288, 192), BF)),
+        out_shape=shape((40, 128), BF),
+        in_specs=[VMEM] + [ANY] * 3,
         compiler_params=VM,
         cost_estimate=cost(1),
         name="add",
-    )(got, own, other)
-
-
-def spread_kernel(own_ref, other_ref, g1, band, out_ref, next_ref):
+    )(got, *after)
+
+
+def spread_kernel(own_ref, other_ref, out_ref):
     own = own_ref[...].astype(F32)
     row = lax.axis_index("lon") * 40 + lax.broadcasted_iota(I32, (40, 128), 0)
     table = (row >= 864) & (row < 1176)
     total = own + jnp.where(table, 0.0, other_ref[...].astype(F32))
     out_ref[...] = jnp.broadcast_to(total.astype(BF)[None], (32, 40, 128))
-    next_ref[0:144, :] = g1[...]
-    next_ref[144:288, :] = band[144:288, :]
-
-
-def spread(own, other, g1, band):
-    return pl.pallas_call(
-        spread_kernel,
-        out_shape=(shape((32, 40, 128), BF), shape((288, 192), BF)),
-        compiler_params=VM,
-        cost_estimate=cost(1),
-        name="spread",
-    )(own, other, g1, band)
+
+
+def spread(own, other):
+    return pl.pallas_call(
+        spread_kernel, out_shape=shape((32, 40, 128), BF), compiler_params=VM, cost_estimate=cost(1), name="spread"
+    )(own, other)
 
 
 def unpack_kernel(weight_scale, table_scale, own_ref, other_ref,
@@ -655,18 +652,17 @@
     part1, score, gcols, grad = backward(gw, proj_weight, qkv_weight, q, k, v, prob)
     other1 = moved(part1, 0, 0, 1)
     table, second, second_send = scatter(score, lo, hi, low, gcols, att, grad)
-    sums = meet(
+    sums, *g = meet(
         part1, other1, xw, first, other_core(first_send), second, other_core(second_send), table, gain_two
     )
-    own, g0, g1, g23 = add(lax.all_to_all(sums.reshape(32, 40, 128), "lon", 0, 0), part1, other1)
-    g_band = moved(g23, -1, 0, 0)
-    totals, g_next = spread(own, moved(own, 2, 0, 0), g1, g_band)
+    back = (moved(g[3], -1, -1, 0), moved(g[2], -1, 0, 0), moved(g[1], 0, -1, 0), g[0])
+    own = add(lax.all_to_all(sums.reshape(32, 40, 128), "lon", 0, 0), back[:3])
+    totals = spread(own, moved(own, 2, 0, 0))
+    result = finish(x, gm, back, gain1)
     got = lax.all_to_all(totals, "lon", 0, 0).reshape(1280, 128)
-    g_sector = moved(g_next, 0, -1, 0)
     qkv_out, proj_out, up_out, down_out, one, two, table_out = unpack(
         weight_scale, table_scale, got, other_core(got)
     )
-    result = finish(x, gm, (g0, g_band, g_sector), gain1, one)
     return (
         result.transpose(2, 0, 1, 3),
         qkv_out,

time: 101 us -> 93.5 us (0.926)
  blocking collectives: 32.9 us -> 15.4 us
  starting transfers between devices: 28.9 us -> 36.3 us
  waiting for transfers between devices: 11.5 us -> 13.8 us
    all_to_all x1 -> x0, blocking collectives: 16.5 us -> none  [local(): lax.all_to_all(sums.reshape(32, 40, 128), 'lon', 0, 0)]
    all_to_all x0 -> x1, starting transfers between devices: none -> 3.91 us  [local(): own = add(lax.all_to_all(sums.reshape(32, 40, 128), 'lon', 0, 0), back[:3])]
    ppermute x11 -> x12, waiting for transfers between devices: 9.36 us -> 12.9 us  [moved(): return lax.ppermute(value, ('lat', 'lon', 'tp'), pairs)]
    ppermute x3, starting transfers between devices: 6.39 us -> 8.68 us  [other_core(): lax.ppermute(value, 'lat', [(a, a ^ 1) for a in range(lax.axis_size('lat'...]
    ppermute x3, waiting for transfers between devices: 2.16 us -> 0.92 us  [other_core(): lax.ppermute(value, 'lat', [(a, a ^ 1) for a in range(lax.axis_size('lat'...]
    ppermute x11 -> x12, starting transfers between devices: 22.6 us -> 23.7 us  [moved(): return lax.ppermute(value, ('lat', 'lon', 'tp'), pairs)]
  transfers between devices with their start and end apart: 14 -> 16, of which waited for: 4 -> 3; matrix products, arithmetic and copies ran while one was open for 0% -> 0% of each run, Pallas kernels for 20% -> 22%
where the time goes in v8:
time: 93.5 us; the launch traced here: 93.3 us
  starting transfers between devices  36.3 us (39%)
  Pallas kernels  26.7 us (29%)
  blocking collectives  15.4 us (16%)
  waiting for transfers between devices  13.8 us (15%)
  between operations  0.94 us (1%)
    ppermute x12, starting transfers between devices, moved(): return lax.ppermute(value, ('lat', 'lon', 'tp'), pairs)  23.7 us
    all_to_all x1, blocking collectives, local(): got = lax.all_to_all(totals, 'lon', 0, 0).reshape(1280, 128)  15.4 us
    ppermute x12, waiting for transfers between devices, moved(): return lax.ppermute(value, ('lat', 'lon', 'tp'), pairs)  12.9 us
    ppermute x3, starting transfers between devices, other_core(): lax.ppermute(value, 'lat', [(a, a ^ 1) for a in range(lax.axis_size('lat'...  8.68 us
    pallas_call x1, Pallas kernels, backward(): pl.pallas_call(backward_kernel, out_shape=(shape((576, 192), BF), shape((...  5.32 us
    pallas_call x1, Pallas kernels, scatter(): pl.pallas_call(scatter_kernel, out_shape=(shape((192, 256), F32), shape((...  5.29 us
    all_to_all x1, starting transfers between devices, local(): own = add(lax.all_to_all(sums.reshape(32, 40, 128), 'lon', 0, 0), back[:3])  3.91 us
    pallas_call x1, Pallas kernels, head(): pl.pallas_call(head_kernel, out_shape=tuple((shape((144, 192), BF) for _...  3.63 us
  transfers between devices with their start and end apart: 16, of which 3 were waited for; matrix products, arithmetic and copies ran while one was open for 0% of the time, Pallas kernels for 22%

profile of v8, /device:TPU:1, one launch (start us, length us, event | category | flops | bytes accessed | tf_op | source)
XLA Modules:
  0.0 93.3 jit_solution(15610232328834380544)
XLA Ops:
  0.7 0.0 copy-start.15
  0.7 3.6 %head.1 = (bf16[144,192]{1,0:T(8,128)(2,1)}, bf16[144,192]{1,0:T(8,128)(2,1)}, bf16[144,192]{1,0:T(8,128)(2,1)}, bf16[144,192]{1,0:T(8,128)(2,1)}, bf16[576,192]...) custom-call(bf16[6,12,8,192]{3,2,1,0:T(8,128)(2,1)} %bitcast.33, ...), custom_call_target="tpu_custom_call" | custom-call | flops 3000000000 | tf_op jit(solution)/shard_map/head/pallas_call | solution.py:139
  4.3 0.0 copy-start
  4.3 0.0 copy-start.1
  4.4 0.0 copy-start.2
  4.4 0.0 copy-start.12
  4.4 2.2 %collective-permute-start = (bf16[576,192]{1,0:T(8,128)(2,1)}, bf16[576,192]{1,0:T(8,128)(2,1)S(1)}, u32[]{:S(2)}, u32[]{:S(2)}) collective-permute-start(bf16[576,192]{1,0:T(8,128)(2,1)} %get-tuple-element.56.own_ref), channel_id=1, source_target_pairs={{1,0},{0,1},{3,2},{2,3},{5,4},{4,5},{7,6},{6,7},{9,8},{8,9},{11,10... | collective-permute-start | bytes 663560 | tf_op jit(solution)/shard_map/ppermute | solution.py:601
  6.6 8.6 %collective-permute-start.6 = (bf16[144,192]{1,0:T(8,128)(2,1)}, bf16[144,192]{1,0:T(8,128)(2,1)S(1)}, u32[]{:S(2)}, u32[]{:S(2)}) collective-permute-start(bf16[144,192]{1,0:T(8,128)(2,1)} %get-tuple-element.52.x0), channel_id=1, source_target_pairs={{66,0},{67,1},{68,2},{69,3},{70,4},{71,5},{72,6},{73,7},{74,8},{75... | collective-permute-start | bytes 165896 | tf_op jit(solution)/shard_map/ppermute | solution.py:601
  15.2 1.9 %collective-permute-start.5 = (bf16[144,192]{1,0:T(8,128)(2,1)}, bf16[144,192]{1,0:T(8,128)(2,1)S(1)}, u32[]{:S(2)}, u32[]{:S(2)}) collective-permute-start(bf16[144,192]{1,0:T(8,128)(2,1)} %get-tuple-element.53.x1), channel_id=1, source_target_pairs={{64,0},{65,1},{66,2},{67,3},{68,4},{69,5},{70,6},{71,7},{72,8},{73... | collective-permute-start | bytes 165896 | tf_op jit(solution)/shard_map/ppermute | solution.py:601
  17.1 0.6 collective-permute-start.4
  17.6 1.4 %collective-permute-start.8 = (bf16[576,128]{1,0:T(8,128)(2,1)}, bf16[576,128]{1,0:T(8,128)(2,1)S(1)}, u32[]{:S(2)}, u32[]{:S(2)}) collective-permute-start(bf16[576,128]{1,0:T(8,128)(2,1)} %get-tuple-element.75), channel_id=1, source_target_pairs={{0,64},{64,0},{128,192},{192,128},{1,65},{65,1},{129,193},{193,129... | collective-permute-start | bytes 442376 | tf_op jit(solution)/shard_map/ppermute | solution.py:614
  19.1 3.0 %gather_first.1 = (f32[1440,128]{1,0:T(8,128)S(1)}, s32[168,128]{1,0:T(8,128)S(1)}, s32[168,128]{1,0:T(8,128)S(1)}, bf16[160,512]{1,0:T(8,128)(2,1)S(1)}, f32[4,144]{1,0:T(4,128)S(1)}) custom-call(s32[144,144]{1,0:T(8,128)S(1)} %copy-done.4, bf16[144,144]{1,0:T(8,128)(2,1)S(1)} %copy-done.15, f32[3,4,3312]{2,1,0:T(4,128)S(1)} %bitcast.26, ...), custom_call_target="tpu_custom_call" | custom-call | flops 500000000 | tf_op jit(solution)/shard_map/gather_first/pallas_call | solution.py:272
  22.1 0.0 collective-permute-done.other_ref
  22.1 0.6 middle.1
  22.7 0.6 collective-permute-start.3
  23.3 0.0 collective-permute-done.6.a3.x3
  23.3 1.6 %collective-permute-start.2 = (bf16[144,192]{1,0:T(8,128)(2,1)S(1)}, bf16[144,192]{1,0:T(8,128)(2,1)S(1)}, u32[]{:S(2)}, u32[]{:S(2)}) collective-permute-start(bf16[144,192]{1,0:T(8,128)(2,1)S(1)} %get-tuple-element.59.m1), channel_id=1, source_target_pairs={{64,0},{65,1},{66,2},{67,3},{68,4},{69,5},{70,6},{71,7},{72,8},{73... | collective-permute-start | bytes 165896 | tf_op jit(solution)/shard_map/ppermute | solution.py:601
  24.9 0.0 collective-permute-done.5.a2.x2
  24.9 1.4 %collective-permute-start.1 = (bf16[144,192]{1,0:T(8,128)(2,1)S(1)}, bf16[144,192]{1,0:T(8,128)(2,1)S(1)}, u32[]{:S(2)}, u32[]{:S(2)}) collective-permute-start(bf16[144,192]{1,0:T(8,128)(2,1)S(1)} %get-tuple-element.60.m2), channel_id=1, source_target_pairs={{2,0},{3,1},{4,2},{5,3},{6,4},{7,5},{8,6},{9,7},{10,8},{11,9},{12,... | collective-permute-start | bytes 165896 | tf_op jit(solution)/shard_map/ppermute | solution.py:601
  26.3 0.0 collective-permute-done.4.a1.x1
  26.3 2.2 %gather_second.1 = (f32[12,144,128]{2,1,0:T(8,128)S(1)}, f32[12,144,128]{2,1,0:T(8,128)S(1)}) custom-call(f32[1440,128]{1,0:T(8,128)S(1)} %get-tuple-element.62.first_stage, s32[168,128]{1,0:T(8,128)S(1)} %get-tuple-element.57.after_ref.lo_ref, s32[168,128]{1,0:T(8,128)S(1)} %get-tuple-element.63.hi_ref, bf16[160,512]{1,0:T(8,128)(2,1)S(1)} %get-tuple-element.64.terms_ref, ...), custom_call_target="tpu_custom_call" | custom-call | flops 4000000000 | tf_op jit(solution)/shard_map/gather_second/pallas_call | solution.py:299
  28.5 0.0 copy-start.9
  28.5 3.0 %forward.1 = (bf16[576,192]{1,0:T(8,128)(2,1)S(1)}, bf16[576,96]{1,0:T(8,128)(2,1)S(1)}, bf16[576,96]{1,0:T(8,128)(2,1)S(1)}, bf16[576,96]{1,0:T(8,128)(2,1)S(1)...) custom-call(bf16[144,192]{1,0:T(8,128)(2,1)S(1)} %copy-done.17, ...), custom_call_target="tpu_custom_call" | custom-call | flops 5000000000 | tf_op jit(solution)/shard_map/forward/pallas_call | solution.py:344
  31.5 0.0 collective-permute-done.2.g2
  31.6 0.0 collective-permute-done.1.g1
  31.6 5.3 %backward.1 = (bf16[576,192]{1,0:T(8,128)(2,1)S(1)}, f32[12,144,144]{2,1,0:T(8,128)S(1)}, bf16[3,576,96]{2,1,0:T(8,128)(2,1)S(1)}, bf16[576,192]{1,0:T(8,128)(2,1)S(1)}) custom-call(bf16[144,192]{1,0:T(8,128)(2,1)S(1)} %get-tuple-element.61.g0.m3, bf16[144,192]{1,0:T(8,128)(2,1)S(1)} %collective-permute-done.1.g1, ...), custom_call_target="tpu_custom_call" | custom-call | flops 7000000000 | tf_op jit(solution)/shard_map/backward/pallas_call | solution.py:400
  36.9 0.5 collective-permute-start.7
  37.4 5.3 %scatter.1 = (f32[192,256]{1,0:T(8,128)S(1)}, bf16[288,128]{1,0:T(8,128)(2,1)S(1)}, bf16[288,128]{1,0:T(8,128)(2,1)S(1)}) custom-call(f32[12,144,144]{2,1,0:T(8,128)S(1)} %get-tuple-element.76.score_ref, s32[168,128]{1,0:T(8,128)S(1)} %get-tuple-element.57.after_ref.lo_ref, s32[168,128]{1,0:T(8,128)S(1)} %get-tuple-element.63.hi_ref, ...), custom_call_target="tpu_custom_call" | custom-call | flops 5000000000 | tf_op jit(solution)/shard_map/scatter/pallas_call | solution.py:444
  42.6 2.6 %collective-permute-start.9 = (bf16[288,128]{1,0:T(8,128)(2,1)S(1)}, bf16[288,128]{1,0:T(8,128)(2,1)S(1)}, u32[]{:S(2)}, u32[]{:S(2)}) collective-permute-start(bf16[288,128]{1,0:T(8,128)(2,1)S(1)} %get-tuple-element.82), channel_id=1, source_target_pairs={{0,64},{64,0},{128,192},{192,128},{1,65},{65,1},{129,193},{193,129... | collective-permute-start | bytes 221192 | tf_op jit(solution)/shard_map/ppermute | solution.py:614
  45.2 0.9 collective-permute-done.9.second_other
  46.1 1.2 %meet.1 = (bf16[1280,128]{1,0:T(8,128)(2,1)}, bf16[144,192]{1,0:T(8,128)(2,1)S(1)}, bf16[144,192]{1,0:T(8,128)(2,1)S(1)}, bf16[144,192]{1,0:T(8,128)(2,1)S(1)}, bf16[144,192]{1,0:T(8,128)(2,1)S(1)}) custom-call(bf16[576,192]{1,0:T(8,128)(2,1)S(1)} %get-tuple-element.73.own_ref, bf16[576,192]{1,0:T(8,128)(2,1)S(1)} %collective-permute-done.7.other_ref, ...), custom_call_target="tpu_custom_call" | custom-call | flops 1000000000 | tf_op jit(solution)/shard_map/meet/pallas_call | solution.py:477
  47.3 3.9 %all-to-all-start = ((bf16[32,40,128]{2,1,0:T(8,128)(2,1)}), bf16[32,40,128]{2,1,0:T(8,128)(2,1)S(1)}, u32[]{:S(2)}, u32[]{:S(2)}) async-start(bf16[32,40,128]{2,1,0:T(8,128)(2,1)} %bitcast.11), calls=%async_computation | async-start | bytes 655360 | tf_op jit(solution)/shard_map/all_to_all | solution.py:659
  51.2 3.7 %collective-permute-start.10 = (bf16[144,192]{1,0:T(8,128)(2,1)S(1)}, bf16[144,192]{1,0:T(8,128)(2,1)S(1)}, u32[]{:S(2)}, u32[]{:S(2)}) collective-permute-start(bf16[144,192]{1,0:T(8,128)(2,1)S(1)} %get-tuple-element.84), channel_id=1, source_target_pairs={{254,0},{255,1},{192,2},{193,3},{194,4},{195,5},{196,6},{197,7},{1... | collective-permute-start | bytes 165896 | tf_op jit(solution)/shard_map/ppermute | solution.py:601
  55.0 0.0 collective-permute-start.11
  55.0 1.2 %collective-permute-start.12 = (bf16[144,192]{1,0:T(8,128)(2,1)S(1)}, bf16[144,192]{1,0:T(8,128)(2,1)S(1)}, u32[]{:S(2)}, u32[]{:S(2)}) collective-permute-start(bf16[144,192]{1,0:T(8,128)(2,1)S(1)} %get-tuple-element.86), channel_id=1, source_target_pairs={{62,0},{63,1},{0,2},{1,3},{2,4},{3,5},{4,6},{5,7},{6,8},{7,9},{8,1... | collective-permute-start | bytes 165896 | tf_op jit(solution)/shard_map/ppermute | solution.py:601
  56.2 10.3 %collective-permute-done.10.g0.b0 = bf16[144,192]{1,0:T(8,128)(2,1)S(1)} collective-permute-done((bf16[144,192]{1,0:T(8,128)(2,1)S(1)}, bf16[144,192]{1,0:T(8,128)(2,1)S(1)}, u32[]{:S(2)}, u32[]{:S(2)}) %collective-permute-start.10) | collective-permute-done | bytes 55328 | tf_op jit(solution)/shard_map/ppermute | solution.py:601
  66.5 0.0 all-to-all-done.got_ref
  66.5 0.1 add.1.own_ref
  66.6 0.0 copy-start.6
  66.6 0.0 copy-start.7
  66.6 0.0 copy-start.8
  66.6 1.6 %collective-permute-start.13 = (bf16[40,128]{1,0:T(8,128)(2,1)S(1)}, bf16[40,128]{1,0:T(8,128)(2,1)S(1)}, u32[]{:S(2)}, u32[]{:S(2)}) collective-permute-start(bf16[40,128]{1,0:T(8,128)(2,1)S(1)} %add.1.own_ref), channel_id=1, source_target_pairs={{128,0},{129,1},{130,2},{131,3},{132,4},{133,5},{134,6},{135,7},{1... | collective-permute-start | bytes 30728 | tf_op jit(solution)/shard_map/ppermute | solution.py:601
  68.2 2.5 %collective-permute-done.13.other_ref = bf16[40,128]{1,0:T(8,128)(2,1)S(1)} collective-permute-done((bf16[40,128]{1,0:T(8,128)(2,1)S(1)}, bf16[40,128]{1,0:T(8,128)(2,1)S(1)}, u32[]{:S(2)}, u32[]{:S(2)}) %collective-permute-start.13) | collective-permute-done | bytes 10272 | tf_op jit(solution)/shard_map/ppermute | solution.py:601
  70.8 15.4 %all_to_all.10 = bf16[32,40,128]{2,1,0:T(8,128)(2,1)S(1)} all-to-all(bf16[32,40,128]{2,1,0:T(8,128)(2,1)S(1)} %spread.1), channel_id=1, replica_groups=mesh['lat'=4,'lon'=32,'tp'=2] {'lon'}, dimensions={0} | all-to-all | bytes 655360 | tf_op jit(solution)/shard_map/all_to_all | solution.py:662
  86.2 4.7 %collective-permute-start.14 = (bf16[1280,128]{1,0:T(8,128)(2,1)S(1)}, bf16[1280,128]{1,0:T(8,128)(2,1)S(1)}, u32[]{:S(2)}, u32[]{:S(2)}) collective-permute-start(bf16[1280,128]{1,0:T(8,128)(2,1)S(1)} %bitcast.20), channel_id=1, source_target_pairs={{0,64},{64,0},{128,192},{192,128},{1,65},{65,1},{129,193},{193,129... | collective-permute-start | bytes 983048 | tf_op jit(solution)/shard_map/ppermute | solution.py:614
  90.9 1.2 %finish.1 = bf16[6,12,8,192]{3,2,1,0:T(8,128)(2,1)} custom-call(bf16[144,192]{1,0:T(8,128)(2,1)S(1)} %copy-done.6, bf16[144,192]{1,0:T(8,128)(2,1)S(1)} %copy-done.7, bf16[144,192]{1,0:T(8,128)(2,1)S(1)} %copy-done.8, bf16[144,192]{1,0:T(8,128)(2,1)S(1)} %copy-done.17, bf16[144,192]{1,0:T(8,128)(2,1)S(1)} %get-tuple-element.58.m0, ...), custom_call_target="tpu_custom_call" | custom-call | flops 1000000000 | tf_op jit(solution)/shard_map/finish/pallas_call | solution.py:502
  92.2 0.0 collective-permute-done.14.other_ref
  92.2 1.1 %unpack.1 = (f32[3,192,96]{2,1,0:T(8,128)}, f32[96,192]{1,0:T(8,128)}, f32[192,384]{1,0:T(8,128)}, f32[192,384]{1,0:T(8,128)}, f32[1,96]{1,0:T(1,128)}, /*index=5*/f32[1,96]{1,0:T(1,128)}, f32[3,4,3312]{2,1,0:T(4,128)}) custom-call(bf16[1280,128]{1,0:T(8,128)(2,1)S(1)} %bitcast.21, bf16[1280,128]{1,0:T(8,128)(2,1)S(1)} %collective-permute-done.14.other_ref), custom_call_target="tpu_custom_call" | custom-call | tf_op jit(solution)/shard_map/unpack/pallas_call | solution.py:577
  (33 shorter events, 0.1 us)
Async XLA Ops:
  0.6 18.4 %copy-start.3 = (f32[1,4,3,3312]{3,1,2,0:T(4,128)S(1)}, f32[1,4,3,3312]{3,1,2,0:T(4,128)}, u32[]{:S(2)}) copy-start(f32[1,4,3,3312]{3,1,2,0:T(4,128)} %param.22) | copy-start | bytes 476932
  0.6 18.4 %copy-start.4 = (s32[144,144]{1,0:T(8,128)S(1)}, s32[144,144]{1,0:T(8,128)}, u32[]{:S(2)}) copy-start(s32[144,144]{1,0:T(8,128)} %index_ref.1) | copy-start | bytes 248836
  0.7 18.4 %copy-start.10 = (s32[8,6,12]{2,0,1:T(8,128)S(1)}, s32[8,6,12]{2,0,1:T(8,128)}, u32[]{:S(2)}) copy-start(s32[8,6,12]{2,0,1:T(8,128)} %param.19) | copy-start | bytes 6916
  0.7 18.4 %copy-start.11 = (s32[8,6,12]{2,0,1:T(8,128)S(1)}, s32[8,6,12]{2,0,1:T(8,128)}, u32[]{:S(2)}) copy-start(s32[8,6,12]{2,0,1:T(8,128)} %param.20) | copy-start | bytes 6916
  0.7 18.4 %copy-start.15 = (bf16[144,144]{1,0:T(8,128)(2,1)S(1)}, bf16[144,144]{1,0:T(8,128)(2,1)}, u32[]{:S(2)}) copy-start(bf16[144,144]{1,0:T(8,128)(2,1)} %constant.4.clone.order_ref) | copy-start | bytes 124420
  4.3 17.8 %copy-start = (bf16[8,6,12,192]{3,0,2,1:T(8,128)(2,1)S(1)}, bf16[8,6,12,192]{3,0,2,1:T(8,128)(2,1)}, u32[]{:S(2)}) copy-start(bf16[8,6,12,192]{3,0,2,1:T(8,128)(2,1)} %param.17) | copy-start | bytes 663556
  4.3 17.8 %copy-start.1 = (bf16[8,6,12,192]{3,0,2,1:T(8,128)(2,1)S(1)}, bf16[8,6,12,192]{3,0,2,1:T(8,128)(2,1)}, u32[]{:S(2)}) copy-start(bf16[8,6,12,192]{3,0,2,1:T(8,128)(2,1)} %param.18) | copy-start | bytes 663556
  4.4 17.8 %copy-start.2 = (bf16[576,192]{1,0:T(8,128)(2,1)S(1)}, bf16[576,192]{1,0:T(8,128)(2,1)}, u32[]{:S(2)}) copy-start(bf16[576,192]{1,0:T(8,128)(2,1)} %get-tuple-element.56.own_ref) | copy-start | bytes 663556
  4.4 17.8 %copy-start.12 = (f32[192]{0:T(256)S(1)}, f32[192]{0:T(256)}, u32[]{:S(2)}) copy-start(f32[192]{0:T(256)} %param.26) | copy-start | bytes 2308
  4.4 17.7 %collective-permute-start = (bf16[576,192]{1,0:T(8,128)(2,1)}, bf16[576,192]{1,0:T(8,128)(2,1)S(1)}, u32[]{:S(2)}, u32[]{:S(2)}) collective-permute-start(bf16[576,192]{1,0:T(8,128)(2,1)} %get-tuple-element.56.own_ref), channel_id=1, source_target_pairs={{1,0},{0,1},{3,2},{2,3},{5,4},{4,5},{7,6},{6,7},{9,8},{8,9},{11,10... | collective-permute-start | bytes 663560 | tf_op jit(solution)/shard_map/ppermute | solution.py:601
  6.6 16.7 %collective-permute-start.6 = (bf16[144,192]{1,0:T(8,128)(2,1)}, bf16[144,192]{1,0:T(8,128)(2,1)S(1)}, u32[]{:S(2)}, u32[]{:S(2)}) collective-permute-start(bf16[144,192]{1,0:T(8,128)(2,1)} %get-tuple-element.52.x0), channel_id=1, source_target_pairs={{66,0},{67,1},{68,2},{69,3},{70,4},{71,5},{72,6},{73,7},{74,8},{75... | collective-permute-start | bytes 165896 | tf_op jit(solution)/shard_map/ppermute | solution.py:601
  15.2 9.7 %collective-permute-start.5 = (bf16[144,192]{1,0:T(8,128)(2,1)}, bf16[144,192]{1,0:T(8,128)(2,1)S(1)}, u32[]{:S(2)}, u32[]{:S(2)}) collective-permute-start(bf16[144,192]{1,0:T(8,128)(2,1)} %get-tuple-element.53.x1), channel_id=1, source_target_pairs={{64,0},{65,1},{66,2},{67,3},{68,4},{69,5},{70,6},{71,7},{72,8},{73... | collective-permute-start | bytes 165896 | tf_op jit(solution)/shard_map/ppermute | solution.py:601
  17.1 9.2 %collective-permute-start.4 = (bf16[144,192]{1,0:T(8,128)(2,1)}, bf16[144,192]{1,0:T(8,128)(2,1)S(1)}, u32[]{:S(2)}, u32[]{:S(2)}) collective-permute-start(bf16[144,192]{1,0:T(8,128)(2,1)} %get-tuple-element.54.x2), channel_id=1, source_target_pairs={{2,0},{3,1},{4,2},{5,3},{6,4},{7,5},{8,6},{9,7},{10,8},{11,9},{12,... | collective-permute-start | bytes 165896 | tf_op jit(solution)/shard_map/ppermute | solution.py:601
  17.6 27.6 %collective-permute-start.8 = (bf16[576,128]{1,0:T(8,128)(2,1)}, bf16[576,128]{1,0:T(8,128)(2,1)S(1)}, u32[]{:S(2)}, u32[]{:S(2)}) collective-permute-start(bf16[576,128]{1,0:T(8,128)(2,1)} %get-tuple-element.75), channel_id=1, source_target_pairs={{0,64},{64,0},{128,192},{192,128},{1,65},{65,1},{129,193},{193,129... | collective-permute-start | bytes 442376 | tf_op jit(solution)/shard_map/ppermute | solution.py:614
  22.7 8.8 %collective-permute-start.3 = (bf16[144,192]{1,0:T(8,128)(2,1)S(1)}, bf16[144,192]{1,0:T(8,128)(2,1)S(1)}, u32[]{:S(2)}, u32[]{:S(2)}) collective-permute-start(bf16[144,192]{1,0:T(8,128)(2,1)S(1)} %get-tuple-element.58.m0), channel_id=1, source_target_pairs={{66,0},{67,1},{68,2},{69,3},{70,4},{71,5},{72,6},{73,7},{74,8},{75... | collective-permute-start | bytes 165896 | tf_op jit(solution)/shard_map/ppermute | solution.py:601
  23.3 8.3 %collective-permute-start.2 = (bf16[144,192]{1,0:T(8,128)(2,1)S(1)}, bf16[144,192]{1,0:T(8,128)(2,1)S(1)}, u32[]{:S(2)}, u32[]{:S(2)}) collective-permute-start(bf16[144,192]{1,0:T(8,128)(2,1)S(1)} %get-tuple-element.59.m1), channel_id=1, source_target_pairs={{64,0},{65,1},{66,2},{67,3},{68,4},{69,5},{70,6},{71,7},{72,8},{73... | collective-permute-start | bytes 165896 | tf_op jit(solution)/shard_map/ppermute | solution.py:601
  24.9 6.7 %collective-permute-start.1 = (bf16[144,192]{1,0:T(8,128)(2,1)S(1)}, bf16[144,192]{1,0:T(8,128)(2,1)S(1)}, u32[]{:S(2)}, u32[]{:S(2)}) collective-permute-start(bf16[144,192]{1,0:T(8,128)(2,1)S(1)} %get-tuple-element.60.m2), channel_id=1, source_target_pairs={{2,0},{3,1},{4,2},{5,3},{6,4},{7,5},{8,6},{9,7},{10,8},{11,9},{12,... | collective-permute-start | bytes 165896 | tf_op jit(solution)/shard_map/ppermute | solution.py:601
  26.3 2.2 %copy-start.5 = (bf16[3,192,96]{2,1,0:T(8,128)(2,1)S(1)}, bf16[3,192,96]{2,1,0:T(8,128)(2,1)}, u32[]{:S(2)}) copy-start(bf16[3,192,96]{2,1,0:T(8,128)(2,1)} %qkv_ref.3) | copy-start | bytes 331780
  26.3 2.2 %copy-start.13 = (f32[192]{0:T(256)S(1)}, f32[192]{0:T(256)}, u32[]{:S(2)}) copy-start(f32[192]{0:T(256)} %param.23) | copy-start | bytes 2308
  26.3 2.3 %copy-start.14 = (bf16[144,144]{1,0:T(8,128)(2,1)S(1)}, bf16[144,144]{1,0:T(8,128)(2,1)}, u32[]{:S(2)}) copy-start(bf16[144,144]{1,0:T(8,128)(2,1)} %constant.5.clone.order_ref) | copy-start | bytes 124420
  26.3 2.3 %copy-start.17 = (bf16[144,192]{1,0:T(8,128)(2,1)S(1)}, bf16[144,192]{1,0:T(8,128)(2,1)}, u32[]{:S(2)}) copy-start(bf16[144,192]{1,0:T(8,128)(2,1)} %get-tuple-element.55.x0.x3) | copy-start | bytes 165892
  28.5 3.0 %copy-start.9 = (bf16[96,192]{1,0:T(8,128)(2,1)S(1)}, bf16[96,192]{1,0:T(8,128)(2,1)}, u32[]{:S(2)}) copy-start(bf16[96,192]{1,0:T(8,128)(2,1)} %proj_ref.1) | copy-start | bytes 110596
  36.9 9.2 %collective-permute-start.7 = (bf16[576,192]{1,0:T(8,128)(2,1)S(1)}, bf16[576,192]{1,0:T(8,128)(2,1)S(1)}, u32[]{:S(2)}, u32[]{:S(2)}) collective-permute-start(bf16[576,192]{1,0:T(8,128)(2,1)S(1)} %get-tuple-element.73.own_ref), channel_id=1, source_target_pairs={{1,0},{0,1},{3,2},{2,3},{5,4},{4,5},{7,6},{6,7},{9,8},{8,9},{11,10... | collective-permute-start | bytes 663560 | tf_op jit(solution)/shard_map/ppermute | solution.py:601
  37.4 8.8 %copy-start.16 = (bf16[576,128]{1,0:T(8,128)(2,1)S(1)}, bf16[576,128]{1,0:T(8,128)(2,1)}, u32[]{:S(2)}) copy-start(bf16[576,128]{1,0:T(8,128)(2,1)} %get-tuple-element.74.first_ref) | copy-start | bytes 442372
  42.6 3.5 %collective-permute-start.9 = (bf16[288,128]{1,0:T(8,128)(2,1)S(1)}, bf16[288,128]{1,0:T(8,128)(2,1)S(1)}, u32[]{:S(2)}, u32[]{:S(2)}) collective-permute-start(bf16[288,128]{1,0:T(8,128)(2,1)S(1)} %get-tuple-element.82), channel_id=1, source_target_pairs={{0,64},{64,0},{128,192},{192,128},{1,65},{65,1},{129,193},{193,129... | collective-permute-start | bytes 221192 | tf_op jit(solution)/shard_map/ppermute | solution.py:614
  47.3 19.2 %all-to-all-start = ((bf16[32,40,128]{2,1,0:T(8,128)(2,1)}), bf16[32,40,128]{2,1,0:T(8,128)(2,1)S(1)}, u32[]{:S(2)}, u32[]{:S(2)}) async-start(bf16[32,40,128]{2,1,0:T(8,128)(2,1)} %bitcast.11), calls=%async_computation | async-start | bytes 655360 | tf_op jit(solution)/shard_map/all_to_all | solution.py:659
  51.2 15.3 %collective-permute-start.10 = (bf16[144,192]{1,0:T(8,128)(2,1)S(1)}, bf16[144,192]{1,0:T(8,128)(2,1)S(1)}, u32[]{:S(2)}, u32[]{:S(2)}) collective-permute-start(bf16[144,192]{1,0:T(8,128)(2,1)S(1)} %get-tuple-element.84), channel_id=1, source_target_pairs={{254,0},{255,1},{192,2},{193,3},{194,4},{195,5},{196,6},{197,7},{1... | collective-permute-start | bytes 165896 | tf_op jit(solution)/shard_map/ppermute | solution.py:601
  55.0 11.5 %collective-permute-start.11 = (bf16[144,192]{1,0:T(8,128)(2,1)S(1)}, bf16[144,192]{1,0:T(8,128)(2,1)S(1)}, u32[]{:S(2)}, u32[]{:S(2)}) collective-permute-start(bf16[144,192]{1,0:T(8,128)(2,1)S(1)} %get-tuple-element.85), channel_id=1, source_target_pairs={{192,0},{193,1},{194,2},{195,3},{196,4},{197,5},{198,6},{199,7},{2... | collective-permute-start | bytes 165896 | tf_op jit(solution)/shard_map/ppermute | solution.py:601
  55.0 11.5 %collective-permute-start.12 = (bf16[144,192]{1,0:T(8,128)(2,1)S(1)}, bf16[144,192]{1,0:T(8,128)(2,1)S(1)}, u32[]{:S(2)}, u32[]{:S(2)}) collective-permute-start(bf16[144,192]{1,0:T(8,128)(2,1)S(1)} %get-tuple-element.86), channel_id=1, source_target_pairs={{62,0},{63,1},{0,2},{1,3},{2,4},{3,5},{4,6},{5,7},{6,8},{7,9},{8,1... | collective-permute-start | bytes 165896 | tf_op jit(solution)/shard_map/ppermute | solution.py:601
  66.6 24.3 %copy-start.6 = (bf16[144,192]{1,0:T(8,128)(2,1)S(1)}, bf16[144,192]{1,0:T(8,128)(2,1)}, u32[]{:S(2)}) copy-start(bf16[144,192]{1,0:T(8,128)(2,1)} %get-tuple-element.52.x0) | copy-start | bytes 165892
  66.6 24.3 %copy-start.7 = (bf16[144,192]{1,0:T(8,128)(2,1)S(1)}, bf16[144,192]{1,0:T(8,128)(2,1)}, u32[]{:S(2)}) copy-start(bf16[144,192]{1,0:T(8,128)(2,1)} %get-tuple-element.53.x1) | copy-start | bytes 165892
  66.6 24.3 %copy-start.8 = (bf16[144,192]{1,0:T(8,128)(2,1)S(1)}, bf16[144,192]{1,0:T(8,128)(2,1)}, u32[]{:S(2)}) copy-start(bf16[144,192]{1,0:T(8,128)(2,1)} %get-tuple-element.54.x2) | copy-start | bytes 165892
  66.6 4.1 %collective-permute-start.13 = (bf16[40,128]{1,0:T(8,128)(2,1)S(1)}, bf16[40,128]{1,0:T(8,128)(2,1)S(1)}, u32[]{:S(2)}, u32[]{:S(2)}) collective-permute-start(bf16[40,128]{1,0:T(8,128)(2,1)S(1)} %add.1.own_ref), channel_id=1, source_target_pairs={{128,0},{129,1},{130,2},{131,3},{132,4},{133,5},{134,6},{135,7},{1... | collective-permute-start | bytes 30728 | tf_op jit(solution)/shard_map/ppermute | solution.py:601
  86.2 6.0 %collective-permute-start.14 = (bf16[1280,128]{1,0:T(8,128)(2,1)S(1)}, bf16[1280,128]{1,0:T(8,128)(2,1)S(1)}, u32[]{:S(2)}, u32[]{:S(2)}) collective-permute-start(bf16[1280,128]{1,0:T(8,128)(2,1)S(1)} %bitcast.20), channel_id=1, source_target_pairs={{0,64},{64,0},{128,192},{192,128},{1,65},{65,1},{129,193},{193,129... | collective-permute-start | bytes 983048 | tf_op jit(solution)/shard_map/ppermute | solution.py:614

commit v9 on v8

--- a/solution.py
+++ b/solution.py
@@ -359,7 +359,7 @@
 
 
 def backward_kernel(g0, g1, g2, g3, order_ref, proj_ref, qkv_ref, q_ref, k_ref, v_ref, prob_ref,
-                    part_ref, score_ref, gcols, grad_ref, scratch, gatt):
+                    part_ref, score_ref, end_ref, gcols, grad_ref, scratch, gatt):
     to_windows((g0, g1, g2, g3), order_ref[...], scratch)
     grad = scratch[...].astype(BF)
     grad_ref[...] = grad
@@ -372,16 +372,17 @@
         for h in range(3):
             cols = slice(h * HD, h * HD + HD)
             prob = prob_ref[w * 3 + h]
-            values.append(dot_tn(prob.astype(BF), above[:, cols]))
+            values.append(dot_tn(above[:, cols], prob.astype(BF)))
             grad_prob = dot_nt(above[:, cols], value[:, cols])
             score = prob * (grad_prob - jnp.sum(grad_prob * prob, axis=-1, keepdims=True))
-            score_ref[w * 3 + h] = score
+            score_ref[w * 3 + h] = score[:, 0:128]
+            end_ref[w * 3 + h, :, 0:16] = score[:, 128:144]
             low_score = (score * (HD ** -0.5)).astype(BF)
             queries.append(dot_nn(low_score, key[:, cols]))
-            keys.append(dot_tn(low_score, query[:, cols]))
+            keys.append(dot_tn(query[:, cols], low_score))
         gcols[0, rows, :] = jnp.concatenate(queries, axis=1).astype(BF)
-        gcols[1, rows, :] = jnp.concatenate(keys, axis=1).astype(BF)
-        gcols[2, rows, :] = jnp.concatenate(values, axis=1).astype(BF)
+        gcols[1, rows, :] = jnp.concatenate(keys, axis=0).T.astype(BF)
+        gcols[2, rows, :] = jnp.concatenate(values, axis=0).T.astype(BF)
         return 0
 
     lax.fori_loop(0, 4, window, 0, unroll=True)
@@ -401,7 +402,8 @@
         backward_kernel,
         out_shape=(
             shape((576, 192), BF),
-            shape((12, 144, 144), F32),
+            shape((12, 144, 128), F32),
+            shape((12, 144, 128), F32),
             shape((3, 576, 96), BF),
             shape((576, 192), BF),
         ),
@@ -412,21 +414,41 @@
     )(*g, level_order(), proj, qkv, q, k, v, prob)
 
 
-def scatter_kernel(score_ref, lo_ref, hi_ref, low_ref, gcols, att_ref, grad_ref,
-                   out_ref, keep_ref, send_ref, grads_ref, tails):
-    out_ref[...] = jnp.zeros((192, 256), F32)
+def scatter_kernel(score_ref, end_ref, lo_ref, hi_ref, after_ref, out_ref, tails):
+    total = jnp.zeros((256, 192), F32)
     place = lax.broadcasted_iota(I32, (16, 128), 0)
+    group = lax.broadcasted_iota(I32, (18, 128), 1) >> 4
     for r in range(12):
-        tails[r] = pack_tail(score_ref[r, :, 128:144].astype(BF))
+        packed = end_ref[r, pl.ds(0, 18, stride=8), :]
+        for j in range(1, 8):
+            moved_on = pltpu.roll(end_ref[r, pl.ds(j, 18, stride=8), :], 16 * j, 1)
+            packed = jnp.where(group == j, moved_on, packed)
+        tails[r, 0:18, :] = packed
     for i in range(9):
         left, right = [], []
         for j in range(18):
             row = slice(i * 18 + j, i * 18 + j + 1)
             here = place == hi_ref[row, :]
             right.append(one_hot(lo_ref[row, :]))
-            lines = [score_ref[r, row, 0:128] if i < 8 else tails[r, j : j + 1, :] for r in range(12)]
+            lines = [score_ref[r, row, :] if i < 8 else tails[r, j : j + 1, :] for r in range(12)]
             left.append(jnp.concatenate([jnp.where(here, line, 0.0).astype(BF) for line in lines], axis=0))
-        out_ref[...] += dot_nt(jnp.concatenate(left, axis=1), jnp.concatenate(right, axis=1))
+        total = total + dot_nt(jnp.concatenate(right, axis=1), jnp.concatenate(left, axis=1))
+    out_ref[...] = total.T
+
+
+def scatter(score, end, lo, hi, after):
+    return pl.pallas_call(
+        scatter_kernel,
+        out_shape=shape((192, 256), F32),
+        in_specs=[VMEM] * 4 + [ANY],
+        scratch_shapes=[pltpu.VMEM((12, 24, 128), F32)],
+        compiler_params=VM,
+        cost_estimate=cost(4),
+        name="scatter",
+    )(score, end, lo, hi, after)
+
+
+def weigh_kernel(low_ref, gcols, att_ref, grad_ref, keep_ref, send_ref, grads_ref):
     gproj = dot_tn(att_ref[...], grad_ref[...]).astype(BF)
     grads_ref[0:96, :] = gproj[:, 0:128]
     grads_ref[96:144, :] = jnp.concatenate([gproj[0:48, 128:192], gproj[48:96, 128:192]], axis=1)
@@ -440,53 +462,58 @@
     send_ref[...] = grads_ref[pl.ds(pl.multiple_of((1 - core) * 288, 16), 288), :]
 
 
-def scatter(score, lo, hi, low, gcols, att, grad):
-    return pl.pallas_call(
-        scatter_kernel,
-        out_shape=(shape((192, 256), F32), shape((288, 128), BF), shape((288, 128), BF)),
-        scratch_shapes=[pltpu.VMEM((576, 128), BF), pltpu.VMEM((12, 24, 128), F32)],
-        compiler_params=VM,
-        cost_estimate=cost(5),
-        name="scatter",
-    )(score, lo, hi, low, gcols, att, grad)
-
-
-def meet_kernel(own_ref, other_ref, x0, x1, x2, x3, first_ref, first_other, second_ref, second_other,
-                table_ref, two_ref, out_ref, g0, g1, g2, g3):
-    gain = jnp.zeros((1, 192), F32)
-    for s, x in enumerate((x0, x1, x2, x3)):
-        rows = slice(s * 144, s * 144 + 144)
-        grad = own_ref[rows, :].astype(F32) + other_ref[rows, :].astype(F32)
-        normed, _ = layer_stats(x[...].astype(F32))
-        gain = gain + jnp.sum(grad * normed, axis=0, keepdims=True)
-        (g0, g1, g2, g3)[s][...] = grad.astype(BF)
+def weigh(low, gcols, att, grad):
+    return pl.pallas_call(
+        weigh_kernel,
+        out_shape=(shape((288, 128), BF), shape((288, 128), BF)),
+        scratch_shapes=[pltpu.VMEM((576, 128), BF)],
+        compiler_params=VM,
+        cost_estimate=cost(0.5),
+        name="weigh",
+    )(low, gcols, att, grad)
+
+
+def gain_rows(line):
+    none = jnp.zeros((1, 64), F32)
+    return [line[:, 0:128], jnp.concatenate([line[:, 128:192], none], axis=1)]
+
+
+def pack_kernel(first_ref, first_other, second_ref, second_other, table_ref, gain_ref, out_ref):
     out_ref[0:576, :] = both(first_ref[...], first_other[...])
     out_ref[576:864, :] = both(second_ref[...], second_other[...])
     rows = []
     for r in range(12):
         pair = table_ref[r * 16 : r * 16 + 13, :]
         rows += [pair[:, 0:128], pair[:, 128:256]]
-    none = jnp.zeros((1, 64), F32)
-    for line in (gain, two_ref[...]):
-        rows += [line[:, 0:128], jnp.concatenate([line[:, 128:192], none], axis=1)]
-    rows += [jnp.zeros((100, 128), F32)]
+    rows += gain_rows(gain_ref[...]) + [jnp.zeros((102, 128), F32)]
     out_ref[864:1280, :] = jnp.concatenate(rows, axis=0).astype(BF)
 
 
-def meet(own, other, x, first, first_other, second, second_other, table, two):
+def pack(first, first_other, second, second_other, table, gain):
+    return pl.pallas_call(
+        pack_kernel, out_shape=shape((1280, 128), BF), compiler_params=VM, cost_estimate=cost(1), name="pack"
+    )(first, first_other, second, second_other, table, gain)
+
+
+def meet_kernel(own_ref, other_ref, x0, x1, x2, x3, g0, g1, g2, g3, gain_out):
+    gain = jnp.zeros((1, 192), F32)
+    for s, (x, g) in enumerate(zip((x0, x1, x2, x3), (g0, g1, g2, g3))):
+        rows = slice(s * 144, s * 144 + 144)
+        grad = own_ref[rows, :].astype(F32) + other_ref[rows, :].astype(F32)
+        normed, _ = layer_stats(x[...].astype(F32))
+        gain = gain + jnp.sum(grad * normed, axis=0, keepdims=True)
+        g[...] = grad.astype(BF)
+    gain_out[...] = jnp.concatenate(gain_rows(gain) + [jnp.zeros((6, 128), F32)], axis=0)
+
+
+def meet(own, other, x):
     return pl.pallas_call(
         meet_kernel,
-        out_shape=(
-            shape((1280, 128), BF),
-            shape((144, 192), BF),
-            shape((144, 192), BF),
-            shape((144, 192), BF),
-            shape((144, 192), BF),
-        ),
+        out_shape=tuple(shape((144, 192), BF) for _ in range(4)) + (shape((8, 128), F32),),
         compiler_params=VM,
         cost_estimate=cost(1),
         name="meet",
-    )(own, other, *x, first, first_other, second, second_other, table, two)
+    )(own, other, *x)
 
 
 def finish_kernel(x0, x1, x2, x3, m0, m1, m2, m3, g0, g1, g2, g3, gain_ref, out_ref):
@@ -508,42 +535,50 @@
     )(*x, *m, *g, gain)
 
 
-def add_kernel(got_ref, b0, b1, b2, out_ref):
+def add_kernel(got_ref, gain_ref, b0, b1, b2, out_ref):
     total = got_ref[0].astype(F32)
     for i in range(1, 32):
         total = total + got_ref[i].astype(F32)
-    out_ref[...] = total.astype(BF)
-
-
-def add(got, after):
+    out_ref[...] = jnp.concatenate([total, gain_ref[...]], axis=0).astype(BF)
+
+
+def add(got, gain, after):
     return pl.pallas_call(
         add_kernel,
-        out_shape=shape((40, 128), BF),
-        in_specs=[VMEM] + [ANY] * 3,
+        out_shape=shape((48, 128), BF),
+        in_specs=[VMEM] * 2 + [ANY] * 3,
         compiler_params=VM,
         cost_estimate=cost(1),
         name="add",
-    )(got, *after)
+    )(got, gain, *after)
 
 
 def spread_kernel(own_ref, other_ref, out_ref):
     own = own_ref[...].astype(F32)
-    row = lax.axis_index("lon") * 40 + lax.broadcasted_iota(I32, (40, 128), 0)
-    table = (row >= 864) & (row < 1176)
+    place = lax.broadcasted_iota(I32, (48, 128), 0)
+    row = lax.axis_index("lon") * 40 + place
+    table = (row >= 864) & (row < 1176) & (place < 40)
     total = own + jnp.where(table, 0.0, other_ref[...].astype(F32))
-    out_ref[...] = jnp.broadcast_to(total.astype(BF)[None], (32, 40, 128))
+    out_ref[...] = jnp.broadcast_to(total.astype(BF)[None], (32, 48, 128))
 
 
 def spread(own, other):
     return pl.pallas_call(
-        spread_kernel, out_shape=shape((32, 40, 128), BF), compiler_params=VM, cost_estimate=cost(1), name="spread"
+        spread_kernel, out_shape=shape((32, 48, 128), BF), compiler_params=VM, cost_estimate=cost(1), name="spread"
     )(own, other)
 
 
 def unpack_kernel(weight_scale, table_scale, own_ref, other_ref,
                   qkv_ref, proj_ref, upg_ref, down_ref, one_ref, two_ref, table_ref):
     swap = lax.rem(lax.axis_index("lat"), 2) == 1
-    own, other = own_ref[0:864, :].astype(F32) * weight_scale, other_ref[0:864, :].astype(F32) * weight_scale
+    fields = []
+    gain = jnp.zeros((8, 128), F32)
+    for ref in (own_ref, other_ref):
+        pieces = [ref[c].astype(F32) for c in range(32)]
+        fields.append(jnp.concatenate([piece[0:40] for piece in pieces], axis=0))
+        for piece in pieces:
+            gain = gain + piece[40:48]
+    own, other = fields[0][0:864] * weight_scale, fields[1][0:864] * weight_scale
     lower, upper = jnp.where(swap, other, own), jnp.where(swap, own, other)
     for j in range(3):
         upg_ref[:, j * 128 : j * 128 + 128] = lower[j * 192 : j * 192 + 192]
@@ -558,7 +593,7 @@
     qkv_ref[2, :, 32:64] = second[336:528, 96:128]
     for i in range(4):
         qkv_ref[2, i * 48 : i * 48 + 48, 64:96] = second[528:576, i * 32 : i * 32 + 32]
-    table = own_ref[864:1184, :].astype(F32)
+    table = fields[0][864:1176]
     for r in range(12):
         for half in range(2):
             piece = table[r * 26 + half * 13 : r * 26 + half * 13 + 13] * table_scale
@@ -566,10 +601,9 @@
                 start = a * 256 + half * 128
                 wide = min(128, 3312 - start)
                 table_ref[r % 3, r // 3 : r // 3 + 1, start : start + wide] = piece[a : a + 1, 0:wide]
-    gains = table[304:320] + other_ref[1168:1184, :].astype(F32)
-    for start, out in ((8, one_ref), (10, two_ref)):
-        line = gains[start : start + 1]
-        later = jnp.concatenate([line[:, 96:128], gains[start + 1 : start + 2, 0:64]], axis=1)
+    for rows, out in ((gain, one_ref), (fields[0][1176:1184] + fields[1][1176:1184], two_ref)):
+        line = rows[0:1]
+        later = jnp.concatenate([line[:, 96:128], rows[1:2, 0:64]], axis=1)
         out[...] = jnp.where(lax.axis_index("tp") == 0, line[:, 0:96], later) * weight_scale
 
 
@@ -649,17 +683,17 @@
     gw = shifted_parts(gm)
     main, tail = gather_second(stage, lo, hi, terms, (gain_two, *xw[1:]))
     low, q, k, v, prob, att = forward(xw, gain1, qkv_weight, main, tail, code)
-    part1, score, gcols, grad = backward(gw, proj_weight, qkv_weight, q, k, v, prob)
+    part1, score, end, gcols, grad = backward(gw, proj_weight, qkv_weight, q, k, v, prob)
     other1 = moved(part1, 0, 0, 1)
-    table, second, second_send = scatter(score, lo, hi, low, gcols, att, grad)
-    sums, *g = meet(
-        part1, other1, xw, first, other_core(first_send), second, other_core(second_send), table, gain_two
-    )
+    second, second_send = weigh(low, gcols, att, grad)
+    table = scatter(score, end, lo, hi, second)
+    sums = pack(first, other_core(first_send), second, other_core(second_send), table, gain_two)
+    *g, gain_one = meet(part1, other1, xw)
     back = (moved(g[3], -1, -1, 0), moved(g[2], -1, 0, 0), moved(g[1], 0, -1, 0), g[0])
-    own = add(lax.all_to_all(sums.reshape(32, 40, 128), "lon", 0, 0), back[:3])
+    own = add(lax.all_to_all(sums.reshape(32, 40, 128), "lon", 0, 0), gain_one, back[:3])
     totals = spread(own, moved(own, 2, 0, 0))
     result = finish(x, gm, back, gain1)
-    got = lax.all_to_all(totals, "lon", 0, 0).reshape(1280, 128)
+    got = lax.all_to_all(totals, "lon", 0, 0)
     qkv_out, proj_out, up_out, down_out, one, two, table_out = unpack(
         weight_scale, table_scale, got, other_core(got)
     )

time: 93.5 us -> 95.3 us (1.019)
  blocking collectives: 15.4 us -> 17.9 us
  Pallas kernels: 26.7 us -> 24.3 us
  waiting for transfers between devices: 13.8 us -> 16 us
    ppermute x12, waiting for transfers between devices: 12.9 us -> 15.9 us  [moved(): return lax.ppermute(value, ('lat', 'lon', 'tp'), pairs)]
    all_to_all x1, blocking collectives: 15.4 us -> 17.9 us  [local(): got = lax.all_to_all(totals, 'lon', 0, 0)]
    pallas_call x4 -> x6, Pallas kernels: 6.56 us -> 4.81 us  [the longest x1 3.02 us: scatter(): pl.pallas_call(scatter_kernel, out_shape=shape((192, 256), F32), in_specs...]
  transfers between devices with their start and end apart: 16 -> 16, of which waited for: 3 -> 5; matrix products, arithmetic and copies ran while one was open for 0% -> 0% of each run, Pallas kernels for 22% -> 20%
where the time goes in v9:
time: 95.3 us; the launch traced here: 95.1 us
  starting transfers between devices  35.8 us (38%)
  Pallas kernels  24.3 us (25%)
  blocking collectives  17.9 us (19%)
  waiting for transfers between devices  16 us (17%)
  between operations  0.97 us (1%)
    ppermute x12, starting transfers between devices, moved(): return lax.ppermute(value, ('lat', 'lon', 'tp'), pairs)  23.3 us
    all_to_all x1, blocking collectives, local(): got = lax.all_to_all(totals, 'lon', 0, 0)  17.9 us
    ppermute x12, waiting for transfers between devices, moved(): return lax.ppermute(value, ('lat', 'lon', 'tp'), pairs)  15.9 us
    ppermute x3, starting transfers between devices, other_core(): lax.ppermute(value, 'lat', [(a, a ^ 1) for a in range(lax.axis_size('lat'...  8.65 us
    pallas_call x1, Pallas kernels, backward(): pl.pallas_call(backward_kernel, out_shape=(shape((576, 192), BF), shape((...  4.6 us
    all_to_all x1, starting transfers between devices, local(): lax.all_to_all(sums.reshape(32, 40, 128), 'lon', 0, 0)  3.91 us
    pallas_call x1, Pallas kernels, head(): pl.pallas_call(head_kernel, out_shape=tuple((shape((144, 192), BF) for _...  3.63 us
    pallas_call x1, Pallas kernels, scatter(): pl.pallas_call(scatter_kernel, out_shape=shape((192, 256), F32), in_specs...  3.02 us
  transfers between devices with their start and end apart: 16, of which 5 were waited for; matrix products, arithmetic and copies ran while one was open for 0% of the time, Pallas kernels for 20%

profile of v9, /device:TPU:1, one launch (start us, length us, event | category | flops | bytes accessed | tf_op | source)
XLA Modules:
  0.0 95.1 jit_solution(612189716729022861)
XLA Ops:
  0.7 0.0 copy-start.15
  0.7 3.6 %head.1 = (bf16[144,192]{1,0:T(8,128)(2,1)}, bf16[144,192]{1,0:T(8,128)(2,1)}, bf16[144,192]{1,0:T(8,128)(2,1)}, bf16[144,192]{1,0:T(8,128)(2,1)}, bf16[576,192]...) custom-call(bf16[6,12,8,192]{3,2,1,0:T(8,128)(2,1)} %bitcast.30, ...), custom_call_target="tpu_custom_call" | custom-call | flops 3000000000 | tf_op jit(solution)/shard_map/head/pallas_call | solution.py:139
  4.3 0.0 copy-start
  4.3 0.0 copy-start.1
  4.4 0.0 copy-start.2
  4.4 0.0 copy-start.12
  4.4 2.2 %collective-permute-start = (bf16[576,192]{1,0:T(8,128)(2,1)}, bf16[576,192]{1,0:T(8,128)(2,1)S(1)}, u32[]{:S(2)}, u32[]{:S(2)}) collective-permute-start(bf16[576,192]{1,0:T(8,128)(2,1)} %get-tuple-element.56.own_ref), channel_id=1, source_target_pairs={{1,0},{0,1},{3,2},{2,3},{5,4},{4,5},{7,6},{6,7},{9,8},{8,9},{11,10... | collective-permute-start | bytes 663560 | tf_op jit(solution)/shard_map/ppermute | solution.py:635
  6.6 8.6 %collective-permute-start.6 = (bf16[144,192]{1,0:T(8,128)(2,1)}, bf16[144,192]{1,0:T(8,128)(2,1)S(1)}, u32[]{:S(2)}, u32[]{:S(2)}) collective-permute-start(bf16[144,192]{1,0:T(8,128)(2,1)} %get-tuple-element.52.x0), channel_id=1, source_target_pairs={{66,0},{67,1},{68,2},{69,3},{70,4},{71,5},{72,6},{73,7},{74,8},{75... | collective-permute-start | bytes 165896 | tf_op jit(solution)/shard_map/ppermute | solution.py:635
  15.2 1.9 %collective-permute-start.5 = (bf16[144,192]{1,0:T(8,128)(2,1)}, bf16[144,192]{1,0:T(8,128)(2,1)S(1)}, u32[]{:S(2)}, u32[]{:S(2)}) collective-permute-start(bf16[144,192]{1,0:T(8,128)(2,1)} %get-tuple-element.53.x1), channel_id=1, source_target_pairs={{64,0},{65,1},{66,2},{67,3},{68,4},{69,5},{70,6},{71,7},{72,8},{73... | collective-permute-start | bytes 165896 | tf_op jit(solution)/shard_map/ppermute | solution.py:635
  17.1 0.6 collective-permute-start.4
  17.6 1.4 %collective-permute-start.11 = (bf16[576,128]{1,0:T(8,128)(2,1)}, bf16[576,128]{1,0:T(8,128)(2,1)S(1)}, u32[]{:S(2)}, u32[]{:S(2)}) collective-permute-start(bf16[576,128]{1,0:T(8,128)(2,1)} %get-tuple-element.79), channel_id=1, source_target_pairs={{0,64},{64,0},{128,192},{192,128},{1,65},{65,1},{129,193},{193,129... | collective-permute-start | bytes 442376 | tf_op jit(solution)/shard_map/ppermute | solution.py:648
  19.1 3.0 %gather_first.1 = (f32[1440,128]{1,0:T(8,128)S(1)}, s32[168,128]{1,0:T(8,128)S(1)}, s32[168,128]{1,0:T(8,128)S(1)}, bf16[160,512]{1,0:T(8,128)(2,1)S(1)}, f32[4,144]{1,0:T(4,128)S(1)}) custom-call(s32[144,144]{1,0:T(8,128)S(1)} %copy-done.4, bf16[144,144]{1,0:T(8,128)(2,1)S(1)} %copy-done.15, f32[3,4,3312]{2,1,0:T(4,128)S(1)} %bitcast.23, ...), custom_call_target="tpu_custom_call" | custom-call | flops 500000000 | tf_op jit(solution)/shard_map/gather_first/pallas_call | solution.py:272
  22.1 0.6 middle.1
  22.7 0.6 collective-permute-start.3
  23.3 0.0 collective-permute-done.6.a3.x3
  23.3 1.6 %collective-permute-start.2 = (bf16[144,192]{1,0:T(8,128)(2,1)S(1)}, bf16[144,192]{1,0:T(8,128)(2,1)S(1)}, u32[]{:S(2)}, u32[]{:S(2)}) collective-permute-start(bf16[144,192]{1,0:T(8,128)(2,1)S(1)} %get-tuple-element.59.m1), channel_id=1, source_target_pairs={{64,0},{65,1},{66,2},{67,3},{68,4},{69,5},{70,6},{71,7},{72,8},{73... | collective-permute-start | bytes 165896 | tf_op jit(solution)/shard_map/ppermute | solution.py:635
  24.9 0.0 collective-permute-done.5.a2.x2
  24.9 1.4 %collective-permute-start.1 = (bf16[144,192]{1,0:T(8,128)(2,1)S(1)}, bf16[144,192]{1,0:T(8,128)(2,1)S(1)}, u32[]{:S(2)}, u32[]{:S(2)}) collective-permute-start(bf16[144,192]{1,0:T(8,128)(2,1)S(1)} %get-tuple-element.60.m2), channel_id=1, source_target_pairs={{2,0},{3,1},{4,2},{5,3},{6,4},{7,5},{8,6},{9,7},{10,8},{11,9},{12,... | collective-permute-start | bytes 165896 | tf_op jit(solution)/shard_map/ppermute | solution.py:635
  26.3 2.2 %gather_second.1 = (f32[12,144,128]{2,1,0:T(8,128)S(1)}, f32[12,144,128]{2,1,0:T(8,128)S(1)}) custom-call(f32[1440,128]{1,0:T(8,128)S(1)} %get-tuple-element.62.first_stage, s32[168,128]{1,0:T(8,128)S(1)} %get-tuple-element.57.after_ref.lo_ref, s32[168,128]{1,0:T(8,128)S(1)} %get-tuple-element.63.hi_ref, bf16[160,512]{1,0:T(8,128)(2,1)S(1)} %get-tuple-element.64.terms_ref, ...), custom_call_target="tpu_custom_call" | custom-call | flops 4000000000 | tf_op jit(solution)/shard_map/gather_second/pallas_call | solution.py:299
  28.5 0.0 copy-start.9
  28.5 3.0 %forward.1 = (bf16[576,192]{1,0:T(8,128)(2,1)S(1)}, bf16[576,96]{1,0:T(8,128)(2,1)S(1)}, bf16[576,96]{1,0:T(8,128)(2,1)S(1)}, bf16[576,96]{1,0:T(8,128)(2,1)S(1)...) custom-call(bf16[144,192]{1,0:T(8,128)(2,1)S(1)} %copy-done.17, ...), custom_call_target="tpu_custom_call" | custom-call | flops 5000000000 | tf_op jit(solution)/shard_map/forward/pallas_call | solution.py:344
  31.6 0.0 collective-permute-done.3.g3
  31.6 0.0 collective-permute-done.2.g2
  31.6 4.6 %backward.1 = (bf16[576,192]{1,0:T(8,128)(2,1)S(1)}, f32[12,144,128]{2,1,0:T(8,128)S(1)}, f32[12,144,128]{2,1,0:T(8,128)S(1)}, bf16[3,576,96]{2,1,0:T(8,128)(2,1)S(1)}, bf16[576,192]{1,0:T(8,128)(2,1)S(1)}) custom-call(bf16[144,192]{1,0:T(8,128)(2,1)S(1)} %get-tuple-element.61.g0.m3, bf16[144,192]{1,0:T(8,128)(2,1)S(1)} %collective-permute-done.1.g1, ...), custom_call_target="tpu_custom_call" | custom-call | flops 7000000000 | tf_op jit(solution)/shard_map/backward/pallas_call | solution.py:401
  36.2 0.5 weigh.1
  36.7 2.1 %collective-permute-start.12 = (bf16[288,128]{1,0:T(8,128)(2,1)S(1)}, bf16[288,128]{1,0:T(8,128)(2,1)S(1)}, u32[]{:S(2)}, u32[]{:S(2)}) collective-permute-start(bf16[288,128]{1,0:T(8,128)(2,1)S(1)} %get-tuple-element.85), channel_id=1, source_target_pairs={{0,64},{64,0},{128,192},{192,128},{1,65},{65,1},{129,193},{193,129... | collective-permute-start | bytes 221192 | tf_op jit(solution)/shard_map/ppermute | solution.py:648
  38.8 3.0 %scatter.1.table_ref = f32[192,256]{1,0:T(8,128)S(1)} custom-call(f32[12,144,128]{2,1,0:T(8,128)S(1)} %get-tuple-element.86.score_ref, f32[12,144,128]{2,1,0:T(8,128)S(1)} %get-tuple-element.87.end_ref, s32[168,128]{1,0:T(8,128)S(1)} %get-tuple-element.57.after_ref.lo_ref, s32[168,128]{1,0:T(8,128)S(1)} %get-tuple-element.63.hi_ref, ...), custom_call_target="tpu_custom_call" | custom-call | flops 4000000000 | tf_op jit(solution)/shard_map/scatter/pallas_call | solution.py:440
  41.8 0.0 collective-permute-done.12.second_other
  41.9 0.8 pack.1
  42.7 3.9 %all-to-all-start = ((bf16[32,40,128]{2,1,0:T(8,128)(2,1)}), bf16[32,40,128]{2,1,0:T(8,128)(2,1)S(1)}, u32[]{:S(2)}, u32[]{:S(2)}) async-start(bf16[32,40,128]{2,1,0:T(8,128)(2,1)} %bitcast.11), calls=%async_computation | async-start | bytes 655360 | tf_op jit(solution)/shard_map/all_to_all | solution.py:693
  46.6 0.7 collective-permute-start.7
  47.3 7.9 %collective-permute-done.7.other_ref = bf16[576,192]{1,0:T(8,128)(2,1)S(1)} collective-permute-done((bf16[576,192]{1,0:T(8,128)(2,1)S(1)}, bf16[576,192]{1,0:T(8,128)(2,1)S(1)}, u32[]{:S(2)}, u32[]{:S(2)}) %collective-permute-start.7) | collective-permute-done | bytes 221216 | tf_op jit(solution)/shard_map/ppermute | solution.py:635
  55.2 0.3 meet.1
  55.5 2.6 %collective-permute-start.8 = (bf16[144,192]{1,0:T(8,128)(2,1)S(1)}, bf16[144,192]{1,0:T(8,128)(2,1)S(1)}, u32[]{:S(2)}, u32[]{:S(2)}) collective-permute-start(bf16[144,192]{1,0:T(8,128)(2,1)S(1)} %get-tuple-element.74), channel_id=1, source_target_pairs={{254,0},{255,1},{192,2},{193,3},{194,4},{195,5},{196,6},{197,7},{1... | collective-permute-start | bytes 165896 | tf_op jit(solution)/shard_map/ppermute | solution.py:635
  58.1 0.0 collective-permute-start.9
  58.1 1.2 %collective-permute-start.10 = (bf16[144,192]{1,0:T(8,128)(2,1)S(1)}, bf16[144,192]{1,0:T(8,128)(2,1)S(1)}, u32[]{:S(2)}, u32[]{:S(2)}) collective-permute-start(bf16[144,192]{1,0:T(8,128)(2,1)S(1)} %get-tuple-element.76), channel_id=1, source_target_pairs={{62,0},{63,1},{0,2},{1,3},{2,4},{3,5},{4,6},{5,7},{6,8},{7,9},{8,1... | collective-permute-start | bytes 165896 | tf_op jit(solution)/shard_map/ppermute | solution.py:635
  59.3 4.7 %collective-permute-done.8.g0.b0 = bf16[144,192]{1,0:T(8,128)(2,1)S(1)} collective-permute-done((bf16[144,192]{1,0:T(8,128)(2,1)S(1)}, bf16[144,192]{1,0:T(8,128)(2,1)S(1)}, u32[]{:S(2)}, u32[]{:S(2)}) %collective-permute-start.8) | collective-permute-done | bytes 55328 | tf_op jit(solution)/shard_map/ppermute | solution.py:635
  64.0 1.2 %collective-permute-done.10.g2.b2 = bf16[144,192]{1,0:T(8,128)(2,1)S(1)} collective-permute-done((bf16[144,192]{1,0:T(8,128)(2,1)S(1)}, bf16[144,192]{1,0:T(8,128)(2,1)S(1)}, u32[]{:S(2)}, u32[]{:S(2)}) %collective-permute-start.10) | collective-permute-done | bytes 55328 | tf_op jit(solution)/shard_map/ppermute | solution.py:635
  65.2 0.1 add.1.own_ref
  65.3 0.0 copy-start.7
  65.3 0.0 copy-start.8
  65.3 2.0 %collective-permute-start.13 = (bf16[48,128]{1,0:T(8,128)(2,1)S(1)}, bf16[48,128]{1,0:T(8,128)(2,1)S(1)}, u32[]{:S(2)}, u32[]{:S(2)}) collective-permute-start(bf16[48,128]{1,0:T(8,128)(2,1)S(1)} %add.1.own_ref), channel_id=1, source_target_pairs={{128,0},{129,1},{130,2},{131,3},{132,4},{133,5},{134,6},{135,7},{1... | collective-permute-start | bytes 36872 | tf_op jit(solution)/shard_map/ppermute | solution.py:635
  67.3 2.2 %collective-permute-done.13.other_ref = bf16[48,128]{1,0:T(8,128)(2,1)S(1)} collective-permute-done((bf16[48,128]{1,0:T(8,128)(2,1)S(1)}, bf16[48,128]{1,0:T(8,128)(2,1)S(1)}, u32[]{:S(2)}, u32[]{:S(2)}) %collective-permute-start.13) | collective-permute-done | bytes 12320 | tf_op jit(solution)/shard_map/ppermute | solution.py:635
  69.5 17.9 %all_to_all.10.own_ref = bf16[32,48,128]{2,1,0:T(8,128)(2,1)S(1)} all-to-all(bf16[32,48,128]{2,1,0:T(8,128)(2,1)S(1)} %spread.1), channel_id=1, replica_groups=mesh['lat'=4,'lon'=32,'tp'=2] {'lon'}, dimensions={0} | all-to-all | bytes 786432 | tf_op jit(solution)/shard_map/all_to_all | solution.py:696
  87.3 5.2 %collective-permute-start.14 = (bf16[32,48,128]{2,1,0:T(8,128)(2,1)S(1)}, bf16[32,48,128]{2,1,0:T(8,128)(2,1)S(1)}, u32[]{:S(2)}, u32[]{:S(2)}) collective-permute-start(bf16[32,48,128]{2,1,0:T(8,128)(2,1)S(1)} %all_to_all.10.own_ref), channel_id=1, source_target_pairs={{0,64},{64,0},{128,192},{192,128},{1,65},{65,1},{129,193},{193,129... | collective-permute-start | bytes 1179656 | tf_op jit(solution)/shard_map/ppermute | solution.py:648
  92.6 1.2 %finish.1 = bf16[6,12,8,192]{3,2,1,0:T(8,128)(2,1)} custom-call(bf16[144,192]{1,0:T(8,128)(2,1)S(1)} %copy-done.6, bf16[144,192]{1,0:T(8,128)(2,1)S(1)} %copy-done.7, bf16[144,192]{1,0:T(8,128)(2,1)S(1)} %copy-done.8, bf16[144,192]{1,0:T(8,128)(2,1)S(1)} %copy-done.17, bf16[144,192]{1,0:T(8,128)(2,1)S(1)} %get-tuple-element.58.m0, ...), custom_call_target="tpu_custom_call" | custom-call | flops 1000000000 | tf_op jit(solution)/shard_map/finish/pallas_call | solution.py:529
  93.8 0.1 collective-permute-done.14.other_ref
  93.9 1.2 %unpack.1 = (f32[3,192,96]{2,1,0:T(8,128)}, f32[96,192]{1,0:T(8,128)}, f32[192,384]{1,0:T(8,128)}, f32[192,384]{1,0:T(8,128)}, f32[1,96]{1,0:T(1,128)}, /*index=5*/f32[1,96]{1,0:T(1,128)}, f32[3,4,3312]{2,1,0:T(4,128)}) custom-call(bf16[32,48,128]{2,1,0:T(8,128)(2,1)S(1)} %all_to_all.10.own_ref, bf16[32,48,128]{2,1,0:T(8,128)(2,1)S(1)} %collective-permute-done.14.other_ref), custom_call_target="tpu_custom_call" | custom-call | tf_op jit(solution)/shard_map/unpack/pallas_call | solution.py:611
  (35 shorter events, 0.1 us)
Async XLA Ops:
  0.6 18.4 %copy-start.3 = (f32[1,4,3,3312]{3,1,2,0:T(4,128)S(1)}, f32[1,4,3,3312]{3,1,2,0:T(4,128)}, u32[]{:S(2)}) copy-start(f32[1,4,3,3312]{3,1,2,0:T(4,128)} %param.22) | copy-start | bytes 476932
  0.6 18.4 %copy-start.4 = (s32[144,144]{1,0:T(8,128)S(1)}, s32[144,144]{1,0:T(8,128)}, u32[]{:S(2)}) copy-start(s32[144,144]{1,0:T(8,128)} %index_ref.1) | copy-start | bytes 248836
  0.7 18.4 %copy-start.10 = (s32[8,6,12]{2,0,1:T(8,128)S(1)}, s32[8,6,12]{2,0,1:T(8,128)}, u32[]{:S(2)}) copy-start(s32[8,6,12]{2,0,1:T(8,128)} %param.19) | copy-start | bytes 6916
  0.7 18.4 %copy-start.11 = (s32[8,6,12]{2,0,1:T(8,128)S(1)}, s32[8,6,12]{2,0,1:T(8,128)}, u32[]{:S(2)}) copy-start(s32[8,6,12]{2,0,1:T(8,128)} %param.20) | copy-start | bytes 6916
  0.7 18.4 %copy-start.15 = (bf16[144,144]{1,0:T(8,128)(2,1)S(1)}, bf16[144,144]{1,0:T(8,128)(2,1)}, u32[]{:S(2)}) copy-start(bf16[144,144]{1,0:T(8,128)(2,1)} %constant.4.clone.order_ref) | copy-start | bytes 124420
  4.3 17.8 %copy-start = (bf16[8,6,12,192]{3,0,2,1:T(8,128)(2,1)S(1)}, bf16[8,6,12,192]{3,0,2,1:T(8,128)(2,1)}, u32[]{:S(2)}) copy-start(bf16[8,6,12,192]{3,0,2,1:T(8,128)(2,1)} %param.17) | copy-start | bytes 663556
  4.3 17.8 %copy-start.1 = (bf16[8,6,12,192]{3,0,2,1:T(8,128)(2,1)S(1)}, bf16[8,6,12,192]{3,0,2,1:T(8,128)(2,1)}, u32[]{:S(2)}) copy-start(bf16[8,6,12,192]{3,0,2,1:T(8,128)(2,1)} %param.18) | copy-start | bytes 663556
  4.4 17.8 %copy-start.2 = (bf16[576,192]{1,0:T(8,128)(2,1)S(1)}, bf16[576,192]{1,0:T(8,128)(2,1)}, u32[]{:S(2)}) copy-start(bf16[576,192]{1,0:T(8,128)(2,1)} %get-tuple-element.56.own_ref) | copy-start | bytes 663556
  4.4 17.7 %copy-start.12 = (f32[192]{0:T(256)S(1)}, f32[192]{0:T(256)}, u32[]{:S(2)}) copy-start(f32[192]{0:T(256)} %param.26) | copy-start | bytes 2308
  4.4 17.7 %collective-permute-start = (bf16[576,192]{1,0:T(8,128)(2,1)}, bf16[576,192]{1,0:T(8,128)(2,1)S(1)}, u32[]{:S(2)}, u32[]{:S(2)}) collective-permute-start(bf16[576,192]{1,0:T(8,128)(2,1)} %get-tuple-element.56.own_ref), channel_id=1, source_target_pairs={{1,0},{0,1},{3,2},{2,3},{5,4},{4,5},{7,6},{6,7},{9,8},{8,9},{11,10... | collective-permute-start | bytes 663560 | tf_op jit(solution)/shard_map/ppermute | solution.py:635
  6.6 16.7 %collective-permute-start.6 = (bf16[144,192]{1,0:T(8,128)(2,1)}, bf16[144,192]{1,0:T(8,128)(2,1)S(1)}, u32[]{:S(2)}, u32[]{:S(2)}) collective-permute-start(bf16[144,192]{1,0:T(8,128)(2,1)} %get-tuple-element.52.x0), channel_id=1, source_target_pairs={{66,0},{67,1},{68,2},{69,3},{70,4},{71,5},{72,6},{73,7},{74,8},{75... | collective-permute-start | bytes 165896 | tf_op jit(solution)/shard_map/ppermute | solution.py:635
  15.2 9.7 %collective-permute-start.5 = (bf16[144,192]{1,0:T(8,128)(2,1)}, bf16[144,192]{1,0:T(8,128)(2,1)S(1)}, u32[]{:S(2)}, u32[]{:S(2)}) collective-permute-start(bf16[144,192]{1,0:T(8,128)(2,1)} %get-tuple-element.53.x1), channel_id=1, source_target_pairs={{64,0},{65,1},{66,2},{67,3},{68,4},{69,5},{70,6},{71,7},{72,8},{73... | collective-permute-start | bytes 165896 | tf_op jit(solution)/shard_map/ppermute | solution.py:635
  17.1 9.2 %collective-permute-start.4 = (bf16[144,192]{1,0:T(8,128)(2,1)}, bf16[144,192]{1,0:T(8,128)(2,1)S(1)}, u32[]{:S(2)}, u32[]{:S(2)}) collective-permute-start(bf16[144,192]{1,0:T(8,128)(2,1)} %get-tuple-element.54.x2), channel_id=1, source_target_pairs={{2,0},{3,1},{4,2},{5,3},{6,4},{7,5},{8,6},{9,7},{10,8},{11,9},{12,... | collective-permute-start | bytes 165896 | tf_op jit(solution)/shard_map/ppermute | solution.py:635
  17.6 24.2 %collective-permute-start.11 = (bf16[576,128]{1,0:T(8,128)(2,1)}, bf16[576,128]{1,0:T(8,128)(2,1)S(1)}, u32[]{:S(2)}, u32[]{:S(2)}) collective-permute-start(bf16[576,128]{1,0:T(8,128)(2,1)} %get-tuple-element.79), channel_id=1, source_target_pairs={{0,64},{64,0},{128,192},{192,128},{1,65},{65,1},{129,193},{193,129... | collective-permute-start | bytes 442376 | tf_op jit(solution)/shard_map/ppermute | solution.py:648
  22.7 8.8 %collective-permute-start.3 = (bf16[144,192]{1,0:T(8,128)(2,1)S(1)}, bf16[144,192]{1,0:T(8,128)(2,1)S(1)}, u32[]{:S(2)}, u32[]{:S(2)}) collective-permute-start(bf16[144,192]{1,0:T(8,128)(2,1)S(1)} %get-tuple-element.58.m0), channel_id=1, source_target_pairs={{66,0},{67,1},{68,2},{69,3},{70,4},{71,5},{72,6},{73,7},{74,8},{75... | collective-permute-start | bytes 165896 | tf_op jit(solution)/shard_map/ppermute | solution.py:635
  23.3 8.3 %collective-permute-start.2 = (bf16[144,192]{1,0:T(8,128)(2,1)S(1)}, bf16[144,192]{1,0:T(8,128)(2,1)S(1)}, u32[]{:S(2)}, u32[]{:S(2)}) collective-permute-start(bf16[144,192]{1,0:T(8,128)(2,1)S(1)} %get-tuple-element.59.m1), channel_id=1, source_target_pairs={{64,0},{65,1},{66,2},{67,3},{68,4},{69,5},{70,6},{71,7},{72,8},{73... | collective-permute-start | bytes 165896 | tf_op jit(solution)/shard_map/ppermute | solution.py:635
  24.9 6.7 %collective-permute-start.1 = (bf16[144,192]{1,0:T(8,128)(2,1)S(1)}, bf16[144,192]{1,0:T(8,128)(2,1)S(1)}, u32[]{:S(2)}, u32[]{:S(2)}) collective-permute-start(bf16[144,192]{1,0:T(8,128)(2,1)S(1)} %get-tuple-element.60.m2), channel_id=1, source_target_pairs={{2,0},{3,1},{4,2},{5,3},{6,4},{7,5},{8,6},{9,7},{10,8},{11,9},{12,... | collective-permute-start | bytes 165896 | tf_op jit(solution)/shard_map/ppermute | solution.py:635
  26.3 2.2 %copy-start.5 = (bf16[3,192,96]{2,1,0:T(8,128)(2,1)S(1)}, bf16[3,192,96]{2,1,0:T(8,128)(2,1)}, u32[]{:S(2)}) copy-start(bf16[3,192,96]{2,1,0:T(8,128)(2,1)} %qkv_ref.3) | copy-start | bytes 331780
  26.3 2.2 %copy-start.13 = (f32[192]{0:T(256)S(1)}, f32[192]{0:T(256)}, u32[]{:S(2)}) copy-start(f32[192]{0:T(256)} %param.23) | copy-start | bytes 2308
  26.3 2.3 %copy-start.14 = (bf16[144,144]{1,0:T(8,128)(2,1)S(1)}, bf16[144,144]{1,0:T(8,128)(2,1)}, u32[]{:S(2)}) copy-start(bf16[144,144]{1,0:T(8,128)(2,1)} %constant.5.clone.order_ref) | copy-start | bytes 124420
  26.3 2.3 %copy-start.17 = (bf16[144,192]{1,0:T(8,128)(2,1)S(1)}, bf16[144,192]{1,0:T(8,128)(2,1)}, u32[]{:S(2)}) copy-start(bf16[144,192]{1,0:T(8,128)(2,1)} %get-tuple-element.55.x0.x3) | copy-start | bytes 165892
  28.5 3.1 %copy-start.9 = (bf16[96,192]{1,0:T(8,128)(2,1)S(1)}, bf16[96,192]{1,0:T(8,128)(2,1)}, u32[]{:S(2)}) copy-start(bf16[96,192]{1,0:T(8,128)(2,1)} %proj_ref.1) | copy-start | bytes 110596
  36.7 5.1 %collective-permute-start.12 = (bf16[288,128]{1,0:T(8,128)(2,1)S(1)}, bf16[288,128]{1,0:T(8,128)(2,1)S(1)}, u32[]{:S(2)}, u32[]{:S(2)}) collective-permute-start(bf16[288,128]{1,0:T(8,128)(2,1)S(1)} %get-tuple-element.85), channel_id=1, source_target_pairs={{0,64},{64,0},{128,192},{192,128},{1,65},{65,1},{129,193},{193,129... | collective-permute-start | bytes 221192 | tf_op jit(solution)/shard_map/ppermute | solution.py:648
  38.8 3.0 %copy-start.16 = (bf16[576,128]{1,0:T(8,128)(2,1)S(1)}, bf16[576,128]{1,0:T(8,128)(2,1)}, u32[]{:S(2)}) copy-start(bf16[576,128]{1,0:T(8,128)(2,1)} %get-tuple-element.78.first_ref) | copy-start | bytes 442372
  42.7 22.5 %all-to-all-start = ((bf16[32,40,128]{2,1,0:T(8,128)(2,1)}), bf16[32,40,128]{2,1,0:T(8,128)(2,1)S(1)}, u32[]{:S(2)}, u32[]{:S(2)}) async-start(bf16[32,40,128]{2,1,0:T(8,128)(2,1)} %bitcast.11), calls=%async_computation | async-start | bytes 655360 | tf_op jit(solution)/shard_map/all_to_all | solution.py:693
  46.6 8.6 %collective-permute-start.7 = (bf16[576,192]{1,0:T(8,128)(2,1)S(1)}, bf16[576,192]{1,0:T(8,128)(2,1)S(1)}, u32[]{:S(2)}, u32[]{:S(2)}) collective-permute-start(bf16[576,192]{1,0:T(8,128)(2,1)S(1)} %get-tuple-element.73.own_ref), channel_id=1, source_target_pairs={{1,0},{0,1},{3,2},{2,3},{5,4},{4,5},{7,6},{6,7},{9,8},{8,9},{11,10... | collective-permute-start | bytes 663560 | tf_op jit(solution)/shard_map/ppermute | solution.py:635
  55.5 8.4 %collective-permute-start.8 = (bf16[144,192]{1,0:T(8,128)(2,1)S(1)}, bf16[144,192]{1,0:T(8,128)(2,1)S(1)}, u32[]{:S(2)}, u32[]{:S(2)}) collective-permute-start(bf16[144,192]{1,0:T(8,128)(2,1)S(1)} %get-tuple-element.74), channel_id=1, source_target_pairs={{254,0},{255,1},{192,2},{193,3},{194,4},{195,5},{196,6},{197,7},{1... | collective-permute-start | bytes 165896 | tf_op jit(solution)/shard_map/ppermute | solution.py:635
  58.1 5.8 %collective-permute-start.9 = (bf16[144,192]{1,0:T(8,128)(2,1)S(1)}, bf16[144,192]{1,0:T(8,128)(2,1)S(1)}, u32[]{:S(2)}, u32[]{:S(2)}) collective-permute-start(bf16[144,192]{1,0:T(8,128)(2,1)S(1)} %get-tuple-element.75), channel_id=1, source_target_pairs={{192,0},{193,1},{194,2},{195,3},{196,4},{197,5},{198,6},{199,7},{2... | collective-permute-start | bytes 165896 | tf_op jit(solution)/shard_map/ppermute | solution.py:635
  58.1 7.0 %collective-permute-start.10 = (bf16[144,192]{1,0:T(8,128)(2,1)S(1)}, bf16[144,192]{1,0:T(8,128)(2,1)S(1)}, u32[]{:S(2)}, u32[]{:S(2)}) collective-permute-start(bf16[144,192]{1,0:T(8,128)(2,1)S(1)} %get-tuple-element.76), channel_id=1, source_target_pairs={{62,0},{63,1},{0,2},{1,3},{2,4},{3,5},{4,6},{5,7},{6,8},{7,9},{8,1... | collective-permute-start | bytes 165896 | tf_op jit(solution)/shard_map/ppermute | solution.py:635
  65.3 27.3 %copy-start.6 = (bf16[144,192]{1,0:T(8,128)(2,1)S(1)}, bf16[144,192]{1,0:T(8,128)(2,1)}, u32[]{:S(2)}) copy-start(bf16[144,192]{1,0:T(8,128)(2,1)} %get-tuple-element.52.x0) | copy-start | bytes 165892
  65.3 27.3 %copy-start.7 = (bf16[144,192]{1,0:T(8,128)(2,1)S(1)}, bf16[144,192]{1,0:T(8,128)(2,1)}, u32[]{:S(2)}) copy-start(bf16[144,192]{1,0:T(8,128)(2,1)} %get-tuple-element.53.x1) | copy-start | bytes 165892
  65.3 27.3 %copy-start.8 = (bf16[144,192]{1,0:T(8,128)(2,1)S(1)}, bf16[144,192]{1,0:T(8,128)(2,1)}, u32[]{:S(2)}) copy-start(bf16[144,192]{1,0:T(8,128)(2,1)} %get-tuple-element.54.x2) | copy-start | bytes 165892
  65.3 4.1 %collective-permute-start.13 = (bf16[48,128]{1,0:T(8,128)(2,1)S(1)}, bf16[48,128]{1,0:T(8,128)(2,1)S(1)}, u32[]{:S(2)}, u32[]{:S(2)}) collective-permute-start(bf16[48,128]{1,0:T(8,128)(2,1)S(1)} %add.1.own_ref), channel_id=1, source_target_pairs={{128,0},{129,1},{130,2},{131,3},{132,4},{133,5},{134,6},{135,7},{1... | collective-permute-start | bytes 36872 | tf_op jit(solution)/shard_map/ppermute | solution.py:635
  87.3 6.6 %collective-permute-start.14 = (bf16[32,48,128]{2,1,0:T(8,128)(2,1)S(1)}, bf16[32,48,128]{2,1,0:T(8,128)(2,1)S(1)}, u32[]{:S(2)}, u32[]{:S(2)}) collective-permute-start(bf16[32,48,128]{2,1,0:T(8,128)(2,1)S(1)} %all_to_all.10.own_ref), channel_id=1, source_target_pairs={{0,64},{64,0},{128,192},{192,128},{1,65},{65,1},{129,193},{193,129... | collective-permute-start | bytes 1179656 | tf_op jit(solution)/shard_map/ppermute | solution.py:648

commit v10 on v9

--- a/solution.py
+++ b/solution.py
@@ -448,7 +448,7 @@
     )(score, end, lo, hi, after)
 
 
-def weigh_kernel(low_ref, gcols, att_ref, grad_ref, keep_ref, send_ref, grads_ref):
+def weigh_kernel(low_ref, gcols, att_ref, grad_ref, first_ref, keep_ref, send_ref, grads_ref):
     gproj = dot_tn(att_ref[...], grad_ref[...]).astype(BF)
     grads_ref[0:96, :] = gproj[:, 0:128]
     grads_ref[96:144, :] = jnp.concatenate([gproj[0:48, 128:192], gproj[48:96, 128:192]], axis=1)
@@ -459,18 +459,19 @@
     grads_ref[528:576, :] = jnp.concatenate([c[i * 48 : i * 48 + 48, 64:96] for i in range(4)], axis=1)
     core = lax.rem(lax.axis_index("lat"), 2)
     keep_ref[...] = grads_ref[pl.ds(pl.multiple_of(core * 288, 16), 288), :]
-    send_ref[...] = grads_ref[pl.ds(pl.multiple_of((1 - core) * 288, 16), 288), :]
-
-
-def weigh(low, gcols, att, grad):
+    send_ref[0:576, :] = first_ref[...]
+    send_ref[576:864, :] = grads_ref[pl.ds(pl.multiple_of((1 - core) * 288, 16), 288), :]
+
+
+def weigh(low, gcols, att, grad, first):
     return pl.pallas_call(
         weigh_kernel,
-        out_shape=(shape((288, 128), BF), shape((288, 128), BF)),
+        out_shape=(shape((288, 128), BF), shape((864, 128), BF)),
         scratch_shapes=[pltpu.VMEM((576, 128), BF)],
         compiler_params=VM,
         cost_estimate=cost(0.5),
         name="weigh",
-    )(low, gcols, att, grad)
+    )(low, gcols, att, grad, first)
 
 
 def gain_rows(line):
@@ -478,9 +479,9 @@
     return [line[:, 0:128], jnp.concatenate([line[:, 128:192], none], axis=1)]
 
 
-def pack_kernel(first_ref, first_other, second_ref, second_other, table_ref, gain_ref, out_ref):
-    out_ref[0:576, :] = both(first_ref[...], first_other[...])
-    out_ref[576:864, :] = both(second_ref[...], second_other[...])
+def pack_kernel(first_ref, second_ref, other_ref, table_ref, gain_ref, out_ref):
+    out_ref[0:576, :] = both(first_ref[...], other_ref[0:576, :])
+    out_ref[576:864, :] = both(second_ref[...], other_ref[576:864, :])
     rows = []
     for r in range(12):
         pair = table_ref[r * 16 : r * 16 + 13, :]
@@ -489,10 +490,10 @@
     out_ref[864:1280, :] = jnp.concatenate(rows, axis=0).astype(BF)
 
 
-def pack(first, first_other, second, second_other, table, gain):
+def pack(first, second, other, table, gain):
     return pl.pallas_call(
         pack_kernel, out_shape=shape((1280, 128), BF), compiler_params=VM, cost_estimate=cost(1), name="pack"
-    )(first, first_other, second, second_other, table, gain)
+    )(first, second, other, table, gain)
 
 
 def meet_kernel(own_ref, other_ref, x0, x1, x2, x3, g0, g1, g2, g3, gain_out):
@@ -511,7 +512,7 @@
         meet_kernel,
         out_shape=tuple(shape((144, 192), BF) for _ in range(4)) + (shape((8, 128), F32),),
         compiler_params=VM,
-        cost_estimate=cost(1),
+        cost_estimate=cost(60),
         name="meet",
     )(own, other, *x)
 
@@ -685,9 +686,9 @@
     low, q, k, v, prob, att = forward(xw, gain1, qkv_weight, main, tail, code)
     part1, score, end, gcols, grad = backward(gw, proj_weight, qkv_weight, q, k, v, prob)
     other1 = moved(part1, 0, 0, 1)
-    second, second_send = weigh(low, gcols, att, grad)
+    second, send = weigh(low, gcols, att, grad, first_send)
     table = scatter(score, end, lo, hi, second)
-    sums = pack(first, other_core(first_send), second, other_core(second_send), table, gain_two)
+    sums = pack(first, second, other_core(send), table, gain_two)
     *g, gain_one = meet(part1, other1, xw)
     back = (moved(g[3], -1, -1, 0), moved(g[2], -1, 0, 0), moved(g[1], 0, -1, 0), g[0])
     own = add(lax.all_to_all(sums.reshape(32, 40, 128), "lon", 0, 0), gain_one, back[:3])

time: 95.3 us -> 90.3 us (0.948)
  waiting for transfers between devices: 16 us -> 13.2 us
  blocking collectives: 17.9 us -> 16.3 us
    ppermute x12, waiting for transfers between devices: 15.9 us -> 13.1 us  [moved(): return lax.ppermute(value, ('lat', 'lon', 'tp'), pairs)]
    ppermute x3 -> x2, starting transfers between devices: 8.65 us -> 6.73 us  [other_core(): lax.ppermute(value, 'lat', [(a, a ^ 1) for a in range(lax.axis_size('lat'...]
    all_to_all x1, blocking collectives: 17.9 us -> 16.3 us  [local(): got = lax.all_to_all(totals, 'lon', 0, 0)]
    ppermute x12, starting transfers between devices: 23.3 us -> 24.3 us  [moved(): return lax.ppermute(value, ('lat', 'lon', 'tp'), pairs)]
  transfers between devices with their start and end apart: 16 -> 15, of which waited for: 5 -> 4; matrix products, arithmetic and copies ran while one was open for 0% -> 0% of each run, Pallas kernels for 20% -> 16%
where the time goes in v10:
time: 90.3 us; the launch traced here: 90.1 us
  starting transfers between devices  35.1 us (39%)
  Pallas kernels  24.3 us (27%)
  blocking collectives  16.3 us (18%)
  waiting for transfers between devices  13.2 us (15%)
  between operations  0.99 us (1%)
    ppermute x12, starting transfers between devices, moved(): return lax.ppermute(value, ('lat', 'lon', 'tp'), pairs)  24.3 us
    all_to_all x1, blocking collectives, local(): got = lax.all_to_all(totals, 'lon', 0, 0)  16.3 us
    ppermute x12, waiting for transfers between devices, moved(): return lax.ppermute(value, ('lat', 'lon', 'tp'), pairs)  13.1 us
    ppermute x2, starting transfers between devices, other_core(): lax.ppermute(value, 'lat', [(a, a ^ 1) for a in range(lax.axis_size('lat'...  6.73 us
    pallas_call x1, Pallas kernels, backward(): pl.pallas_call(backward_kernel, out_shape=(shape((576, 192), BF), shape((...  4.61 us
    all_to_all x1, starting transfers between devices, local(): lax.all_to_all(sums.reshape(32, 40, 128), 'lon', 0, 0)  4.1 us
    pallas_call x1, Pallas kernels, head(): pl.pallas_call(head_kernel, out_shape=tuple((shape((144, 192), BF) for _...  3.63 us
    pallas_call x1, Pallas kernels, scatter(): pl.pallas_call(scatter_kernel, out_shape=shape((192, 256), F32), in_specs...  3.02 us
  transfers between devices with their start and end apart: 15, of which 4 were waited for; matrix products, arithmetic and copies ran while one was open for 0% of the time, Pallas kernels for 16%

profile of v10, /device:TPU:1, one launch (start us, length us, event | category | flops | bytes accessed | tf_op | source)
XLA Modules:
  0.0 90.1 jit_solution(16093633311533309188)
XLA Ops:
  0.7 0.0 copy-start.15
  0.7 3.6 %head.1 = (bf16[144,192]{1,0:T(8,128)(2,1)}, bf16[144,192]{1,0:T(8,128)(2,1)}, bf16[144,192]{1,0:T(8,128)(2,1)}, bf16[144,192]{1,0:T(8,128)(2,1)}, bf16[576,192]...) custom-call(bf16[6,12,8,192]{3,2,1,0:T(8,128)(2,1)} %bitcast.30, ...), custom_call_target="tpu_custom_call" | custom-call | flops 3000000000 | tf_op jit(solution)/shard_map/head/pallas_call | solution.py:139
  4.3 0.0 copy-start
  4.3 0.0 copy-start.1
  4.4 0.0 copy-start.2
  4.4 0.0 copy-start.12
  4.4 2.2 %collective-permute-start = (bf16[576,192]{1,0:T(8,128)(2,1)}, bf16[576,192]{1,0:T(8,128)(2,1)S(1)}, u32[]{:S(2)}, u32[]{:S(2)}) collective-permute-start(bf16[576,192]{1,0:T(8,128)(2,1)} %get-tuple-element.56.own_ref), channel_id=1, source_target_pairs={{1,0},{0,1},{3,2},{2,3},{5,4},{4,5},{7,6},{6,7},{9,8},{8,9},{11,10... | collective-permute-start | bytes 663560 | tf_op jit(solution)/shard_map/ppermute | solution.py:636
  6.6 8.6 %collective-permute-start.6 = (bf16[144,192]{1,0:T(8,128)(2,1)}, bf16[144,192]{1,0:T(8,128)(2,1)S(1)}, u32[]{:S(2)}, u32[]{:S(2)}) collective-permute-start(bf16[144,192]{1,0:T(8,128)(2,1)} %get-tuple-element.52.x0), channel_id=1, source_target_pairs={{66,0},{67,1},{68,2},{69,3},{70,4},{71,5},{72,6},{73,7},{74,8},{75... | collective-permute-start | bytes 165896 | tf_op jit(solution)/shard_map/ppermute | solution.py:636
  15.2 1.9 %collective-permute-start.5 = (bf16[144,192]{1,0:T(8,128)(2,1)}, bf16[144,192]{1,0:T(8,128)(2,1)S(1)}, u32[]{:S(2)}, u32[]{:S(2)}) collective-permute-start(bf16[144,192]{1,0:T(8,128)(2,1)} %get-tuple-element.53.x1), channel_id=1, source_target_pairs={{64,0},{65,1},{66,2},{67,3},{68,4},{69,5},{70,6},{71,7},{72,8},{73... | collective-permute-start | bytes 165896 | tf_op jit(solution)/shard_map/ppermute | solution.py:636
  17.1 0.6 collective-permute-start.4
  17.7 3.0 %gather_first.1 = (f32[1440,128]{1,0:T(8,128)S(1)}, s32[168,128]{1,0:T(8,128)S(1)}, s32[168,128]{1,0:T(8,128)S(1)}, bf16[160,512]{1,0:T(8,128)(2,1)S(1)}, f32[4,144]{1,0:T(4,128)S(1)}) custom-call(s32[144,144]{1,0:T(8,128)S(1)} %copy-done.4, bf16[144,144]{1,0:T(8,128)(2,1)S(1)} %copy-done.15, f32[3,4,3312]{2,1,0:T(4,128)S(1)} %bitcast.23, ...), custom_call_target="tpu_custom_call" | custom-call | flops 500000000 | tf_op jit(solution)/shard_map/gather_first/pallas_call | solution.py:272
  20.7 0.0 collective-permute-done.other_ref
  20.7 0.6 middle.1
  21.3 2.0 %collective-permute-start.3 = (bf16[144,192]{1,0:T(8,128)(2,1)S(1)}, bf16[144,192]{1,0:T(8,128)(2,1)S(1)}, u32[]{:S(2)}, u32[]{:S(2)}) collective-permute-start(bf16[144,192]{1,0:T(8,128)(2,1)S(1)} %get-tuple-element.58.m0), channel_id=1, source_target_pairs={{66,0},{67,1},{68,2},{69,3},{70,4},{71,5},{72,6},{73,7},{74,8},{75... | collective-permute-start | bytes 165896 | tf_op jit(solution)/shard_map/ppermute | solution.py:636
  23.3 1.6 %collective-permute-start.2 = (bf16[144,192]{1,0:T(8,128)(2,1)S(1)}, bf16[144,192]{1,0:T(8,128)(2,1)S(1)}, u32[]{:S(2)}, u32[]{:S(2)}) collective-permute-start(bf16[144,192]{1,0:T(8,128)(2,1)S(1)} %get-tuple-element.59.m1), channel_id=1, source_target_pairs={{64,0},{65,1},{66,2},{67,3},{68,4},{69,5},{70,6},{71,7},{72,8},{73... | collective-permute-start | bytes 165896 | tf_op jit(solution)/shard_map/ppermute | solution.py:636
  24.9 0.0 collective-permute-done.6.a3.x3
  24.9 1.4 %collective-permute-start.1 = (bf16[144,192]{1,0:T(8,128)(2,1)S(1)}, bf16[144,192]{1,0:T(8,128)(2,1)S(1)}, u32[]{:S(2)}, u32[]{:S(2)}) collective-permute-start(bf16[144,192]{1,0:T(8,128)(2,1)S(1)} %get-tuple-element.60.m2), channel_id=1, source_target_pairs={{2,0},{3,1},{4,2},{5,3},{6,4},{7,5},{8,6},{9,7},{10,8},{11,9},{12,... | collective-permute-start | bytes 165896 | tf_op jit(solution)/shard_map/ppermute | solution.py:636
  26.2 0.0 collective-permute-done.5.a2.x2
  26.2 0.0 copy-start.13
  26.2 0.0 copy-start.14
  26.3 2.2 %gather_second.1 = (f32[12,144,128]{2,1,0:T(8,128)S(1)}, f32[12,144,128]{2,1,0:T(8,128)S(1)}) custom-call(f32[1440,128]{1,0:T(8,128)S(1)} %get-tuple-element.62.first_stage, s32[168,128]{1,0:T(8,128)S(1)} %get-tuple-element.57.after_ref.lo_ref, s32[168,128]{1,0:T(8,128)S(1)} %get-tuple-element.63.hi_ref, bf16[160,512]{1,0:T(8,128)(2,1)S(1)} %get-tuple-element.64.terms_ref, ...), custom_call_target="tpu_custom_call" | custom-call | flops 4000000000 | tf_op jit(solution)/shard_map/gather_second/pallas_call | solution.py:299
  28.5 0.0 copy-start.9
  28.5 3.0 %forward.1 = (bf16[576,192]{1,0:T(8,128)(2,1)S(1)}, bf16[576,96]{1,0:T(8,128)(2,1)S(1)}, bf16[576,96]{1,0:T(8,128)(2,1)S(1)}, bf16[576,96]{1,0:T(8,128)(2,1)S(1)...) custom-call(bf16[144,192]{1,0:T(8,128)(2,1)S(1)} %copy-done.18, ...), custom_call_target="tpu_custom_call" | custom-call | flops 5000000000 | tf_op jit(solution)/shard_map/forward/pallas_call | solution.py:344
  31.5 0.0 collective-permute-done.3.g3
  31.6 0.0 collective-permute-done.1.g1
  31.6 0.0 copy-start.16
  31.6 4.6 %backward.1 = (bf16[576,192]{1,0:T(8,128)(2,1)S(1)}, f32[12,144,128]{2,1,0:T(8,128)S(1)}, f32[12,144,128]{2,1,0:T(8,128)S(1)}, bf16[3,576,96]{2,1,0:T(8,128)(2,1)S(1)}, bf16[576,192]{1,0:T(8,128)(2,1)S(1)}) custom-call(bf16[144,192]{1,0:T(8,128)(2,1)S(1)} %get-tuple-element.61.g0.m3, bf16[144,192]{1,0:T(8,128)(2,1)S(1)} %collective-permute-done.1.g1, ...), custom_call_target="tpu_custom_call" | custom-call | flops 7000000000 | tf_op jit(solution)/shard_map/backward/pallas_call | solution.py:401
  36.2 0.6 weigh.1
  36.8 2.1 %collective-permute-start.11 = (bf16[864,128]{1,0:T(8,128)(2,1)S(1)}, bf16[864,128]{1,0:T(8,128)(2,1)S(1)}, u32[]{:S(2)}, u32[]{:S(2)}) collective-permute-start(bf16[864,128]{1,0:T(8,128)(2,1)S(1)} %get-tuple-element.85), channel_id=1, source_target_pairs={{0,64},{64,0},{128,192},{192,128},{1,65},{65,1},{129,193},{193,129... | collective-permute-start | bytes 663560 | tf_op jit(solution)/shard_map/ppermute | solution.py:649
  38.8 0.4 collective-permute-start.7
  39.3 3.0 %scatter.1.table_ref = f32[192,256]{1,0:T(8,128)S(1)} custom-call(f32[12,144,128]{2,1,0:T(8,128)S(1)} %get-tuple-element.86.score_ref, f32[12,144,128]{2,1,0:T(8,128)S(1)} %get-tuple-element.87.end_ref, s32[168,128]{1,0:T(8,128)S(1)} %get-tuple-element.57.after_ref.lo_ref, s32[168,128]{1,0:T(8,128)S(1)} %get-tuple-element.63.hi_ref, ...), custom_call_target="tpu_custom_call" | custom-call | flops 4000000000 | tf_op jit(solution)/shard_map/scatter/pallas_call | solution.py:440
  42.3 0.8 pack.1
  43.1 4.1 %all-to-all-start = ((bf16[32,40,128]{2,1,0:T(8,128)(2,1)}), bf16[32,40,128]{2,1,0:T(8,128)(2,1)S(1)}, u32[]{:S(2)}, u32[]{:S(2)}) async-start(bf16[32,40,128]{2,1,0:T(8,128)(2,1)} %bitcast.11), calls=%async_computation | async-start | bytes 655360 | tf_op jit(solution)/shard_map/all_to_all | solution.py:694
  47.2 0.2 collective-permute-done.7.other_ref
  47.4 0.3 meet.1
  47.8 2.9 %collective-permute-start.8 = (bf16[144,192]{1,0:T(8,128)(2,1)S(1)}, bf16[144,192]{1,0:T(8,128)(2,1)S(1)}, u32[]{:S(2)}, u32[]{:S(2)}) collective-permute-start(bf16[144,192]{1,0:T(8,128)(2,1)S(1)} %get-tuple-element.74), channel_id=1, source_target_pairs={{254,0},{255,1},{192,2},{193,3},{194,4},{195,5},{196,6},{197,7},{1... | collective-permute-start | bytes 165896 | tf_op jit(solution)/shard_map/ppermute | solution.py:636
  50.7 1.2 %collective-permute-start.10 = (bf16[144,192]{1,0:T(8,128)(2,1)S(1)}, bf16[144,192]{1,0:T(8,128)(2,1)S(1)}, u32[]{:S(2)}, u32[]{:S(2)}) collective-permute-start(bf16[144,192]{1,0:T(8,128)(2,1)S(1)} %get-tuple-element.76), channel_id=1, source_target_pairs={{62,0},{63,1},{0,2},{1,3},{2,4},{3,5},{4,6},{5,7},{6,8},{7,9},{8,1... | collective-permute-start | bytes 165896 | tf_op jit(solution)/shard_map/ppermute | solution.py:636
  51.9 10.4 %collective-permute-done.8.g0.b0 = bf16[144,192]{1,0:T(8,128)(2,1)S(1)} collective-permute-done((bf16[144,192]{1,0:T(8,128)(2,1)S(1)}, bf16[144,192]{1,0:T(8,128)(2,1)S(1)}, u32[]{:S(2)}, u32[]{:S(2)}) %collective-permute-start.8) | collective-permute-done | bytes 55328 | tf_op jit(solution)/shard_map/ppermute | solution.py:636
  62.3 0.1 add.1.own_ref
  62.4 0.0 copy-start.7
  62.4 0.0 copy-start.8
  62.4 1.6 %collective-permute-start.12 = (bf16[48,128]{1,0:T(8,128)(2,1)S(1)}, bf16[48,128]{1,0:T(8,128)(2,1)S(1)}, u32[]{:S(2)}, u32[]{:S(2)}) collective-permute-start(bf16[48,128]{1,0:T(8,128)(2,1)S(1)} %add.1.own_ref), channel_id=1, source_target_pairs={{128,0},{129,1},{130,2},{131,3},{132,4},{133,5},{134,6},{135,7},{1... | collective-permute-start | bytes 36872 | tf_op jit(solution)/shard_map/ppermute | solution.py:636
  64.0 2.5 %collective-permute-done.12.other_ref = bf16[48,128]{1,0:T(8,128)(2,1)S(1)} collective-permute-done((bf16[48,128]{1,0:T(8,128)(2,1)S(1)}, bf16[48,128]{1,0:T(8,128)(2,1)S(1)}, u32[]{:S(2)}, u32[]{:S(2)}) %collective-permute-start.12) | collective-permute-done | bytes 12320 | tf_op jit(solution)/shard_map/ppermute | solution.py:636
  66.6 16.3 %all_to_all.10.own_ref = bf16[32,48,128]{2,1,0:T(8,128)(2,1)S(1)} all-to-all(bf16[32,48,128]{2,1,0:T(8,128)(2,1)S(1)} %spread.1), channel_id=1, replica_groups=mesh['lat'=4,'lon'=32,'tp'=2] {'lon'}, dimensions={0} | all-to-all | bytes 786432 | tf_op jit(solution)/shard_map/all_to_all | solution.py:697
  82.9 4.7 %collective-permute-start.13 = (bf16[32,48,128]{2,1,0:T(8,128)(2,1)S(1)}, bf16[32,48,128]{2,1,0:T(8,128)(2,1)S(1)}, u32[]{:S(2)}, u32[]{:S(2)}) collective-permute-start(bf16[32,48,128]{2,1,0:T(8,128)(2,1)S(1)} %all_to_all.10.own_ref), channel_id=1, source_target_pairs={{0,64},{64,0},{128,192},{192,128},{1,65},{65,1},{129,193},{193,129... | collective-permute-start | bytes 1179656 | tf_op jit(solution)/shard_map/ppermute | solution.py:649
  87.6 1.2 %finish.1 = bf16[6,12,8,192]{3,2,1,0:T(8,128)(2,1)} custom-call(bf16[144,192]{1,0:T(8,128)(2,1)S(1)} %copy-done.6, bf16[144,192]{1,0:T(8,128)(2,1)S(1)} %copy-done.7, bf16[144,192]{1,0:T(8,128)(2,1)S(1)} %copy-done.8, bf16[144,192]{1,0:T(8,128)(2,1)S(1)} %copy-done.18, bf16[144,192]{1,0:T(8,128)(2,1)S(1)} %get-tuple-element.58.m0, ...), custom_call_target="tpu_custom_call" | custom-call | flops 1000000000 | tf_op jit(solution)/shard_map/finish/pallas_call | solution.py:530
  88.8 0.1 collective-permute-done.13.other_ref
  88.9 1.2 %unpack.1 = (f32[3,192,96]{2,1,0:T(8,128)}, f32[96,192]{1,0:T(8,128)}, f32[192,384]{1,0:T(8,128)}, f32[192,384]{1,0:T(8,128)}, f32[1,96]{1,0:T(1,128)}, /*index=5*/f32[1,96]{1,0:T(1,128)}, f32[3,4,3312]{2,1,0:T(4,128)}) custom-call(bf16[32,48,128]{2,1,0:T(8,128)(2,1)S(1)} %all_to_all.10.own_ref, bf16[32,48,128]{2,1,0:T(8,128)(2,1)S(1)} %collective-permute-done.13.other_ref), custom_call_target="tpu_custom_call" | custom-call | tf_op jit(solution)/shard_map/unpack/pallas_call | solution.py:612
  (35 shorter events, 0.1 us)
Async XLA Ops:
  0.6 17.0 %copy-start.3 = (f32[1,4,3,3312]{3,1,2,0:T(4,128)S(1)}, f32[1,4,3,3312]{3,1,2,0:T(4,128)}, u32[]{:S(2)}) copy-start(f32[1,4,3,3312]{3,1,2,0:T(4,128)} %param.22) | copy-start | bytes 476932
  0.6 17.0 %copy-start.4 = (s32[144,144]{1,0:T(8,128)S(1)}, s32[144,144]{1,0:T(8,128)}, u32[]{:S(2)}) copy-start(s32[144,144]{1,0:T(8,128)} %index_ref.1) | copy-start | bytes 248836
  0.7 17.0 %copy-start.10 = (s32[8,6,12]{2,0,1:T(8,128)S(1)}, s32[8,6,12]{2,0,1:T(8,128)}, u32[]{:S(2)}) copy-start(s32[8,6,12]{2,0,1:T(8,128)} %param.19) | copy-start | bytes 6916
  0.7 17.0 %copy-start.11 = (s32[8,6,12]{2,0,1:T(8,128)S(1)}, s32[8,6,12]{2,0,1:T(8,128)}, u32[]{:S(2)}) copy-start(s32[8,6,12]{2,0,1:T(8,128)} %param.20) | copy-start | bytes 6916
  0.7 17.0 %copy-start.15 = (bf16[144,144]{1,0:T(8,128)(2,1)S(1)}, bf16[144,144]{1,0:T(8,128)(2,1)}, u32[]{:S(2)}) copy-start(bf16[144,144]{1,0:T(8,128)(2,1)} %constant.4.clone.order_ref) | copy-start | bytes 124420
  4.3 16.4 %copy-start = (bf16[8,6,12,192]{3,0,2,1:T(8,128)(2,1)S(1)}, bf16[8,6,12,192]{3,0,2,1:T(8,128)(2,1)}, u32[]{:S(2)}) copy-start(bf16[8,6,12,192]{3,0,2,1:T(8,128)(2,1)} %param.17) | copy-start | bytes 663556
  4.3 16.4 %copy-start.1 = (bf16[8,6,12,192]{3,0,2,1:T(8,128)(2,1)S(1)}, bf16[8,6,12,192]{3,0,2,1:T(8,128)(2,1)}, u32[]{:S(2)}) copy-start(bf16[8,6,12,192]{3,0,2,1:T(8,128)(2,1)} %param.18) | copy-start | bytes 663556
  4.4 16.4 %copy-start.2 = (bf16[576,192]{1,0:T(8,128)(2,1)S(1)}, bf16[576,192]{1,0:T(8,128)(2,1)}, u32[]{:S(2)}) copy-start(bf16[576,192]{1,0:T(8,128)(2,1)} %get-tuple-element.56.own_ref) | copy-start | bytes 663556
  4.4 16.4 %copy-start.12 = (f32[192]{0:T(256)S(1)}, f32[192]{0:T(256)}, u32[]{:S(2)}) copy-start(f32[192]{0:T(256)} %param.26) | copy-start | bytes 2308
  4.4 16.3 %collective-permute-start = (bf16[576,192]{1,0:T(8,128)(2,1)}, bf16[576,192]{1,0:T(8,128)(2,1)S(1)}, u32[]{:S(2)}, u32[]{:S(2)}) collective-permute-start(bf16[576,192]{1,0:T(8,128)(2,1)} %get-tuple-element.56.own_ref), channel_id=1, source_target_pairs={{1,0},{0,1},{3,2},{2,3},{5,4},{4,5},{7,6},{6,7},{9,8},{8,9},{11,10... | collective-permute-start | bytes 663560 | tf_op jit(solution)/shard_map/ppermute | solution.py:636
  6.6 18.3 %collective-permute-start.6 = (bf16[144,192]{1,0:T(8,128)(2,1)}, bf16[144,192]{1,0:T(8,128)(2,1)S(1)}, u32[]{:S(2)}, u32[]{:S(2)}) collective-permute-start(bf16[144,192]{1,0:T(8,128)(2,1)} %get-tuple-element.52.x0), channel_id=1, source_target_pairs={{66,0},{67,1},{68,2},{69,3},{70,4},{71,5},{72,6},{73,7},{74,8},{75... | collective-permute-start | bytes 165896 | tf_op jit(solution)/shard_map/ppermute | solution.py:636
  15.2 11.0 %collective-permute-start.5 = (bf16[144,192]{1,0:T(8,128)(2,1)}, bf16[144,192]{1,0:T(8,128)(2,1)S(1)}, u32[]{:S(2)}, u32[]{:S(2)}) collective-permute-start(bf16[144,192]{1,0:T(8,128)(2,1)} %get-tuple-element.53.x1), channel_id=1, source_target_pairs={{64,0},{65,1},{66,2},{67,3},{68,4},{69,5},{70,6},{71,7},{72,8},{73... | collective-permute-start | bytes 165896 | tf_op jit(solution)/shard_map/ppermute | solution.py:636
  17.1 9.1 %collective-permute-start.4 = (bf16[144,192]{1,0:T(8,128)(2,1)}, bf16[144,192]{1,0:T(8,128)(2,1)S(1)}, u32[]{:S(2)}, u32[]{:S(2)}) collective-permute-start(bf16[144,192]{1,0:T(8,128)(2,1)} %get-tuple-element.54.x2), channel_id=1, source_target_pairs={{2,0},{3,1},{4,2},{5,3},{6,4},{7,5},{8,6},{9,7},{10,8},{11,9},{12,... | collective-permute-start | bytes 165896 | tf_op jit(solution)/shard_map/ppermute | solution.py:636
  21.3 10.2 %collective-permute-start.3 = (bf16[144,192]{1,0:T(8,128)(2,1)S(1)}, bf16[144,192]{1,0:T(8,128)(2,1)S(1)}, u32[]{:S(2)}, u32[]{:S(2)}) collective-permute-start(bf16[144,192]{1,0:T(8,128)(2,1)S(1)} %get-tuple-element.58.m0), channel_id=1, source_target_pairs={{66,0},{67,1},{68,2},{69,3},{70,4},{71,5},{72,6},{73,7},{74,8},{75... | collective-permute-start | bytes 165896 | tf_op jit(solution)/shard_map/ppermute | solution.py:636
  23.3 8.3 %collective-permute-start.2 = (bf16[144,192]{1,0:T(8,128)(2,1)S(1)}, bf16[144,192]{1,0:T(8,128)(2,1)S(1)}, u32[]{:S(2)}, u32[]{:S(2)}) collective-permute-start(bf16[144,192]{1,0:T(8,128)(2,1)S(1)} %get-tuple-element.59.m1), channel_id=1, source_target_pairs={{64,0},{65,1},{66,2},{67,3},{68,4},{69,5},{70,6},{71,7},{72,8},{73... | collective-permute-start | bytes 165896 | tf_op jit(solution)/shard_map/ppermute | solution.py:636
  24.9 6.7 %collective-permute-start.1 = (bf16[144,192]{1,0:T(8,128)(2,1)S(1)}, bf16[144,192]{1,0:T(8,128)(2,1)S(1)}, u32[]{:S(2)}, u32[]{:S(2)}) collective-permute-start(bf16[144,192]{1,0:T(8,128)(2,1)S(1)} %get-tuple-element.60.m2), channel_id=1, source_target_pairs={{2,0},{3,1},{4,2},{5,3},{6,4},{7,5},{8,6},{9,7},{10,8},{11,9},{12,... | collective-permute-start | bytes 165896 | tf_op jit(solution)/shard_map/ppermute | solution.py:636
  26.2 2.3 %copy-start.5 = (bf16[3,192,96]{2,1,0:T(8,128)(2,1)S(1)}, bf16[3,192,96]{2,1,0:T(8,128)(2,1)}, u32[]{:S(2)}) copy-start(bf16[3,192,96]{2,1,0:T(8,128)(2,1)} %qkv_ref.3) | copy-start | bytes 331780
  26.2 2.3 %copy-start.13 = (f32[192]{0:T(256)S(1)}, f32[192]{0:T(256)}, u32[]{:S(2)}) copy-start(f32[192]{0:T(256)} %param.23) | copy-start | bytes 2308
  26.2 2.3 %copy-start.14 = (bf16[144,144]{1,0:T(8,128)(2,1)S(1)}, bf16[144,144]{1,0:T(8,128)(2,1)}, u32[]{:S(2)}) copy-start(bf16[144,144]{1,0:T(8,128)(2,1)} %constant.5.clone.order_ref) | copy-start | bytes 124420
  26.3 2.3 %copy-start.18 = (bf16[144,192]{1,0:T(8,128)(2,1)S(1)}, bf16[144,192]{1,0:T(8,128)(2,1)}, u32[]{:S(2)}) copy-start(bf16[144,192]{1,0:T(8,128)(2,1)} %get-tuple-element.55.x0.x3) | copy-start | bytes 165892
  28.5 3.1 %copy-start.9 = (bf16[96,192]{1,0:T(8,128)(2,1)S(1)}, bf16[96,192]{1,0:T(8,128)(2,1)}, u32[]{:S(2)}) copy-start(bf16[96,192]{1,0:T(8,128)(2,1)} %proj_ref.1) | copy-start | bytes 110596
  31.6 4.6 %copy-start.16 = (bf16[576,128]{1,0:T(8,128)(2,1)S(1)}, bf16[576,128]{1,0:T(8,128)(2,1)}, u32[]{:S(2)}) copy-start(bf16[576,128]{1,0:T(8,128)(2,1)} %get-tuple-element.83.first_ref) | copy-start | bytes 442372
  36.8 5.5 %collective-permute-start.11 = (bf16[864,128]{1,0:T(8,128)(2,1)S(1)}, bf16[864,128]{1,0:T(8,128)(2,1)S(1)}, u32[]{:S(2)}, u32[]{:S(2)}) collective-permute-start(bf16[864,128]{1,0:T(8,128)(2,1)S(1)} %get-tuple-element.85), channel_id=1, source_target_pairs={{0,64},{64,0},{128,192},{192,128},{1,65},{65,1},{129,193},{193,129... | collective-permute-start | bytes 663560 | tf_op jit(solution)/shard_map/ppermute | solution.py:649
  38.8 8.6 %collective-permute-start.7 = (bf16[576,192]{1,0:T(8,128)(2,1)S(1)}, bf16[576,192]{1,0:T(8,128)(2,1)S(1)}, u32[]{:S(2)}, u32[]{:S(2)}) collective-permute-start(bf16[576,192]{1,0:T(8,128)(2,1)S(1)} %get-tuple-element.73.own_ref), channel_id=1, source_target_pairs={{1,0},{0,1},{3,2},{2,3},{5,4},{4,5},{7,6},{6,7},{9,8},{8,9},{11,10... | collective-permute-start | bytes 663560 | tf_op jit(solution)/shard_map/ppermute | solution.py:636
  39.3 3.0 %copy-start.17 = (bf16[576,128]{1,0:T(8,128)(2,1)S(1)}, bf16[576,128]{1,0:T(8,128)(2,1)}, u32[]{:S(2)}) copy-start(bf16[576,128]{1,0:T(8,128)(2,1)} %get-tuple-element.78.first_ref) | copy-start | bytes 442372
  43.1 19.1 %all-to-all-start = ((bf16[32,40,128]{2,1,0:T(8,128)(2,1)}), bf16[32,40,128]{2,1,0:T(8,128)(2,1)S(1)}, u32[]{:S(2)}, u32[]{:S(2)}) async-start(bf16[32,40,128]{2,1,0:T(8,128)(2,1)} %bitcast.11), calls=%async_computation | async-start | bytes 655360 | tf_op jit(solution)/shard_map/all_to_all | solution.py:694
  47.8 14.5 %collective-permute-start.8 = (bf16[144,192]{1,0:T(8,128)(2,1)S(1)}, bf16[144,192]{1,0:T(8,128)(2,1)S(1)}, u32[]{:S(2)}, u32[]{:S(2)}) collective-permute-start(bf16[144,192]{1,0:T(8,128)(2,1)S(1)} %get-tuple-element.74), channel_id=1, source_target_pairs={{254,0},{255,1},{192,2},{193,3},{194,4},{195,5},{196,6},{197,7},{1... | collective-permute-start | bytes 165896 | tf_op jit(solution)/shard_map/ppermute | solution.py:636
  50.7 11.6 %collective-permute-start.9 = (bf16[144,192]{1,0:T(8,128)(2,1)S(1)}, bf16[144,192]{1,0:T(8,128)(2,1)S(1)}, u32[]{:S(2)}, u32[]{:S(2)}) collective-permute-start(bf16[144,192]{1,0:T(8,128)(2,1)S(1)} %get-tuple-element.75), channel_id=1, source_target_pairs={{192,0},{193,1},{194,2},{195,3},{196,4},{197,5},{198,6},{199,7},{2... | collective-permute-start | bytes 165896 | tf_op jit(solution)/shard_map/ppermute | solution.py:636
  50.7 11.6 %collective-permute-start.10 = (bf16[144,192]{1,0:T(8,128)(2,1)S(1)}, bf16[144,192]{1,0:T(8,128)(2,1)S(1)}, u32[]{:S(2)}, u32[]{:S(2)}) collective-permute-start(bf16[144,192]{1,0:T(8,128)(2,1)S(1)} %get-tuple-element.76), channel_id=1, source_target_pairs={{62,0},{63,1},{0,2},{1,3},{2,4},{3,5},{4,6},{5,7},{6,8},{7,9},{8,1... | collective-permute-start | bytes 165896 | tf_op jit(solution)/shard_map/ppermute | solution.py:636
  62.3 25.2 %copy-start.6 = (bf16[144,192]{1,0:T(8,128)(2,1)S(1)}, bf16[144,192]{1,0:T(8,128)(2,1)}, u32[]{:S(2)}) copy-start(bf16[144,192]{1,0:T(8,128)(2,1)} %get-tuple-element.52.x0) | copy-start | bytes 165892
  62.4 25.2 %copy-start.7 = (bf16[144,192]{1,0:T(8,128)(2,1)S(1)}, bf16[144,192]{1,0:T(8,128)(2,1)}, u32[]{:S(2)}) copy-start(bf16[144,192]{1,0:T(8,128)(2,1)} %get-tuple-element.53.x1) | copy-start | bytes 165892
  62.4 25.2 %copy-start.8 = (bf16[144,192]{1,0:T(8,128)(2,1)S(1)}, bf16[144,192]{1,0:T(8,128)(2,1)}, u32[]{:S(2)}) copy-start(bf16[144,192]{1,0:T(8,128)(2,1)} %get-tuple-element.54.x2) | copy-start | bytes 165892
  62.4 4.1 %collective-permute-start.12 = (bf16[48,128]{1,0:T(8,128)(2,1)S(1)}, bf16[48,128]{1,0:T(8,128)(2,1)S(1)}, u32[]{:S(2)}, u32[]{:S(2)}) collective-permute-start(bf16[48,128]{1,0:T(8,128)(2,1)S(1)} %add.1.own_ref), channel_id=1, source_target_pairs={{128,0},{129,1},{130,2},{131,3},{132,4},{133,5},{134,6},{135,7},{1... | collective-permute-start | bytes 36872 | tf_op jit(solution)/shard_map/ppermute | solution.py:636
  82.9 6.0 %collective-permute-start.13 = (bf16[32,48,128]{2,1,0:T(8,128)(2,1)S(1)}, bf16[32,48,128]{2,1,0:T(8,128)(2,1)S(1)}, u32[]{:S(2)}, u32[]{:S(2)}) collective-permute-start(bf16[32,48,128]{2,1,0:T(8,128)(2,1)S(1)} %all_to_all.10.own_ref), channel_id=1, source_target_pairs={{0,64},{64,0},{128,192},{192,128},{1,65},{65,1},{129,193},{193,129... | collective-permute-start | bytes 1179656 | tf_op jit(solution)/shard_map/ppermute | solution.py:649

commit v11 on v10

--- a/solution.py
+++ b/solution.py
@@ -33,6 +33,18 @@
     return (own.astype(F32) + other.astype(F32)).astype(BF)
 
 
+def fold(rows):
+    return jnp.concatenate(
+        [rows[:, 0:128], jnp.concatenate([rows[0:288, 128:192], rows[288:576, 128:192]], axis=1)], axis=0
+    )
+
+
+def unfold(rows):
+    return jnp.concatenate(
+        [rows[0:576], jnp.concatenate([rows[576:864, 0:64], rows[576:864, 64:128]], axis=0)], axis=1
+    )
+
+
 def dot_nn(a, b):
     return lax.dot_general(a, b, (((1,), (0,)), ((), ())), preferred_element_type=F32)
 
@@ -84,12 +96,16 @@
 
 def to_windows(parts, order, scratch):
     for s in range(4):
-        rows = dot_nn(order, parts[s][...])
+        rows = dot_nn(order, parts[s])
         for w in range(4):
             scratch[w * 144 + s * 36 : w * 144 + s * 36 + 36, :] = rows[w * 36 : w * 36 + 36]
 
 
-def head_kernel(x_hbm, mid_hbm, up_hbm, gain_hbm, fc1_hbm, fc2_hbm, o0, o1, o2, o3, part_hbm, keep_hbm, send_hbm,
+def window_parts(own, band, sector):
+    return (own[...], sector[0:144, :], band[0:144, :], sector[144:288, :])
+
+
+def head_kernel(x_hbm, mid_hbm, up_hbm, gain_hbm, fc1_hbm, fc2_hbm, o10, o2, o3, part_hbm, keep_hbm, send_hbm,
                 x_ref, mid_ref, up_ref, gain_ref, fc1_ref, fc2_ref, xq_ref, part_ref, grads_ref, x_s, mid_s, up_s, sem):
     pairs = (
         (mid_hbm, mid_ref),
@@ -112,15 +128,16 @@
     for copy in copies[3:]:
         copy.wait()
     to_quarters(x_ref, x_s)
+    for place, q in enumerate((1, 0, 2, 3)):
+        xq_ref[place * 144 : place * 144 + 144, :] = x_s[q * 144 : q * 144 + 144, :].astype(BF)
     writes = []
-    for q, out in enumerate((o0, o1, o2, o3)):
-        xq_ref[q] = x_s[q * 144 : q * 144 + 144, :].astype(BF)
-        writes.append(pltpu.make_async_copy(xq_ref.at[q], out, sem.at[8 + q]))
+    for i, (start, size, out) in enumerate(((0, 288, o10), (288, 144, o2), (432, 144, o3))):
+        writes.append(pltpu.make_async_copy(xq_ref.at[pl.ds(start, size)], out, sem.at[8 + i]))
         writes[-1].start()
     to_quarters(up_ref, up_s)
     up = up_s[...].astype(BF)
     grad_pre = (dot_nn(up, fc2_ref[...]) * slopes).astype(BF)
-    part_ref[...] = dot_nt(grad_pre, fc1_ref[...]).astype(BF)
+    part_ref[...] = fold(dot_nt(grad_pre, fc1_ref[...]).astype(BF))
     writes.append(pltpu.make_async_copy(part_ref, part_hbm, sem.at[6]))
     writes[-1].start()
     for start, grads in ((0, dot_tn(lowered, grad_pre)), (576, dot_tn(up, active.astype(BF)))):
@@ -138,10 +155,16 @@
 def head(x, mid, up, gain, fc1, fc2):
     return pl.pallas_call(
         head_kernel,
-        out_shape=tuple(shape((144, 192), BF) for _ in range(4))
-        + (shape((576, 192), BF), shape((576, 128), BF), shape((576, 128), BF)),
+        out_shape=(
+            shape((288, 192), BF),
+            shape((144, 192), BF),
+            shape((144, 192), BF),
+            shape((864, 128), BF),
+            shape((576, 128), BF),
+            shape((576, 128), BF),
+        ),
         in_specs=[ANY] * 6,
-        out_specs=tuple(ANY for _ in range(7)),
+        out_specs=tuple(ANY for _ in range(6)),
         scratch_shapes=[
             pltpu.VMEM((6, 12, 8, 192), BF),
             pltpu.VMEM((6, 12, 8, 192), BF),
@@ -149,8 +172,8 @@
             pltpu.VMEM((1, 192), F32),
             pltpu.VMEM((192, 384), BF),
             pltpu.VMEM((192, 384), BF),
-            pltpu.VMEM((4, 144, 192), BF),
             pltpu.VMEM((576, 192), BF),
+            pltpu.VMEM((864, 128), BF),
             pltpu.VMEM((1152, 128), BF),
             pltpu.VMEM((576, 192), F32),
             pltpu.VMEM((576, 192), F32),
@@ -163,27 +186,30 @@
     )(x, mid, up, gain, fc1, fc2)
 
 
-def middle_kernel(mid_ref, up_ref, own_ref, other_ref, gain_ref, after_ref, o0, o1, o2, o3, gain_out, mid_s, up_s):
+def middle_kernel(mid_ref, up_ref, own_ref, other_ref, gain_ref, x2_ref, band_ref, after_ref,
+                  o0, o1, o2, o3, gain_out, x_out, mid_s, up_s):
+    x_out[0:144, :] = x2_ref[...]
+    x_out[144:288, :] = band_ref[144:288, :]
     to_quarters(mid_ref, mid_s)
     to_quarters(up_ref, up_s)
     normed, inverse = layer_stats(mid_s[...])
-    grad = own_ref[...].astype(F32) + other_ref[...].astype(F32)
+    grad = unfold(own_ref[...].astype(F32) + other_ref[...].astype(F32))
     gain_out[...] = jnp.sum(grad * normed, axis=0, keepdims=True)
     out = up_s[...] + norm_backward(grad, gain_ref[...], normed, inverse)
     for q, o in enumerate((o0, o1, o2, o3)):
         o[...] = out[q * 144 : q * 144 + 144].astype(BF)
 
 
-def middle(mid, up, own, other, gain, after):
+def middle(mid, up, own, other, gain, x2, band, after):
     return pl.pallas_call(
         middle_kernel,
-        out_shape=tuple(shape((144, 192), BF) for _ in range(4)) + (shape((1, 192), F32),),
-        in_specs=[VMEM] * 5 + [ANY],
+        out_shape=tuple(shape((144, 192), BF) for _ in range(4)) + (shape((1, 192), F32), shape((288, 192), BF)),
+        in_specs=[VMEM] * 7 + [ANY],
         scratch_shapes=[pltpu.VMEM((576, 192), F32)] * 2,
         compiler_params=VM,
         cost_estimate=cost(1),
         name="middle",
-    )(mid, up, own, other, gain, after)
+    )(mid, up, own, other, gain, x2, band, after)
 
 
 def window_order():
@@ -265,14 +291,14 @@
         lines += [picked[lat * 4 : lat * 4 + 4] for lat in range(6)]
     lines = jnp.concatenate(lines, axis=1)
     code_ref[...] = dot_nt(lines.astype(BF), order)
-    look_up(terms_ref[...], lo_ref, hi_ref, stage, 0, 5)
+    look_up(terms_ref[...], lo_ref, hi_ref, stage, 0, 7)
 
 
 def gather_first(index, bias, ids, valid):
     return pl.pallas_call(
         gather_first_kernel,
         out_shape=(
-            shape((90 * 16, 128), F32),
+            shape((126 * 16, 128), F32),
             shape((168, 128), I32),
             shape((168, 128), I32),
             shape((160, 512), BF),
@@ -285,12 +311,12 @@
     )(index, jnp.asarray(window_order(), BF), bias, ids, valid)
 
 
-def gather_second_kernel(first_stage, lo_ref, hi_ref, terms_ref, a0, a1, a2, a3, main_ref, tail_ref, stage):
-    look_up(terms_ref[...], lo_ref, hi_ref, stage, 90, 4)
+def gather_second_kernel(first_stage, lo_ref, hi_ref, terms_ref, a0, a1, main_ref, tail_ref, stage):
+    look_up(terms_ref[...], lo_ref, hi_ref, stage, 126, 2)
     for r in range(12):
-        main_ref[r, 0:90, :] = first_stage[pl.ds(r, 90, stride=16), :]
-        main_ref[r, 90:144, :] = stage[pl.ds(r, 54, stride=16), :]
-        packed = stage[pl.ds(54 * 16 + r, 18, stride=16), :]
+        main_ref[r, 0:126, :] = first_stage[pl.ds(r, 126, stride=16), :]
+        main_ref[r, 126:144, :] = stage[pl.ds(r, 18, stride=16), :]
+        packed = stage[pl.ds(18 * 16 + r, 18, stride=16), :]
         for s in range(8):
             tail_ref[r, pl.ds(s, 18, stride=8), :] = pltpu.roll(packed, 128 - 16 * s, 1) if s else packed
 
@@ -299,17 +325,17 @@
     return pl.pallas_call(
         gather_second_kernel,
         out_shape=(shape((12, 144, 128), F32), shape((12, 144, 128), F32)),
-        in_specs=[VMEM] * 4 + [ANY] * 4,
-        scratch_shapes=[pltpu.VMEM((72 * 16, 128), F32)],
-        compiler_params=VM,
-        cost_estimate=cost(4),
+        in_specs=[VMEM] * 4 + [ANY] * 2,
+        scratch_shapes=[pltpu.VMEM((36 * 16, 128), F32)],
+        compiler_params=VM,
+        cost_estimate=cost(0.2),
         name="gather_second",
     )(first_stage, lo, hi, terms, *after)
 
 
-def forward_kernel(x0, x1, x2, x3, order_ref, gain_ref, qkv_ref, main_ref, tail_ref, code_ref,
+def forward_kernel(own_ref, band_ref, sector_ref, order_ref, gain_ref, qkv_ref, main_ref, tail_ref, code_ref,
                    low_ref, q_ref, k_ref, v_ref, prob_ref, att_ref, scratch):
-    to_windows((x0, x1, x2, x3), order_ref[...], scratch)
+    to_windows(window_parts(own_ref, band_ref, sector_ref), order_ref[...], scratch)
     normed, _ = layer_stats(scratch[...])
     low = (normed * gain_ref[...]).astype(BF)
     low_ref[...] = low
@@ -360,7 +386,7 @@
 
 def backward_kernel(g0, g1, g2, g3, order_ref, proj_ref, qkv_ref, q_ref, k_ref, v_ref, prob_ref,
                     part_ref, score_ref, end_ref, gcols, grad_ref, scratch, gatt):
-    to_windows((g0, g1, g2, g3), order_ref[...], scratch)
+    to_windows((g0[...], g1[...], g2[...], g3[...]), order_ref[...], scratch)
     grad = scratch[...].astype(BF)
     grad_ref[...] = grad
     gatt[...] = dot_nt(grad, proj_ref[...]).astype(BF)
@@ -391,17 +417,19 @@
         term = dot_nt(gcols[j], qkv_ref[j])
         total = term if total is None else total + term
     scratch[...] = total
+    moved_back = []
     for s in range(4):
         pieces = [scratch[w * 144 + s * 36 : w * 144 + s * 36 + 36, :] for w in range(4)]
         piece = jnp.concatenate(pieces, axis=0).astype(BF)
-        part_ref[s * 144 : s * 144 + 144, :] = dot_tn(order_ref[...], piece).astype(BF)
+        moved_back.append(dot_tn(order_ref[...], piece).astype(BF))
+    part_ref[...] = fold(jnp.concatenate(moved_back, axis=0))
 
 
 def backward(g, proj, qkv, q, k, v, prob):
     return pl.pallas_call(
         backward_kernel,
         out_shape=(
-            shape((576, 192), BF),
+            shape((864, 128), BF),
             shape((12, 144, 128), F32),
             shape((12, 144, 128), F32),
             shape((3, 576, 96), BF),
@@ -496,12 +524,12 @@
     )(first, second, other, table, gain)
 
 
-def meet_kernel(own_ref, other_ref, x0, x1, x2, x3, g0, g1, g2, g3, gain_out):
+def meet_kernel(own_ref, other_ref, x_own, x_band, x_sector, g0, g1, g2, g3, gain_out):
     gain = jnp.zeros((1, 192), F32)
-    for s, (x, g) in enumerate(zip((x0, x1, x2, x3), (g0, g1, g2, g3))):
-        rows = slice(s * 144, s * 144 + 144)
-        grad = own_ref[rows, :].astype(F32) + other_ref[rows, :].astype(F32)
-        normed, _ = layer_stats(x[...].astype(F32))
+    total = unfold(own_ref[...].astype(F32) + other_ref[...].astype(F32))
+    for s, (x, g) in enumerate(zip(window_parts(x_own, x_band, x_sector), (g0, g1, g2, g3))):
+        grad = total[s * 144 : s * 144 + 144]
+        normed, _ = layer_stats(x.astype(F32))
         gain = gain + jnp.sum(grad * normed, axis=0, keepdims=True)
         g[...] = grad.astype(BF)
     gain_out[...] = jnp.concatenate(gain_rows(gain) + [jnp.zeros((6, 128), F32)], axis=0)
@@ -517,9 +545,11 @@
     )(own, other, *x)
 
 
-def finish_kernel(x0, x1, x2, x3, m0, m1, m2, m3, g0, g1, g2, g3, gain_ref, out_ref):
-    for q, (x, m, g) in enumerate(zip((x0, x1, x2, x3), (m0, m1, m2, m3), (g0, g1, g2, g3))):
-        normed, inverse = layer_stats(x[...].astype(F32))
+def finish_kernel(x10, x2, x3, m0, m1, m2, m3, g0, g1, g2, g3, gain_ref, out_ref, token_ref):
+    token_ref[...] = jnp.zeros((8, 128), F32)
+    xs = (x10[144:288, :], x10[0:144, :], x2[...], x3[...])
+    for q, (x, m, g) in enumerate(zip(xs, (m0, m1, m2, m3), (g0, g1, g2, g3))):
+        normed, inverse = layer_stats(x.astype(F32))
         rows = m[...].astype(F32) + norm_backward(g[...].astype(F32), gain_ref[...], normed, inverse)
         for lat in range(3):
             piece = rows[lat * 48 : lat * 48 + 48].reshape(6, 8, 192)
@@ -529,7 +559,7 @@
 def finish(x, m, g, gain):
     return pl.pallas_call(
         finish_kernel,
-        out_shape=shape((6, 12, 8, 192), BF),
+        out_shape=(shape((6, 12, 8, 192), BF), shape((8, 128), F32)),
         compiler_params=VM,
         cost_estimate=cost(1),
         name="finish",
@@ -554,7 +584,7 @@
     )(got, gain, *after)
 
 
-def spread_kernel(own_ref, other_ref, out_ref):
+def spread_kernel(own_ref, other_ref, after_ref, out_ref):
     own = own_ref[...].astype(F32)
     place = lax.broadcasted_iota(I32, (48, 128), 0)
     row = lax.axis_index("lon") * 40 + place
@@ -563,14 +593,36 @@
     out_ref[...] = jnp.broadcast_to(total.astype(BF)[None], (32, 48, 128))
 
 
-def spread(own, other):
-    return pl.pallas_call(
-        spread_kernel, out_shape=shape((32, 48, 128), BF), compiler_params=VM, cost_estimate=cost(1), name="spread"
-    )(own, other)
-
-
-def unpack_kernel(weight_scale, table_scale, own_ref, other_ref,
-                  qkv_ref, proj_ref, upg_ref, down_ref, one_ref, two_ref, table_ref):
+def spread(own, other, after):
+    return pl.pallas_call(
+        spread_kernel,
+        out_shape=shape((32, 48, 128), BF),
+        in_specs=[VMEM] * 2 + [ANY],
+        compiler_params=VM,
+        cost_estimate=cost(1),
+        name="spread",
+    )(own, other, after)
+
+
+def table_kernel(table_scale, got_ref, table_ref):
+    rows = jnp.concatenate([got_ref[c].astype(F32)[0:40] for c in range(21, 30)], axis=0)[24:336] * table_scale
+    for r in range(12):
+        for a in range(26):
+            row, wide = r * 26 + (a % 2) * 13 + a // 2, min(128, 3312 - a * 128)
+            table_ref[r % 3, r // 3 : r // 3 + 1, a * 128 : a * 128 + wide] = rows[row : row + 1, 0:wide]
+
+
+def unpack_table(table_scale, got):
+    return pl.pallas_call(
+        functools.partial(table_kernel, table_scale),
+        out_shape=shape((3, 4, 3312), F32),
+        compiler_params=VM,
+        cost_estimate=cost(0.5),
+        name="table",
+    )(got)
+
+
+def unpack_kernel(weight_scale, own_ref, other_ref, qkv_ref, proj_ref, upg_ref, down_ref, one_ref, two_ref):
     swap = lax.rem(lax.axis_index("lat"), 2) == 1
     fields = []
     gain = jnp.zeros((8, 128), F32)
@@ -594,23 +646,15 @@
     qkv_ref[2, :, 32:64] = second[336:528, 96:128]
     for i in range(4):
         qkv_ref[2, i * 48 : i * 48 + 48, 64:96] = second[528:576, i * 32 : i * 32 + 32]
-    table = fields[0][864:1176]
-    for r in range(12):
-        for half in range(2):
-            piece = table[r * 26 + half * 13 : r * 26 + half * 13 + 13] * table_scale
-            for a in range(13):
-                start = a * 256 + half * 128
-                wide = min(128, 3312 - start)
-                table_ref[r % 3, r // 3 : r // 3 + 1, start : start + wide] = piece[a : a + 1, 0:wide]
     for rows, out in ((gain, one_ref), (fields[0][1176:1184] + fields[1][1176:1184], two_ref)):
         line = rows[0:1]
         later = jnp.concatenate([line[:, 96:128], rows[1:2, 0:64]], axis=1)
         out[...] = jnp.where(lax.axis_index("tp") == 0, line[:, 0:96], later) * weight_scale
 
 
-def unpack(weight_scale, table_scale, got, other):
-    return pl.pallas_call(
-        functools.partial(unpack_kernel, weight_scale, table_scale),
+def unpack(weight_scale, got, other):
+    return pl.pallas_call(
+        functools.partial(unpack_kernel, weight_scale),
         out_shape=(
             shape((3, 192, 96), F32),
             shape((96, 192), F32),
@@ -618,7 +662,6 @@
             shape((192, 384), F32),
             shape((1, 96), F32),
             shape((1, 96), F32),
-            shape((3, 4, 3312), F32),
         ),
         compiler_params=VM,
         name="unpack",
@@ -674,15 +717,17 @@
         return field.transpose(1, 2, 0, 3)
 
     x_in, mid_in, up_in = turned(inputs), turned(residual_mid), turned(grad_out)
-    *x, part2, first, first_send = head(x_in, mid_in, up_in, gain2, fc1_weight, fc2_weight.T)
+    x10, x2, x3, part2, first, first_send = head(x_in, mid_in, up_in, gain2, fc1_weight, fc2_weight.T)
     other2 = moved(part2, 0, 0, 1)
-    xw = shifted_parts(x)
+    x_band = moved(x10, 1, 0, 0)
     stage, lo, hi, terms, code = gather_first(
         bias_index, pos_bias[0].transpose(1, 0, 2), mask_ids.transpose(1, 0, 2), key_valid.transpose(1, 0, 2)
     )
-    *gm, gain_two = middle(mid_in, up_in, part2, other2, gain2, lo)
+    *gm, gain_two, x_next = middle(mid_in, up_in, part2, other2, gain2, x2, x_band, lo)
+    x_sector = moved(x_next, 0, 1, 0)
+    xw = (x3, x_band, x_sector)
     gw = shifted_parts(gm)
-    main, tail = gather_second(stage, lo, hi, terms, (gain_two, *xw[1:]))
+    main, tail = gather_second(stage, lo, hi, terms, (gain_two, x_band))
     low, q, k, v, prob, att = forward(xw, gain1, qkv_weight, main, tail, code)
     part1, score, end, gcols, grad = backward(gw, proj_weight, qkv_weight, q, k, v, prob)
     other1 = moved(part1, 0, 0, 1)
@@ -692,12 +737,11 @@
     *g, gain_one = meet(part1, other1, xw)
     back = (moved(g[3], -1, -1, 0), moved(g[2], -1, 0, 0), moved(g[1], 0, -1, 0), g[0])
     own = add(lax.all_to_all(sums.reshape(32, 40, 128), "lon", 0, 0), gain_one, back[:3])
-    totals = spread(own, moved(own, 2, 0, 0))
-    result = finish(x, gm, back, gain1)
+    result, token = finish((x10, x2, x3), gm, back, gain1)
+    totals = spread(own, moved(own, 2, 0, 0), token)
     got = lax.all_to_all(totals, "lon", 0, 0)
-    qkv_out, proj_out, up_out, down_out, one, two, table_out = unpack(
-        weight_scale, table_scale, got, other_core(got)
-    )
+    table_out = unpack_table(table_scale, got)
+    qkv_out, proj_out, up_out, down_out, one, two = unpack(weight_scale, got, other_core(got))
     return (
         result.transpose(2, 0, 1, 3),
         qkv_out,

time: 90.3 us -> 90.8 us (level)
  starting transfers between devices: 35.1 us -> 32 us
  waiting for transfers between devices: 13.2 us -> 15.6 us
    ppermute x12 -> x11, starting transfers between devices: 24.3 us -> 21.4 us  [moved(): return lax.ppermute(value, ('lat', 'lon', 'tp'), pairs)]
    ppermute x2, starting transfers between devices: 6.73 us -> 4.57 us  [other_core(): lax.ppermute(value, 'lat', [(a, a ^ 1) for a in range(lax.axis_size('lat'...]
    all_to_all x1, starting transfers between devices: 4.1 us -> 6.02 us  [local(): lax.all_to_all(sums.reshape(32, 40, 128), 'lon', 0, 0)]
    ppermute x12 -> x11, waiting for transfers between devices: 13.1 us -> 15 us  [moved(): return lax.ppermute(value, ('lat', 'lon', 'tp'), pairs)]
    pallas_call x6 -> x7, Pallas kernels: 13.7 us -> 15.2 us  [the longest x1 4.68 us: backward(): pl.pallas_call(backward_kernel, out_shape=(shape((864, 128), BF), shape((...]
  transfers between devices with their start and end apart: 15 -> 14, of which waited for: 4 -> 6; matrix products, arithmetic and copies ran while one was open for 0% -> 0% of each run, Pallas kernels for 16% -> 16%
where the time goes in v11:
time: 90.8 us; the launch traced here: 90.6 us
  starting transfers between devices  32 us (35%)
  Pallas kernels  25.1 us (28%)
  blocking collectives  16.8 us (19%)
  waiting for transfers between devices  15.6 us (17%)
  between operations  0.97 us (1%)
    ppermute x11, starting transfers between devices, moved(): return lax.ppermute(value, ('lat', 'lon', 'tp'), pairs)  21.4 us
    all_to_all x1, blocking collectives, local(): got = lax.all_to_all(totals, 'lon', 0, 0)  16.8 us
    ppermute x11, waiting for transfers between devices, moved(): return lax.ppermute(value, ('lat', 'lon', 'tp'), pairs)  15 us
    all_to_all x1, starting transfers between devices, local(): lax.all_to_all(sums.reshape(32, 40, 128), 'lon', 0, 0)  6.02 us
    pallas_call x1, Pallas kernels, backward(): pl.pallas_call(backward_kernel, out_shape=(shape((864, 128), BF), shape((...  4.68 us
    ppermute x2, starting transfers between devices, other_core(): lax.ppermute(value, 'lat', [(a, a ^ 1) for a in range(lax.axis_size('lat'...  4.57 us
    pallas_call x1, Pallas kernels, gather_first(): pl.pallas_call(gather_first_kernel, out_shape=(shape((126 * 16, 128), F32...  3.78 us
    pallas_call x1, Pallas kernels, head(): pl.pallas_call(head_kernel, out_shape=(shape((288, 192), BF), shape((144,...  3.66 us
  transfers between devices with their start and end apart: 14, of which 6 were waited for; matrix products, arithmetic and copies ran while one was open for 0% of the time, Pallas kernels for 16%

profile of v11, /device:TPU:1, one launch (start us, length us, event | category | flops | bytes accessed | tf_op | source)
XLA Modules:
  0.0 90.6 jit_solution(9215884914804041846)
XLA Ops:
  0.7 0.0 copy-start.13
  0.7 3.7 %head.1 = (bf16[288,192]{1,0:T(8,128)(2,1)}, bf16[144,192]{1,0:T(8,128)(2,1)}, bf16[144,192]{1,0:T(8,128)(2,1)}, bf16[864,128]{1,0:T(8,128)(2,1)}, bf16[576,128]{1,0:T(8,128)(2,1)}, /*index=5*/bf16[576,128]{1,0:T(8,128)(2,1)}) custom-call(bf16[6,12,8,192]{3,2,1,0:T(8,128)(2,1)} %bitcast.30, bf16[6,12,8,192]{3,2,1,0:T(8,128)(2,1)} %bitcast.19, ...), custom_call_target="tpu_custom_call" | custom-call | flops 3000000000 | tf_op jit(solution)/shard_map/head/pallas_call | solution.py:156
  4.4 0.0 copy-start
  4.4 0.0 copy-start.1
  4.4 0.0 copy-start.2
  4.4 0.0 copy-start.10
  4.4 0.0 copy-start.16
  4.4 2.2 %collective-permute-start = (bf16[864,128]{1,0:T(8,128)(2,1)}, bf16[864,128]{1,0:T(8,128)(2,1)S(1)}, u32[]{:S(2)}, u32[]{:S(2)}) collective-permute-start(bf16[864,128]{1,0:T(8,128)(2,1)} %get-tuple-element.56.own_ref), channel_id=1, source_target_pairs={{1,0},{0,1},{3,2},{2,3},{5,4},{4,5},{7,6},{6,7},{9,8},{8,9},{11,10... | collective-permute-start | bytes 663560 | tf_op jit(solution)/shard_map/ppermute | solution.py:679
  6.6 1.2 %collective-permute-start.1 = (bf16[288,192]{1,0:T(8,128)(2,1)}, bf16[288,192]{1,0:T(8,128)(2,1)S(1)}, u32[]{:S(2)}, u32[]{:S(2)}) collective-permute-start(bf16[288,192]{1,0:T(8,128)(2,1)} %get-tuple-element.53.x10), channel_id=1, source_target_pairs={{64,0},{65,1},{66,2},{67,3},{68,4},{69,5},{70,6},{71,7},{72,8},{73... | collective-permute-start | bytes 331784 | tf_op jit(solution)/shard_map/ppermute | solution.py:679
  7.8 3.8 %gather_first.1 = (f32[2016,128]{1,0:T(8,128)S(1)}, s32[168,128]{1,0:T(8,128)S(1)}, s32[168,128]{1,0:T(8,128)S(1)}, bf16[160,512]{1,0:T(8,128)(2,1)S(1)}, f32[4,144]{1,0:T(4,128)S(1)}) custom-call(s32[144,144]{1,0:T(8,128)S(1)} %copy-done.4, bf16[144,144]{1,0:T(8,128)(2,1)S(1)} %copy-done.13, f32[3,4,3312]{2,1,0:T(4,128)S(1)} %bitcast.23, ...), custom_call_target="tpu_custom_call" | custom-call | flops 500000000 | tf_op jit(solution)/shard_map/gather_first/pallas_call | solution.py:298
  11.6 5.1 %collective-permute-done.1.band_ref.a1.x_band = bf16[288,192]{1,0:T(8,128)(2,1)S(1)} collective-permute-done((bf16[288,192]{1,0:T(8,128)(2,1)}, bf16[288,192]{1,0:T(8,128)(2,1)S(1)}, u32[]{:S(2)}, u32[]{:S(2)}) %collective-permute-start.1) | collective-permute-done | bytes 110624 | tf_op jit(solution)/shard_map/ppermute | solution.py:679
  16.8 0.0 copy-start.5
  16.8 0.0 copy-start.11
  16.8 0.0 copy-start.12
  16.8 0.0 copy-start.17
  16.8 0.6 middle.1
  17.4 7.8 %collective-permute-start.5 = (bf16[288,192]{1,0:T(8,128)(2,1)S(1)}, bf16[288,192]{1,0:T(8,128)(2,1)S(1)}, u32[]{:S(2)}, u32[]{:S(2)}) collective-permute-start(bf16[288,192]{1,0:T(8,128)(2,1)S(1)} %get-tuple-element.62), channel_id=1, source_target_pairs={{2,0},{3,1},{4,2},{5,3},{6,4},{7,5},{8,6},{9,7},{10,8},{11,9},{12,... | collective-permute-start | bytes 331784 | tf_op jit(solution)/shard_map/ppermute | solution.py:679
  25.2 0.0 collective-permute-start.4
  25.2 1.0 %collective-permute-start.3 = (bf16[144,192]{1,0:T(8,128)(2,1)S(1)}, bf16[144,192]{1,0:T(8,128)(2,1)S(1)}, u32[]{:S(2)}, u32[]{:S(2)}) collective-permute-start(bf16[144,192]{1,0:T(8,128)(2,1)S(1)} %get-tuple-element.59.m1), channel_id=1, source_target_pairs={{64,0},{65,1},{66,2},{67,3},{68,4},{69,5},{70,6},{71,7},{72,8},{73... | collective-permute-start | bytes 165896 | tf_op jit(solution)/shard_map/ppermute | solution.py:679
  26.3 0.3 collective-permute-start.2
  26.5 1.4 %gather_second.1 = (f32[12,144,128]{2,1,0:T(8,128)S(1)}, f32[12,144,128]{2,1,0:T(8,128)S(1)}) custom-call(f32[2016,128]{1,0:T(8,128)S(1)} %get-tuple-element.63.first_stage, s32[168,128]{1,0:T(8,128)S(1)} %get-tuple-element.57.after_ref.lo_ref, s32[168,128]{1,0:T(8,128)S(1)} %get-tuple-element.64.hi_ref, bf16[160,512]{1,0:T(8,128)(2,1)S(1)} %get-tuple-element.65.terms_ref, ...), custom_call_target="tpu_custom_call" | custom-call | flops 200000000 | tf_op jit(solution)/shard_map/gather_second/pallas_call | solution.py:325
  28.0 0.0 collective-permute-done.5.sector_ref.x_sector
  28.0 0.0 copy-start.7
  28.0 3.0 %forward.1 = (bf16[576,192]{1,0:T(8,128)(2,1)S(1)}, bf16[576,96]{1,0:T(8,128)(2,1)S(1)}, bf16[576,96]{1,0:T(8,128)(2,1)S(1)}, bf16[576,96]{1,0:T(8,128)(2,1)S(1)...) custom-call(bf16[144,192]{1,0:T(8,128)(2,1)S(1)} %copy-done.17, ...), custom_call_target="tpu_custom_call" | custom-call | flops 5000000000 | tf_op jit(solution)/shard_map/forward/pallas_call | solution.py:370
  31.0 0.9 collective-permute-done.4.g3
  31.9 0.0 copy-start.14
  32.0 4.7 %backward.1 = (bf16[864,128]{1,0:T(8,128)(2,1)S(1)}, f32[12,144,128]{2,1,0:T(8,128)S(1)}, f32[12,144,128]{2,1,0:T(8,128)S(1)}, bf16[3,576,96]{2,1,0:T(8,128)(2,1)S(1)}, bf16[576,192]{1,0:T(8,128)(2,1)S(1)}) custom-call(bf16[144,192]{1,0:T(8,128)(2,1)S(1)} %get-tuple-element.61.g0.m3, bf16[144,192]{1,0:T(8,128)(2,1)S(1)} %collective-permute-done.2.g1, ...), custom_call_target="tpu_custom_call" | custom-call | flops 7000000000 | tf_op jit(solution)/shard_map/backward/pallas_call | solution.py:429
  36.6 0.5 weigh.1
  37.2 0.1 collective-permute-start.10
  37.3 0.1 collective-permute-start.6
  37.4 0.0 copy-start.15
  37.4 3.0 %scatter.1.table_ref = f32[192,256]{1,0:T(8,128)S(1)} custom-call(f32[12,144,128]{2,1,0:T(8,128)S(1)} %get-tuple-element.88.score_ref, f32[12,144,128]{2,1,0:T(8,128)S(1)} %get-tuple-element.89.end_ref, s32[168,128]{1,0:T(8,128)S(1)} %get-tuple-element.57.after_ref.lo_ref, s32[168,128]{1,0:T(8,128)S(1)} %get-tuple-element.64.hi_ref, ...), custom_call_target="tpu_custom_call" | custom-call | flops 4000000000 | tf_op jit(solution)/shard_map/scatter/pallas_call | solution.py:468
  40.4 0.8 pack.1
  41.3 6.0 %all-to-all-start = ((bf16[32,40,128]{2,1,0:T(8,128)(2,1)}), bf16[32,40,128]{2,1,0:T(8,128)(2,1)S(1)}, u32[]{:S(2)}, u32[]{:S(2)}) async-start(bf16[32,40,128]{2,1,0:T(8,128)(2,1)} %bitcast.11), calls=%async_computation | async-start | bytes 655360 | tf_op jit(solution)/shard_map/all_to_all | solution.py:739
  47.3 0.4 meet.1
  47.7 4.8 %collective-permute-start.7 = (bf16[144,192]{1,0:T(8,128)(2,1)S(1)}, bf16[144,192]{1,0:T(8,128)(2,1)S(1)}, u32[]{:S(2)}, u32[]{:S(2)}) collective-permute-start(bf16[144,192]{1,0:T(8,128)(2,1)S(1)} %get-tuple-element.75), channel_id=1, source_target_pairs={{254,0},{255,1},{192,2},{193,3},{194,4},{195,5},{196,6},{197,7},{1... | collective-permute-start | bytes 165896 | tf_op jit(solution)/shard_map/ppermute | solution.py:679
  52.5 1.2 %collective-permute-start.9 = (bf16[144,192]{1,0:T(8,128)(2,1)S(1)}, bf16[144,192]{1,0:T(8,128)(2,1)S(1)}, u32[]{:S(2)}, u32[]{:S(2)}) collective-permute-start(bf16[144,192]{1,0:T(8,128)(2,1)S(1)} %get-tuple-element.77), channel_id=1, source_target_pairs={{62,0},{63,1},{0,2},{1,3},{2,4},{3,5},{4,6},{5,7},{6,8},{7,9},{8,1... | collective-permute-start | bytes 165896 | tf_op jit(solution)/shard_map/ppermute | solution.py:679
  53.7 8.6 %collective-permute-done.7.g0.b0 = bf16[144,192]{1,0:T(8,128)(2,1)S(1)} collective-permute-done((bf16[144,192]{1,0:T(8,128)(2,1)S(1)}, bf16[144,192]{1,0:T(8,128)(2,1)S(1)}, u32[]{:S(2)}, u32[]{:S(2)}) %collective-permute-start.7) | collective-permute-done | bytes 55328 | tf_op jit(solution)/shard_map/ppermute | solution.py:679
  62.3 0.3 collective-permute-done.9.g2.b2
  62.6 0.1 add.1.own_ref
  62.6 2.8 %collective-permute-start.11 = (bf16[48,128]{1,0:T(8,128)(2,1)S(1)}, bf16[48,128]{1,0:T(8,128)(2,1)S(1)}, u32[]{:S(2)}, u32[]{:S(2)}) collective-permute-start(bf16[48,128]{1,0:T(8,128)(2,1)S(1)} %add.1.own_ref), channel_id=1, source_target_pairs={{128,0},{129,1},{130,2},{131,3},{132,4},{133,5},{134,6},{135,7},{1... | collective-permute-start | bytes 36872 | tf_op jit(solution)/shard_map/ppermute | solution.py:679
  65.4 1.2 %finish.1 = (bf16[6,12,8,192]{3,2,1,0:T(8,128)(2,1)}, f32[8,128]{1,0:T(8,128)S(1)}) custom-call(bf16[288,192]{1,0:T(8,128)(2,1)S(1)} %copy-done.6, bf16[144,192]{1,0:T(8,128)(2,1)S(1)} %copy-done.16, bf16[144,192]{1,0:T(8,128)(2,1)S(1)} %copy-done.17, bf16[144,192]{1,0:T(8,128)(2,1)S(1)} %get-tuple-element.58.m0, bf16[144,192]{1,0:T(8,128)(2,1)S(1)} %get-tuple-element.59.m1, ...), custom_call_target="tpu_custom_call" | custom-call | flops 1000000000 | tf_op jit(solution)/shard_map/finish/pallas_call | solution.py:560
  66.7 0.1 collective-permute-done.11.other_ref
  66.8 16.8 %all_to_all.10.own_ref.got_ref = bf16[32,48,128]{2,1,0:T(8,128)(2,1)S(1)} all-to-all(bf16[32,48,128]{2,1,0:T(8,128)(2,1)S(1)} %spread.1), channel_id=1, replica_groups=mesh['lat'=4,'lon'=32,'tp'=2] {'lon'}, dimensions={0} | all-to-all | bytes 786432 | tf_op jit(solution)/shard_map/all_to_all | solution.py:742
  83.6 4.5 %collective-permute-start.12 = (bf16[32,48,128]{2,1,0:T(8,128)(2,1)S(1)}, bf16[32,48,128]{2,1,0:T(8,128)(2,1)S(1)}, u32[]{:S(2)}, u32[]{:S(2)}) collective-permute-start(bf16[32,48,128]{2,1,0:T(8,128)(2,1)S(1)} %all_to_all.10.own_ref.got_ref), channel_id=1, source_target_pairs={{0,64},{64,0},{128,192},{192,128},{1,65},{65,1},{129,193},{193,129... | collective-permute-start | bytes 1179656 | tf_op jit(solution)/shard_map/ppermute | solution.py:692
  88.1 0.8 table.1
  88.9 0.6 collective-permute-done.12.other_ref
  89.5 1.1 %unpack.1 = (f32[3,192,96]{2,1,0:T(8,128)}, f32[96,192]{1,0:T(8,128)}, f32[192,384]{1,0:T(8,128)}, f32[192,384]{1,0:T(8,128)}, f32[1,96]{1,0:T(1,128)}, /*index=5*/f32[1,96]{1,0:T(1,128)}) custom-call(bf16[32,48,128]{2,1,0:T(8,128)(2,1)S(1)} %all_to_all.10.own_ref.got_ref, bf16[32,48,128]{2,1,0:T(8,128)(2,1)S(1)} %collective-permute-done.12.other_ref), custom_call_target="tpu_custom_call" | custom-call | tf_op jit(solution)/shard_map/unpack/pallas_call | solution.py:656
  (32 shorter events, 0.1 us)
Async XLA Ops:
  0.6 7.2 %copy-start.3 = (f32[1,4,3,3312]{3,1,2,0:T(4,128)S(1)}, f32[1,4,3,3312]{3,1,2,0:T(4,128)}, u32[]{:S(2)}) copy-start(f32[1,4,3,3312]{3,1,2,0:T(4,128)} %param.22) | copy-start | bytes 476932
  0.6 7.2 %copy-start.4 = (s32[144,144]{1,0:T(8,128)S(1)}, s32[144,144]{1,0:T(8,128)}, u32[]{:S(2)}) copy-start(s32[144,144]{1,0:T(8,128)} %index_ref.1) | copy-start | bytes 248836
  0.7 7.2 %copy-start.8 = (s32[8,6,12]{2,0,1:T(8,128)S(1)}, s32[8,6,12]{2,0,1:T(8,128)}, u32[]{:S(2)}) copy-start(s32[8,6,12]{2,0,1:T(8,128)} %param.19) | copy-start | bytes 6916
  0.7 7.2 %copy-start.9 = (s32[8,6,12]{2,0,1:T(8,128)S(1)}, s32[8,6,12]{2,0,1:T(8,128)}, u32[]{:S(2)}) copy-start(s32[8,6,12]{2,0,1:T(8,128)} %param.20) | copy-start | bytes 6916
  0.7 7.2 %copy-start.13 = (bf16[144,144]{1,0:T(8,128)(2,1)S(1)}, bf16[144,144]{1,0:T(8,128)(2,1)}, u32[]{:S(2)}) copy-start(bf16[144,144]{1,0:T(8,128)(2,1)} %constant.4.clone.order_ref) | copy-start | bytes 124420
  4.4 12.4 %copy-start = (bf16[8,6,12,192]{3,0,2,1:T(8,128)(2,1)S(1)}, bf16[8,6,12,192]{3,0,2,1:T(8,128)(2,1)}, u32[]{:S(2)}) copy-start(bf16[8,6,12,192]{3,0,2,1:T(8,128)(2,1)} %param.17) | copy-start | bytes 663556
  4.4 12.4 %copy-start.1 = (bf16[8,6,12,192]{3,0,2,1:T(8,128)(2,1)S(1)}, bf16[8,6,12,192]{3,0,2,1:T(8,128)(2,1)}, u32[]{:S(2)}) copy-start(bf16[8,6,12,192]{3,0,2,1:T(8,128)(2,1)} %param.18) | copy-start | bytes 663556
  4.4 12.4 %copy-start.2 = (bf16[864,128]{1,0:T(8,128)(2,1)S(1)}, bf16[864,128]{1,0:T(8,128)(2,1)}, u32[]{:S(2)}) copy-start(bf16[864,128]{1,0:T(8,128)(2,1)} %get-tuple-element.56.own_ref) | copy-start | bytes 663556
  4.4 12.4 %copy-start.10 = (f32[192]{0:T(256)S(1)}, f32[192]{0:T(256)}, u32[]{:S(2)}) copy-start(f32[192]{0:T(256)} %param.26) | copy-start | bytes 2308
  4.4 12.4 %copy-start.16 = (bf16[144,192]{1,0:T(8,128)(2,1)S(1)}, bf16[144,192]{1,0:T(8,128)(2,1)}, u32[]{:S(2)}) copy-start(bf16[144,192]{1,0:T(8,128)(2,1)} %get-tuple-element.54.x2_ref.x2) | copy-start | bytes 165892
  4.4 12.3 %collective-permute-start = (bf16[864,128]{1,0:T(8,128)(2,1)}, bf16[864,128]{1,0:T(8,128)(2,1)S(1)}, u32[]{:S(2)}, u32[]{:S(2)}) collective-permute-start(bf16[864,128]{1,0:T(8,128)(2,1)} %get-tuple-element.56.own_ref), channel_id=1, source_target_pairs={{1,0},{0,1},{3,2},{2,3},{5,4},{4,5},{7,6},{6,7},{9,8},{8,9},{11,10... | collective-permute-start | bytes 663560 | tf_op jit(solution)/shard_map/ppermute | solution.py:679
  6.6 10.1 %collective-permute-start.1 = (bf16[288,192]{1,0:T(8,128)(2,1)}, bf16[288,192]{1,0:T(8,128)(2,1)S(1)}, u32[]{:S(2)}, u32[]{:S(2)}) collective-permute-start(bf16[288,192]{1,0:T(8,128)(2,1)} %get-tuple-element.53.x10), channel_id=1, source_target_pairs={{64,0},{65,1},{66,2},{67,3},{68,4},{69,5},{70,6},{71,7},{72,8},{73... | collective-permute-start | bytes 331784 | tf_op jit(solution)/shard_map/ppermute | solution.py:679
  16.8 11.2 %copy-start.5 = (bf16[3,192,96]{2,1,0:T(8,128)(2,1)S(1)}, bf16[3,192,96]{2,1,0:T(8,128)(2,1)}, u32[]{:S(2)}) copy-start(bf16[3,192,96]{2,1,0:T(8,128)(2,1)} %qkv_ref.3) | copy-start | bytes 331780
  16.8 11.2 %copy-start.11 = (f32[192]{0:T(256)S(1)}, f32[192]{0:T(256)}, u32[]{:S(2)}) copy-start(f32[192]{0:T(256)} %param.23) | copy-start | bytes 2308
  16.8 11.2 %copy-start.12 = (bf16[144,144]{1,0:T(8,128)(2,1)S(1)}, bf16[144,144]{1,0:T(8,128)(2,1)}, u32[]{:S(2)}) copy-start(bf16[144,144]{1,0:T(8,128)(2,1)} %constant.5.clone.order_ref) | copy-start | bytes 124420
  16.8 11.2 %copy-start.17 = (bf16[144,192]{1,0:T(8,128)(2,1)S(1)}, bf16[144,192]{1,0:T(8,128)(2,1)}, u32[]{:S(2)}) copy-start(bf16[144,192]{1,0:T(8,128)(2,1)} %get-tuple-element.55.own_ref.x_own.x3) | copy-start | bytes 165892
  17.4 10.6 %collective-permute-start.5 = (bf16[288,192]{1,0:T(8,128)(2,1)S(1)}, bf16[288,192]{1,0:T(8,128)(2,1)S(1)}, u32[]{:S(2)}, u32[]{:S(2)}) collective-permute-start(bf16[288,192]{1,0:T(8,128)(2,1)S(1)} %get-tuple-element.62), channel_id=1, source_target_pairs={{2,0},{3,1},{4,2},{5,3},{6,4},{7,5},{8,6},{9,7},{10,8},{11,9},{12,... | collective-permute-start | bytes 331784 | tf_op jit(solution)/shard_map/ppermute | solution.py:679
  25.2 6.7 %collective-permute-start.4 = (bf16[144,192]{1,0:T(8,128)(2,1)S(1)}, bf16[144,192]{1,0:T(8,128)(2,1)S(1)}, u32[]{:S(2)}, u32[]{:S(2)}) collective-permute-start(bf16[144,192]{1,0:T(8,128)(2,1)S(1)} %get-tuple-element.58.m0), channel_id=1, source_target_pairs={{66,0},{67,1},{68,2},{69,3},{70,4},{71,5},{72,6},{73,7},{74,8},{75... | collective-permute-start | bytes 165896 | tf_op jit(solution)/shard_map/ppermute | solution.py:679
  25.2 6.7 %collective-permute-start.3 = (bf16[144,192]{1,0:T(8,128)(2,1)S(1)}, bf16[144,192]{1,0:T(8,128)(2,1)S(1)}, u32[]{:S(2)}, u32[]{:S(2)}) collective-permute-start(bf16[144,192]{1,0:T(8,128)(2,1)S(1)} %get-tuple-element.59.m1), channel_id=1, source_target_pairs={{64,0},{65,1},{66,2},{67,3},{68,4},{69,5},{70,6},{71,7},{72,8},{73... | collective-permute-start | bytes 165896 | tf_op jit(solution)/shard_map/ppermute | solution.py:679
  26.3 5.7 %collective-permute-start.2 = (bf16[144,192]{1,0:T(8,128)(2,1)S(1)}, bf16[144,192]{1,0:T(8,128)(2,1)S(1)}, u32[]{:S(2)}, u32[]{:S(2)}) collective-permute-start(bf16[144,192]{1,0:T(8,128)(2,1)S(1)} %get-tuple-element.60.m2), channel_id=1, source_target_pairs={{2,0},{3,1},{4,2},{5,3},{6,4},{7,5},{8,6},{9,7},{10,8},{11,9},{12,... | collective-permute-start | bytes 165896 | tf_op jit(solution)/shard_map/ppermute | solution.py:679
  28.0 3.9 %copy-start.7 = (bf16[96,192]{1,0:T(8,128)(2,1)S(1)}, bf16[96,192]{1,0:T(8,128)(2,1)}, u32[]{:S(2)}) copy-start(bf16[96,192]{1,0:T(8,128)(2,1)} %proj_ref.1) | copy-start | bytes 110596
  31.9 4.7 %copy-start.14 = (bf16[576,128]{1,0:T(8,128)(2,1)S(1)}, bf16[576,128]{1,0:T(8,128)(2,1)}, u32[]{:S(2)}) copy-start(bf16[576,128]{1,0:T(8,128)(2,1)} %get-tuple-element.85.first_ref) | copy-start | bytes 442372
  37.2 3.2 %collective-permute-start.10 = (bf16[864,128]{1,0:T(8,128)(2,1)S(1)}, bf16[864,128]{1,0:T(8,128)(2,1)S(1)}, u32[]{:S(2)}, u32[]{:S(2)}) collective-permute-start(bf16[864,128]{1,0:T(8,128)(2,1)S(1)} %get-tuple-element.87), channel_id=1, source_target_pairs={{0,64},{64,0},{128,192},{192,128},{1,65},{65,1},{129,193},{193,129... | collective-permute-start | bytes 663560 | tf_op jit(solution)/shard_map/ppermute | solution.py:692
  37.3 10.0 %collective-permute-start.6 = (bf16[864,128]{1,0:T(8,128)(2,1)S(1)}, bf16[864,128]{1,0:T(8,128)(2,1)S(1)}, u32[]{:S(2)}, u32[]{:S(2)}) collective-permute-start(bf16[864,128]{1,0:T(8,128)(2,1)S(1)} %get-tuple-element.74.own_ref), channel_id=1, source_target_pairs={{1,0},{0,1},{3,2},{2,3},{5,4},{4,5},{7,6},{6,7},{9,8},{8,9},{11,10... | collective-permute-start | bytes 663560 | tf_op jit(solution)/shard_map/ppermute | solution.py:679
  37.4 3.0 %copy-start.15 = (bf16[576,128]{1,0:T(8,128)(2,1)S(1)}, bf16[576,128]{1,0:T(8,128)(2,1)}, u32[]{:S(2)}) copy-start(bf16[576,128]{1,0:T(8,128)(2,1)} %get-tuple-element.80.first_ref) | copy-start | bytes 442372
  41.3 21.3 %all-to-all-start = ((bf16[32,40,128]{2,1,0:T(8,128)(2,1)}), bf16[32,40,128]{2,1,0:T(8,128)(2,1)S(1)}, u32[]{:S(2)}, u32[]{:S(2)}) async-start(bf16[32,40,128]{2,1,0:T(8,128)(2,1)} %bitcast.11), calls=%async_computation | async-start | bytes 655360 | tf_op jit(solution)/shard_map/all_to_all | solution.py:739
  47.7 14.6 %collective-permute-start.7 = (bf16[144,192]{1,0:T(8,128)(2,1)S(1)}, bf16[144,192]{1,0:T(8,128)(2,1)S(1)}, u32[]{:S(2)}, u32[]{:S(2)}) collective-permute-start(bf16[144,192]{1,0:T(8,128)(2,1)S(1)} %get-tuple-element.75), channel_id=1, source_target_pairs={{254,0},{255,1},{192,2},{193,3},{194,4},{195,5},{196,6},{197,7},{1... | collective-permute-start | bytes 165896 | tf_op jit(solution)/shard_map/ppermute | solution.py:679
  52.5 9.8 %collective-permute-start.8 = (bf16[144,192]{1,0:T(8,128)(2,1)S(1)}, bf16[144,192]{1,0:T(8,128)(2,1)S(1)}, u32[]{:S(2)}, u32[]{:S(2)}) collective-permute-start(bf16[144,192]{1,0:T(8,128)(2,1)S(1)} %get-tuple-element.76), channel_id=1, source_target_pairs={{192,0},{193,1},{194,2},{195,3},{196,4},{197,5},{198,6},{199,7},{2... | collective-permute-start | bytes 165896 | tf_op jit(solution)/shard_map/ppermute | solution.py:679
  52.5 10.1 %collective-permute-start.9 = (bf16[144,192]{1,0:T(8,128)(2,1)S(1)}, bf16[144,192]{1,0:T(8,128)(2,1)S(1)}, u32[]{:S(2)}, u32[]{:S(2)}) collective-permute-start(bf16[144,192]{1,0:T(8,128)(2,1)S(1)} %get-tuple-element.77), channel_id=1, source_target_pairs={{62,0},{63,1},{0,2},{1,3},{2,4},{3,5},{4,6},{5,7},{6,8},{7,9},{8,1... | collective-permute-start | bytes 165896 | tf_op jit(solution)/shard_map/ppermute | solution.py:679
  62.6 2.8 %copy-start.6 = (bf16[288,192]{1,0:T(8,128)(2,1)S(1)}, bf16[288,192]{1,0:T(8,128)(2,1)}, u32[]{:S(2)}) copy-start(bf16[288,192]{1,0:T(8,128)(2,1)} %get-tuple-element.53.x10) | copy-start | bytes 331780
  62.6 4.1 %collective-permute-start.11 = (bf16[48,128]{1,0:T(8,128)(2,1)S(1)}, bf16[48,128]{1,0:T(8,128)(2,1)S(1)}, u32[]{:S(2)}, u32[]{:S(2)}) collective-permute-start(bf16[48,128]{1,0:T(8,128)(2,1)S(1)} %add.1.own_ref), channel_id=1, source_target_pairs={{128,0},{129,1},{130,2},{131,3},{132,4},{133,5},{134,6},{135,7},{1... | collective-permute-start | bytes 36872 | tf_op jit(solution)/shard_map/ppermute | solution.py:679
  83.6 5.8 %collective-permute-start.12 = (bf16[32,48,128]{2,1,0:T(8,128)(2,1)S(1)}, bf16[32,48,128]{2,1,0:T(8,128)(2,1)S(1)}, u32[]{:S(2)}, u32[]{:S(2)}) collective-permute-start(bf16[32,48,128]{2,1,0:T(8,128)(2,1)S(1)} %all_to_all.10.own_ref.got_ref), channel_id=1, source_target_pairs={{0,64},{64,0},{128,192},{192,128},{1,65},{65,1},{129,193},{193,129... | collective-permute-start | bytes 1179656 | tf_op jit(solution)/shard_map/ppermute | solution.py:692

commit v12 on v10

--- a/solution.py
+++ b/solution.py
@@ -89,15 +89,14 @@
             scratch[w * 144 + s * 36 : w * 144 + s * 36 + 36, :] = rows[w * 36 : w * 36 + 36]
 
 
-def head_kernel(x_hbm, mid_hbm, up_hbm, gain_hbm, fc1_hbm, fc2_hbm, o0, o1, o2, o3, part_hbm, keep_hbm, send_hbm,
-                x_ref, mid_ref, up_ref, gain_ref, fc1_ref, fc2_ref, xq_ref, part_ref, grads_ref, x_s, mid_s, up_s, sem):
+def head_kernel(mid_hbm, up_hbm, gain_hbm, fc1_hbm, fc2_hbm, part_hbm, keep_hbm, send_hbm,
+                mid_ref, up_ref, gain_ref, fc1_ref, fc2_ref, part_ref, grads_ref, mid_s, up_s, sem):
     pairs = (
         (mid_hbm, mid_ref),
         (gain_hbm, gain_ref),
         (fc1_hbm, fc1_ref),
         (up_hbm, up_ref),
         (fc2_hbm, fc2_ref),
-        (x_hbm, x_ref),
     )
     copies = [pltpu.make_async_copy(a, b, sem.at[i]) for i, (a, b) in enumerate(pairs)]
     for copy in copies:
@@ -111,12 +110,7 @@
     active, slopes = gelu_pair(pre)
     for copy in copies[3:]:
         copy.wait()
-    to_quarters(x_ref, x_s)
     writes = []
-    for q, out in enumerate((o0, o1, o2, o3)):
-        xq_ref[q] = x_s[q * 144 : q * 144 + 144, :].astype(BF)
-        writes.append(pltpu.make_async_copy(xq_ref.at[q], out, sem.at[8 + q]))
-        writes[-1].start()
     to_quarters(up_ref, up_s)
     up = up_s[...].astype(BF)
     grad_pre = (dot_nn(up, fc2_ref[...]) * slopes).astype(BF)
@@ -129,38 +123,34 @@
     core = lax.rem(lax.axis_index("lat"), 2)
     for i, (half, out) in enumerate(((core, keep_hbm), (1 - core, send_hbm))):
         piece = grads_ref.at[pl.ds(pl.multiple_of(half * 576, 16), 576)]
-        writes.append(pltpu.make_async_copy(piece, out, sem.at[12 + i]))
+        writes.append(pltpu.make_async_copy(piece, out, sem.at[7 + i]))
         writes[-1].start()
     for write in writes:
         write.wait()
 
 
-def head(x, mid, up, gain, fc1, fc2):
+def head(mid, up, gain, fc1, fc2):
     return pl.pallas_call(
         head_kernel,
-        out_shape=tuple(shape((144, 192), BF) for _ in range(4))
-        + (shape((576, 192), BF), shape((576, 128), BF), shape((576, 128), BF)),
-        in_specs=[ANY] * 6,
-        out_specs=tuple(ANY for _ in range(7)),
+        out_shape=(shape((576, 192), BF), shape((576, 128), BF), shape((576, 128), BF)),
+        in_specs=[ANY] * 5,
+        out_specs=(ANY, ANY, ANY),
         scratch_shapes=[
-            pltpu.VMEM((6, 12, 8, 192), BF),
             pltpu.VMEM((6, 12, 8, 192), BF),
             pltpu.VMEM((6, 12, 8, 192), BF),
             pltpu.VMEM((1, 192), F32),
             pltpu.VMEM((192, 384), BF),
             pltpu.VMEM((192, 384), BF),
-            pltpu.VMEM((4, 144, 192), BF),
             pltpu.VMEM((576, 192), BF),
             pltpu.VMEM((1152, 128), BF),
             pltpu.VMEM((576, 192), F32),
             pltpu.VMEM((576, 192), F32),
-            pltpu.VMEM((576, 192), F32),
-            pltpu.SemaphoreType.DMA((14,)),
+            pltpu.SemaphoreType.DMA((9,)),
         ],
         compiler_params=ALL,
         cost_estimate=cost(3),
         name="head",
-    )(x, mid, up, gain, fc1, fc2)
+    )(mid, up, gain, fc1, fc2)
 
 
 def middle_kernel(mid_ref, up_ref, own_ref, other_ref, gain_ref, after_ref, o0, o1, o2, o3, gain_out, mid_s, up_s):
@@ -233,8 +223,11 @@
     lax.fori_loop(0, steps, step, 0, unroll=True)
 
 
-def gather_first_kernel(index_ref, order_ref, bias_ref, ids_ref, valid_ref,
-                        stage, lo_ref, hi_ref, terms_ref, code_ref, table):
+def gather_first_kernel(index_ref, order_ref, bias_ref, ids_ref, valid_ref, x_ref,
+                        stage, lo_ref, hi_ref, terms_ref, code_ref, o0, o1, o2, o3, table, x_s):
+    to_quarters(x_ref, x_s)
+    for q, out in enumerate((o0, o1, o2, o3)):
+        out[...] = x_s[q * 144 : q * 144 + 144, :].astype(BF)
     index = index_ref[...]
     order = order_ref[...]
     pieces = []
@@ -268,7 +261,7 @@
     look_up(terms_ref[...], lo_ref, hi_ref, stage, 0, 5)
 
 
-def gather_first(index, bias, ids, valid):
+def gather_first(index, bias, ids, valid, x):
     return pl.pallas_call(
         gather_first_kernel,
         out_shape=(
@@ -277,12 +270,13 @@
             shape((168, 128), I32),
             shape((160, 512), BF),
             shape((4, 144), F32),
-        ),
-        scratch_shapes=[pltpu.VMEM((160, 256), F32)],
+        )
+        + tuple(shape((144, 192), BF) for _ in range(4)),
+        scratch_shapes=[pltpu.VMEM((160, 256), F32), pltpu.VMEM((576, 192), F32)],
         compiler_params=VM,
         cost_estimate=cost(0.5),
         name="gather_first",
-    )(index, jnp.asarray(window_order(), BF), bias, ids, valid)
+    )(index, jnp.asarray(window_order(), BF), bias, ids, valid, x)
 
 
 def gather_second_kernel(first_stage, lo_ref, hi_ref, terms_ref, a0, a1, a2, a3, main_ref, tail_ref, stage):
@@ -674,12 +668,12 @@
         return field.transpose(1, 2, 0, 3)
 
     x_in, mid_in, up_in = turned(inputs), turned(residual_mid), turned(grad_out)
-    *x, part2, first, first_send = head(x_in, mid_in, up_in, gain2, fc1_weight, fc2_weight.T)
+    part2, first, first_send = head(mid_in, up_in, gain2, fc1_weight, fc2_weight.T)
     other2 = moved(part2, 0, 0, 1)
+    stage, lo, hi, terms, code, *x = gather_first(
+        bias_index, pos_bias[0].transpose(1, 0, 2), mask_ids.transpose(1, 0, 2), key_valid.transpose(1, 0, 2), x_in
+    )
     xw = shifted_parts(x)
-    stage, lo, hi, terms, code = gather_first(
-        bias_index, pos_bias[0].transpose(1, 0, 2), mask_ids.transpose(1, 0, 2), key_valid.transpose(1, 0, 2)
-    )
     *gm, gain_two = middle(mid_in, up_in, part2, other2, gain2, lo)
     gw = shifted_parts(gm)
     main, tail = gather_second(stage, lo, hi, terms, (gain_two, *xw[1:]))

time: 90.3 us -> 90.1 us (level)
  waiting for transfers between devices: 13.2 us -> 12.1 us
    ppermute x12, starting transfers between devices: 24.3 us -> 26.7 us  [moved(): return lax.ppermute(value, ('lat', 'lon', 'tp'), pairs)]
    ppermute x2, starting transfers between devices: 6.73 us -> 5.05 us  [other_core(): lax.ppermute(value, 'lat', [(a, a ^ 1) for a in range(lax.axis_size('lat'...]
    ppermute x12, waiting for transfers between devices: 13.1 us -> 12 us  [moved(): return lax.ppermute(value, ('lat', 'lon', 'tp'), pairs)]
where the time goes in v12:
time: 90.1 us; the launch traced here: 89.9 us
  starting transfers between devices  35.9 us (40%)
  Pallas kernels  24.1 us (27%)
  blocking collectives  16.8 us (19%)
  waiting for transfers between devices  12.1 us (13%)
  between operations  0.95 us (1%)
    ppermute x12, starting transfers between devices, moved(): return lax.ppermute(value, ('lat', 'lon', 'tp'), pairs)  26.7 us
    all_to_all x1, blocking collectives, local(): got = lax.all_to_all(totals, 'lon', 0, 0)  16.8 us
    ppermute x12, waiting for transfers between devices, moved(): return lax.ppermute(value, ('lat', 'lon', 'tp'), pairs)  12 us
    ppermute x2, starting transfers between devices, other_core(): lax.ppermute(value, 'lat', [(a, a ^ 1) for a in range(lax.axis_size('lat'...  5.05 us
    pallas_call x1, Pallas kernels, backward(): pl.pallas_call(backward_kernel, out_shape=(shape((576, 192), BF), shape((...  4.61 us
    all_to_all x1, starting transfers between devices, local(): lax.all_to_all(sums.reshape(32, 40, 128), 'lon', 0, 0)  4.11 us
    pallas_call x1, Pallas kernels, head(): pl.pallas_call(head_kernel, out_shape=(shape((576, 192), BF), shape((576,...  3.43 us
    pallas_call x1, Pallas kernels, gather_first(): pl.pallas_call(gather_first_kernel, out_shape=(shape((90 * 16, 128), F32)...  3.05 us
  transfers between devices with their start and end apart: 15, of which 4 were waited for; matrix products, arithmetic and copies ran while one was open for 0% of the time, Pallas kernels for 16%

profile of v12, /device:TPU:1, one launch (start us, length us, event | category | flops | bytes accessed | tf_op | source)
XLA Modules:
  0.0 89.9 jit_solution(10856466915664003954)
XLA Ops:
  0.7 0.0 copy-start.13
  0.7 3.4 %head.1 = (bf16[576,192]{1,0:T(8,128)(2,1)}, bf16[576,128]{1,0:T(8,128)(2,1)}, bf16[576,128]{1,0:T(8,128)(2,1)}) custom-call(bf16[6,12,8,192]{3,2,1,0:T(8,128)(2,1)} %bitcast.20, bf16[6,12,8,192]{3,2,1,0:T(8,128)(2,1)} %bitcast.22, f32[1,192]{1,0:T(1,128)} %bitcast.27, bf16[192,384]{1,0:T(8,128)(2,1)} %fc1_hbm.1, bf16[192,384]{1,0:T(8,128)(2,1)} %bitcast.33), custom_call_target="tpu_custom_call" | custom-call | flops 3000000000 | tf_op jit(solution)/shard_map/head/pallas_call | solution.py:133
  4.1 0.0 copy-start.1
  4.1 0.0 copy-start.2
  4.2 0.0 copy-start.3
  4.2 0.0 copy-start.10
  4.2 2.2 %collective-permute-start = (bf16[576,192]{1,0:T(8,128)(2,1)}, bf16[576,192]{1,0:T(8,128)(2,1)S(1)}, u32[]{:S(2)}, u32[]{:S(2)}) collective-permute-start(bf16[576,192]{1,0:T(8,128)(2,1)} %get-tuple-element.56.own_ref), channel_id=1, source_target_pairs={{1,0},{0,1},{3,2},{2,3},{5,4},{4,5},{7,6},{6,7},{9,8},{8,9},{11,10... | collective-permute-start | bytes 663560 | tf_op jit(solution)/shard_map/ppermute | solution.py:630
  6.4 3.0 %gather_first.1 = (f32[1440,128]{1,0:T(8,128)S(1)}, s32[168,128]{1,0:T(8,128)S(1)}, s32[168,128]{1,0:T(8,128)S(1)}, bf16[160,512]{1,0:T(8,128)(2,1)S(1)}, f32[4,...) custom-call(s32[144,144]{1,0:T(8,128)S(1)} %copy-done.5, ...), custom_call_target="tpu_custom_call" | custom-call | flops 500000000 | tf_op jit(solution)/shard_map/gather_first/pallas_call | solution.py:265
  9.5 8.7 %collective-permute-start.6 = (bf16[144,192]{1,0:T(8,128)(2,1)S(1)}, bf16[144,192]{1,0:T(8,128)(2,1)S(1)}, u32[]{:S(2)}, u32[]{:S(2)}) collective-permute-start(bf16[144,192]{1,0:T(8,128)(2,1)S(1)} %get-tuple-element.52.x0), channel_id=1, source_target_pairs={{66,0},{67,1},{68,2},{69,3},{70,4},{71,5},{72,6},{73,7},{74,8},{75... | collective-permute-start | bytes 165896 | tf_op jit(solution)/shard_map/ppermute | solution.py:630
  18.2 1.9 %collective-permute-start.5 = (bf16[144,192]{1,0:T(8,128)(2,1)S(1)}, bf16[144,192]{1,0:T(8,128)(2,1)S(1)}, u32[]{:S(2)}, u32[]{:S(2)}) collective-permute-start(bf16[144,192]{1,0:T(8,128)(2,1)S(1)} %get-tuple-element.53.x1), channel_id=1, source_target_pairs={{64,0},{65,1},{66,2},{67,3},{68,4},{69,5},{70,6},{71,7},{72,8},{73... | collective-permute-start | bytes 165896 | tf_op jit(solution)/shard_map/ppermute | solution.py:630
  20.1 0.5 collective-permute-start.4
  20.6 0.0 collective-permute-done.other_ref
  20.6 0.6 middle.1
  21.2 1.9 %collective-permute-start.3 = (bf16[144,192]{1,0:T(8,128)(2,1)S(1)}, bf16[144,192]{1,0:T(8,128)(2,1)S(1)}, u32[]{:S(2)}, u32[]{:S(2)}) collective-permute-start(bf16[144,192]{1,0:T(8,128)(2,1)S(1)} %get-tuple-element.58.m0), channel_id=1, source_target_pairs={{66,0},{67,1},{68,2},{69,3},{70,4},{71,5},{72,6},{73,7},{74,8},{75... | collective-permute-start | bytes 165896 | tf_op jit(solution)/shard_map/ppermute | solution.py:630
  23.1 1.6 %collective-permute-start.2 = (bf16[144,192]{1,0:T(8,128)(2,1)S(1)}, bf16[144,192]{1,0:T(8,128)(2,1)S(1)}, u32[]{:S(2)}, u32[]{:S(2)}) collective-permute-start(bf16[144,192]{1,0:T(8,128)(2,1)S(1)} %get-tuple-element.59.m1), channel_id=1, source_target_pairs={{64,0},{65,1},{66,2},{67,3},{68,4},{69,5},{70,6},{71,7},{72,8},{73... | collective-permute-start | bytes 165896 | tf_op jit(solution)/shard_map/ppermute | solution.py:630
  24.7 0.0 collective-permute-done.6.a3.x3
  24.7 2.7 %collective-permute-start.1 = (bf16[144,192]{1,0:T(8,128)(2,1)S(1)}, bf16[144,192]{1,0:T(8,128)(2,1)S(1)}, u32[]{:S(2)}, u32[]{:S(2)}) collective-permute-start(bf16[144,192]{1,0:T(8,128)(2,1)S(1)} %get-tuple-element.60.m2), channel_id=1, source_target_pairs={{2,0},{3,1},{4,2},{5,3},{6,4},{7,5},{8,6},{9,7},{10,8},{11,9},{12,... | collective-permute-start | bytes 165896 | tf_op jit(solution)/shard_map/ppermute | solution.py:630
  27.4 0.0 collective-permute-done.5.a2.x2
  27.4 0.0 collective-permute-done.4.a1.x1
  27.4 0.0 copy-start.11
  27.4 0.0 copy-start.12
  27.5 2.1 %gather_second.1 = (f32[12,144,128]{2,1,0:T(8,128)S(1)}, f32[12,144,128]{2,1,0:T(8,128)S(1)}) custom-call(f32[1440,128]{1,0:T(8,128)S(1)} %get-tuple-element.62.first_stage, s32[168,128]{1,0:T(8,128)S(1)} %get-tuple-element.57.after_ref.lo_ref, s32[168,128]{1,0:T(8,128)S(1)} %get-tuple-element.63.hi_ref, bf16[160,512]{1,0:T(8,128)(2,1)S(1)} %get-tuple-element.64.terms_ref, ...), custom_call_target="tpu_custom_call" | custom-call | flops 4000000000 | tf_op jit(solution)/shard_map/gather_second/pallas_call | solution.py:293
  29.6 0.0 copy-start.7
  29.7 3.0 %forward.1 = (bf16[576,192]{1,0:T(8,128)(2,1)S(1)}, bf16[576,96]{1,0:T(8,128)(2,1)S(1)}, bf16[576,96]{1,0:T(8,128)(2,1)S(1)}, bf16[576,96]{1,0:T(8,128)(2,1)S(1)...) custom-call(bf16[144,192]{1,0:T(8,128)(2,1)S(1)} %get-tuple-element.55.x0.x3, ...), custom_call_target="tpu_custom_call" | custom-call | flops 5000000000 | tf_op jit(solution)/shard_map/forward/pallas_call | solution.py:338
  32.7 0.0 collective-permute-done.1.g1
  32.7 0.0 copy-start.14
  32.7 4.6 %backward.1 = (bf16[576,192]{1,0:T(8,128)(2,1)S(1)}, f32[12,144,128]{2,1,0:T(8,128)S(1)}, f32[12,144,128]{2,1,0:T(8,128)S(1)}, bf16[3,576,96]{2,1,0:T(8,128)(2,1)S(1)}, bf16[576,192]{1,0:T(8,128)(2,1)S(1)}) custom-call(bf16[144,192]{1,0:T(8,128)(2,1)S(1)} %get-tuple-element.61.g0.m3, bf16[144,192]{1,0:T(8,128)(2,1)S(1)} %collective-permute-done.1.g1, ...), custom_call_target="tpu_custom_call" | custom-call | flops 7000000000 | tf_op jit(solution)/shard_map/backward/pallas_call | solution.py:395
  37.3 0.6 weigh.1
  37.9 0.7 collective-permute-start.11
  38.6 0.4 collective-permute-start.7
  39.0 3.0 %scatter.1.table_ref = f32[192,256]{1,0:T(8,128)S(1)} custom-call(f32[12,144,128]{2,1,0:T(8,128)S(1)} %get-tuple-element.86.score_ref, f32[12,144,128]{2,1,0:T(8,128)S(1)} %get-tuple-element.87.end_ref, s32[168,128]{1,0:T(8,128)S(1)} %get-tuple-element.57.after_ref.lo_ref, s32[168,128]{1,0:T(8,128)S(1)} %get-tuple-element.63.hi_ref, ...), custom_call_target="tpu_custom_call" | custom-call | flops 4000000000 | tf_op jit(solution)/shard_map/scatter/pallas_call | solution.py:434
  42.0 0.0 collective-permute-done.11.other_ref
  42.0 0.8 pack.1
  42.8 4.1 %all-to-all-start = ((bf16[32,40,128]{2,1,0:T(8,128)(2,1)}), bf16[32,40,128]{2,1,0:T(8,128)(2,1)S(1)}, u32[]{:S(2)}, u32[]{:S(2)}) async-start(bf16[32,40,128]{2,1,0:T(8,128)(2,1)} %bitcast.11), calls=%async_computation | async-start | bytes 655360 | tf_op jit(solution)/shard_map/all_to_all | solution.py:688
  46.9 0.2 collective-permute-done.7.other_ref
  47.1 0.3 meet.1
  47.5 3.5 %collective-permute-start.8 = (bf16[144,192]{1,0:T(8,128)(2,1)S(1)}, bf16[144,192]{1,0:T(8,128)(2,1)S(1)}, u32[]{:S(2)}, u32[]{:S(2)}) collective-permute-start(bf16[144,192]{1,0:T(8,128)(2,1)S(1)} %get-tuple-element.74), channel_id=1, source_target_pairs={{254,0},{255,1},{192,2},{193,3},{194,4},{195,5},{196,6},{197,7},{1... | collective-permute-start | bytes 165896 | tf_op jit(solution)/shard_map/ppermute | solution.py:630
  50.9 0.0 collective-permute-start.9
  50.9 1.2 %collective-permute-start.10 = (bf16[144,192]{1,0:T(8,128)(2,1)S(1)}, bf16[144,192]{1,0:T(8,128)(2,1)S(1)}, u32[]{:S(2)}, u32[]{:S(2)}) collective-permute-start(bf16[144,192]{1,0:T(8,128)(2,1)S(1)} %get-tuple-element.76), channel_id=1, source_target_pairs={{62,0},{63,1},{0,2},{1,3},{2,4},{3,5},{4,6},{5,7},{6,8},{7,9},{8,1... | collective-permute-start | bytes 165896 | tf_op jit(solution)/shard_map/ppermute | solution.py:630
  52.1 9.8 %collective-permute-done.8.g0.b0 = bf16[144,192]{1,0:T(8,128)(2,1)S(1)} collective-permute-done((bf16[144,192]{1,0:T(8,128)(2,1)S(1)}, bf16[144,192]{1,0:T(8,128)(2,1)S(1)}, u32[]{:S(2)}, u32[]{:S(2)}) %collective-permute-start.8) | collective-permute-done | bytes 55328 | tf_op jit(solution)/shard_map/ppermute | solution.py:630
  62.0 0.1 add.1.own_ref
  62.0 2.2 %collective-permute-start.12 = (bf16[48,128]{1,0:T(8,128)(2,1)S(1)}, bf16[48,128]{1,0:T(8,128)(2,1)S(1)}, u32[]{:S(2)}, u32[]{:S(2)}) collective-permute-start(bf16[48,128]{1,0:T(8,128)(2,1)S(1)} %add.1.own_ref), channel_id=1, source_target_pairs={{128,0},{129,1},{130,2},{131,3},{132,4},{133,5},{134,6},{135,7},{1... | collective-permute-start | bytes 36872 | tf_op jit(solution)/shard_map/ppermute | solution.py:630
  64.2 2.0 %collective-permute-done.12.other_ref = bf16[48,128]{1,0:T(8,128)(2,1)S(1)} collective-permute-done((bf16[48,128]{1,0:T(8,128)(2,1)S(1)}, bf16[48,128]{1,0:T(8,128)(2,1)S(1)}, u32[]{:S(2)}, u32[]{:S(2)}) %collective-permute-start.12) | collective-permute-done | bytes 12320 | tf_op jit(solution)/shard_map/ppermute | solution.py:630
  66.2 16.8 %all_to_all.10.own_ref = bf16[32,48,128]{2,1,0:T(8,128)(2,1)S(1)} all-to-all(bf16[32,48,128]{2,1,0:T(8,128)(2,1)S(1)} %spread.1), channel_id=1, replica_groups=mesh['lat'=4,'lon'=32,'tp'=2] {'lon'}, dimensions={0} | all-to-all | bytes 786432 | tf_op jit(solution)/shard_map/all_to_all | solution.py:691
  83.0 4.4 %collective-permute-start.13 = (bf16[32,48,128]{2,1,0:T(8,128)(2,1)S(1)}, bf16[32,48,128]{2,1,0:T(8,128)(2,1)S(1)}, u32[]{:S(2)}, u32[]{:S(2)}) collective-permute-start(bf16[32,48,128]{2,1,0:T(8,128)(2,1)S(1)} %all_to_all.10.own_ref), channel_id=1, source_target_pairs={{0,64},{64,0},{128,192},{192,128},{1,65},{65,1},{129,193},{193,129... | collective-permute-start | bytes 1179656 | tf_op jit(solution)/shard_map/ppermute | solution.py:643
  87.3 1.2 %finish.1 = bf16[6,12,8,192]{3,2,1,0:T(8,128)(2,1)} custom-call(bf16[144,192]{1,0:T(8,128)(2,1)S(1)} %get-tuple-element.52.x0, bf16[144,192]{1,0:T(8,128)(2,1)S(1)} %get-tuple-element.53.x1, bf16[144,192]{1,0:T(8,128)(2,1)S(1)} %get-tuple-element.54.x2, bf16[144,192]{1,0:T(8,128)(2,1)S(1)} %get-tuple-element.55.x0.x3, ...), custom_call_target="tpu_custom_call" | custom-call | flops 1000000000 | tf_op jit(solution)/shard_map/finish/pallas_call | solution.py:524
  88.6 0.1 collective-permute-done.13.other_ref
  88.7 1.2 %unpack.1 = (f32[3,192,96]{2,1,0:T(8,128)}, f32[96,192]{1,0:T(8,128)}, f32[192,384]{1,0:T(8,128)}, f32[192,384]{1,0:T(8,128)}, f32[1,96]{1,0:T(1,128)}, /*index=5*/f32[1,96]{1,0:T(1,128)}, f32[3,4,3312]{2,1,0:T(4,128)}) custom-call(bf16[32,48,128]{2,1,0:T(8,128)(2,1)S(1)} %all_to_all.10.own_ref, bf16[32,48,128]{2,1,0:T(8,128)(2,1)S(1)} %collective-permute-done.13.other_ref), custom_call_target="tpu_custom_call" | custom-call | tf_op jit(solution)/shard_map/unpack/pallas_call | solution.py:606
  (29 shorter events, 0.1 us)
Async XLA Ops:
  0.6 5.8 %copy-start = (bf16[8,6,12,192]{3,0,2,1:T(8,128)(2,1)S(1)}, bf16[8,6,12,192]{3,0,2,1:T(8,128)(2,1)}, u32[]{:S(2)}) copy-start(bf16[8,6,12,192]{3,0,2,1:T(8,128)(2,1)} %param.16) | copy-start | bytes 663556
  0.6 5.8 %copy-start.4 = (f32[1,4,3,3312]{3,1,2,0:T(4,128)S(1)}, f32[1,4,3,3312]{3,1,2,0:T(4,128)}, u32[]{:S(2)}) copy-start(f32[1,4,3,3312]{3,1,2,0:T(4,128)} %param.22) | copy-start | bytes 476932
  0.7 5.8 %copy-start.5 = (s32[144,144]{1,0:T(8,128)S(1)}, s32[144,144]{1,0:T(8,128)}, u32[]{:S(2)}) copy-start(s32[144,144]{1,0:T(8,128)} %index_ref.1) | copy-start | bytes 248836
  0.7 5.7 %copy-start.8 = (s32[8,6,12]{2,0,1:T(8,128)S(1)}, s32[8,6,12]{2,0,1:T(8,128)}, u32[]{:S(2)}) copy-start(s32[8,6,12]{2,0,1:T(8,128)} %param.19) | copy-start | bytes 6916
  0.7 5.7 %copy-start.9 = (s32[8,6,12]{2,0,1:T(8,128)S(1)}, s32[8,6,12]{2,0,1:T(8,128)}, u32[]{:S(2)}) copy-start(s32[8,6,12]{2,0,1:T(8,128)} %param.20) | copy-start | bytes 6916
  0.7 5.7 %copy-start.13 = (bf16[144,144]{1,0:T(8,128)(2,1)S(1)}, bf16[144,144]{1,0:T(8,128)(2,1)}, u32[]{:S(2)}) copy-start(bf16[144,144]{1,0:T(8,128)(2,1)} %constant.4.clone.order_ref) | copy-start | bytes 124420
  4.1 16.5 %copy-start.1 = (bf16[8,6,12,192]{3,0,2,1:T(8,128)(2,1)S(1)}, bf16[8,6,12,192]{3,0,2,1:T(8,128)(2,1)}, u32[]{:S(2)}) copy-start(bf16[8,6,12,192]{3,0,2,1:T(8,128)(2,1)} %param.17) | copy-start | bytes 663556
  4.1 16.5 %copy-start.2 = (bf16[8,6,12,192]{3,0,2,1:T(8,128)(2,1)S(1)}, bf16[8,6,12,192]{3,0,2,1:T(8,128)(2,1)}, u32[]{:S(2)}) copy-start(bf16[8,6,12,192]{3,0,2,1:T(8,128)(2,1)} %param.18) | copy-start | bytes 663556
  4.2 16.5 %copy-start.3 = (bf16[576,192]{1,0:T(8,128)(2,1)S(1)}, bf16[576,192]{1,0:T(8,128)(2,1)}, u32[]{:S(2)}) copy-start(bf16[576,192]{1,0:T(8,128)(2,1)} %get-tuple-element.56.own_ref) | copy-start | bytes 663556
  4.2 16.5 %copy-start.10 = (f32[192]{0:T(256)S(1)}, f32[192]{0:T(256)}, u32[]{:S(2)}) copy-start(f32[192]{0:T(256)} %param.26) | copy-start | bytes 2308
  4.2 16.4 %collective-permute-start = (bf16[576,192]{1,0:T(8,128)(2,1)}, bf16[576,192]{1,0:T(8,128)(2,1)S(1)}, u32[]{:S(2)}, u32[]{:S(2)}) collective-permute-start(bf16[576,192]{1,0:T(8,128)(2,1)} %get-tuple-element.56.own_ref), channel_id=1, source_target_pairs={{1,0},{0,1},{3,2},{2,3},{5,4},{4,5},{7,6},{6,7},{9,8},{8,9},{11,10... | collective-permute-start | bytes 663560 | tf_op jit(solution)/shard_map/ppermute | solution.py:630
  9.5 15.2 %collective-permute-start.6 = (bf16[144,192]{1,0:T(8,128)(2,1)S(1)}, bf16[144,192]{1,0:T(8,128)(2,1)S(1)}, u32[]{:S(2)}, u32[]{:S(2)}) collective-permute-start(bf16[144,192]{1,0:T(8,128)(2,1)S(1)} %get-tuple-element.52.x0), channel_id=1, source_target_pairs={{66,0},{67,1},{68,2},{69,3},{70,4},{71,5},{72,6},{73,7},{74,8},{75... | collective-permute-start | bytes 165896 | tf_op jit(solution)/shard_map/ppermute | solution.py:630
  18.2 9.2 %collective-permute-start.5 = (bf16[144,192]{1,0:T(8,128)(2,1)S(1)}, bf16[144,192]{1,0:T(8,128)(2,1)S(1)}, u32[]{:S(2)}, u32[]{:S(2)}) collective-permute-start(bf16[144,192]{1,0:T(8,128)(2,1)S(1)} %get-tuple-element.53.x1), channel_id=1, source_target_pairs={{64,0},{65,1},{66,2},{67,3},{68,4},{69,5},{70,6},{71,7},{72,8},{73... | collective-permute-start | bytes 165896 | tf_op jit(solution)/shard_map/ppermute | solution.py:630
  20.1 7.4 %collective-permute-start.4 = (bf16[144,192]{1,0:T(8,128)(2,1)S(1)}, bf16[144,192]{1,0:T(8,128)(2,1)S(1)}, u32[]{:S(2)}, u32[]{:S(2)}) collective-permute-start(bf16[144,192]{1,0:T(8,128)(2,1)S(1)} %get-tuple-element.54.x2), channel_id=1, source_target_pairs={{2,0},{3,1},{4,2},{5,3},{6,4},{7,5},{8,6},{9,7},{10,8},{11,9},{12,... | collective-permute-start | bytes 165896 | tf_op jit(solution)/shard_map/ppermute | solution.py:630
  21.2 11.4 %collective-permute-start.3 = (bf16[144,192]{1,0:T(8,128)(2,1)S(1)}, bf16[144,192]{1,0:T(8,128)(2,1)S(1)}, u32[]{:S(2)}, u32[]{:S(2)}) collective-permute-start(bf16[144,192]{1,0:T(8,128)(2,1)S(1)} %get-tuple-element.58.m0), channel_id=1, source_target_pairs={{66,0},{67,1},{68,2},{69,3},{70,4},{71,5},{72,6},{73,7},{74,8},{75... | collective-permute-start | bytes 165896 | tf_op jit(solution)/shard_map/ppermute | solution.py:630
  23.1 9.6 %collective-permute-start.2 = (bf16[144,192]{1,0:T(8,128)(2,1)S(1)}, bf16[144,192]{1,0:T(8,128)(2,1)S(1)}, u32[]{:S(2)}, u32[]{:S(2)}) collective-permute-start(bf16[144,192]{1,0:T(8,128)(2,1)S(1)} %get-tuple-element.59.m1), channel_id=1, source_target_pairs={{64,0},{65,1},{66,2},{67,3},{68,4},{69,5},{70,6},{71,7},{72,8},{73... | collective-permute-start | bytes 165896 | tf_op jit(solution)/shard_map/ppermute | solution.py:630
  24.7 8.0 %collective-permute-start.1 = (bf16[144,192]{1,0:T(8,128)(2,1)S(1)}, bf16[144,192]{1,0:T(8,128)(2,1)S(1)}, u32[]{:S(2)}, u32[]{:S(2)}) collective-permute-start(bf16[144,192]{1,0:T(8,128)(2,1)S(1)} %get-tuple-element.60.m2), channel_id=1, source_target_pairs={{2,0},{3,1},{4,2},{5,3},{6,4},{7,5},{8,6},{9,7},{10,8},{11,9},{12,... | collective-permute-start | bytes 165896 | tf_op jit(solution)/shard_map/ppermute | solution.py:630
  27.4 2.2 %copy-start.6 = (bf16[3,192,96]{2,1,0:T(8,128)(2,1)S(1)}, bf16[3,192,96]{2,1,0:T(8,128)(2,1)}, u32[]{:S(2)}) copy-start(bf16[3,192,96]{2,1,0:T(8,128)(2,1)} %qkv_ref.3) | copy-start | bytes 331780
  27.4 2.2 %copy-start.11 = (f32[192]{0:T(256)S(1)}, f32[192]{0:T(256)}, u32[]{:S(2)}) copy-start(f32[192]{0:T(256)} %param.23) | copy-start | bytes 2308
  27.4 2.2 %copy-start.12 = (bf16[144,144]{1,0:T(8,128)(2,1)S(1)}, bf16[144,144]{1,0:T(8,128)(2,1)}, u32[]{:S(2)}) copy-start(bf16[144,144]{1,0:T(8,128)(2,1)} %constant.5.clone.order_ref) | copy-start | bytes 124420
  29.6 3.1 %copy-start.7 = (bf16[96,192]{1,0:T(8,128)(2,1)S(1)}, bf16[96,192]{1,0:T(8,128)(2,1)}, u32[]{:S(2)}) copy-start(bf16[96,192]{1,0:T(8,128)(2,1)} %proj_ref.1) | copy-start | bytes 110596
  32.7 4.6 %copy-start.14 = (bf16[576,128]{1,0:T(8,128)(2,1)S(1)}, bf16[576,128]{1,0:T(8,128)(2,1)}, u32[]{:S(2)}) copy-start(bf16[576,128]{1,0:T(8,128)(2,1)} %get-tuple-element.83.first_ref) | copy-start | bytes 442372
  37.9 4.1 %collective-permute-start.11 = (bf16[864,128]{1,0:T(8,128)(2,1)S(1)}, bf16[864,128]{1,0:T(8,128)(2,1)S(1)}, u32[]{:S(2)}, u32[]{:S(2)}) collective-permute-start(bf16[864,128]{1,0:T(8,128)(2,1)S(1)} %get-tuple-element.85), channel_id=1, source_target_pairs={{0,64},{64,0},{128,192},{192,128},{1,65},{65,1},{129,193},{193,129... | collective-permute-start | bytes 663560 | tf_op jit(solution)/shard_map/ppermute | solution.py:643
  38.6 8.6 %collective-permute-start.7 = (bf16[576,192]{1,0:T(8,128)(2,1)S(1)}, bf16[576,192]{1,0:T(8,128)(2,1)S(1)}, u32[]{:S(2)}, u32[]{:S(2)}) collective-permute-start(bf16[576,192]{1,0:T(8,128)(2,1)S(1)} %get-tuple-element.73.own_ref), channel_id=1, source_target_pairs={{1,0},{0,1},{3,2},{2,3},{5,4},{4,5},{7,6},{6,7},{9,8},{8,9},{11,10... | collective-permute-start | bytes 663560 | tf_op jit(solution)/shard_map/ppermute | solution.py:630
  39.0 3.0 %copy-start.15 = (bf16[576,128]{1,0:T(8,128)(2,1)S(1)}, bf16[576,128]{1,0:T(8,128)(2,1)}, u32[]{:S(2)}) copy-start(bf16[576,128]{1,0:T(8,128)(2,1)} %get-tuple-element.78.first_ref) | copy-start | bytes 442372
  42.8 19.1 %all-to-all-start = ((bf16[32,40,128]{2,1,0:T(8,128)(2,1)}), bf16[32,40,128]{2,1,0:T(8,128)(2,1)S(1)}, u32[]{:S(2)}, u32[]{:S(2)}) async-start(bf16[32,40,128]{2,1,0:T(8,128)(2,1)} %bitcast.11), calls=%async_computation | async-start | bytes 655360 | tf_op jit(solution)/shard_map/all_to_all | solution.py:688
  47.5 14.5 %collective-permute-start.8 = (bf16[144,192]{1,0:T(8,128)(2,1)S(1)}, bf16[144,192]{1,0:T(8,128)(2,1)S(1)}, u32[]{:S(2)}, u32[]{:S(2)}) collective-permute-start(bf16[144,192]{1,0:T(8,128)(2,1)S(1)} %get-tuple-element.74), channel_id=1, source_target_pairs={{254,0},{255,1},{192,2},{193,3},{194,4},{195,5},{196,6},{197,7},{1... | collective-permute-start | bytes 165896 | tf_op jit(solution)/shard_map/ppermute | solution.py:630
  50.9 11.0 %collective-permute-start.9 = (bf16[144,192]{1,0:T(8,128)(2,1)S(1)}, bf16[144,192]{1,0:T(8,128)(2,1)S(1)}, u32[]{:S(2)}, u32[]{:S(2)}) collective-permute-start(bf16[144,192]{1,0:T(8,128)(2,1)S(1)} %get-tuple-element.75), channel_id=1, source_target_pairs={{192,0},{193,1},{194,2},{195,3},{196,4},{197,5},{198,6},{199,7},{2... | collective-permute-start | bytes 165896 | tf_op jit(solution)/shard_map/ppermute | solution.py:630
  50.9 11.0 %collective-permute-start.10 = (bf16[144,192]{1,0:T(8,128)(2,1)S(1)}, bf16[144,192]{1,0:T(8,128)(2,1)S(1)}, u32[]{:S(2)}, u32[]{:S(2)}) collective-permute-start(bf16[144,192]{1,0:T(8,128)(2,1)S(1)} %get-tuple-element.76), channel_id=1, source_target_pairs={{62,0},{63,1},{0,2},{1,3},{2,4},{3,5},{4,6},{5,7},{6,8},{7,9},{8,1... | collective-permute-start | bytes 165896 | tf_op jit(solution)/shard_map/ppermute | solution.py:630
  62.0 4.1 %collective-permute-start.12 = (bf16[48,128]{1,0:T(8,128)(2,1)S(1)}, bf16[48,128]{1,0:T(8,128)(2,1)S(1)}, u32[]{:S(2)}, u32[]{:S(2)}) collective-permute-start(bf16[48,128]{1,0:T(8,128)(2,1)S(1)} %add.1.own_ref), channel_id=1, source_target_pairs={{128,0},{129,1},{130,2},{131,3},{132,4},{133,5},{134,6},{135,7},{1... | collective-permute-start | bytes 36872 | tf_op jit(solution)/shard_map/ppermute | solution.py:630
  83.0 5.7 %collective-permute-start.13 = (bf16[32,48,128]{2,1,0:T(8,128)(2,1)S(1)}, bf16[32,48,128]{2,1,0:T(8,128)(2,1)S(1)}, u32[]{:S(2)}, u32[]{:S(2)}) collective-permute-start(bf16[32,48,128]{2,1,0:T(8,128)(2,1)S(1)} %all_to_all.10.own_ref), channel_id=1, source_target_pairs={{0,64},{64,0},{128,192},{192,128},{1,65},{65,1},{129,193},{193,129... | collective-permute-start | bytes 1179656 | tf_op jit(solution)/shard_map/ppermute | solution.py:643

commit v13 on v12

--- a/solution.py
+++ b/solution.py
@@ -258,14 +258,14 @@
         lines += [picked[lat * 4 : lat * 4 + 4] for lat in range(6)]
     lines = jnp.concatenate(lines, axis=1)
     code_ref[...] = dot_nt(lines.astype(BF), order)
-    look_up(terms_ref[...], lo_ref, hi_ref, stage, 0, 5)
+    look_up(terms_ref[...], lo_ref, hi_ref, stage, 0, 7)
 
 
 def gather_first(index, bias, ids, valid, x):
     return pl.pallas_call(
         gather_first_kernel,
         out_shape=(
-            shape((90 * 16, 128), F32),
+            shape((126 * 16, 128), F32),
             shape((168, 128), I32),
             shape((168, 128), I32),
             shape((160, 512), BF),
@@ -280,11 +280,11 @@
 
 
 def gather_second_kernel(first_stage, lo_ref, hi_ref, terms_ref, a0, a1, a2, a3, main_ref, tail_ref, stage):
-    look_up(terms_ref[...], lo_ref, hi_ref, stage, 90, 4)
+    look_up(terms_ref[...], lo_ref, hi_ref, stage, 126, 2)
     for r in range(12):
-        main_ref[r, 0:90, :] = first_stage[pl.ds(r, 90, stride=16), :]
-        main_ref[r, 90:144, :] = stage[pl.ds(r, 54, stride=16), :]
-        packed = stage[pl.ds(54 * 16 + r, 18, stride=16), :]
+        main_ref[r, 0:126, :] = first_stage[pl.ds(r, 126, stride=16), :]
+        main_ref[r, 126:144, :] = stage[pl.ds(r, 18, stride=16), :]
+        packed = stage[pl.ds(18 * 16 + r, 18, stride=16), :]
         for s in range(8):
             tail_ref[r, pl.ds(s, 18, stride=8), :] = pltpu.roll(packed, 128 - 16 * s, 1) if s else packed
 
@@ -294,7 +294,7 @@
         gather_second_kernel,
         out_shape=(shape((12, 144, 128), F32), shape((12, 144, 128), F32)),
         in_specs=[VMEM] * 4 + [ANY] * 4,
-        scratch_shapes=[pltpu.VMEM((72 * 16, 128), F32)],
+        scratch_shapes=[pltpu.VMEM((36 * 16, 128), F32)],
         compiler_params=VM,
         cost_estimate=cost(4),
         name="gather_second",

time: 90.1 us -> 90.7 us (level)
    all_to_all x1, starting transfers between devices: 4.11 us -> 5.04 us  [local(): lax.all_to_all(sums.reshape(32, 40, 128), 'lon', 0, 0)]
  transfers between devices with their start and end apart: 15 -> 15, of which waited for: 4 -> 3; matrix products, arithmetic and copies ran while one was open for 0% -> 0% of each run, Pallas kernels for 16% -> 16%
where the time goes in v13:
time: 90.7 us; the launch traced here: 90.4 us
  starting transfers between devices  35.9 us (40%)
  Pallas kernels  24.1 us (27%)
  blocking collectives  16.5 us (18%)
  waiting for transfers between devices  12.9 us (14%)
  between operations  0.96 us (1%)
    ppermute x12, starting transfers between devices, moved(): return lax.ppermute(value, ('lat', 'lon', 'tp'), pairs)  26.3 us
    all_to_all x1, blocking collectives, local(): got = lax.all_to_all(totals, 'lon', 0, 0)  16.5 us
    ppermute x12, waiting for transfers between devices, moved(): return lax.ppermute(value, ('lat', 'lon', 'tp'), pairs)  12.8 us
    all_to_all x1, starting transfers between devices, local(): lax.all_to_all(sums.reshape(32, 40, 128), 'lon', 0, 0)  5.04 us
    pallas_call x1, Pallas kernels, backward(): pl.pallas_call(backward_kernel, out_shape=(shape((576, 192), BF), shape((...  4.6 us
    ppermute x2, starting transfers between devices, other_core(): lax.ppermute(value, 'lat', [(a, a ^ 1) for a in range(lax.axis_size('lat'...  4.57 us
    pallas_call x1, Pallas kernels, gather_first(): pl.pallas_call(gather_first_kernel, out_shape=(shape((126 * 16, 128), F32...  3.83 us
    pallas_call x1, Pallas kernels, head(): pl.pallas_call(head_kernel, out_shape=(shape((576, 192), BF), shape((576,...  3.43 us
  transfers between devices with their start and end apart: 15, of which 3 were waited for; matrix products, arithmetic and copies ran while one was open for 0% of the time, Pallas kernels for 16%

profile of v13, /device:TPU:1, one launch (start us, length us, event | category | flops | bytes accessed | tf_op | source)
XLA Modules:
  0.0 90.4 jit_solution(5366909053340961790)
XLA Ops:
  0.7 0.0 copy-start.13
  0.7 3.4 %head.1 = (bf16[576,192]{1,0:T(8,128)(2,1)}, bf16[576,128]{1,0:T(8,128)(2,1)}, bf16[576,128]{1,0:T(8,128)(2,1)}) custom-call(bf16[6,12,8,192]{3,2,1,0:T(8,128)(2,1)} %bitcast.20, bf16[6,12,8,192]{3,2,1,0:T(8,128)(2,1)} %bitcast.22, f32[1,192]{1,0:T(1,128)} %bitcast.27, bf16[192,384]{1,0:T(8,128)(2,1)} %fc1_hbm.1, bf16[192,384]{1,0:T(8,128)(2,1)} %bitcast.33), custom_call_target="tpu_custom_call" | custom-call | flops 3000000000 | tf_op jit(solution)/shard_map/head/pallas_call | solution.py:133
  4.1 0.0 copy-start.1
  4.1 0.0 copy-start.2
  4.2 0.0 copy-start.3
  4.2 0.0 copy-start.10
  4.2 2.2 %collective-permute-start = (bf16[576,192]{1,0:T(8,128)(2,1)}, bf16[576,192]{1,0:T(8,128)(2,1)S(1)}, u32[]{:S(2)}, u32[]{:S(2)}) collective-permute-start(bf16[576,192]{1,0:T(8,128)(2,1)} %get-tuple-element.56.own_ref), channel_id=1, source_target_pairs={{1,0},{0,1},{3,2},{2,3},{5,4},{4,5},{7,6},{6,7},{9,8},{8,9},{11,10... | collective-permute-start | bytes 663560 | tf_op jit(solution)/shard_map/ppermute | solution.py:630
  6.4 3.8 %gather_first.1 = (f32[2016,128]{1,0:T(8,128)S(1)}, s32[168,128]{1,0:T(8,128)S(1)}, s32[168,128]{1,0:T(8,128)S(1)}, bf16[160,512]{1,0:T(8,128)(2,1)S(1)}, f32[4,...) custom-call(s32[144,144]{1,0:T(8,128)S(1)} %copy-done.5, ...), custom_call_target="tpu_custom_call" | custom-call | flops 500000000 | tf_op jit(solution)/shard_map/gather_first/pallas_call | solution.py:265
  10.3 8.7 %collective-permute-start.6 = (bf16[144,192]{1,0:T(8,128)(2,1)S(1)}, bf16[144,192]{1,0:T(8,128)(2,1)S(1)}, u32[]{:S(2)}, u32[]{:S(2)}) collective-permute-start(bf16[144,192]{1,0:T(8,128)(2,1)S(1)} %get-tuple-element.52.x0), channel_id=1, source_target_pairs={{66,0},{67,1},{68,2},{69,3},{70,4},{71,5},{72,6},{73,7},{74,8},{75... | collective-permute-start | bytes 165896 | tf_op jit(solution)/shard_map/ppermute | solution.py:630
  19.0 1.9 %collective-permute-start.5 = (bf16[144,192]{1,0:T(8,128)(2,1)S(1)}, bf16[144,192]{1,0:T(8,128)(2,1)S(1)}, u32[]{:S(2)}, u32[]{:S(2)}) collective-permute-start(bf16[144,192]{1,0:T(8,128)(2,1)S(1)} %get-tuple-element.53.x1), channel_id=1, source_target_pairs={{64,0},{65,1},{66,2},{67,3},{68,4},{69,5},{70,6},{71,7},{72,8},{73... | collective-permute-start | bytes 165896 | tf_op jit(solution)/shard_map/ppermute | solution.py:630
  20.8 0.5 collective-permute-start.4
  21.4 0.0 collective-permute-done.other_ref
  21.4 0.6 middle.1
  22.0 1.6 %collective-permute-start.3 = (bf16[144,192]{1,0:T(8,128)(2,1)S(1)}, bf16[144,192]{1,0:T(8,128)(2,1)S(1)}, u32[]{:S(2)}, u32[]{:S(2)}) collective-permute-start(bf16[144,192]{1,0:T(8,128)(2,1)S(1)} %get-tuple-element.58.m0), channel_id=1, source_target_pairs={{66,0},{67,1},{68,2},{69,3},{70,4},{71,5},{72,6},{73,7},{74,8},{75... | collective-permute-start | bytes 165896 | tf_op jit(solution)/shard_map/ppermute | solution.py:630
  23.6 1.0 %collective-permute-start.2 = (bf16[144,192]{1,0:T(8,128)(2,1)S(1)}, bf16[144,192]{1,0:T(8,128)(2,1)S(1)}, u32[]{:S(2)}, u32[]{:S(2)}) collective-permute-start(bf16[144,192]{1,0:T(8,128)(2,1)S(1)} %get-tuple-element.59.m1), channel_id=1, source_target_pairs={{64,0},{65,1},{66,2},{67,3},{68,4},{69,5},{70,6},{71,7},{72,8},{73... | collective-permute-start | bytes 165896 | tf_op jit(solution)/shard_map/ppermute | solution.py:630
  24.7 3.5 %collective-permute-start.1 = (bf16[144,192]{1,0:T(8,128)(2,1)S(1)}, bf16[144,192]{1,0:T(8,128)(2,1)S(1)}, u32[]{:S(2)}, u32[]{:S(2)}) collective-permute-start(bf16[144,192]{1,0:T(8,128)(2,1)S(1)} %get-tuple-element.60.m2), channel_id=1, source_target_pairs={{2,0},{3,1},{4,2},{5,3},{6,4},{7,5},{8,6},{9,7},{10,8},{11,9},{12,... | collective-permute-start | bytes 165896 | tf_op jit(solution)/shard_map/ppermute | solution.py:630
  28.2 0.0 collective-permute-done.5.a2.x2
  28.2 0.0 copy-start.11
  28.2 0.0 copy-start.12
  28.2 1.4 %gather_second.1 = (f32[12,144,128]{2,1,0:T(8,128)S(1)}, f32[12,144,128]{2,1,0:T(8,128)S(1)}) custom-call(f32[2016,128]{1,0:T(8,128)S(1)} %get-tuple-element.62.first_stage, s32[168,128]{1,0:T(8,128)S(1)} %get-tuple-element.57.after_ref.lo_ref, s32[168,128]{1,0:T(8,128)S(1)} %get-tuple-element.63.hi_ref, bf16[160,512]{1,0:T(8,128)(2,1)S(1)} %get-tuple-element.64.terms_ref, ...), custom_call_target="tpu_custom_call" | custom-call | flops 4000000000 | tf_op jit(solution)/shard_map/gather_second/pallas_call | solution.py:293
  29.7 0.0 copy-start.7
  29.7 3.0 %forward.1 = (bf16[576,192]{1,0:T(8,128)(2,1)S(1)}, bf16[576,96]{1,0:T(8,128)(2,1)S(1)}, bf16[576,96]{1,0:T(8,128)(2,1)S(1)}, bf16[576,96]{1,0:T(8,128)(2,1)S(1)...) custom-call(bf16[144,192]{1,0:T(8,128)(2,1)S(1)} %get-tuple-element.55.x0.x3, ...), custom_call_target="tpu_custom_call" | custom-call | flops 5000000000 | tf_op jit(solution)/shard_map/forward/pallas_call | solution.py:338
  32.7 0.0 collective-permute-done.3.g3
  32.7 0.0 collective-permute-done.1.g1
  32.7 0.0 copy-start.14
  32.7 4.6 %backward.1 = (bf16[576,192]{1,0:T(8,128)(2,1)S(1)}, f32[12,144,128]{2,1,0:T(8,128)S(1)}, f32[12,144,128]{2,1,0:T(8,128)S(1)}, bf16[3,576,96]{2,1,0:T(8,128)(2,1)S(1)}, bf16[576,192]{1,0:T(8,128)(2,1)S(1)}) custom-call(bf16[144,192]{1,0:T(8,128)(2,1)S(1)} %get-tuple-element.61.g0.m3, bf16[144,192]{1,0:T(8,128)(2,1)S(1)} %collective-permute-done.1.g1, ...), custom_call_target="tpu_custom_call" | custom-call | flops 7000000000 | tf_op jit(solution)/shard_map/backward/pallas_call | solution.py:395
  37.4 0.6 weigh.1
  37.9 0.1 collective-permute-start.11
  38.0 0.5 collective-permute-start.7
  38.5 3.0 %scatter.1.table_ref = f32[192,256]{1,0:T(8,128)S(1)} custom-call(f32[12,144,128]{2,1,0:T(8,128)S(1)} %get-tuple-element.86.score_ref, f32[12,144,128]{2,1,0:T(8,128)S(1)} %get-tuple-element.87.end_ref, s32[168,128]{1,0:T(8,128)S(1)} %get-tuple-element.57.after_ref.lo_ref, s32[168,128]{1,0:T(8,128)S(1)} %get-tuple-element.63.hi_ref, ...), custom_call_target="tpu_custom_call" | custom-call | flops 4000000000 | tf_op jit(solution)/shard_map/scatter/pallas_call | solution.py:434
  41.5 0.8 pack.1
  42.3 5.0 %all-to-all-start = ((bf16[32,40,128]{2,1,0:T(8,128)(2,1)}), bf16[32,40,128]{2,1,0:T(8,128)(2,1)S(1)}, u32[]{:S(2)}, u32[]{:S(2)}) async-start(bf16[32,40,128]{2,1,0:T(8,128)(2,1)} %bitcast.11), calls=%async_computation | async-start | bytes 655360 | tf_op jit(solution)/shard_map/all_to_all | solution.py:688
  47.4 0.3 meet.1
  47.7 3.6 %collective-permute-start.8 = (bf16[144,192]{1,0:T(8,128)(2,1)S(1)}, bf16[144,192]{1,0:T(8,128)(2,1)S(1)}, u32[]{:S(2)}, u32[]{:S(2)}) collective-permute-start(bf16[144,192]{1,0:T(8,128)(2,1)S(1)} %get-tuple-element.74), channel_id=1, source_target_pairs={{254,0},{255,1},{192,2},{193,3},{194,4},{195,5},{196,6},{197,7},{1... | collective-permute-start | bytes 165896 | tf_op jit(solution)/shard_map/ppermute | solution.py:630
  51.3 0.0 collective-permute-start.9
  51.3 1.2 %collective-permute-start.10 = (bf16[144,192]{1,0:T(8,128)(2,1)S(1)}, bf16[144,192]{1,0:T(8,128)(2,1)S(1)}, u32[]{:S(2)}, u32[]{:S(2)}) collective-permute-start(bf16[144,192]{1,0:T(8,128)(2,1)S(1)} %get-tuple-element.76), channel_id=1, source_target_pairs={{62,0},{63,1},{0,2},{1,3},{2,4},{3,5},{4,6},{5,7},{6,8},{7,9},{8,1... | collective-permute-start | bytes 165896 | tf_op jit(solution)/shard_map/ppermute | solution.py:630
  52.5 10.1 %collective-permute-done.8.g0.b0 = bf16[144,192]{1,0:T(8,128)(2,1)S(1)} collective-permute-done((bf16[144,192]{1,0:T(8,128)(2,1)S(1)}, bf16[144,192]{1,0:T(8,128)(2,1)S(1)}, u32[]{:S(2)}, u32[]{:S(2)}) %collective-permute-start.8) | collective-permute-done | bytes 55328 | tf_op jit(solution)/shard_map/ppermute | solution.py:630
  62.6 0.0 collective-permute-done.9.g1.b1
  62.6 0.0 collective-permute-done.10.g2.b2
  62.6 0.0 all-to-all-done.got_ref
  62.6 0.1 add.1.own_ref
  62.7 1.5 %collective-permute-start.12 = (bf16[48,128]{1,0:T(8,128)(2,1)S(1)}, bf16[48,128]{1,0:T(8,128)(2,1)S(1)}, u32[]{:S(2)}, u32[]{:S(2)}) collective-permute-start(bf16[48,128]{1,0:T(8,128)(2,1)S(1)} %add.1.own_ref), channel_id=1, source_target_pairs={{128,0},{129,1},{130,2},{131,3},{132,4},{133,5},{134,6},{135,7},{1... | collective-permute-start | bytes 36872 | tf_op jit(solution)/shard_map/ppermute | solution.py:630
  64.2 2.6 %collective-permute-done.12.other_ref = bf16[48,128]{1,0:T(8,128)(2,1)S(1)} collective-permute-done((bf16[48,128]{1,0:T(8,128)(2,1)S(1)}, bf16[48,128]{1,0:T(8,128)(2,1)S(1)}, u32[]{:S(2)}, u32[]{:S(2)}) %collective-permute-start.12) | collective-permute-done | bytes 12320 | tf_op jit(solution)/shard_map/ppermute | solution.py:630
  66.9 16.5 %all_to_all.10.own_ref = bf16[32,48,128]{2,1,0:T(8,128)(2,1)S(1)} all-to-all(bf16[32,48,128]{2,1,0:T(8,128)(2,1)S(1)} %spread.1), channel_id=1, replica_groups=mesh['lat'=4,'lon'=32,'tp'=2] {'lon'}, dimensions={0} | all-to-all | bytes 786432 | tf_op jit(solution)/shard_map/all_to_all | solution.py:691
  83.4 4.5 %collective-permute-start.13 = (bf16[32,48,128]{2,1,0:T(8,128)(2,1)S(1)}, bf16[32,48,128]{2,1,0:T(8,128)(2,1)S(1)}, u32[]{:S(2)}, u32[]{:S(2)}) collective-permute-start(bf16[32,48,128]{2,1,0:T(8,128)(2,1)S(1)} %all_to_all.10.own_ref), channel_id=1, source_target_pairs={{0,64},{64,0},{128,192},{192,128},{1,65},{65,1},{129,193},{193,129... | collective-permute-start | bytes 1179656 | tf_op jit(solution)/shard_map/ppermute | solution.py:643
  87.9 1.2 %finish.1 = bf16[6,12,8,192]{3,2,1,0:T(8,128)(2,1)} custom-call(bf16[144,192]{1,0:T(8,128)(2,1)S(1)} %get-tuple-element.52.x0, bf16[144,192]{1,0:T(8,128)(2,1)S(1)} %get-tuple-element.53.x1, bf16[144,192]{1,0:T(8,128)(2,1)S(1)} %get-tuple-element.54.x2, bf16[144,192]{1,0:T(8,128)(2,1)S(1)} %get-tuple-element.55.x0.x3, ...), custom_call_target="tpu_custom_call" | custom-call | flops 1000000000 | tf_op jit(solution)/shard_map/finish/pallas_call | solution.py:524
  89.1 0.1 collective-permute-done.13.other_ref
  89.2 1.2 %unpack.1 = (f32[3,192,96]{2,1,0:T(8,128)}, f32[96,192]{1,0:T(8,128)}, f32[192,384]{1,0:T(8,128)}, f32[192,384]{1,0:T(8,128)}, f32[1,96]{1,0:T(1,128)}, /*index=5*/f32[1,96]{1,0:T(1,128)}, f32[3,4,3312]{2,1,0:T(4,128)}) custom-call(bf16[32,48,128]{2,1,0:T(8,128)(2,1)S(1)} %all_to_all.10.own_ref, bf16[32,48,128]{2,1,0:T(8,128)(2,1)S(1)} %collective-permute-done.13.other_ref), custom_call_target="tpu_custom_call" | custom-call | tf_op jit(solution)/shard_map/unpack/pallas_call | solution.py:606
  (29 shorter events, 0.1 us)
Async XLA Ops:
  0.6 5.8 %copy-start = (bf16[8,6,12,192]{3,0,2,1:T(8,128)(2,1)S(1)}, bf16[8,6,12,192]{3,0,2,1:T(8,128)(2,1)}, u32[]{:S(2)}) copy-start(bf16[8,6,12,192]{3,0,2,1:T(8,128)(2,1)} %param.16) | copy-start | bytes 663556
  0.6 5.8 %copy-start.4 = (f32[1,4,3,3312]{3,1,2,0:T(4,128)S(1)}, f32[1,4,3,3312]{3,1,2,0:T(4,128)}, u32[]{:S(2)}) copy-start(f32[1,4,3,3312]{3,1,2,0:T(4,128)} %param.22) | copy-start | bytes 476932
  0.7 5.8 %copy-start.5 = (s32[144,144]{1,0:T(8,128)S(1)}, s32[144,144]{1,0:T(8,128)}, u32[]{:S(2)}) copy-start(s32[144,144]{1,0:T(8,128)} %index_ref.1) | copy-start | bytes 248836
  0.7 5.7 %copy-start.8 = (s32[8,6,12]{2,0,1:T(8,128)S(1)}, s32[8,6,12]{2,0,1:T(8,128)}, u32[]{:S(2)}) copy-start(s32[8,6,12]{2,0,1:T(8,128)} %param.19) | copy-start | bytes 6916
  0.7 5.7 %copy-start.9 = (s32[8,6,12]{2,0,1:T(8,128)S(1)}, s32[8,6,12]{2,0,1:T(8,128)}, u32[]{:S(2)}) copy-start(s32[8,6,12]{2,0,1:T(8,128)} %param.20) | copy-start | bytes 6916
  0.7 5.7 %copy-start.13 = (bf16[144,144]{1,0:T(8,128)(2,1)S(1)}, bf16[144,144]{1,0:T(8,128)(2,1)}, u32[]{:S(2)}) copy-start(bf16[144,144]{1,0:T(8,128)(2,1)} %constant.4.clone.order_ref) | copy-start | bytes 124420
  4.1 17.3 %copy-start.1 = (bf16[8,6,12,192]{3,0,2,1:T(8,128)(2,1)S(1)}, bf16[8,6,12,192]{3,0,2,1:T(8,128)(2,1)}, u32[]{:S(2)}) copy-start(bf16[8,6,12,192]{3,0,2,1:T(8,128)(2,1)} %param.17) | copy-start | bytes 663556
  4.1 17.2 %copy-start.2 = (bf16[8,6,12,192]{3,0,2,1:T(8,128)(2,1)S(1)}, bf16[8,6,12,192]{3,0,2,1:T(8,128)(2,1)}, u32[]{:S(2)}) copy-start(bf16[8,6,12,192]{3,0,2,1:T(8,128)(2,1)} %param.18) | copy-start | bytes 663556
  4.2 17.2 %copy-start.3 = (bf16[576,192]{1,0:T(8,128)(2,1)S(1)}, bf16[576,192]{1,0:T(8,128)(2,1)}, u32[]{:S(2)}) copy-start(bf16[576,192]{1,0:T(8,128)(2,1)} %get-tuple-element.56.own_ref) | copy-start | bytes 663556
  4.2 17.2 %copy-start.10 = (f32[192]{0:T(256)S(1)}, f32[192]{0:T(256)}, u32[]{:S(2)}) copy-start(f32[192]{0:T(256)} %param.26) | copy-start | bytes 2308
  4.2 17.2 %collective-permute-start = (bf16[576,192]{1,0:T(8,128)(2,1)}, bf16[576,192]{1,0:T(8,128)(2,1)S(1)}, u32[]{:S(2)}, u32[]{:S(2)}) collective-permute-start(bf16[576,192]{1,0:T(8,128)(2,1)} %get-tuple-element.56.own_ref), channel_id=1, source_target_pairs={{1,0},{0,1},{3,2},{2,3},{5,4},{4,5},{7,6},{6,7},{9,8},{8,9},{11,10... | collective-permute-start | bytes 663560 | tf_op jit(solution)/shard_map/ppermute | solution.py:630
  10.3 14.4 %collective-permute-start.6 = (bf16[144,192]{1,0:T(8,128)(2,1)S(1)}, bf16[144,192]{1,0:T(8,128)(2,1)S(1)}, u32[]{:S(2)}, u32[]{:S(2)}) collective-permute-start(bf16[144,192]{1,0:T(8,128)(2,1)S(1)} %get-tuple-element.52.x0), channel_id=1, source_target_pairs={{66,0},{67,1},{68,2},{69,3},{70,4},{71,5},{72,6},{73,7},{74,8},{75... | collective-permute-start | bytes 165896 | tf_op jit(solution)/shard_map/ppermute | solution.py:630
  19.0 9.2 %collective-permute-start.5 = (bf16[144,192]{1,0:T(8,128)(2,1)S(1)}, bf16[144,192]{1,0:T(8,128)(2,1)S(1)}, u32[]{:S(2)}, u32[]{:S(2)}) collective-permute-start(bf16[144,192]{1,0:T(8,128)(2,1)S(1)} %get-tuple-element.53.x1), channel_id=1, source_target_pairs={{64,0},{65,1},{66,2},{67,3},{68,4},{69,5},{70,6},{71,7},{72,8},{73... | collective-permute-start | bytes 165896 | tf_op jit(solution)/shard_map/ppermute | solution.py:630
  20.8 7.4 %collective-permute-start.4 = (bf16[144,192]{1,0:T(8,128)(2,1)S(1)}, bf16[144,192]{1,0:T(8,128)(2,1)S(1)}, u32[]{:S(2)}, u32[]{:S(2)}) collective-permute-start(bf16[144,192]{1,0:T(8,128)(2,1)S(1)} %get-tuple-element.54.x2), channel_id=1, source_target_pairs={{2,0},{3,1},{4,2},{5,3},{6,4},{7,5},{8,6},{9,7},{10,8},{11,9},{12,... | collective-permute-start | bytes 165896 | tf_op jit(solution)/shard_map/ppermute | solution.py:630
  22.0 10.7 %collective-permute-start.3 = (bf16[144,192]{1,0:T(8,128)(2,1)S(1)}, bf16[144,192]{1,0:T(8,128)(2,1)S(1)}, u32[]{:S(2)}, u32[]{:S(2)}) collective-permute-start(bf16[144,192]{1,0:T(8,128)(2,1)S(1)} %get-tuple-element.58.m0), channel_id=1, source_target_pairs={{66,0},{67,1},{68,2},{69,3},{70,4},{71,5},{72,6},{73,7},{74,8},{75... | collective-permute-start | bytes 165896 | tf_op jit(solution)/shard_map/ppermute | solution.py:630
  23.6 9.1 %collective-permute-start.2 = (bf16[144,192]{1,0:T(8,128)(2,1)S(1)}, bf16[144,192]{1,0:T(8,128)(2,1)S(1)}, u32[]{:S(2)}, u32[]{:S(2)}) collective-permute-start(bf16[144,192]{1,0:T(8,128)(2,1)S(1)} %get-tuple-element.59.m1), channel_id=1, source_target_pairs={{64,0},{65,1},{66,2},{67,3},{68,4},{69,5},{70,6},{71,7},{72,8},{73... | collective-permute-start | bytes 165896 | tf_op jit(solution)/shard_map/ppermute | solution.py:630
  24.7 8.0 %collective-permute-start.1 = (bf16[144,192]{1,0:T(8,128)(2,1)S(1)}, bf16[144,192]{1,0:T(8,128)(2,1)S(1)}, u32[]{:S(2)}, u32[]{:S(2)}) collective-permute-start(bf16[144,192]{1,0:T(8,128)(2,1)S(1)} %get-tuple-element.60.m2), channel_id=1, source_target_pairs={{2,0},{3,1},{4,2},{5,3},{6,4},{7,5},{8,6},{9,7},{10,8},{11,9},{12,... | collective-permute-start | bytes 165896 | tf_op jit(solution)/shard_map/ppermute | solution.py:630
  28.2 1.5 %copy-start.6 = (bf16[3,192,96]{2,1,0:T(8,128)(2,1)S(1)}, bf16[3,192,96]{2,1,0:T(8,128)(2,1)}, u32[]{:S(2)}) copy-start(bf16[3,192,96]{2,1,0:T(8,128)(2,1)} %qkv_ref.3) | copy-start | bytes 331780
  28.2 1.5 %copy-start.11 = (f32[192]{0:T(256)S(1)}, f32[192]{0:T(256)}, u32[]{:S(2)}) copy-start(f32[192]{0:T(256)} %param.23) | copy-start | bytes 2308
  28.2 1.5 %copy-start.12 = (bf16[144,144]{1,0:T(8,128)(2,1)S(1)}, bf16[144,144]{1,0:T(8,128)(2,1)}, u32[]{:S(2)}) copy-start(bf16[144,144]{1,0:T(8,128)(2,1)} %constant.5.clone.order_ref) | copy-start | bytes 124420
  29.7 3.0 %copy-start.7 = (bf16[96,192]{1,0:T(8,128)(2,1)S(1)}, bf16[96,192]{1,0:T(8,128)(2,1)}, u32[]{:S(2)}) copy-start(bf16[96,192]{1,0:T(8,128)(2,1)} %proj_ref.1) | copy-start | bytes 110596
  32.7 4.6 %copy-start.14 = (bf16[576,128]{1,0:T(8,128)(2,1)S(1)}, bf16[576,128]{1,0:T(8,128)(2,1)}, u32[]{:S(2)}) copy-start(bf16[576,128]{1,0:T(8,128)(2,1)} %get-tuple-element.83.first_ref) | copy-start | bytes 442372
  37.9 3.6 %collective-permute-start.11 = (bf16[864,128]{1,0:T(8,128)(2,1)S(1)}, bf16[864,128]{1,0:T(8,128)(2,1)S(1)}, u32[]{:S(2)}, u32[]{:S(2)}) collective-permute-start(bf16[864,128]{1,0:T(8,128)(2,1)S(1)} %get-tuple-element.85), channel_id=1, source_target_pairs={{0,64},{64,0},{128,192},{192,128},{1,65},{65,1},{129,193},{193,129... | collective-permute-start | bytes 663560 | tf_op jit(solution)/shard_map/ppermute | solution.py:643
  38.0 9.4 %collective-permute-start.7 = (bf16[576,192]{1,0:T(8,128)(2,1)S(1)}, bf16[576,192]{1,0:T(8,128)(2,1)S(1)}, u32[]{:S(2)}, u32[]{:S(2)}) collective-permute-start(bf16[576,192]{1,0:T(8,128)(2,1)S(1)} %get-tuple-element.73.own_ref), channel_id=1, source_target_pairs={{1,0},{0,1},{3,2},{2,3},{5,4},{4,5},{7,6},{6,7},{9,8},{8,9},{11,10... | collective-permute-start | bytes 663560 | tf_op jit(solution)/shard_map/ppermute | solution.py:630
  38.5 3.0 %copy-start.15 = (bf16[576,128]{1,0:T(8,128)(2,1)S(1)}, bf16[576,128]{1,0:T(8,128)(2,1)}, u32[]{:S(2)}) copy-start(bf16[576,128]{1,0:T(8,128)(2,1)} %get-tuple-element.78.first_ref) | copy-start | bytes 442372
  42.3 20.3 %all-to-all-start = ((bf16[32,40,128]{2,1,0:T(8,128)(2,1)}), bf16[32,40,128]{2,1,0:T(8,128)(2,1)S(1)}, u32[]{:S(2)}, u32[]{:S(2)}) async-start(bf16[32,40,128]{2,1,0:T(8,128)(2,1)} %bitcast.11), calls=%async_computation | async-start | bytes 655360 | tf_op jit(solution)/shard_map/all_to_all | solution.py:688
  47.7 14.9 %collective-permute-start.8 = (bf16[144,192]{1,0:T(8,128)(2,1)S(1)}, bf16[144,192]{1,0:T(8,128)(2,1)S(1)}, u32[]{:S(2)}, u32[]{:S(2)}) collective-permute-start(bf16[144,192]{1,0:T(8,128)(2,1)S(1)} %get-tuple-element.74), channel_id=1, source_target_pairs={{254,0},{255,1},{192,2},{193,3},{194,4},{195,5},{196,6},{197,7},{1... | collective-permute-start | bytes 165896 | tf_op jit(solution)/shard_map/ppermute | solution.py:630
  51.3 11.3 %collective-permute-start.9 = (bf16[144,192]{1,0:T(8,128)(2,1)S(1)}, bf16[144,192]{1,0:T(8,128)(2,1)S(1)}, u32[]{:S(2)}, u32[]{:S(2)}) collective-permute-start(bf16[144,192]{1,0:T(8,128)(2,1)S(1)} %get-tuple-element.75), channel_id=1, source_target_pairs={{192,0},{193,1},{194,2},{195,3},{196,4},{197,5},{198,6},{199,7},{2... | collective-permute-start | bytes 165896 | tf_op jit(solution)/shard_map/ppermute | solution.py:630
  51.3 11.3 %collective-permute-start.10 = (bf16[144,192]{1,0:T(8,128)(2,1)S(1)}, bf16[144,192]{1,0:T(8,128)(2,1)S(1)}, u32[]{:S(2)}, u32[]{:S(2)}) collective-permute-start(bf16[144,192]{1,0:T(8,128)(2,1)S(1)} %get-tuple-element.76), channel_id=1, source_target_pairs={{62,0},{63,1},{0,2},{1,3},{2,4},{3,5},{4,6},{5,7},{6,8},{7,9},{8,1... | collective-permute-start | bytes 165896 | tf_op jit(solution)/shard_map/ppermute | solution.py:630
  62.7 4.1 %collective-permute-start.12 = (bf16[48,128]{1,0:T(8,128)(2,1)S(1)}, bf16[48,128]{1,0:T(8,128)(2,1)S(1)}, u32[]{:S(2)}, u32[]{:S(2)}) collective-permute-start(bf16[48,128]{1,0:T(8,128)(2,1)S(1)} %add.1.own_ref), channel_id=1, source_target_pairs={{128,0},{129,1},{130,2},{131,3},{132,4},{133,5},{134,6},{135,7},{1... | collective-permute-start | bytes 36872 | tf_op jit(solution)/shard_map/ppermute | solution.py:630
  83.4 5.8 %collective-permute-start.13 = (bf16[32,48,128]{2,1,0:T(8,128)(2,1)S(1)}, bf16[32,48,128]{2,1,0:T(8,128)(2,1)S(1)}, u32[]{:S(2)}, u32[]{:S(2)}) collective-permute-start(bf16[32,48,128]{2,1,0:T(8,128)(2,1)S(1)} %all_to_all.10.own_ref), channel_id=1, source_target_pairs={{0,64},{64,0},{128,192},{192,128},{1,65},{65,1},{129,193},{193,129... | collective-permute-start | bytes 1179656 | tf_op jit(solution)/shard_map/ppermute | solution.py:643

commit v14 on v12

--- a/solution.py
+++ b/solution.py
@@ -31,6 +31,18 @@
 
 def both(own, other):
     return (own.astype(F32) + other.astype(F32)).astype(BF)
+
+
+def fold(rows):
+    return jnp.concatenate(
+        [rows[:, 0:128], jnp.concatenate([rows[0:72, 128:192], rows[72:144, 128:192]], axis=1)], axis=0
+    )
+
+
+def unfold(rows):
+    return jnp.concatenate(
+        [rows[0:144], jnp.concatenate([rows[144:216, 0:64], rows[144:216, 64:128]], axis=0)], axis=1
+    )
 
 
 def dot_nn(a, b):
@@ -265,7 +277,7 @@
     return pl.pallas_call(
         gather_first_kernel,
         out_shape=(
-            shape((90 * 16, 128), F32),
+            shape((96 * 16, 128), F32),
             shape((168, 128), I32),
             shape((168, 128), I32),
             shape((160, 512), BF),
@@ -292,9 +304,9 @@
 def gather_second(first_stage, lo, hi, terms, after):
     return pl.pallas_call(
         gather_second_kernel,
-        out_shape=(shape((12, 144, 128), F32), shape((12, 144, 128), F32)),
+        out_shape=(shape((12, 144, 128), F32), shape((12, 192, 128), F32)),
         in_specs=[VMEM] * 4 + [ANY] * 4,
-        scratch_shapes=[pltpu.VMEM((72 * 16, 128), F32)],
+        scratch_shapes=[pltpu.VMEM((80 * 16, 128), F32)],
         compiler_params=VM,
         cost_estimate=cost(4),
         name="gather_second",
@@ -321,7 +333,7 @@
         heads = []
         for h in range(3):
             cols = slice(h * HD, h * HD + HD)
-            bias = jnp.concatenate([main_ref[w * 3 + h], tail_ref[w * 3 + h][:, 0:16]], axis=1)
+            bias = jnp.concatenate([main_ref[w * 3 + h], tail_ref[w * 3 + h, 0:144, 0:16]], axis=1)
             scores = dot_nt(query[:, cols], key[:, cols]) * (HD ** -0.5) + bias
             scores = jnp.where(allowed, scores, EXCLUDED)
             expo = jnp.exp(scores - jnp.max(scores, axis=-1, keepdims=True))
@@ -370,7 +382,7 @@
             grad_prob = dot_nt(above[:, cols], value[:, cols])
             score = prob * (grad_prob - jnp.sum(grad_prob * prob, axis=-1, keepdims=True))
             score_ref[w * 3 + h] = score[:, 0:128]
-            end_ref[w * 3 + h, :, 0:16] = score[:, 128:144]
+            end_ref[w * 3 + h, 0:144, 0:16] = score[:, 128:144]
             low_score = (score * (HD ** -0.5)).astype(BF)
             queries.append(dot_nn(low_score, key[:, cols]))
             keys.append(dot_tn(query[:, cols], low_score))
@@ -397,7 +409,7 @@
         out_shape=(
             shape((576, 192), BF),
             shape((12, 144, 128), F32),
-            shape((12, 144, 128), F32),
+            shape((12, 192, 128), F32),
             shape((3, 576, 96), BF),
             shape((576, 192), BF),
         ),
@@ -497,14 +509,14 @@
         grad = own_ref[rows, :].astype(F32) + other_ref[rows, :].astype(F32)
         normed, _ = layer_stats(x[...].astype(F32))
         gain = gain + jnp.sum(grad * normed, axis=0, keepdims=True)
-        g[...] = grad.astype(BF)
+        g[...] = fold(grad).astype(BF)
     gain_out[...] = jnp.concatenate(gain_rows(gain) + [jnp.zeros((6, 128), F32)], axis=0)
 
 
 def meet(own, other, x):
     return pl.pallas_call(
         meet_kernel,
-        out_shape=tuple(shape((144, 192), BF) for _ in range(4)) + (shape((8, 128), F32),),
+        out_shape=tuple(shape((216, 128), BF) for _ in range(4)) + (shape((8, 128), F32),),
         compiler_params=VM,
         cost_estimate=cost(60),
         name="meet",
@@ -514,7 +526,7 @@
 def finish_kernel(x0, x1, x2, x3, m0, m1, m2, m3, g0, g1, g2, g3, gain_ref, out_ref):
     for q, (x, m, g) in enumerate(zip((x0, x1, x2, x3), (m0, m1, m2, m3), (g0, g1, g2, g3))):
         normed, inverse = layer_stats(x[...].astype(F32))
-        rows = m[...].astype(F32) + norm_backward(g[...].astype(F32), gain_ref[...], normed, inverse)
+        rows = m[...].astype(F32) + norm_backward(unfold(g[...].astype(F32)), gain_ref[...], normed, inverse)
         for lat in range(3):
             piece = rows[lat * 48 : lat * 48 + 48].reshape(6, 8, 192)
             out_ref[(q // 2) * 3 + lat, (q % 2) * 6 : (q % 2) * 6 + 6] = piece.astype(BF)

time: 90.1 us -> 89.5 us (level)
  waiting for transfers between devices: 12.1 us -> 11.1 us
  transfers between devices with their start and end apart: 15 -> 15, of which waited for: 4 -> 3; matrix products, arithmetic and copies ran while one was open for 0% -> 0% of each run, Pallas kernels for 16% -> 16%
where the time goes in v14:
time: 89.5 us; the launch traced here: 89.3 us
  starting transfers between devices  35.9 us (40%)
  Pallas kernels  24.4 us (27%)
  blocking collectives  16.7 us (19%)
  waiting for transfers between devices  11.1 us (12%)
  between operations  0.95 us (1%)
    ppermute x12, starting transfers between devices, moved(): return lax.ppermute(value, ('lat', 'lon', 'tp'), pairs)  26.8 us
    all_to_all x1, blocking collectives, local(): got = lax.all_to_all(totals, 'lon', 0, 0)  16.7 us
    ppermute x12, waiting for transfers between devices, moved(): return lax.ppermute(value, ('lat', 'lon', 'tp'), pairs)  11.1 us
    ppermute x2, starting transfers between devices, other_core(): lax.ppermute(value, 'lat', [(a, a ^ 1) for a in range(lax.axis_size('lat'...  5.03 us
    pallas_call x1, Pallas kernels, backward(): pl.pallas_call(backward_kernel, out_shape=(shape((576, 192), BF), shape((...  4.61 us
    all_to_all x1, starting transfers between devices, local(): lax.all_to_all(sums.reshape(32, 40, 128), 'lon', 0, 0)  4.13 us
    pallas_call x1, Pallas kernels, head(): pl.pallas_call(head_kernel, out_shape=(shape((576, 192), BF), shape((576,...  3.43 us
    pallas_call x1, Pallas kernels, gather_first(): pl.pallas_call(gather_first_kernel, out_shape=(shape((96 * 16, 128), F32)...  3.05 us
  transfers between devices with their start and end apart: 15, of which 3 were waited for; matrix products, arithmetic and copies ran while one was open for 0% of the time, Pallas kernels for 16%

profile of v14, /device:TPU:1, one launch (start us, length us, event | category | flops | bytes accessed | tf_op | source)
XLA Modules:
  0.0 89.3 jit_solution(15221347780667775713)
XLA Ops:
  0.7 0.0 copy-start.13
  0.7 3.4 %head.1 = (bf16[576,192]{1,0:T(8,128)(2,1)}, bf16[576,128]{1,0:T(8,128)(2,1)}, bf16[576,128]{1,0:T(8,128)(2,1)}) custom-call(bf16[6,12,8,192]{3,2,1,0:T(8,128)(2,1)} %bitcast.20, bf16[6,12,8,192]{3,2,1,0:T(8,128)(2,1)} %bitcast.22, f32[1,192]{1,0:T(1,128)} %bitcast.27, bf16[192,384]{1,0:T(8,128)(2,1)} %fc1_hbm.1, bf16[192,384]{1,0:T(8,128)(2,1)} %bitcast.33), custom_call_target="tpu_custom_call" | custom-call | flops 3000000000 | tf_op jit(solution)/shard_map/head/pallas_call | solution.py:145
  4.1 0.0 copy-start.1
  4.1 0.0 copy-start.2
  4.2 0.0 copy-start.3
  4.2 0.0 copy-start.10
  4.2 2.2 %collective-permute-start = (bf16[576,192]{1,0:T(8,128)(2,1)}, bf16[576,192]{1,0:T(8,128)(2,1)S(1)}, u32[]{:S(2)}, u32[]{:S(2)}) collective-permute-start(bf16[576,192]{1,0:T(8,128)(2,1)} %get-tuple-element.56.own_ref), channel_id=1, source_target_pairs={{1,0},{0,1},{3,2},{2,3},{5,4},{4,5},{7,6},{6,7},{9,8},{8,9},{11,10... | collective-permute-start | bytes 663560 | tf_op jit(solution)/shard_map/ppermute | solution.py:642
  6.4 3.0 %gather_first.1 = (f32[1536,128]{1,0:T(8,128)S(1)}, s32[168,128]{1,0:T(8,128)S(1)}, s32[168,128]{1,0:T(8,128)S(1)}, bf16[160,512]{1,0:T(8,128)(2,1)S(1)}, f32[4,...) custom-call(s32[144,144]{1,0:T(8,128)S(1)} %copy-done.5, ...), custom_call_target="tpu_custom_call" | custom-call | flops 500000000 | tf_op jit(solution)/shard_map/gather_first/pallas_call | solution.py:277
  9.5 8.7 %collective-permute-start.6 = (bf16[144,192]{1,0:T(8,128)(2,1)S(1)}, bf16[144,192]{1,0:T(8,128)(2,1)S(1)}, u32[]{:S(2)}, u32[]{:S(2)}) collective-permute-start(bf16[144,192]{1,0:T(8,128)(2,1)S(1)} %get-tuple-element.52.x0), channel_id=1, source_target_pairs={{66,0},{67,1},{68,2},{69,3},{70,4},{71,5},{72,6},{73,7},{74,8},{75... | collective-permute-start | bytes 165896 | tf_op jit(solution)/shard_map/ppermute | solution.py:642
  18.2 1.9 %collective-permute-start.5 = (bf16[144,192]{1,0:T(8,128)(2,1)S(1)}, bf16[144,192]{1,0:T(8,128)(2,1)S(1)}, u32[]{:S(2)}, u32[]{:S(2)}) collective-permute-start(bf16[144,192]{1,0:T(8,128)(2,1)S(1)} %get-tuple-element.53.x1), channel_id=1, source_target_pairs={{64,0},{65,1},{66,2},{67,3},{68,4},{69,5},{70,6},{71,7},{72,8},{73... | collective-permute-start | bytes 165896 | tf_op jit(solution)/shard_map/ppermute | solution.py:642
  20.1 0.5 collective-permute-start.4
  20.6 0.6 middle.1
  21.2 1.9 %collective-permute-start.3 = (bf16[144,192]{1,0:T(8,128)(2,1)S(1)}, bf16[144,192]{1,0:T(8,128)(2,1)S(1)}, u32[]{:S(2)}, u32[]{:S(2)}) collective-permute-start(bf16[144,192]{1,0:T(8,128)(2,1)S(1)} %get-tuple-element.58.m0), channel_id=1, source_target_pairs={{66,0},{67,1},{68,2},{69,3},{70,4},{71,5},{72,6},{73,7},{74,8},{75... | collective-permute-start | bytes 165896 | tf_op jit(solution)/shard_map/ppermute | solution.py:642
  23.1 1.6 %collective-permute-start.2 = (bf16[144,192]{1,0:T(8,128)(2,1)S(1)}, bf16[144,192]{1,0:T(8,128)(2,1)S(1)}, u32[]{:S(2)}, u32[]{:S(2)}) collective-permute-start(bf16[144,192]{1,0:T(8,128)(2,1)S(1)} %get-tuple-element.59.m1), channel_id=1, source_target_pairs={{64,0},{65,1},{66,2},{67,3},{68,4},{69,5},{70,6},{71,7},{72,8},{73... | collective-permute-start | bytes 165896 | tf_op jit(solution)/shard_map/ppermute | solution.py:642
  24.7 0.0 collective-permute-done.6.a3.x3
  24.7 2.7 %collective-permute-start.1 = (bf16[144,192]{1,0:T(8,128)(2,1)S(1)}, bf16[144,192]{1,0:T(8,128)(2,1)S(1)}, u32[]{:S(2)}, u32[]{:S(2)}) collective-permute-start(bf16[144,192]{1,0:T(8,128)(2,1)S(1)} %get-tuple-element.60.m2), channel_id=1, source_target_pairs={{2,0},{3,1},{4,2},{5,3},{6,4},{7,5},{8,6},{9,7},{10,8},{11,9},{12,... | collective-permute-start | bytes 165896 | tf_op jit(solution)/shard_map/ppermute | solution.py:642
  27.4 0.0 collective-permute-done.4.a1.x1
  27.4 0.0 copy-start.11
  27.4 0.0 copy-start.12
  27.5 2.1 %gather_second.1 = (f32[12,144,128]{2,1,0:T(8,128)S(1)}, f32[12,192,128]{2,1,0:T(8,128)S(1)}) custom-call(f32[1536,128]{1,0:T(8,128)S(1)} %get-tuple-element.62.first_stage, s32[168,128]{1,0:T(8,128)S(1)} %get-tuple-element.57.after_ref.lo_ref, s32[168,128]{1,0:T(8,128)S(1)} %get-tuple-element.63.hi_ref, bf16[160,512]{1,0:T(8,128)(2,1)S(1)} %get-tuple-element.64.terms_ref, ...), custom_call_target="tpu_custom_call" | custom-call | flops 4000000000 | tf_op jit(solution)/shard_map/gather_second/pallas_call | solution.py:305
  29.6 0.0 copy-start.7
  29.7 3.0 %forward.1 = (bf16[576,192]{1,0:T(8,128)(2,1)S(1)}, bf16[576,96]{1,0:T(8,128)(2,1)S(1)}, bf16[576,96]{1,0:T(8,128)(2,1)S(1)}, bf16[576,96]{1,0:T(8,128)(2,1)S(1)...) custom-call(bf16[144,192]{1,0:T(8,128)(2,1)S(1)} %get-tuple-element.55.x0.x3, ...), custom_call_target="tpu_custom_call" | custom-call | flops 5000000000 | tf_op jit(solution)/shard_map/forward/pallas_call | solution.py:350
  32.7 0.0 collective-permute-done.1.g1
  32.7 0.0 copy-start.14
  32.7 4.6 %backward.1 = (bf16[576,192]{1,0:T(8,128)(2,1)S(1)}, f32[12,144,128]{2,1,0:T(8,128)S(1)}, f32[12,192,128]{2,1,0:T(8,128)S(1)}, bf16[3,576,96]{2,1,0:T(8,128)(2,1)S(1)}, bf16[576,192]{1,0:T(8,128)(2,1)S(1)}) custom-call(bf16[144,192]{1,0:T(8,128)(2,1)S(1)} %get-tuple-element.61.g0.m3, bf16[144,192]{1,0:T(8,128)(2,1)S(1)} %collective-permute-done.1.g1, ...), custom_call_target="tpu_custom_call" | custom-call | flops 7000000000 | tf_op jit(solution)/shard_map/backward/pallas_call | solution.py:407
  37.3 0.5 weigh.1
  37.9 0.7 collective-permute-start.11
  38.5 0.4 collective-permute-start.7
  39.0 3.0 %scatter.1.table_ref = f32[192,256]{1,0:T(8,128)S(1)} custom-call(f32[12,144,128]{2,1,0:T(8,128)S(1)} %get-tuple-element.86.score_ref, f32[12,192,128]{2,1,0:T(8,128)S(1)} %get-tuple-element.87.end_ref, s32[168,128]{1,0:T(8,128)S(1)} %get-tuple-element.57.after_ref.lo_ref, s32[168,128]{1,0:T(8,128)S(1)} %get-tuple-element.63.hi_ref, ...), custom_call_target="tpu_custom_call" | custom-call | flops 4000000000 | tf_op jit(solution)/shard_map/scatter/pallas_call | solution.py:446
  42.0 0.0 collective-permute-done.11.other_ref
  42.0 0.8 pack.1
  42.8 4.1 %all-to-all-start = ((bf16[32,40,128]{2,1,0:T(8,128)(2,1)}), bf16[32,40,128]{2,1,0:T(8,128)(2,1)S(1)}, u32[]{:S(2)}, u32[]{:S(2)}) async-start(bf16[32,40,128]{2,1,0:T(8,128)(2,1)} %bitcast.11), calls=%async_computation | async-start | bytes 655360 | tf_op jit(solution)/shard_map/all_to_all | solution.py:700
  46.9 0.2 collective-permute-done.7.other_ref
  47.1 0.4 meet.1
  47.6 3.5 %collective-permute-start.8 = (bf16[216,128]{1,0:T(8,128)(2,1)S(1)}, bf16[216,128]{1,0:T(8,128)(2,1)S(1)}, u32[]{:S(2)}, u32[]{:S(2)}) collective-permute-start(bf16[216,128]{1,0:T(8,128)(2,1)S(1)} %get-tuple-element.74), channel_id=1, source_target_pairs={{254,0},{255,1},{192,2},{193,3},{194,4},{195,5},{196,6},{197,7},{1... | collective-permute-start | bytes 165896 | tf_op jit(solution)/shard_map/ppermute | solution.py:642
  51.0 0.0 collective-permute-start.9
  51.0 1.2 %collective-permute-start.10 = (bf16[216,128]{1,0:T(8,128)(2,1)S(1)}, bf16[216,128]{1,0:T(8,128)(2,1)S(1)}, u32[]{:S(2)}, u32[]{:S(2)}) collective-permute-start(bf16[216,128]{1,0:T(8,128)(2,1)S(1)} %get-tuple-element.76), channel_id=1, source_target_pairs={{62,0},{63,1},{0,2},{1,3},{2,4},{3,5},{4,6},{5,7},{6,8},{7,9},{8,1... | collective-permute-start | bytes 165896 | tf_op jit(solution)/shard_map/ppermute | solution.py:642
  52.2 9.0 %collective-permute-done.8.g0.b0 = bf16[216,128]{1,0:T(8,128)(2,1)S(1)} collective-permute-done((bf16[216,128]{1,0:T(8,128)(2,1)S(1)}, bf16[216,128]{1,0:T(8,128)(2,1)S(1)}, u32[]{:S(2)}, u32[]{:S(2)}) %collective-permute-start.8) | collective-permute-done | bytes 55328 | tf_op jit(solution)/shard_map/ppermute | solution.py:642
  61.2 0.0 collective-permute-done.9.g1.b1
  61.2 0.0 collective-permute-done.10.g2.b2
  61.2 0.0 all-to-all-done.got_ref
  61.2 0.1 add.1.own_ref
  61.3 2.2 %collective-permute-start.12 = (bf16[48,128]{1,0:T(8,128)(2,1)S(1)}, bf16[48,128]{1,0:T(8,128)(2,1)S(1)}, u32[]{:S(2)}, u32[]{:S(2)}) collective-permute-start(bf16[48,128]{1,0:T(8,128)(2,1)S(1)} %add.1.own_ref), channel_id=1, source_target_pairs={{128,0},{129,1},{130,2},{131,3},{132,4},{133,5},{134,6},{135,7},{1... | collective-permute-start | bytes 36872 | tf_op jit(solution)/shard_map/ppermute | solution.py:642
  63.5 1.9 %collective-permute-done.12.other_ref = bf16[48,128]{1,0:T(8,128)(2,1)S(1)} collective-permute-done((bf16[48,128]{1,0:T(8,128)(2,1)S(1)}, bf16[48,128]{1,0:T(8,128)(2,1)S(1)}, u32[]{:S(2)}, u32[]{:S(2)}) %collective-permute-start.12) | collective-permute-done | bytes 12320 | tf_op jit(solution)/shard_map/ppermute | solution.py:642
  65.5 16.7 %all_to_all.10.own_ref = bf16[32,48,128]{2,1,0:T(8,128)(2,1)S(1)} all-to-all(bf16[32,48,128]{2,1,0:T(8,128)(2,1)S(1)} %spread.1), channel_id=1, replica_groups=mesh['lat'=4,'lon'=32,'tp'=2] {'lon'}, dimensions={0} | all-to-all | bytes 786432 | tf_op jit(solution)/shard_map/all_to_all | solution.py:703
  82.2 4.4 %collective-permute-start.13 = (bf16[32,48,128]{2,1,0:T(8,128)(2,1)S(1)}, bf16[32,48,128]{2,1,0:T(8,128)(2,1)S(1)}, u32[]{:S(2)}, u32[]{:S(2)}) collective-permute-start(bf16[32,48,128]{2,1,0:T(8,128)(2,1)S(1)} %all_to_all.10.own_ref), channel_id=1, source_target_pairs={{0,64},{64,0},{128,192},{192,128},{1,65},{65,1},{129,193},{193,129... | collective-permute-start | bytes 1179656 | tf_op jit(solution)/shard_map/ppermute | solution.py:655
  86.6 1.5 %finish.1 = bf16[6,12,8,192]{3,2,1,0:T(8,128)(2,1)} custom-call(bf16[144,192]{1,0:T(8,128)(2,1)S(1)} %get-tuple-element.52.x0, bf16[144,192]{1,0:T(8,128)(2,1)S(1)} %get-tuple-element.53.x1, bf16[144,192]{1,0:T(8,128)(2,1)S(1)} %get-tuple-element.54.x2, bf16[144,192]{1,0:T(8,128)(2,1)S(1)} %get-tuple-element.55.x0.x3, ...), custom_call_target="tpu_custom_call" | custom-call | flops 1000000000 | tf_op jit(solution)/shard_map/finish/pallas_call | solution.py:536
  88.1 1.2 %unpack.1 = (f32[3,192,96]{2,1,0:T(8,128)}, f32[96,192]{1,0:T(8,128)}, f32[192,384]{1,0:T(8,128)}, f32[192,384]{1,0:T(8,128)}, f32[1,96]{1,0:T(1,128)}, /*index=5*/f32[1,96]{1,0:T(1,128)}, f32[3,4,3312]{2,1,0:T(4,128)}) custom-call(bf16[32,48,128]{2,1,0:T(8,128)(2,1)S(1)} %all_to_all.10.own_ref, bf16[32,48,128]{2,1,0:T(8,128)(2,1)S(1)} %collective-permute-done.13.other_ref), custom_call_target="tpu_custom_call" | custom-call | tf_op jit(solution)/shard_map/unpack/pallas_call | solution.py:618
  (29 shorter events, 0.1 us)
Async XLA Ops:
  0.6 5.8 %copy-start = (bf16[8,6,12,192]{3,0,2,1:T(8,128)(2,1)S(1)}, bf16[8,6,12,192]{3,0,2,1:T(8,128)(2,1)}, u32[]{:S(2)}) copy-start(bf16[8,6,12,192]{3,0,2,1:T(8,128)(2,1)} %param.16) | copy-start | bytes 663556
  0.6 5.8 %copy-start.4 = (f32[1,4,3,3312]{3,1,2,0:T(4,128)S(1)}, f32[1,4,3,3312]{3,1,2,0:T(4,128)}, u32[]{:S(2)}) copy-start(f32[1,4,3,3312]{3,1,2,0:T(4,128)} %param.22) | copy-start | bytes 476932
  0.7 5.8 %copy-start.5 = (s32[144,144]{1,0:T(8,128)S(1)}, s32[144,144]{1,0:T(8,128)}, u32[]{:S(2)}) copy-start(s32[144,144]{1,0:T(8,128)} %index_ref.1) | copy-start | bytes 248836
  0.7 5.7 %copy-start.8 = (s32[8,6,12]{2,0,1:T(8,128)S(1)}, s32[8,6,12]{2,0,1:T(8,128)}, u32[]{:S(2)}) copy-start(s32[8,6,12]{2,0,1:T(8,128)} %param.19) | copy-start | bytes 6916
  0.7 5.7 %copy-start.9 = (s32[8,6,12]{2,0,1:T(8,128)S(1)}, s32[8,6,12]{2,0,1:T(8,128)}, u32[]{:S(2)}) copy-start(s32[8,6,12]{2,0,1:T(8,128)} %param.20) | copy-start | bytes 6916
  0.7 5.7 %copy-start.13 = (bf16[144,144]{1,0:T(8,128)(2,1)S(1)}, bf16[144,144]{1,0:T(8,128)(2,1)}, u32[]{:S(2)}) copy-start(bf16[144,144]{1,0:T(8,128)(2,1)} %constant.4.clone.order_ref) | copy-start | bytes 124420
  4.1 16.5 %copy-start.1 = (bf16[8,6,12,192]{3,0,2,1:T(8,128)(2,1)S(1)}, bf16[8,6,12,192]{3,0,2,1:T(8,128)(2,1)}, u32[]{:S(2)}) copy-start(bf16[8,6,12,192]{3,0,2,1:T(8,128)(2,1)} %param.17) | copy-start | bytes 663556
  4.1 16.5 %copy-start.2 = (bf16[8,6,12,192]{3,0,2,1:T(8,128)(2,1)S(1)}, bf16[8,6,12,192]{3,0,2,1:T(8,128)(2,1)}, u32[]{:S(2)}) copy-start(bf16[8,6,12,192]{3,0,2,1:T(8,128)(2,1)} %param.18) | copy-start | bytes 663556
  4.2 16.5 %copy-start.3 = (bf16[576,192]{1,0:T(8,128)(2,1)S(1)}, bf16[576,192]{1,0:T(8,128)(2,1)}, u32[]{:S(2)}) copy-start(bf16[576,192]{1,0:T(8,128)(2,1)} %get-tuple-element.56.own_ref) | copy-start | bytes 663556
  4.2 16.5 %copy-start.10 = (f32[192]{0:T(256)S(1)}, f32[192]{0:T(256)}, u32[]{:S(2)}) copy-start(f32[192]{0:T(256)} %param.26) | copy-start | bytes 2308
  4.2 16.4 %collective-permute-start = (bf16[576,192]{1,0:T(8,128)(2,1)}, bf16[576,192]{1,0:T(8,128)(2,1)S(1)}, u32[]{:S(2)}, u32[]{:S(2)}) collective-permute-start(bf16[576,192]{1,0:T(8,128)(2,1)} %get-tuple-element.56.own_ref), channel_id=1, source_target_pairs={{1,0},{0,1},{3,2},{2,3},{5,4},{4,5},{7,6},{6,7},{9,8},{8,9},{11,10... | collective-permute-start | bytes 663560 | tf_op jit(solution)/shard_map/ppermute | solution.py:642
  9.5 15.2 %collective-permute-start.6 = (bf16[144,192]{1,0:T(8,128)(2,1)S(1)}, bf16[144,192]{1,0:T(8,128)(2,1)S(1)}, u32[]{:S(2)}, u32[]{:S(2)}) collective-permute-start(bf16[144,192]{1,0:T(8,128)(2,1)S(1)} %get-tuple-element.52.x0), channel_id=1, source_target_pairs={{66,0},{67,1},{68,2},{69,3},{70,4},{71,5},{72,6},{73,7},{74,8},{75... | collective-permute-start | bytes 165896 | tf_op jit(solution)/shard_map/ppermute | solution.py:642
  18.2 9.2 %collective-permute-start.5 = (bf16[144,192]{1,0:T(8,128)(2,1)S(1)}, bf16[144,192]{1,0:T(8,128)(2,1)S(1)}, u32[]{:S(2)}, u32[]{:S(2)}) collective-permute-start(bf16[144,192]{1,0:T(8,128)(2,1)S(1)} %get-tuple-element.53.x1), channel_id=1, source_target_pairs={{64,0},{65,1},{66,2},{67,3},{68,4},{69,5},{70,6},{71,7},{72,8},{73... | collective-permute-start | bytes 165896 | tf_op jit(solution)/shard_map/ppermute | solution.py:642
  20.1 7.4 %collective-permute-start.4 = (bf16[144,192]{1,0:T(8,128)(2,1)S(1)}, bf16[144,192]{1,0:T(8,128)(2,1)S(1)}, u32[]{:S(2)}, u32[]{:S(2)}) collective-permute-start(bf16[144,192]{1,0:T(8,128)(2,1)S(1)} %get-tuple-element.54.x2), channel_id=1, source_target_pairs={{2,0},{3,1},{4,2},{5,3},{6,4},{7,5},{8,6},{9,7},{10,8},{11,9},{12,... | collective-permute-start | bytes 165896 | tf_op jit(solution)/shard_map/ppermute | solution.py:642
  21.2 11.4 %collective-permute-start.3 = (bf16[144,192]{1,0:T(8,128)(2,1)S(1)}, bf16[144,192]{1,0:T(8,128)(2,1)S(1)}, u32[]{:S(2)}, u32[]{:S(2)}) collective-permute-start(bf16[144,192]{1,0:T(8,128)(2,1)S(1)} %get-tuple-element.58.m0), channel_id=1, source_target_pairs={{66,0},{67,1},{68,2},{69,3},{70,4},{71,5},{72,6},{73,7},{74,8},{75... | collective-permute-start | bytes 165896 | tf_op jit(solution)/shard_map/ppermute | solution.py:642
  23.1 9.6 %collective-permute-start.2 = (bf16[144,192]{1,0:T(8,128)(2,1)S(1)}, bf16[144,192]{1,0:T(8,128)(2,1)S(1)}, u32[]{:S(2)}, u32[]{:S(2)}) collective-permute-start(bf16[144,192]{1,0:T(8,128)(2,1)S(1)} %get-tuple-element.59.m1), channel_id=1, source_target_pairs={{64,0},{65,1},{66,2},{67,3},{68,4},{69,5},{70,6},{71,7},{72,8},{73... | collective-permute-start | bytes 165896 | tf_op jit(solution)/shard_map/ppermute | solution.py:642
  24.7 8.0 %collective-permute-start.1 = (bf16[144,192]{1,0:T(8,128)(2,1)S(1)}, bf16[144,192]{1,0:T(8,128)(2,1)S(1)}, u32[]{:S(2)}, u32[]{:S(2)}) collective-permute-start(bf16[144,192]{1,0:T(8,128)(2,1)S(1)} %get-tuple-element.60.m2), channel_id=1, source_target_pairs={{2,0},{3,1},{4,2},{5,3},{6,4},{7,5},{8,6},{9,7},{10,8},{11,9},{12,... | collective-permute-start | bytes 165896 | tf_op jit(solution)/shard_map/ppermute | solution.py:642
  27.4 2.2 %copy-start.6 = (bf16[3,192,96]{2,1,0:T(8,128)(2,1)S(1)}, bf16[3,192,96]{2,1,0:T(8,128)(2,1)}, u32[]{:S(2)}) copy-start(bf16[3,192,96]{2,1,0:T(8,128)(2,1)} %qkv_ref.3) | copy-start | bytes 331780
  27.4 2.2 %copy-start.11 = (f32[192]{0:T(256)S(1)}, f32[192]{0:T(256)}, u32[]{:S(2)}) copy-start(f32[192]{0:T(256)} %param.23) | copy-start | bytes 2308
  27.4 2.2 %copy-start.12 = (bf16[144,144]{1,0:T(8,128)(2,1)S(1)}, bf16[144,144]{1,0:T(8,128)(2,1)}, u32[]{:S(2)}) copy-start(bf16[144,144]{1,0:T(8,128)(2,1)} %constant.5.clone.order_ref) | copy-start | bytes 124420
  29.6 3.0 %copy-start.7 = (bf16[96,192]{1,0:T(8,128)(2,1)S(1)}, bf16[96,192]{1,0:T(8,128)(2,1)}, u32[]{:S(2)}) copy-start(bf16[96,192]{1,0:T(8,128)(2,1)} %proj_ref.1) | copy-start | bytes 110596
  32.7 4.6 %copy-start.14 = (bf16[576,128]{1,0:T(8,128)(2,1)S(1)}, bf16[576,128]{1,0:T(8,128)(2,1)}, u32[]{:S(2)}) copy-start(bf16[576,128]{1,0:T(8,128)(2,1)} %get-tuple-element.83.first_ref) | copy-start | bytes 442372
  37.9 4.1 %collective-permute-start.11 = (bf16[864,128]{1,0:T(8,128)(2,1)S(1)}, bf16[864,128]{1,0:T(8,128)(2,1)S(1)}, u32[]{:S(2)}, u32[]{:S(2)}) collective-permute-start(bf16[864,128]{1,0:T(8,128)(2,1)S(1)} %get-tuple-element.85), channel_id=1, source_target_pairs={{0,64},{64,0},{128,192},{192,128},{1,65},{65,1},{129,193},{193,129... | collective-permute-start | bytes 663560 | tf_op jit(solution)/shard_map/ppermute | solution.py:655
  38.5 8.6 %collective-permute-start.7 = (bf16[576,192]{1,0:T(8,128)(2,1)S(1)}, bf16[576,192]{1,0:T(8,128)(2,1)S(1)}, u32[]{:S(2)}, u32[]{:S(2)}) collective-permute-start(bf16[576,192]{1,0:T(8,128)(2,1)S(1)} %get-tuple-element.73.own_ref), channel_id=1, source_target_pairs={{1,0},{0,1},{3,2},{2,3},{5,4},{4,5},{7,6},{6,7},{9,8},{8,9},{11,10... | collective-permute-start | bytes 663560 | tf_op jit(solution)/shard_map/ppermute | solution.py:642
  39.0 3.0 %copy-start.15 = (bf16[576,128]{1,0:T(8,128)(2,1)S(1)}, bf16[576,128]{1,0:T(8,128)(2,1)}, u32[]{:S(2)}) copy-start(bf16[576,128]{1,0:T(8,128)(2,1)} %get-tuple-element.78.first_ref) | copy-start | bytes 442372
  42.8 18.4 %all-to-all-start = ((bf16[32,40,128]{2,1,0:T(8,128)(2,1)}), bf16[32,40,128]{2,1,0:T(8,128)(2,1)S(1)}, u32[]{:S(2)}, u32[]{:S(2)}) async-start(bf16[32,40,128]{2,1,0:T(8,128)(2,1)} %bitcast.11), calls=%async_computation | async-start | bytes 655360 | tf_op jit(solution)/shard_map/all_to_all | solution.py:700
  47.6 13.7 %collective-permute-start.8 = (bf16[216,128]{1,0:T(8,128)(2,1)S(1)}, bf16[216,128]{1,0:T(8,128)(2,1)S(1)}, u32[]{:S(2)}, u32[]{:S(2)}) collective-permute-start(bf16[216,128]{1,0:T(8,128)(2,1)S(1)} %get-tuple-element.74), channel_id=1, source_target_pairs={{254,0},{255,1},{192,2},{193,3},{194,4},{195,5},{196,6},{197,7},{1... | collective-permute-start | bytes 165896 | tf_op jit(solution)/shard_map/ppermute | solution.py:642
  51.0 10.2 %collective-permute-start.9 = (bf16[216,128]{1,0:T(8,128)(2,1)S(1)}, bf16[216,128]{1,0:T(8,128)(2,1)S(1)}, u32[]{:S(2)}, u32[]{:S(2)}) collective-permute-start(bf16[216,128]{1,0:T(8,128)(2,1)S(1)} %get-tuple-element.75), channel_id=1, source_target_pairs={{192,0},{193,1},{194,2},{195,3},{196,4},{197,5},{198,6},{199,7},{2... | collective-permute-start | bytes 165896 | tf_op jit(solution)/shard_map/ppermute | solution.py:642
  51.0 10.2 %collective-permute-start.10 = (bf16[216,128]{1,0:T(8,128)(2,1)S(1)}, bf16[216,128]{1,0:T(8,128)(2,1)S(1)}, u32[]{:S(2)}, u32[]{:S(2)}) collective-permute-start(bf16[216,128]{1,0:T(8,128)(2,1)S(1)} %get-tuple-element.76), channel_id=1, source_target_pairs={{62,0},{63,1},{0,2},{1,3},{2,4},{3,5},{4,6},{5,7},{6,8},{7,9},{8,1... | collective-permute-start | bytes 165896 | tf_op jit(solution)/shard_map/ppermute | solution.py:642
  61.3 4.1 %collective-permute-start.12 = (bf16[48,128]{1,0:T(8,128)(2,1)S(1)}, bf16[48,128]{1,0:T(8,128)(2,1)S(1)}, u32[]{:S(2)}, u32[]{:S(2)}) collective-permute-start(bf16[48,128]{1,0:T(8,128)(2,1)S(1)} %add.1.own_ref), channel_id=1, source_target_pairs={{128,0},{129,1},{130,2},{131,3},{132,4},{133,5},{134,6},{135,7},{1... | collective-permute-start | bytes 36872 | tf_op jit(solution)/shard_map/ppermute | solution.py:642
  82.2 5.9 %collective-permute-start.13 = (bf16[32,48,128]{2,1,0:T(8,128)(2,1)S(1)}, bf16[32,48,128]{2,1,0:T(8,128)(2,1)S(1)}, u32[]{:S(2)}, u32[]{:S(2)}) collective-permute-start(bf16[32,48,128]{2,1,0:T(8,128)(2,1)S(1)} %all_to_all.10.own_ref), channel_id=1, source_target_pairs={{0,64},{64,0},{128,192},{192,128},{1,65},{65,1},{129,193},{193,129... | collective-permute-start | bytes 1179656 | tf_op jit(solution)/shard_map/ppermute | solution.py:655
